TPU v7x, 32 devices: a whole 2x2x4 slice. The times are simulated.
32 devices in a mesh: seq: 8 (over z, core), head: 4 (over y, x).
Axes of the slice: x: 2, y: 2, z: 4, core: 2. Of those that a mesh axis runs over, the one named last changes fastest.
Arguments:
- tokens: bfloat16 [8192, 4096], P('seq', 'head'), may hold values from -6 to 6
- w_qkv: bfloat16 [3, 4096, 4096], P(None, None, 'head'), may hold values from -0.09375 to 0.09375
- w_out: bfloat16 [4096, 4096], P('head'), may hold values from -0.125 to 0.125
- decay_rate: float32 [32, 8192], P('head', 'seq'), may hold values from 0 to 1, as said below
- prior_state: float32 [32, 128, 128], P('head'), may hold values from -256 to 256
Outputs:
- mixed: bfloat16 [8192, 4096], P('seq', 'head')
Inputs may be any that keep to these rules, and one draw needn't show every extreme that they name: `decay_rate`: rates of each head for each position; every rate is positive.
All inputs are finite; a program needn't handle non-finite values.
Results may differ from a plain program's by a relative error of at most 0.02.
Values may be sent and summed in bfloat16 or wider, within the bound.
No kernel may reach another device: no remote copies, remote signals or barrier semaphores. Data moves between devices by JAX's collectives and lax.ppermute only.
A program may use at most 128 MiB of HBM per device.

v0:
```python
import jax
import jax.numpy as jnp
from jax import lax
from jax.sharding import PartitionSpec as P


def prefix(x, axis, join, neutral):
    place = lax.axis_index(axis)
    gathered = jax.tree.map(
        lambda a, kind: lax.all_gather(a.astype(kind), axis), x, (jnp.bfloat16, jnp.bfloat16)
    )
    state = jax.tree.map(lambda a, e: jnp.zeros_like(a) + jnp.asarray(e, a.dtype), x, neutral)

    def one(turn, state):
        return join(
            state,
            jax.tree.map(
                lambda a, own: lax.dynamic_index_in_dim(a, turn, 0, False).astype(own.dtype),
                gathered,
                x,
            ),
        )

    return lax.fori_loop(0, place, one, state)


def local(tokens, w_qkv, w_out, decay_rate, prior_state):
    tok_rows = tokens.shape[0]
    head_count = decay_rate.shape[0]
    head_size = prior_state.shape[1]
    projected = jnp.einsum(
        "tr,cre->cte",
        lax.all_gather(tokens, "head", axis=1, tiled=True),
        w_qkv,
        preferred_element_type=jnp.float32,
    ).astype(jnp.bfloat16)
    queries = projected[0].reshape(tok_rows, head_count, head_size)
    keys_local = projected[1].reshape(tok_rows, head_count, head_size)
    values_local = projected[2].reshape(tok_rows, head_count, head_size)
    cumulative = jnp.cumsum(decay_rate, axis=1)
    tail_sum = cumulative[:, -1:]
    key_scale = jnp.exp(cumulative - tail_sum).T[:, :, None]
    scaled_keys = (keys_local.astype(jnp.float32) * key_scale).astype(jnp.bfloat16)
    end_state = jnp.einsum(
        "thd,the->hde", scaled_keys, values_local, preferred_element_type=jnp.float32
    )
    end_decay = jnp.exp(-tail_sum[:, 0])
    scores = jnp.einsum("thd,uhd->htu", queries, keys_local, preferred_element_type=jnp.float32)
    decay_gap = cumulative[:, :, None] - cumulative[:, None, :]
    causal = lax.broadcasted_iota(jnp.int32, (tok_rows, tok_rows), 0) >= lax.broadcasted_iota(
        jnp.int32, (tok_rows, tok_rows), 1
    )
    weights = jnp.where(causal[None], scores * jnp.exp(-jnp.maximum(decay_gap, 0.0)), 0.0).astype(
        jnp.bfloat16
    )
    within = jnp.einsum("htu,uhd->thd", weights, values_local, preferred_element_type=jnp.float32)
    identity = (jnp.ones_like(end_decay), jnp.zeros_like(end_state))

    def combine(earlier, later):
        return (earlier[0] * later[0], later[0][:, None, None] * earlier[1] + later[1])

    decay_before, state_before = prefix((end_decay, end_state), "seq", combine, identity)
    entering = state_before + decay_before[:, None, None] * prior_state
    from_state = jnp.einsum(
        "thd,hde->the", queries, entering.astype(jnp.bfloat16), preferred_element_type=jnp.float32
    )
    from_state = from_state * jnp.exp(-cumulative).T[:, :, None]
    combined = within + from_state
    normed = combined * lax.rsqrt(jnp.mean(combined * combined, axis=2, keepdims=True) + 1e-06)
    normed = normed.astype(jnp.bfloat16).reshape(tok_rows, head_count * head_size)
    partial_value = jnp.dot(normed, w_out, preferred_element_type=jnp.float32)
    return lax.psum_scatter(
        partial_value.astype(jnp.bfloat16), "head", scatter_dimension=1, tiled=True
    )


def solution(mesh):
    in_specs = (
        P("seq", "head"),
        P(None, None, "head"),
        P("head", None),
        P("head", "seq"),
        P("head", None, None),
    )
    out_specs = P("seq", "head")
    return jax.shard_map(local, mesh=mesh, in_specs=in_specs, out_specs=out_specs, check_vma=False)
```

profile of v0, /device:TPU:8, one launch (start us, length us, event | category | flops | bytes accessed | tf_op | source)
XLA Modules:
  0.0 301.8 jit_solution(14494729811705583887)
XLA Ops:
  6.5 0.7 all-gather.5.cloned.1.call-update
  7.3 0.0 all-gather.7.cloned.1.call-start
  7.3 0.8 copy.21
  8.1 2.3 reduce-window.6
  10.3 0.2 slice_reduce_fusion
  10.5 0.2 reduce-window.9
  10.6 0.1 add_bitcast_fusion
  10.7 0.1 slice.28
  10.8 0.1 copy.32
  10.9 0.1 exponential_bitcast_fusion
  11.0 87.1 %all-gather.5.cloned.1.call-done = bf16[1024,4096]{1,0:T(8,128)(2,1)} async-done(((bf16[1024,1024]{1,0:T(8,128)(2,1)}), bf16[1024,4096]{1,0:T(8,128)(2,1)}) %all-gather.5.cloned.1.call-update) | async-done | bytes 8388624 | tf_op jit(solution)/shard_map/all_gather | solution.py:33
  98.1 32.0 %convert_bitcast_fusion = bf16[3,1024,1024]{1,2,0:T(8,128)(2,1)S(1)} fusion(bf16[3,4096,1024]{2,1,0:T(8,128)(2,1)} %param.8, bf16[1024,4096]{1,0:T(8,128)(2,1)} %all-gather.5.cloned.1.call-done), kind=kOutput, calls=%fused_computation.8 | convolution fusion | flops 25772949504 | bytes 39845888 | tf_op jit(solution)/shard_map/tr,cre->cte/dot_general | solution.py:31
  130.1 0.7 fusion.16
  130.9 1.3 copy-done
  132.2 0.7 copy-done.1
  132.9 1.5 fusion.11
  134.3 0.0 all-gather.7.cloned.1.call-update
  134.3 0.0 reduce-scatter.2.cloned.1.call-start
  134.4 0.6 dynamic-slice
  135.6 0.2 dynamic-update-slice
  135.8 13.1 %all-reduce = bf16[64]{0:T(256)(128)(2,1)S(1)} all-reduce(bf16[64]{0:T(256)(128)(2,1)S(1)} %dynamic-update-slice), channel_id=2, replica_groups=mesh['seq'=8,'head'=4] {'seq'}, use_global_device_ids=true, to_apply=%add | all-reduce | flops 64 | bytes 256
  148.9 0.1 reshape.88
  149.0 1.3 iota_compare_fusion
  150.3 13.4 %all-gather.7.cloned.1.call-done = bf16[64,128,128]{2,1,0:T(8,128)(2,1)} async-done(((bf16[8,128,128]{2,1,0:T(8,128)(2,1)}), bf16[64,128,128]{2,1,0:T(8,128)(2,1)}) %all-gather.7.cloned.1.call-update) | async-done | bytes 2097168 | tf_op jit(solution)/shard_map/all_gather | solution.py:10
  163.8 2.5 while.12
  163.8 1.1 convert_add_fusion.2
  165.0 1.1 convert_add_fusion.2
  166.3 2.8 fusion.12
  169.0 17.2 %multiply_reduce_fusion = (f32[1024,8]{0,1:T(8,128)S(1)}, f32[1024,8,128]{0,2,1:T(8,128)}) fusion(f32[1024,8]{0,1:T(8,128)S(1)} %get-tuple-element.58, f32[8,128,1024]{2,1,0:T(8,128)} %fusion.12, bf16[1024,8,128]{0,2,1:T(8,128)(2,1)} %bitcast.60, f32[8,1024]{1,0:T(8,128)S(1)} %bitcast.63, pred[1024,1024]{1,0:T(8,128)(4,1)} %iota_compare_fusion, ...), kind=kOutput, calls=%fused_computation.13 | convolution fusion | flops 4349485056 | bytes 15826944 | tf_op jit(solution)/shard_map/htu,uhd->thd/dot_general | solution.py:56
  186.2 2.8 multiply_convert_fusion
  189.0 14.6 %convolution_convert_fusion = bf16[1024,4096]{1,0:T(8,128)(2,1)} fusion(bf16[1024,1024]{0,1:T(8,128)(2,1)S(1)} %bitcast.56, bf16[1024,4096]{1,0:T(8,128)(2,1)} %param.9), kind=kOutput, calls=%fused_computation.7 | convolution fusion | flops 8594128896 | bytes 18874368 | tf_op jit(solution)/shard_map/dot_general | solution.py:71
  203.6 91.6 %reduce-scatter.2.cloned.1.call-done = bf16[1024,1024]{1,0:T(8,128)(2,1)} async-done(((bf16[1024,4096]{1,0:T(8,128)(2,1)}), bf16[1024,1024]{1,0:T(8,128)(2,1)}) %reduce-scatter.2.cloned.1.call-update) | async-done | bytes 2097168 | tf_op jit(solution)/shard_map/reduce_scatter | solution.py:72
  (16 shorter events, 0.1 us)
Async XLA Ops:
  6.5 91.5 %all-gather.5.cloned.1.call-start = ((), (), s32[]{:S(2)}) async-start(), calls=%async_computation.1 | async-start | bytes 10485760 | tf_op jit(solution)/shard_map/all_gather | solution.py:33
  7.3 156.5 %all-gather.7.cloned.1.call-start = ((), (), s32[]{:S(2)}) async-start(), calls=%async_computation.3 | async-start | bytes 2359296 | tf_op jit(solution)/shard_map/all_gather | solution.py:10
  130.8 1.3 copy-start
  130.9 2.0 copy-start.1
  130.9 3.5 %copy-start.3 = (u32[32]{0:T(128)S(1)}, u32[32]{0:T(128)}, u32[]{:S(2)}) copy-start(u32[32]{0:T(128)} %constant.36) | copy-start | bytes 388
  134.3 160.9 %reduce-scatter.2.cloned.1.call-start = ((), (), s32[]{:S(2)}) async-start(), calls=%async_computation.2 | async-start | bytes 10485760 | tf_op jit(solution)/shard_map/reduce_scatter | solution.py:72
  135.6 30.7 %copy-start.2 = (f32[8,128,128]{2,1,0:T(8,128)S(1)}, f32[8,128,128]{2,1,0:T(8,128)}, u32[]{:S(2)}) copy-start(f32[8,128,128]{2,1,0:T(8,128)} %param.11) | copy-start | bytes 1572868
Sparse Core Ops, SparseCore 0:
  9.2 88.8 all-gather.4
  134.5 29.2 all-gather.6
  203.7 91.4 reduce-scatter.1
where the time goes:
time: 304 us; the launch traced here: 302 us
  waiting for transfers between devices  193 us (63%)
  matrix products  68 us (22%)
  between operations  13.8 us (5%)
  blocking collectives  13.1 us (4%)
  other arithmetic  8.95 us (3%)
  local copies, waits for them, and re-layouts  4.75 us (2%)
    reduce_scatter x1, waiting for transfers between devices, local(): lax.psum_scatter(partial_value.astype(jnp.bfloat16), 'head', scatter_dime...  91.6 us
    all_gather x1, waiting for transfers between devices, local(): lax.all_gather(tokens, 'head', axis=1, tiled=True)  87.1 us
    dot_general x1, matrix products, local(): jnp.einsum('tr,cre->cte', lax.all_gather(tokens, 'head', axis=1, tiled=Tr...  32 us
    dot_general x1, matrix products, local(): jnp.einsum('htu,uhd->thd', weights, values_local, preferred_element_type=...  17.2 us
    dot_general x1, matrix products, local(): partial_value = jnp.dot(normed, w_out, preferred_element_type=jnp.float32)  14.6 us
    all_gather x1, waiting for transfers between devices, prefix(): lax.all_gather(a.astype(kind), axis)  13.4 us
    unnamed x1, blocking collectives  13.1 us
  transfers between devices with their start and end apart: 3, of which 3 were waited for; matrix products, arithmetic and copies ran while one was open for 2% of the time, Pallas kernels for 0%

commit v1 on v0

v1 whole, which is shorter than its diff:
```python
import functools

import jax
import jax.numpy as jnp
from jax import lax
from jax.experimental import pallas as pl
from jax.experimental.pallas import tpu as pltpu
from jax.sharding import PartitionSpec as P

BF16, F32 = jnp.bfloat16, jnp.float32
VMEM_LIMIT = 40 * 1024 * 1024


def dot(a, b, contract=((1,), (0,))):
    return lax.dot_general(a, b, (contract, ((), ())), preferred_element_type=F32)


def rows_of(refs):
    if len(refs) == 1:
        return refs[0][...]
    return jnp.concatenate([ref[...] for ref in refs], axis=0)


def chunk_kernel(layout, offs, *refs):
    count = sum(layout)
    piece_refs, refs = refs[:count], refs[count:]
    w_ref, row_ref, col_ref, state_ref, q_ref, within_ref, state_out_ref = refs
    pieces, at = [], 0
    for parts in layout:
        pieces.append(piece_refs[at : at + parts])
        at += parts
    width = piece_refs[0].shape[1]
    rows = q_ref.shape[0]
    heads, size = state_ref.shape[0], state_ref.shape[1]

    def project(c):
        total = None
        for i, piece in enumerate(pieces):
            start = pl.multiple_of(offs[i], width)
            term = dot(rows_of(piece), w_ref[c, pl.ds(start, width), :])
            total = term if total is None else total + term
        return total.astype(BF16)

    q_all, k_all, v_all = project(0), project(1), project(2)
    q_ref[...] = q_all
    causal = lax.broadcasted_iota(jnp.int32, (rows, rows), 0) >= lax.broadcasted_iota(
        jnp.int32, (rows, rows), 1
    )
    for a in range(heads):
        lanes = slice(a * size, (a + 1) * size)
        q, k, v = q_all[:, lanes], k_all[:, lanes], v_all[:, lanes]
        along, down = row_ref[0, a : a + 1, :], col_ref[0, :, a : a + 1]
        decay = jnp.exp(jnp.minimum(along - down, 0.0))
        weights = jnp.where(causal, dot(q, k, ((1,), (1,))) * decay, 0.0).astype(BF16)
        state = state_ref[a]
        within = dot(weights, v) + dot(q, state.astype(BF16)) * jnp.exp(-down)
        within_ref[:, lanes] = within
        last = down[rows - 1 :, :]
        scaled = (k.astype(F32) * jnp.exp(down - last)).astype(BF16)
        state_out_ref[a] = jnp.exp(-last) * state + dot(scaled, v, ((0,), (0,)))


def chunk_call(offs, pieces, w_qkv, along, down, state):
    rows = pieces[0][0].shape[0] if len(pieces[0]) == 1 else sum(p.shape[0] for p in pieces[0])
    heads, size = state.shape[0], state.shape[1]
    group = along.shape[1]
    steps = heads // group
    cols = group * size
    flat = [p for piece in pieces for p in piece]
    depth = w_qkv.shape[1]
    whole = [pl.BlockSpec(p.shape, lambda j, o: (0, 0)) for p in flat]
    flops = 2 * rows * depth * 3 * heads * size + 4 * heads * rows * size * (rows + size)
    return pl.pallas_call(
        functools.partial(chunk_kernel, tuple(len(p) for p in pieces)),
        out_shape=(
            jax.ShapeDtypeStruct((rows, heads * size), BF16),
            jax.ShapeDtypeStruct((rows, heads * size), F32),
            jax.ShapeDtypeStruct(state.shape, F32),
        ),
        grid_spec=pltpu.PrefetchScalarGridSpec(
            num_scalar_prefetch=1,
            grid=(steps,),
            in_specs=whole
            + [
                pl.BlockSpec((3, depth, cols), lambda j, o: (0, 0, j)),
                pl.BlockSpec((1, group, rows), lambda j, o: (j, 0, 0)),
                pl.BlockSpec((1, rows, group), lambda j, o: (j, 0, 0)),
                pl.BlockSpec((group, size, size), lambda j, o: (j, 0, 0)),
            ],
            out_specs=[
                pl.BlockSpec((rows, cols), lambda j, o: (0, j)),
                pl.BlockSpec((rows, cols), lambda j, o: (0, j)),
                pl.BlockSpec((group, size, size), lambda j, o: (j, 0, 0)),
            ],
        ),
        compiler_params=pltpu.CompilerParams(vmem_limit_bytes=VMEM_LIMIT),
        cost_estimate=pl.CostEstimate(
            flops=flops, bytes_accessed=w_qkv.size * 2 + rows * depth * 2, transcendentals=0
        ),
        name="chunk",
    )(offs, *flat, w_qkv, along, down, state)


def head_kernel(block, q_ref, within_ref, entering_ref, down_ref, w_ref, normed_ref, out_ref):
    heads, size = entering_ref.shape[0], entering_ref.shape[1]
    fade = jnp.exp(-down_ref[...])
    for a in range(heads):
        lanes = slice(a * size, (a + 1) * size)
        combined = within_ref[:, lanes] + dot(q_ref[:, lanes], entering_ref[a]) * fade[:, a : a + 1]
        power = jnp.mean(combined * combined, axis=1, keepdims=True)
        normed_ref[:, lanes] = (combined * lax.rsqrt(power + 1e-06)).astype(BF16)
    out_ref[...] = dot(normed_ref[...], w_ref[...]).astype(BF16)


def head_call(block, q, within, entering, down, w_out, width):
    rows, cols = q.shape
    heads = entering.shape[0]
    tile = min(rows, 256)
    return pl.pallas_call(
        head_kernel,
        out_shape=(
            jax.ShapeDtypeStruct((rows, cols), BF16),
            jax.ShapeDtypeStruct((rows, width), BF16),
        ),
        grid_spec=pltpu.PrefetchScalarGridSpec(
            num_scalar_prefetch=1,
            grid=(rows // tile,),
            in_specs=[
                pl.BlockSpec((tile, cols), lambda i, b: (i, 0)),
                pl.BlockSpec((tile, cols), lambda i, b: (i, 0)),
                pl.BlockSpec(entering.shape, lambda i, b: (0, 0, 0)),
                pl.BlockSpec((tile, heads), lambda i, b: (i, 0)),
                pl.BlockSpec((cols, width), lambda i, b: (0, b[0])),
            ],
            out_specs=[
                pl.BlockSpec((tile, cols), lambda i, b: (i, 0)),
                pl.BlockSpec((tile, width), lambda i, b: (i, 0)),
            ],
        ),
        compiler_params=pltpu.CompilerParams(vmem_limit_bytes=VMEM_LIMIT),
        cost_estimate=pl.CostEstimate(
            flops=2 * rows * cols * (width + 128),
            bytes_accessed=cols * width * 2 + rows * cols * 8 + rows * width * 2,
            transcendentals=0,
        ),
        name="heads",
    )(block, q, within, entering, down, w_out)


def out_kernel(block, normed_ref, w_ref, *refs):
    total = dot(normed_ref[...], w_ref[...])
    for ref in refs[:-1]:
        total = total + ref[...].astype(F32)
    refs[-1][...] = total.astype(BF16)


def out_call(block, normed, w_out, width, *arrived):
    rows, cols = normed.shape
    tile = min(width, 256)
    per = width // tile
    return pl.pallas_call(
        out_kernel,
        out_shape=jax.ShapeDtypeStruct((rows, width), BF16),
        grid_spec=pltpu.PrefetchScalarGridSpec(
            num_scalar_prefetch=1,
            grid=(per,),
            in_specs=[
                pl.BlockSpec((rows, cols), lambda j, b: (0, 0)),
                pl.BlockSpec((cols, tile), lambda j, b: (0, b[0] * per + j)),
            ]
            + [pl.BlockSpec((rows, tile), lambda j, b: (0, j)) for _ in arrived],
            out_specs=pl.BlockSpec((rows, tile), lambda j, b: (0, j)),
        ),
        compiler_params=pltpu.CompilerParams(vmem_limit_bytes=VMEM_LIMIT),
        cost_estimate=pl.CostEstimate(
            flops=2 * rows * cols * width,
            bytes_accessed=cols * width * 2 + rows * (cols + width * (1 + len(arrived))) * 2,
            transcendentals=0,
        ),
        name="project_out",
    )(block, normed, w_out, *arrived)


def local(n_head, n_seq, tokens, w_qkv, w_out, decay_rate, prior_state):
    rows, width = tokens.shape
    heads, size = prior_state.shape[0], prior_state.shape[1]
    square = n_head == 4
    place = lax.axis_index("head")
    chunk = min(rows, 256)
    chunks = rows // chunk
    group = 2 if heads % 2 == 0 else 1

    over_x = functools.partial(lax.ppermute, axis_name="head", perm=[(i, i ^ 1) for i in range(n_head)])
    over_y = functools.partial(lax.ppermute, axis_name="head", perm=[(i, i ^ 2) for i in range(n_head)])

    pieces = []
    if square:
        offs = jnp.stack([place, place ^ 1, place ^ 2, place ^ 3]).astype(jnp.int32) * width
        half = chunk // 2
        for c in range(chunks):
            own = tokens[c * chunk : (c + 1) * chunk]
            from_x, from_y = over_x(own), over_y(own)
            far = (over_y(from_x[:half]), over_x(from_y[half:]))
            pieces.append(((own,), (from_x,), (from_y,), far))
    else:
        offs = jnp.zeros((1,), jnp.int32)
        for c in range(chunks):
            own = tokens[c * chunk : (c + 1) * chunk]
            pieces.append(((lax.all_gather(own, "head", axis=1, tiled=True),),))

    inside = jnp.cumsum(decay_rate.reshape(heads, chunks, chunk), axis=2)
    sums = inside[:, :, -1]
    before = jnp.cumsum(sums, axis=1) - sums
    cumulative = (inside + before[:, :, None]).reshape(heads, rows)
    down_all = cumulative.T
    tail = jnp.sum(sums, axis=1)
    along = inside.reshape(heads // group, group, chunks, chunk)

    pos = lax.axis_index("seq")
    core = pos % 2
    n_chips = n_seq // 2
    swap = functools.partial(lax.ppermute, axis_name="seq", perm=[(i, i ^ 1) for i in range(n_seq)])

    def later(x, step):
        return lax.ppermute(x, "seq", perm=[(i, i + 2 * step) for i in range(n_seq - 2 * step)])

    tail_other = swap(tail)
    tail_chip = tail + tail_other
    tails = [later(tail_chip, s) for s in range(1, n_chips)]

    state = jnp.zeros((heads, size, size), F32)
    queries, withins = [], []
    for c in range(chunks):
        q, within, state = chunk_call(
            offs,
            pieces[c],
            w_qkv,
            along[:, :, c, :],
            along[:, :, c, :].transpose(0, 2, 1),
            state,
        )
        queries.append(q)
        withins.append(within)

    other = swap(state.astype(BF16)).astype(F32)
    first = jnp.where(core == 0, state, other)
    second = jnp.where(core == 0, other, state)
    tail_first = jnp.where(core == 0, tail, tail_other)
    tail_second = jnp.where(core == 0, tail_other, tail)
    share = heads // 2

    def mine(x):
        return lax.dynamic_slice_in_dim(x, core * share, share, 0)

    chip_state = (
        jnp.exp(-mine(tail_second))[:, None, None] * mine(first) + mine(second)
    ).astype(BF16)
    gap = jnp.zeros((share,), F32)
    chip_entering = jnp.zeros((share, size, size), F32)
    for s in range(1, n_chips):
        chip_entering += jnp.exp(-gap)[:, None, None] * later(chip_state, s).astype(F32)
        gap += mine(tails[s - 1])
    chip_entering += jnp.exp(-gap)[:, None, None] * mine(prior_state)
    there = swap(chip_entering.astype(BF16)).astype(F32)
    entering = jnp.concatenate(
        [jnp.where(core == 0, chip_entering, there), jnp.where(core == 0, there, chip_entering)]
    )
    entering = jnp.where(
        core == 0, entering, jnp.exp(-tail_first)[:, None, None] * entering + first
    ).astype(BF16)

    def block(flip):
        return (place ^ flip).astype(jnp.int32).reshape(1)

    if not square:
        q, within = jnp.concatenate(queries), jnp.concatenate(withins)
        normed, _ = head_call(block(0), q, within, entering, down_all, w_out, width)
        partial = dot(normed, w_out).astype(BF16)
        return lax.psum_scatter(partial, "head", scatter_dimension=1, tiled=True)

    cut = rows // 2
    per = chunks // 2
    normed, far = [], []
    for r in range(2):
        q = jnp.concatenate(queries[r * per : (r + 1) * per])
        within = jnp.concatenate(withins[r * per : (r + 1) * per])
        down = down_all[r * cut : (r + 1) * cut]
        n, p = head_call(block(3), q, within, entering, down, w_out, width)
        normed.append(n)
        far.append(p)
    via_x, via_y = over_x(far[0]), over_y(far[1])
    near_x = over_x(out_call(block(1), normed[0], w_out, width))
    near_y = over_y(out_call(block(2), normed[1], w_out, width))
    sum_x = over_x(out_call(block(1), normed[1], w_out, width, via_y))
    sum_y = over_y(out_call(block(2), normed[0], w_out, width, via_x))
    own_a = out_call(block(0), normed[0], w_out, width, near_x)
    own_b = out_call(block(0), normed[1], w_out, width, near_y)
    return jnp.concatenate(
        [
            (own_a.astype(F32) + sum_y.astype(F32)).astype(BF16),
            (own_b.astype(F32) + sum_x.astype(F32)).astype(BF16),
        ]
    )


def solution(mesh):
    in_specs = (
        P("seq", "head"),
        P(None, None, "head"),
        P("head", None),
        P("head", "seq"),
        P("head", None, None),
    )
    body = functools.partial(local, mesh.shape["head"], mesh.shape["seq"])
    return jax.shard_map(
        body, mesh=mesh, in_specs=in_specs, out_specs=P("seq", "head"), check_vma=False
    )
```

time: 304 us -> 229 us (0.75)
  waiting for transfers between devices: 193 us -> 84.8 us
  Pallas kernels: 0 us -> 78.6 us
  matrix products: 68 us -> 0 us
  starting transfers between devices: 0.08 us -> 44 us
  between operations: 13.8 us -> 0.57 us
  blocking collectives: 13.1 us -> 0 us
  local copies, waits for them, and re-layouts: 4.75 us -> 12 us
    all_gather x2 -> x0, waiting for transfers between devices: 100 us -> none  [the longest x1 87.1 us: local(): lax.all_gather(tokens, 'head', axis=1, tiled=True)]
    reduce_scatter x1 -> x0, waiting for transfers between devices: 91.6 us -> none  [local(): lax.psum_scatter(partial_value.astype(jnp.bfloat16), 'head', scatter_dime...]
    ppermute x0 -> x31, waiting for transfers between devices: none -> 84.8 us  [the longest x8 24.8 us: local(): from_x, from_y = (over_x(own), over_y(own))]
    pallas_call x0 -> x12, Pallas kernels: none -> 78.6 us  [the longest x4 56.3 us: chunk_call(): pl.pallas_call(functools.partial(chunk_kernel, tuple((len(p) for p in pie...]
    dot_general x5 -> x0, matrix products: 68 us -> none  [the longest x1 32 us: local(): jnp.einsum('tr,cre->cte', lax.all_gather(tokens, 'head', axis=1, tiled=Tr...]
    ppermute x0 -> x31, starting transfers between devices: none -> 44 us  [the longest x6 17 us: later(): lax.ppermute(x, 'seq', perm=[(i, i + 2 * step) for i in range(n_seq - 2 *...]
    unnamed x1 -> x0, blocking collectives: 13.1 us -> none
    slice x3 -> x12, local copies, waits for them, and re-layouts: 0.94 us -> 9 us  [the longest x8 6.29 us: local(): far = (over_y(from_x[:half]), over_x(from_y[half:]))]
  transfers between devices with their start and end apart: 3 -> 31, of which waited for: 3 -> 13; matrix products, arithmetic and copies ran while one was open for 2% -> 6% of each run, Pallas kernels for 0% -> 33%
where the time goes in v1:
time: 229 us; the launch traced here: 228 us
  waiting for transfers between devices  84.8 us (37%)
  Pallas kernels  78.6 us (34%)
  starting transfers between devices  44 us (19%)
  local copies, waits for them, and re-layouts  12 us (5%)
  other arithmetic  7.72 us (3%)
    pallas_call x4, Pallas kernels, chunk_call(): pl.pallas_call(functools.partial(chunk_kernel, tuple((len(p) for p in pie...  56.3 us
    ppermute x8, waiting for transfers between devices, local(): from_x, from_y = (over_x(own), over_y(own))  24.8 us
    ppermute x1, waiting for transfers between devices, local(): sum_y = over_y(out_call(block(2), normed[0], w_out, width, via_x))  19 us
    ppermute x6, starting transfers between devices, later(): lax.ppermute(x, 'seq', perm=[(i, i + 2 * step) for i in range(n_seq - 2 *...  17 us
    ppermute x2, waiting for transfers between devices, local(): via_x, via_y = (over_x(far[0]), over_y(far[1]))  14 us
    pallas_call x6, Pallas kernels, out_call(): pl.pallas_call(out_kernel, out_shape=jax.ShapeDtypeStruct((rows, width),...  13.7 us
    ppermute x1, waiting for transfers between devices, local(): near_x = over_x(out_call(block(1), normed[0], w_out, width))  13.3 us
    ppermute x8, starting transfers between devices, local(): from_x, from_y = (over_x(own), over_y(own))  10.1 us
  transfers between devices with their start and end apart: 31, of which 13 were waited for; matrix products, arithmetic and copies ran while one was open for 6% of the time, Pallas kernels for 33%

profile of v1, /device:TPU:8, one launch (start us, length us, event | category | flops | bytes accessed | tf_op | source)
XLA Modules:
  0.0 227.6 jit_solution(12152645978580081584)
XLA Ops:
  0.0 2.5 %fusion.6 = (bf16[256,1024]{1,0:T(8,128)(2,1)S(1)}, bf16[256,1024]{1,0:T(8,128)(2,1)S(1)}, bf16[256,1024]{1,0:T(8,128)(2,1)}, bf16[256,1024]{1,0:T(8,128)(2,1)S(1)}) fusion(bf16[1024,1024]{1,0:T(8,128)(2,1)} %param.5), kind=kLoop, calls=%fused_computation.34 | loop fusion | bytes 4194304 | tf_op jit(solution)/shard_map/slice | solution.py:201
  8.0 2.3 reduce-window.6
  10.7 6.7 %collective-permute-done.refs_1_ = bf16[256,1024]{1,0:T(8,128)(2,1)} collective-permute-done((bf16[256,1024]{1,0:T(8,128)(2,1)S(1)}, bf16[256,1024]{1,0:T(8,128)(2,1)}, u32[]{:S(2)}, u32[]{:S(2)}) %collective-permute-start) | collective-permute-done | bytes 524320 | tf_op jit(solution)/shard_map/ppermute | solution.py:202
  20.4 8.1 %collective-permute-done.4.refs_1_ = bf16[256,1024]{1,0:T(8,128)(2,1)S(1)} collective-permute-done((bf16[256,1024]{1,0:T(8,128)(2,1)S(1)}, bf16[256,1024]{1,0:T(8,128)(2,1)S(1)}, u32[]{:S(2)}, u32[]{:S(2)}) %collective-permute-start.4) | collective-permute-done | bytes 524320 | tf_op jit(solution)/shard_map/ppermute | solution.py:202
  30.4 1.7 slice.88
  32.1 1.7 slice.89
  34.3 5.5 %collective-permute-done.13.refs_1_ = bf16[256,1024]{1,0:T(8,128)(2,1)S(1)} collective-permute-done((bf16[256,1024]{1,0:T(8,128)(2,1)}, bf16[256,1024]{1,0:T(8,128)(2,1)S(1)}, u32[]{:S(2)}, u32[]{:S(2)}) %collective-permute-start.13) | collective-permute-done | bytes 524320 | tf_op jit(solution)/shard_map/ppermute | solution.py:202
  46.6 4.5 %collective-permute-done.9.refs_1_ = bf16[256,1024]{1,0:T(8,128)(2,1)} collective-permute-done((bf16[256,1024]{1,0:T(8,128)(2,1)S(1)}, bf16[256,1024]{1,0:T(8,128)(2,1)}, u32[]{:S(2)}, u32[]{:S(2)}) %collective-permute-start.9) | collective-permute-done | bytes 524320 | tf_op jit(solution)/shard_map/ppermute | solution.py:202
  56.1 2.0 collective-permute-done.2.refs_3_
  60.3 14.1 %chunk.4 = (bf16[256,1024]{1,0:T(8,128)(2,1)S(1)}, f32[256,1024]{1,0:T(8,128)S(1)}, f32[8,128,128]{2,1,0:T(8,128)S(1)}) custom-call(s32[4]{0:T(128)S(1)} %add_multiply_fusion.offs, bf16[256,1024]{1,0:T(8,128)(2,1)S(1)} %copy-done.3, bf16[256,1024]{1,0:T(8,128)(2,1)} %collective-permute-done.refs_1_, bf16[256,1024]{1,0:T(8,128)(2,1)} %collective-permute-done.1.refs_2_, ...), custom_call_target="tpu_custom_call" | custom-call | flops 6845104128 | bytes 27262976 | tf_op jit(solution)/shard_map/chunk/pallas_call | solution.py:73
  76.4 13.7 %chunk.5 = (bf16[256,1024]{1,0:T(8,128)(2,1)S(1)}, f32[256,1024]{1,0:T(8,128)S(1)}, f32[8,128,128]{2,1,0:T(8,128)S(1)}) custom-call(s32[4]{0:T(128)S(1)} %add_multiply_fusion.offs, bf16[256,1024]{1,0:T(8,128)(2,1)S(1)} %copy-done.1, bf16[256,1024]{1,0:T(8,128)(2,1)S(1)} %copy-done.5, bf16[256,1024]{1,0:T(8,128)(2,1)S(1)} %copy-done.7, ...), custom_call_target="tpu_custom_call" | custom-call | flops 6845104128 | bytes 27262976 | tf_op jit(solution)/shard_map/chunk/pallas_call | solution.py:73
  90.2 14.2 %chunk.6 = (bf16[256,1024]{1,0:T(8,128)(2,1)S(1)}, f32[256,1024]{1,0:T(8,128)S(1)}, f32[8,128,128]{2,1,0:T(8,128)S(1)}) custom-call(s32[4]{0:T(128)S(1)} %add_multiply_fusion.offs, bf16[256,1024]{1,0:T(8,128)(2,1)} %get-tuple-element.41.refs_0_, bf16[256,1024]{1,0:T(8,128)(2,1)S(1)} %collective-permute-done.13.refs_1_, ...), custom_call_target="tpu_custom_call" | custom-call | flops 6845104128 | bytes 27262976 | tf_op jit(solution)/shard_map/chunk/pallas_call | solution.py:73
  104.5 14.2 %chunk.7 = (bf16[256,1024]{1,0:T(8,128)(2,1)S(1)}, f32[256,1024]{1,0:T(8,128)S(1)}, f32[8,128,128]{2,1,0:T(8,128)S(1)}) custom-call(s32[4]{0:T(128)S(1)} %add_multiply_fusion.offs, bf16[256,1024]{1,0:T(8,128)(2,1)S(1)} %get-tuple-element.42.refs_0_, bf16[256,1024]{1,0:T(8,128)(2,1)} %collective-permute-done.9.refs_1_, ...), custom_call_target="tpu_custom_call" | custom-call | flops 6845104128 | bytes 27262976 | tf_op jit(solution)/shard_map/chunk/pallas_call | solution.py:73
  118.9 3.5 %collective-permute-start.19 = (f32[8]{0:T(128)S(1)}, f32[8]{0:T(128)S(1)}, u32[]{:S(2)}, u32[]{:S(2)}) collective-permute-start(f32[8]{0:T(128)S(1)} %get-tuple-element.52), channel_id=1, source_target_pairs={{0,8},{4,12},{8,16},{12,20},{16,24},{20,28},{1,9},{5,13},{9,17},{1... | collective-permute-start | bytes 104 | tf_op jit(solution)/shard_map/ppermute | solution.py:225
  122.4 2.3 %collective-permute-start.21 = (f32[8]{0:T(128)S(1)}, f32[8]{0:T(128)S(1)}, u32[]{:S(2)}, u32[]{:S(2)}) collective-permute-start(f32[8]{0:T(128)S(1)} %get-tuple-element.52), channel_id=1, source_target_pairs={{0,16},{4,20},{8,24},{12,28},{1,17},{5,21},{9,25},{13,29},{2,18},{... | collective-permute-start | bytes 104 | tf_op jit(solution)/shard_map/ppermute | solution.py:225
  126.3 6.2 %collective-permute-start.18 = (bf16[4,128,128]{2,1,0:T(8,128)(2,1)S(1)}, bf16[4,128,128]{2,1,0:T(8,128)(2,1)S(1)}, u32[]{:S(2)}, u32[]{:S(2)}) collective-permute-start(bf16[4,128,128]{2,1,0:T(8,128)(2,1)S(1)} %fusion.1), channel_id=1, source_target_pairs={{0,8},{4,12},{8,16},{12,20},{16,24},{20,28},{1,9},{5,13},{9,17},{1... | collective-permute-start | bytes 393224 | tf_op jit(solution)/shard_map/ppermute | solution.py:225
  132.5 3.5 %collective-permute-start.20 = (bf16[4,128,128]{2,1,0:T(8,128)(2,1)S(1)}, bf16[4,128,128]{2,1,0:T(8,128)(2,1)S(1)}, u32[]{:S(2)}, u32[]{:S(2)}) collective-permute-start(bf16[4,128,128]{2,1,0:T(8,128)(2,1)S(1)} %fusion.1), channel_id=1, source_target_pairs={{0,16},{4,20},{8,24},{12,28},{1,17},{5,21},{9,25},{13,29},{2,18},{... | collective-permute-start | bytes 393224 | tf_op jit(solution)/shard_map/ppermute | solution.py:225
  137.1 6.8 %collective-permute-done.20 = bf16[4,128,128]{2,1,0:T(8,128)(2,1)S(1)} collective-permute-done((bf16[4,128,128]{2,1,0:T(8,128)(2,1)S(1)}, bf16[4,128,128]{2,1,0:T(8,128)(2,1)S(1)}, u32[]{:S(2)}, u32[]{:S(2)}) %collective-permute-start.20) | collective-permute-done | bytes 131104 | tf_op jit(solution)/shard_map/ppermute | solution.py:225
  145.8 4.3 %heads.2 = (bf16[512,1024]{1,0:T(8,128)(2,1)S(1)}, bf16[512,1024]{1,0:T(8,128)(2,1)S(1)}) custom-call(s32[1]{0:T(128)} %bitcast.1.block, bf16[512,1024]{1,0:T(8,128)(2,1)S(1)} %pad_maximum_fusion.3.q_ref, f32[512,1024]{1,0:T(8,128)S(1)} %pad_maximum_fusion.within_ref, bf16[8,128,128]{2,1,0:T(8,128)(2,1)S(1)} %select_convert_fusion.entering_ref, ...), custom_call_target="tpu_custom_call" | custom-call | flops 1207959552 | bytes 7340032 | tf_op jit(solution)/shard_map/heads/pallas_call | solution.py:119
  151.0 4.3 %heads.3 = (bf16[512,1024]{1,0:T(8,128)(2,1)S(1)}, bf16[512,1024]{1,0:T(8,128)(2,1)S(1)}) custom-call(s32[1]{0:T(128)} %bitcast.1.block, bf16[512,1024]{1,0:T(8,128)(2,1)S(1)} %pad_maximum_fusion.4.q_ref, f32[512,1024]{1,0:T(8,128)S(1)} %pad_maximum_fusion.1.within_ref, bf16[8,128,128]{2,1,0:T(8,128)(2,1)S(1)} %select_convert_fusion.entering_ref, ...), custom_call_target="tpu_custom_call" | custom-call | flops 1207959552 | bytes 7340032 | tf_op jit(solution)/shard_map/heads/pallas_call | solution.py:119
  156.8 2.2 project_out.6
  160.6 2.2 project_out.9
  163.4 12.8 %collective-permute-done.26.refs_0_ = bf16[512,1024]{1,0:T(8,128)(2,1)S(1)} collective-permute-done((bf16[512,1024]{1,0:T(8,128)(2,1)S(1)}, bf16[512,1024]{1,0:T(8,128)(2,1)S(1)}, u32[]{:S(2)}, u32[]{:S(2)}) %collective-permute-start.26) | collective-permute-done | bytes 1048608 | tf_op jit(solution)/shard_map/ppermute | solution.py:291
  176.2 2.3 %project_out.8 = bf16[512,1024]{1,0:T(8,128)(2,1)S(1)} custom-call(s32[1]{0:T(128)} %bitcast.3.block, bf16[512,1024]{1,0:T(8,128)(2,1)S(1)} %get-tuple-element.29.normed_ref, bf16[1024,4096]{1,0:T(8,128)(2,1)S(1)} %bitcast.29, bf16[512,1024]{1,0:T(8,128)(2,1)S(1)} %collective-permute-done.26.refs_0_), custom_call_target="tpu_custom_call" | custom-call | flops 1073741824 | bytes 5242880 | tf_op jit(solution)/shard_map/project_out/pallas_call | solution.py:161
  181.4 2.3 %project_out.11 = bf16[512,1024]{1,0:T(8,128)(2,1)S(1)} custom-call(s32[1]{0:T(128)} %bitcast.2.block, bf16[512,1024]{1,0:T(8,128)(2,1)S(1)} %get-tuple-element.35.normed_ref, bf16[1024,4096]{1,0:T(8,128)(2,1)S(1)} %bitcast.29, bf16[512,1024]{1,0:T(8,128)(2,1)S(1)} %collective-permute-done.29.refs_0_), custom_call_target="tpu_custom_call" | custom-call | flops 1073741824 | bytes 5242880 | tf_op jit(solution)/shard_map/project_out/pallas_call | solution.py:161
  183.7 1.6 collective-permute-start.30
  185.3 13.3 %collective-permute-done.25.refs_0_ = bf16[512,1024]{1,0:T(8,128)(2,1)S(1)} collective-permute-done((bf16[512,1024]{1,0:T(8,128)(2,1)S(1)}, bf16[512,1024]{1,0:T(8,128)(2,1)S(1)}, u32[]{:S(2)}, u32[]{:S(2)}) %collective-permute-start.25) | collective-permute-done | bytes 1048608 | tf_op jit(solution)/shard_map/ppermute | solution.py:292
  198.6 2.3 %project_out.7 = bf16[512,1024]{1,0:T(8,128)(2,1)S(1)} custom-call(s32[1]{0:T(128)} %bitcast.block, bf16[512,1024]{1,0:T(8,128)(2,1)S(1)} %get-tuple-element.29.normed_ref, bf16[1024,4096]{1,0:T(8,128)(2,1)S(1)} %bitcast.29, bf16[512,1024]{1,0:T(8,128)(2,1)S(1)} %collective-permute-done.25.refs_0_), custom_call_target="tpu_custom_call" | custom-call | flops 1073741824 | bytes 5242880 | tf_op jit(solution)/shard_map/project_out/pallas_call | solution.py:161
  201.0 2.9 %collective-permute-done.28.refs_0_ = bf16[512,1024]{1,0:T(8,128)(2,1)S(1)} collective-permute-done((bf16[512,1024]{1,0:T(8,128)(2,1)S(1)}, bf16[512,1024]{1,0:T(8,128)(2,1)S(1)}, u32[]{:S(2)}, u32[]{:S(2)}) %collective-permute-start.28) | collective-permute-done | bytes 1048608 | tf_op jit(solution)/shard_map/ppermute | solution.py:293
  203.8 2.3 %project_out.10 = bf16[512,1024]{1,0:T(8,128)(2,1)S(1)} custom-call(s32[1]{0:T(128)} %bitcast.block, bf16[512,1024]{1,0:T(8,128)(2,1)S(1)} %get-tuple-element.35.normed_ref, bf16[1024,4096]{1,0:T(8,128)(2,1)S(1)} %bitcast.29, bf16[512,1024]{1,0:T(8,128)(2,1)S(1)} %collective-permute-done.28.refs_0_), custom_call_target="tpu_custom_call" | custom-call | flops 1073741824 | bytes 5242880 | tf_op jit(solution)/shard_map/project_out/pallas_call | solution.py:161
  206.2 19.0 %collective-permute-done.27 = bf16[512,1024]{1,0:T(8,128)(2,1)S(1)} collective-permute-done((bf16[512,1024]{1,0:T(8,128)(2,1)S(1)}, bf16[512,1024]{1,0:T(8,128)(2,1)S(1)}, u32[]{:S(2)}, u32[]{:S(2)}) %collective-permute-start.27) | collective-permute-done | bytes 1048608 | tf_op jit(solution)/shard_map/ppermute | solution.py:295
  226.0 1.6 pad_maximum_fusion.2
  (118 shorter events, 40.0 us)
Async XLA Ops:
  2.5 14.9 %collective-permute-start = (bf16[256,1024]{1,0:T(8,128)(2,1)S(1)}, bf16[256,1024]{1,0:T(8,128)(2,1)}, u32[]{:S(2)}, u32[]{:S(2)}) collective-permute-start(bf16[256,1024]{1,0:T(8,128)(2,1)S(1)} %get-tuple-element.39.refs_0_), channel_id=1, source_target_pairs={{0,1},{1,0},{2,3},{3,2},{4,5},{5,4},{6,7},{7,6},{8,9},{9,8},{10,11... | collective-permute-start | bytes 1572872 | tf_op jit(solution)/shard_map/ppermute | solution.py:202
  4.0 15.0 %collective-permute-start.1 = (bf16[256,1024]{1,0:T(8,128)(2,1)S(1)}, bf16[256,1024]{1,0:T(8,128)(2,1)}, u32[]{:S(2)}, u32[]{:S(2)}) collective-permute-start(bf16[256,1024]{1,0:T(8,128)(2,1)S(1)} %get-tuple-element.39.refs_0_), channel_id=1, source_target_pairs={{0,2},{1,3},{2,0},{3,1},{4,6},{5,7},{6,4},{7,5},{8,10},{9,11},{10,... | collective-permute-start | bytes 1572872 | tf_op jit(solution)/shard_map/ppermute | solution.py:202
  5.5 23.0 %collective-permute-start.4 = (bf16[256,1024]{1,0:T(8,128)(2,1)S(1)}, bf16[256,1024]{1,0:T(8,128)(2,1)S(1)}, u32[]{:S(2)}, u32[]{:S(2)}) collective-permute-start(bf16[256,1024]{1,0:T(8,128)(2,1)S(1)} %get-tuple-element.40.refs_0_), channel_id=1, source_target_pairs={{0,1},{1,0},{2,3},{3,2},{4,5},{5,4},{6,7},{7,6},{8,9},{9,8},{10,11... | collective-permute-start | bytes 1572872 | tf_op jit(solution)/shard_map/ppermute | solution.py:202
  6.0 27.7 %collective-permute-start.5 = (bf16[256,1024]{1,0:T(8,128)(2,1)S(1)}, bf16[256,1024]{1,0:T(8,128)(2,1)S(1)}, u32[]{:S(2)}, u32[]{:S(2)}) collective-permute-start(bf16[256,1024]{1,0:T(8,128)(2,1)S(1)} %get-tuple-element.40.refs_0_), channel_id=1, source_target_pairs={{0,2},{1,3},{2,0},{3,1},{4,6},{5,7},{6,4},{7,5},{8,10},{9,11},{10,... | collective-permute-start | bytes 1572872 | tf_op jit(solution)/shard_map/ppermute | solution.py:202
  6.5 33.2 %collective-permute-start.13 = (bf16[256,1024]{1,0:T(8,128)(2,1)}, bf16[256,1024]{1,0:T(8,128)(2,1)S(1)}, u32[]{:S(2)}, u32[]{:S(2)}) collective-permute-start(bf16[256,1024]{1,0:T(8,128)(2,1)} %get-tuple-element.41.refs_0_), channel_id=1, source_target_pairs={{0,1},{1,0},{2,3},{3,2},{4,5},{5,4},{6,7},{7,6},{8,9},{9,8},{10,11... | collective-permute-start | bytes 1572872 | tf_op jit(solution)/shard_map/ppermute | solution.py:202
  17.4 28.1 %collective-permute-start.14 = (bf16[256,1024]{1,0:T(8,128)(2,1)}, bf16[256,1024]{1,0:T(8,128)(2,1)}, u32[]{:S(2)}, u32[]{:S(2)}) collective-permute-start(bf16[256,1024]{1,0:T(8,128)(2,1)} %get-tuple-element.41.refs_0_), channel_id=1, source_target_pairs={{0,2},{1,3},{2,0},{3,1},{4,6},{5,7},{6,4},{7,5},{8,10},{9,11},{10,... | collective-permute-start | bytes 1572872 | tf_op jit(solution)/shard_map/ppermute | solution.py:202
  18.9 32.2 %collective-permute-start.9 = (bf16[256,1024]{1,0:T(8,128)(2,1)S(1)}, bf16[256,1024]{1,0:T(8,128)(2,1)}, u32[]{:S(2)}, u32[]{:S(2)}) collective-permute-start(bf16[256,1024]{1,0:T(8,128)(2,1)S(1)} %get-tuple-element.42.refs_0_), channel_id=1, source_target_pairs={{0,1},{1,0},{2,3},{3,2},{4,5},{5,4},{6,7},{7,6},{8,9},{9,8},{10,11... | collective-permute-start | bytes 1572872 | tf_op jit(solution)/shard_map/ppermute | solution.py:202
  28.5 25.1 %collective-permute-start.10 = (bf16[256,1024]{1,0:T(8,128)(2,1)S(1)}, bf16[256,1024]{1,0:T(8,128)(2,1)}, u32[]{:S(2)}, u32[]{:S(2)}) collective-permute-start(bf16[256,1024]{1,0:T(8,128)(2,1)S(1)} %get-tuple-element.42.refs_0_), channel_id=1, source_target_pairs={{0,2},{1,3},{2,0},{3,1},{4,6},{5,7},{6,4},{7,5},{8,10},{9,11},{10,... | collective-permute-start | bytes 1572872 | tf_op jit(solution)/shard_map/ppermute | solution.py:202
  33.7 24.4 %collective-permute-start.2 = (bf16[128,1024]{1,0:T(8,128)(2,1)}, bf16[128,1024]{1,0:T(8,128)(2,1)S(1)}, u32[]{:S(2)}, u32[]{:S(2)}) collective-permute-start(bf16[128,1024]{1,0:T(8,128)(2,1)} %slice.88), channel_id=1, source_target_pairs={{0,2},{1,3},{2,0},{3,1},{4,6},{5,7},{6,4},{7,5},{8,10},{9,11},{10,... | collective-permute-start | bytes 786440 | tf_op jit(solution)/shard_map/ppermute | solution.py:203
  39.8 19.9 %collective-permute-start.3 = (bf16[128,1024]{1,0:T(8,128)(2,1)}, bf16[128,1024]{1,0:T(8,128)(2,1)}, u32[]{:S(2)}, u32[]{:S(2)}) collective-permute-start(bf16[128,1024]{1,0:T(8,128)(2,1)} %slice.89), channel_id=1, source_target_pairs={{0,1},{1,0},{2,3},{3,2},{4,5},{5,4},{6,7},{7,6},{8,9},{9,8},{10,11... | collective-permute-start | bytes 786440 | tf_op jit(solution)/shard_map/ppermute | solution.py:203
  45.5 73.3 %collective-permute-start.8 = (f32[8]{0:T(128)S(1)}, f32[8]{0:T(128)S(1)}, u32[]{:S(2)}, u32[]{:S(2)}) collective-permute-start(f32[8]{0:T(128)S(1)} %slice_reduce_fusion.1), channel_id=1, source_target_pairs={{0,4},{4,0},{8,12},{12,8},{16,20},{20,16},{24,28},{28,24},{1,5},{5... | collective-permute-start | bytes 104 | tf_op jit(solution)/shard_map/ppermute | solution.py:227
  51.1 23.2 %collective-permute-start.6 = (bf16[128,1024]{1,0:T(8,128)(2,1)S(1)}, bf16[128,1024]{1,0:T(8,128)(2,1)S(1)}, u32[]{:S(2)}, u32[]{:S(2)}) collective-permute-start(bf16[128,1024]{1,0:T(8,128)(2,1)S(1)} %slice.93), channel_id=1, source_target_pairs={{0,2},{1,3},{2,0},{3,1},{4,6},{5,7},{6,4},{7,5},{8,10},{9,11},{10,... | collective-permute-start | bytes 786440 | tf_op jit(solution)/shard_map/ppermute | solution.py:203
  53.6 21.3 %collective-permute-start.7 = (bf16[128,1024]{1,0:T(8,128)(2,1)S(1)}, bf16[128,1024]{1,0:T(8,128)(2,1)S(1)}, u32[]{:S(2)}, u32[]{:S(2)}) collective-permute-start(bf16[128,1024]{1,0:T(8,128)(2,1)S(1)} %slice.94), channel_id=1, source_target_pairs={{0,1},{1,0},{2,3},{3,2},{4,5},{5,4},{6,7},{7,6},{8,9},{9,8},{10,11... | collective-permute-start | bytes 786440 | tf_op jit(solution)/shard_map/ppermute | solution.py:203
  58.2 32.0 %collective-permute-start.15 = (bf16[128,1024]{1,0:T(8,128)(2,1)S(1)}, bf16[128,1024]{1,0:T(8,128)(2,1)S(1)}, u32[]{:S(2)}, u32[]{:S(2)}) collective-permute-start(bf16[128,1024]{1,0:T(8,128)(2,1)S(1)} %slice.100), channel_id=1, source_target_pairs={{0,2},{1,3},{2,0},{3,1},{4,6},{5,7},{6,4},{7,5},{8,10},{9,11},{10,... | collective-permute-start | bytes 786440 | tf_op jit(solution)/shard_map/ppermute | solution.py:203
  59.7 30.5 %collective-permute-start.16 = (bf16[128,1024]{1,0:T(8,128)(2,1)S(1)}, bf16[128,1024]{1,0:T(8,128)(2,1)S(1)}, u32[]{:S(2)}, u32[]{:S(2)}) collective-permute-start(bf16[128,1024]{1,0:T(8,128)(2,1)S(1)} %slice.101), channel_id=1, source_target_pairs={{0,1},{1,0},{2,3},{3,2},{4,5},{5,4},{6,7},{7,6},{8,9},{9,8},{10,11... | collective-permute-start | bytes 786440 | tf_op jit(solution)/shard_map/ppermute | solution.py:203
  74.4 30.1 %collective-permute-start.11 = (bf16[128,1024]{1,0:T(8,128)(2,1)S(1)}, bf16[128,1024]{1,0:T(8,128)(2,1)S(1)}, u32[]{:S(2)}, u32[]{:S(2)}) collective-permute-start(bf16[128,1024]{1,0:T(8,128)(2,1)S(1)} %slice.97), channel_id=1, source_target_pairs={{0,2},{1,3},{2,0},{3,1},{4,6},{5,7},{6,4},{7,5},{8,10},{9,11},{10,... | collective-permute-start | bytes 786440 | tf_op jit(solution)/shard_map/ppermute | solution.py:203
  74.9 29.6 %collective-permute-start.12 = (bf16[128,1024]{1,0:T(8,128)(2,1)S(1)}, bf16[128,1024]{1,0:T(8,128)(2,1)S(1)}, u32[]{:S(2)}, u32[]{:S(2)}) collective-permute-start(bf16[128,1024]{1,0:T(8,128)(2,1)S(1)} %slice.98), channel_id=1, source_target_pairs={{0,1},{1,0},{2,3},{3,2},{4,5},{5,4},{6,7},{7,6},{8,9},{9,8},{10,11... | collective-permute-start | bytes 786440 | tf_op jit(solution)/shard_map/ppermute | solution.py:203
  90.2 55.5 %slice-start = ((s8[8388608]{0:T(1024)(128)(4,1)}), s8[4194304]{0:T(1024)(128)(4,1)S(1)}, s32[]{:S(2)}) async-start(s8[8388608]{0:T(1024)(128)(4,1)} %bitcast.28), calls=%async_computation | async-start | bytes 8388608
  118.8 7.3 %collective-permute-start.17 = (bf16[8,128,128]{2,1,0:T(8,128)(2,1)S(1)}, bf16[8,128,128]{2,1,0:T(8,128)(2,1)S(1)}, u32[]{:S(2)}, u32[]{:S(2)}) collective-permute-start(bf16[8,128,128]{2,1,0:T(8,128)(2,1)S(1)} %convert_element_type.45), channel_id=1, source_target_pairs={{0,4},{4,0},{8,12},{12,8},{16,20},{20,16},{24,28},{28,24},{1,5},{5... | collective-permute-start | bytes 786440 | tf_op jit(solution)/shard_map/ppermute | solution.py:245
  118.9 6.6 %collective-permute-start.19 = (f32[8]{0:T(128)S(1)}, f32[8]{0:T(128)S(1)}, u32[]{:S(2)}, u32[]{:S(2)}) collective-permute-start(f32[8]{0:T(128)S(1)} %get-tuple-element.52), channel_id=1, source_target_pairs={{0,8},{4,12},{8,16},{12,20},{16,24},{20,28},{1,9},{5,13},{9,17},{1... | collective-permute-start | bytes 104 | tf_op jit(solution)/shard_map/ppermute | solution.py:225
  122.4 3.6 %collective-permute-start.21 = (f32[8]{0:T(128)S(1)}, f32[8]{0:T(128)S(1)}, u32[]{:S(2)}, u32[]{:S(2)}) collective-permute-start(f32[8]{0:T(128)S(1)} %get-tuple-element.52), channel_id=1, source_target_pairs={{0,16},{4,20},{8,24},{12,28},{1,17},{5,21},{9,25},{13,29},{2,18},{... | collective-permute-start | bytes 104 | tf_op jit(solution)/shard_map/ppermute | solution.py:225
  124.7 1.3 collective-permute-start.23
  126.3 10.9 %collective-permute-start.18 = (bf16[4,128,128]{2,1,0:T(8,128)(2,1)S(1)}, bf16[4,128,128]{2,1,0:T(8,128)(2,1)S(1)}, u32[]{:S(2)}, u32[]{:S(2)}) collective-permute-start(bf16[4,128,128]{2,1,0:T(8,128)(2,1)S(1)} %fusion.1), channel_id=1, source_target_pairs={{0,8},{4,12},{8,16},{12,20},{16,24},{20,28},{1,9},{5,13},{9,17},{1... | collective-permute-start | bytes 393224 | tf_op jit(solution)/shard_map/ppermute | solution.py:225
  132.5 11.5 %collective-permute-start.20 = (bf16[4,128,128]{2,1,0:T(8,128)(2,1)S(1)}, bf16[4,128,128]{2,1,0:T(8,128)(2,1)S(1)}, u32[]{:S(2)}, u32[]{:S(2)}) collective-permute-start(bf16[4,128,128]{2,1,0:T(8,128)(2,1)S(1)} %fusion.1), channel_id=1, source_target_pairs={{0,16},{4,20},{8,24},{12,28},{1,17},{5,21},{9,25},{13,29},{2,18},{... | collective-permute-start | bytes 393224 | tf_op jit(solution)/shard_map/ppermute | solution.py:225
  136.0 8.0 %collective-permute-start.22 = (bf16[4,128,128]{2,1,0:T(8,128)(2,1)S(1)}, bf16[4,128,128]{2,1,0:T(8,128)(2,1)S(1)}, u32[]{:S(2)}, u32[]{:S(2)}) collective-permute-start(bf16[4,128,128]{2,1,0:T(8,128)(2,1)S(1)} %fusion.1), channel_id=1, source_target_pairs={{0,24},{4,28},{1,25},{5,29},{2,26},{6,30},{3,27},{7,31}} | collective-permute-start | bytes 393224 | tf_op jit(solution)/shard_map/ppermute | solution.py:225
  144.2 1.4 collective-permute-start.24
  150.1 26.1 %collective-permute-start.26 = (bf16[512,1024]{1,0:T(8,128)(2,1)S(1)}, bf16[512,1024]{1,0:T(8,128)(2,1)S(1)}, u32[]{:S(2)}, u32[]{:S(2)}) collective-permute-start(bf16[512,1024]{1,0:T(8,128)(2,1)S(1)} %get-tuple-element.30), channel_id=1, source_target_pairs={{0,1},{1,0},{2,3},{3,2},{4,5},{5,4},{6,7},{7,6},{8,9},{9,8},{10,11... | collective-permute-start | bytes 3145736 | tf_op jit(solution)/shard_map/ppermute | solution.py:291
  155.3 26.1 %collective-permute-start.29 = (bf16[512,1024]{1,0:T(8,128)(2,1)S(1)}, bf16[512,1024]{1,0:T(8,128)(2,1)S(1)}, u32[]{:S(2)}, u32[]{:S(2)}) collective-permute-start(bf16[512,1024]{1,0:T(8,128)(2,1)S(1)} %get-tuple-element.36), channel_id=1, source_target_pairs={{0,2},{1,3},{2,0},{3,1},{4,6},{5,7},{6,4},{7,5},{8,10},{9,11},{10,... | collective-permute-start | bytes 3145736 | tf_op jit(solution)/shard_map/ppermute | solution.py:291
  159.0 39.6 %collective-permute-start.25 = (bf16[512,1024]{1,0:T(8,128)(2,1)S(1)}, bf16[512,1024]{1,0:T(8,128)(2,1)S(1)}, u32[]{:S(2)}, u32[]{:S(2)}) collective-permute-start(bf16[512,1024]{1,0:T(8,128)(2,1)S(1)} %project_out.6), channel_id=1, source_target_pairs={{0,1},{1,0},{2,3},{3,2},{4,5},{5,4},{6,7},{7,6},{8,9},{9,8},{10,11... | collective-permute-start | bytes 3145736 | tf_op jit(solution)/shard_map/ppermute | solution.py:292
  162.8 41.0 %collective-permute-start.28 = (bf16[512,1024]{1,0:T(8,128)(2,1)S(1)}, bf16[512,1024]{1,0:T(8,128)(2,1)S(1)}, u32[]{:S(2)}, u32[]{:S(2)}) collective-permute-start(bf16[512,1024]{1,0:T(8,128)(2,1)S(1)} %project_out.9), channel_id=1, source_target_pairs={{0,2},{1,3},{2,0},{3,1},{4,6},{5,7},{6,4},{7,5},{8,10},{9,11},{10,... | collective-permute-start | bytes 3145736 | tf_op jit(solution)/shard_map/ppermute | solution.py:293
  178.5 46.7 %collective-permute-start.27 = (bf16[512,1024]{1,0:T(8,128)(2,1)S(1)}, bf16[512,1024]{1,0:T(8,128)(2,1)S(1)}, u32[]{:S(2)}, u32[]{:S(2)}) collective-permute-start(bf16[512,1024]{1,0:T(8,128)(2,1)S(1)} %project_out.8), channel_id=1, source_target_pairs={{0,2},{1,3},{2,0},{3,1},{4,6},{5,7},{6,4},{7,5},{8,10},{9,11},{10,... | collective-permute-start | bytes 3145736 | tf_op jit(solution)/shard_map/ppermute | solution.py:295
  183.7 41.9 %collective-permute-start.30 = (bf16[512,1024]{1,0:T(8,128)(2,1)S(1)}, bf16[512,1024]{1,0:T(8,128)(2,1)S(1)}, u32[]{:S(2)}, u32[]{:S(2)}) collective-permute-start(bf16[512,1024]{1,0:T(8,128)(2,1)S(1)} %project_out.11), channel_id=1, source_target_pairs={{0,1},{1,0},{2,3},{3,2},{4,5},{5,4},{6,7},{7,6},{8,9},{9,8},{10,11... | collective-permute-start | bytes 3145736 | tf_op jit(solution)/shard_map/ppermute | solution.py:294
  (11 other events, 194.5 us)

commit v2 on v0

v2 whole, which is shorter than its diff:
```python
import functools

import jax
import jax.numpy as jnp
from jax import lax
from jax.experimental import pallas as pl
from jax.experimental.pallas import tpu as pltpu
from jax.sharding import PartitionSpec as P

BF16, F32 = jnp.bfloat16, jnp.float32
PARAMS = pltpu.CompilerParams(vmem_limit_bytes=40 * 1024 * 1024)


def dot(a, b, contract=((1,), (0,))):
    return lax.dot_general(a, b, (contract, ((), ())), preferred_element_type=F32)


def after(x, *earlier):
    return lax.optimization_barrier((x, *earlier))[0]


def struct(shape, dtype):
    return jax.ShapeDtypeStruct(shape, dtype)


def fixed(shape):
    return pl.BlockSpec(shape, lambda j, o: (0,) * len(shape))


def call(kernel, name, steps, scalars, ins, in_specs, outs, out_specs, flops, scratch=(), aliases=None, light=False):
    moved = sum(a.size * a.dtype.itemsize for a in ins) + sum(
        o.size * jnp.dtype(o.dtype).itemsize for o in outs
    )
    return pl.pallas_call(
        kernel,
        out_shape=tuple(outs),
        grid_spec=pltpu.PrefetchScalarGridSpec(
            num_scalar_prefetch=1,
            grid=(steps,),
            in_specs=in_specs,
            out_specs=out_specs,
            scratch_shapes=list(scratch),
        ),
        input_output_aliases=aliases or {},
        compiler_params=PARAMS,
        cost_estimate=pl.CostEstimate(
            flops=1 if light else flops, bytes_accessed=1 if light else moved, transcendentals=0
        ),
        name=name,
    )(scalars, *ins)


def decay_kernel(chunk, _, rate_ref, along_ref, inside_ref, down_ref, tail_ref):
    heads, rows = rate_ref.shape
    lane = lax.broadcasted_iota(jnp.int32, (heads, chunk), 1)
    base = jnp.zeros((heads, 1), F32)
    insides, wholes = [], []
    for c in range(rows // chunk):
        x = rate_ref[:, c * chunk : (c + 1) * chunk]
        step = 1
        while step < chunk:
            x = x + jnp.where(lane >= step, pltpu.roll(x, step, 1), 0.0)
            step *= 2
        insides.append(x)
        wholes.append(x + base)
        base = base + x[:, chunk - 1 :]
    inside = jnp.concatenate(insides, axis=1)
    along_ref[...] = inside
    inside_ref[...] = inside.T
    down_ref[...] = jnp.concatenate(wholes, axis=1).T
    tail_ref[...] = jnp.broadcast_to(base, tail_ref.shape)


def decay_call(rate, chunk):
    heads, rows = rate.shape
    return call(
        functools.partial(decay_kernel, chunk),
        "decay",
        1,
        jnp.zeros((1,), jnp.int32),
        (rate,),
        [fixed((heads, rows))],
        (
            struct((heads, rows), F32),
            struct((rows, heads), F32),
            struct((rows, heads), F32),
            struct((heads, 128), F32),
        ),
        [fixed((heads, rows)), fixed((rows, heads)), fixed((rows, heads)), fixed((heads, 128))],
        heads * rows * 16,
    )


def column(table, head):
    lane = lax.broadcasted_iota(jnp.int32, table.shape, 1)
    return jnp.sum(jnp.where(lane == head, table, 0.0), axis=1, keepdims=True)


def scores(q, k, v, along, down, state):
    rows = q.shape[0]
    causal = lax.broadcasted_iota(jnp.int32, (rows, rows), 0) >= lax.broadcasted_iota(
        jnp.int32, (rows, rows), 1
    )
    decay = jnp.exp(jnp.minimum(along - down, 0.0))
    weights = jnp.where(causal, dot(q, k, ((1,), (1,))) * decay, 0.0).astype(BF16)
    return dot(weights, v) + dot(q, state.astype(BF16)) * jnp.exp(-down)


def advance(k, v, down, state):
    last = down[down.shape[0] - 1 :, :]
    scaled = (k.astype(F32) * jnp.exp(down - last)).astype(BF16)
    return jnp.exp(-last) * state + dot(scaled, v, ((0,), (0,)))


def first_kernel(layout, chunk, group, size, _, *refs):
    count = sum(layout)
    x_refs, w_refs, refs = refs[:count], refs[count : count + len(layout)], refs[count + len(layout) :]
    along_ref, inside_ref, q_ref, within_ref, state_ref, held = refs
    j = pl.program_id(0)
    rows, depth = held.shape[1], held.shape[2]

    @pl.when(j == 0)
    def _():
        at = 0
        for i, parts in enumerate(layout):
            tall = rows // parts
            for p in range(parts):
                held[i, p * tall : (p + 1) * tall, :] = x_refs[at][...]
                at += 1

    def project(c):
        total = dot(held[0], w_refs[0][c])
        for i in range(1, len(layout)):
            total = total + dot(held[i], w_refs[i][c])
        return total.astype(BF16)

    q_all, k_all, v_all = project(0), project(1), project(2)
    q_ref[...] = q_all
    for a in range(group):
        head = j * group + a
        lanes = slice(a * size, (a + 1) * size)
        state = jnp.zeros((size, size), F32)
        for c in range(rows // chunk):
            here = slice(c * chunk, (c + 1) * chunk)
            q, k, v = q_all[here, lanes], k_all[here, lanes], v_all[here, lanes]
            down = column(inside_ref[here, :], head)
            along = along_ref[pl.ds(head, 1), here]
            within_ref[here, lanes] = scores(q, k, v, along, down, state)
            state = advance(k, v, down, state)
        state_ref[a] = state


def first_call(places, blocks, pieces, w_qkv, along, inside, rows, chunk, size, group):
    heads = along.shape[0]
    cols = group * size
    flat = [p for piece in pieces for p in piece]
    depth = flat[0].shape[1]

    def block(i):
        return pl.BlockSpec((3, depth, cols), lambda j, o: (0, o[blocks[i]] if blocks else 0, j))

    wide = pl.BlockSpec((rows, cols), lambda j, o: (0, j))
    return call(
        functools.partial(first_kernel, tuple(len(p) for p in pieces), chunk, group, size),
        "first",
        heads // group,
        places,
        (*flat, *[w_qkv] * len(pieces), along, inside),
        [
            pl.BlockSpec((rows // len(piece), depth), lambda j, o: (0, 0))
            for piece in pieces
            for _ in piece
        ]
        + [block(i) for i in range(len(pieces))]
        + [fixed((heads, rows)), fixed((rows, heads))],
        (
            struct((rows, heads * size), BF16),
            struct((rows, heads * size), F32),
            struct((heads, size, size), F32),
        ),
        [wide, wide, pl.BlockSpec((group, size, size), lambda j, o: (j, 0, 0))],
        2 * rows * w_qkv.size,
        scratch=[pltpu.VMEM((len(pieces), rows, depth), BF16)],
    )


def part_kernel(layout, added, _, *refs):
    count = sum(layout)
    x_refs, w_refs = refs[:count], refs[count : count + len(layout)]
    out_ref, held = refs[-2], refs[-1]
    rows = held.shape[1]

    @pl.when(pl.program_id(0) == 0)
    def _():
        at = 0
        for i, parts in enumerate(layout):
            tall = rows // parts
            for p in range(parts):
                held[i, p * tall : (p + 1) * tall, :] = x_refs[at][...]
                at += 1

    for c in range(3):
        total = dot(held[0], w_refs[0][c])
        for i in range(1, len(layout)):
            total = total + dot(held[i], w_refs[i][c])
        if added:
            total = total + refs[-3][c]
        out_ref[c] = total


def part_call(places, blocks, pieces, w_qkv, rows, row_block, cols, before=None):
    flat = [p for piece in pieces for p in piece]
    depth = flat[0].shape[1]
    width = w_qkv.shape[2]

    def block(i):
        return pl.BlockSpec((3, depth, cols), lambda j, o: (0, o[blocks[i]], j))

    acc = pl.BlockSpec((3, rows, cols), lambda j, o: (0, 0, j))
    ins = [*flat, *[w_qkv] * len(pieces)]
    specs = [
        pl.BlockSpec((rows // len(piece), depth), lambda j, o: (row_block, 0))
        for piece in pieces
        for _ in piece
    ] + [block(i) for i in range(len(pieces))]
    if before is not None:
        ins.append(before)
        specs.append(acc)
    (out,) = call(
        functools.partial(part_kernel, tuple(len(p) for p in pieces), before is not None),
        "part",
        width // cols,
        places,
        ins,
        specs,
        (struct((3, rows, width), F32),),
        [acc],
        2 * rows * depth * len(pieces) * width * 3,
        scratch=[pltpu.VMEM((len(pieces), rows, depth), BF16)],
        aliases=None if before is None else {len(ins): 0},
    )
    return out


def state_kernel(chunk, group, size, _, *refs):
    xa, xb, wk, wv, acc_k, acc_v, inside_ref, state_ref = refs[:8]
    k_ref, v_ref, mid_ref, end_ref, sent_ref, held = refs[8:]
    j = pl.program_id(0)
    rows = held.shape[0]

    @pl.when(j == 0)
    def _():
        held[: rows // 2, :] = xa[...]
        held[rows // 2 :, :] = xb[...]

    k_all = (acc_k[0] + dot(held[...], wk[0])).astype(BF16)
    v_all = (acc_v[0] + dot(held[...], wv[0])).astype(BF16)
    k_ref[...] = k_all
    v_ref[...] = v_all
    for a in range(group):
        head = j * group + a
        lanes = slice(a * size, (a + 1) * size)
        state = state_ref[a]
        for c in range(rows // chunk):
            here = slice(c * chunk, (c + 1) * chunk)
            mid_ref[c, a] = state
            state = advance(
                k_all[here, lanes], v_all[here, lanes], column(inside_ref[here, :], head), state
            )
        end_ref[a] = state
        sent_ref[a] = state.astype(BF16)


def state_call(places, far, w_qkv, acc, inside, state, chunk, group):
    _, rows, width = acc.shape
    heads, size = state.shape[0], state.shape[1]
    depth = far[0].shape[1]
    cols = group * size
    wide = pl.BlockSpec((rows, cols), lambda j, o: (0, j))
    small = pl.BlockSpec((group, size, size), lambda j, o: (j, 0, 0))
    chunks = rows // chunk
    return call(
        functools.partial(state_kernel, chunk, group, size),
        "states",
        heads // group,
        places,
        (*far, w_qkv, w_qkv, acc, acc, inside, state),
        [fixed(far[0].shape), fixed(far[1].shape)]
        + [pl.BlockSpec((1, depth, cols), lambda j, o, c=c: (c, o[3], j)) for c in (1, 2)]
        + [pl.BlockSpec((1, rows, cols), lambda j, o, c=c: (c, 0, j)) for c in (1, 2)]
        + [pl.BlockSpec((rows, heads), lambda j, o: (1, 0)), small],
        (
            struct((rows, width), BF16),
            struct((rows, width), BF16),
            struct((chunks, heads, size, size), F32),
            struct(state.shape, F32),
            struct(state.shape, BF16),
        ),
        [
            wide,
            wide,
            pl.BlockSpec((chunks, group, size, size), lambda j, o: (0, j, 0, 0)),
            small,
            small,
        ],
        4 * rows * depth * width,
        scratch=[pltpu.VMEM((rows, depth), BF16)],
    )


def later_kernel(chunk, group, size, _, *refs):
    xa, xb, wq, acc_q, k_ref, v_ref, along_ref, inside_ref, mid_ref, q_ref, within_ref, held = refs
    j = pl.program_id(0)
    rows = held.shape[0]

    @pl.when(j == 0)
    def _():
        held[: rows // 2, :] = xa[...]
        held[rows // 2 :, :] = xb[...]

    q_all = (acc_q[0] + dot(held[...], wq[0])).astype(BF16)
    q_ref[...] = q_all
    for a in range(group):
        head = j * group + a
        lanes = slice(a * size, (a + 1) * size)
        for c in range(rows // chunk):
            here = slice(c * chunk, (c + 1) * chunk)
            within_ref[here, lanes] = scores(
                q_all[here, lanes],
                k_ref[here, lanes],
                v_ref[here, lanes],
                along_ref[pl.ds(head, 1), here],
                column(inside_ref[here, :], head),
                mid_ref[c, a],
            )


def later_call(places, far, w_qkv, acc, k, v, along, inside, mid, group):
    _, rows, width = acc.shape
    chunks, heads, size = mid.shape[0], mid.shape[1], mid.shape[2]
    chunk = rows // chunks
    depth = far[0].shape[1]
    cols = group * size
    wide = pl.BlockSpec((rows, cols), lambda j, o: (0, j))
    return call(
        functools.partial(later_kernel, chunk, group, size),
        "later",
        heads // group,
        places,
        (*far, w_qkv, acc, k, v, along, inside, mid),
        [
            fixed(far[0].shape),
            fixed(far[1].shape),
            pl.BlockSpec((1, depth, cols), lambda j, o: (0, o[3], j)),
            pl.BlockSpec((1, rows, cols), lambda j, o: (0, 0, j)),
            wide,
            wide,
            pl.BlockSpec((heads, rows), lambda j, o: (0, 1)),
            pl.BlockSpec((rows, heads), lambda j, o: (1, 0)),
            pl.BlockSpec((chunks, group, size, size), lambda j, o: (0, j, 0, 0)),
        ],
        (struct((rows, width), BF16), struct((rows, width), F32)),
        [wide, wide],
        2 * rows * depth * width + 4 * rows * (chunk + size) * width,
        scratch=[pltpu.VMEM((rows, depth), BF16)],
    )


def normalise(rows, q_ref, within_ref, entering_ref, down_ref, normed_ref):
    heads, size = entering_ref.shape[0], entering_ref.shape[1]
    fade = jnp.exp(-down_ref[...])
    for a in range(heads):
        lanes = slice(a * size, (a + 1) * size)
        combined = within_ref[:, lanes] + dot(q_ref[:, lanes], entering_ref[a]) * fade[:, a : a + 1]
        power = jnp.mean(combined * combined, axis=1, keepdims=True)
        normed_ref[rows, lanes] = (combined * lax.rsqrt(power + 1e-06)).astype(BF16)


def head_kernel(_, q_ref, within_ref, entering_ref, down_ref, w_ref, normed_ref, *parts):
    tall = q_ref.shape[0]
    for p, part in enumerate(parts):

        @pl.when(pl.program_id(0) == p)
        def _(p=p, part=part):
            rows = slice(p * tall, (p + 1) * tall)
            normalise(rows, q_ref, within_ref, entering_ref, down_ref, normed_ref)
            part[...] = dot(normed_ref[rows, :], w_ref[...]).astype(BF16)


def head_call(places, block, q, within, entering, down, w_out, width, tile):
    rows, cols = q.shape
    heads = entering.shape[0]
    parts = rows // tile
    part = pl.BlockSpec((tile, cols), lambda i, o: (i, 0))
    return call(
        head_kernel,
        "heads",
        parts,
        places,
        (q, within, entering, down, w_out),
        [
            part,
            part,
            fixed(entering.shape),
            pl.BlockSpec((tile, heads), lambda i, o: (i, 0)),
            pl.BlockSpec((cols, width), lambda i, o: (0, o[block])),
        ],
        (struct((rows, cols), BF16), *[struct((tile, width), BF16)] * parts),
        [fixed((rows, cols))] + [fixed((tile, width))] * parts,
        2 * rows * cols * (width + 128),
        light=True,
    )


def near_kernel(
    _, q_ref, within_ref, entering_ref, down_ref, first_ref, w_ref, normed_ref, *out_refs
):
    far_refs, near_refs = out_refs[:2], out_refs[2:]
    tall = q_ref.shape[0]
    for p in range(2):
        rows = slice(p * tall, (p + 1) * tall)

        @pl.when(pl.program_id(0) == p)
        def _(p=p, rows=rows):
            normalise(rows, q_ref, within_ref, entering_ref, down_ref, normed_ref)
            far_refs[p][...] = dot(normed_ref[rows, :], w_ref[...]).astype(BF16)

        @pl.when(pl.program_id(0) == 2 + p)
        def _(p=p, rows=rows):
            near_refs[p][:tall, :] = dot(first_ref[rows, :], w_ref[...]).astype(BF16)
            near_refs[p][tall:, :] = dot(normed_ref[rows, :], w_ref[...]).astype(BF16)


def near_call(places, q, within, entering, down, first, w_out, width):
    rows, cols = q.shape
    tall = rows // 2
    heads = entering.shape[0]
    part = pl.BlockSpec((tall, cols), lambda i, o: (jnp.minimum(i, 1), 0))
    return call(
        near_kernel,
        "heads_near",
        4,
        places,
        (q, within, entering, down, first, w_out),
        [
            part,
            part,
            fixed(entering.shape),
            pl.BlockSpec((tall, heads), lambda i, o: (2 + jnp.minimum(i, 1), 0)),
            fixed((rows, cols)),
            pl.BlockSpec((cols, width), lambda i, o: (0, o[jnp.where(i < 2, 3, i - 1)])),
        ],
        (
            struct((rows, cols), BF16),
            struct((tall, width), BF16),
            struct((tall, width), BF16),
            struct((rows, width), BF16),
            struct((rows, width), BF16),
        ),
        [
            fixed((rows, cols)),
            fixed((tall, width)),
            fixed((tall, width)),
            fixed((rows, width)),
            fixed((rows, width)),
        ],
        2 * rows * cols * (3 * width + 128),
        light=True,
    )


def out_kernel(count, kept, _, *refs):
    w_ref, out_ref = refs[count], refs[-1]
    arrived = refs[count + 1 : -1]
    tall = refs[0].shape[0]
    for i in range(count):
        total = dot(refs[i][...], w_ref[...])
        for ref, which in zip(arrived, kept, strict=True):
            if i in which:
                at = which.index(i) * tall
                total = total + ref[at : at + tall, :].astype(F32)
        out_ref[i * tall : (i + 1) * tall, :] = total.astype(BF16)


def out_call(places, block, normed, tall, w_out, width, arrived=()):
    cols = normed[0][0].shape[1]
    rows = tall * len(normed)
    tile = min(width, 256)
    per = width // tile
    return call(
        functools.partial(out_kernel, len(normed), tuple(w for _, w in arrived)),
        "project_out",
        per,
        places,
        (*[n for n, _ in normed], w_out, *[a for a, _ in arrived]),
        [pl.BlockSpec((tall, cols), lambda j, o, at=at: (at, 0)) for _, at in normed]
        + [pl.BlockSpec((cols, tile), lambda j, o: (0, o[block] * per + j))]
        + [pl.BlockSpec((a.shape[0], tile), lambda j, o: (0, j)) for a, _ in arrived],
        (struct((rows, width), BF16),),
        [pl.BlockSpec((rows, tile), lambda j, o: (0, j))],
        2 * rows * cols * width,
        light=True,
    )[0]


def last_kernel(_, kept_ref, a_ref, b_ref, out_ref):
    tall = a_ref.shape[0]
    out_ref[:tall, :] = (kept_ref[:tall, :].astype(F32) + a_ref[...].astype(F32)).astype(BF16)
    out_ref[tall:, :] = (kept_ref[tall:, :].astype(F32) + b_ref[...].astype(F32)).astype(BF16)


def last_call(kept, a, b, half):
    rows, width = kept.shape
    tile = min(width, 256)
    pair = pl.BlockSpec((rows // 2, tile), lambda j, o: (half, j))
    quarter = pl.BlockSpec((rows // 4, tile), lambda j, o: (0, j))
    return call(
        last_kernel,
        "last_add",
        width // tile,
        jnp.zeros((1,), jnp.int32),
        (kept, a, b),
        [pair, quarter, quarter],
        (struct(kept.shape, BF16),),
        [pair],
        rows * width,
        aliases={1: 0},
    )[0]


def local(n_head, n_seq, tokens, w_qkv, w_out, decay_rate, prior_state):
    rows, width = tokens.shape
    heads, size = prior_state.shape[0], prior_state.shape[1]
    square = n_head == 4
    place = lax.axis_index("head").astype(jnp.int32)
    quarter = rows // 4
    group = 2 if heads % 2 == 0 else 1
    cols = group * size

    over_x = functools.partial(lax.ppermute, axis_name="head", perm=[(i, i ^ 1) for i in range(n_head)])
    over_y = functools.partial(lax.ppermute, axis_name="head", perm=[(i, i ^ 2) for i in range(n_head)])

    flips = (0, 1, 2, 3) if square else (0,)
    places = jnp.stack([place ^ f for f in flips])

    along, inside, down, tail = decay_call(decay_rate, quarter)
    tail = tail[:, 0]
    pos = lax.axis_index("seq")
    core = pos % 2
    n_chips = n_seq // 2
    swap = functools.partial(lax.ppermute, axis_name="seq", perm=[(i, i ^ 1) for i in range(n_seq)])

    def later(x, step):
        return lax.ppermute(x, "seq", perm=[(i, i + 2 * step) for i in range(n_seq - 2 * step)])

    tail_other = swap(tail)
    tail_chip = tail + tail_other
    tails = [later(tail_chip, s) for s in range(1, n_chips)]

    if square:
        q0, q1 = tokens[:quarter], tokens[quarter : 2 * quarter]
        x0, y1 = over_x(q0), over_y(q1)
        acc = part_call(places, (0,), [(tokens,)], w_qkv, 2 * quarter, 1, cols)
        rest = after(tokens, acc)
        q2, q3 = rest[2 * quarter : 3 * quarter], rest[3 * quarter :]
        x1, y0 = over_x(after(q1, acc)), over_y(after(q0, acc))
        fy0, fx1 = over_y(x0), over_x(y1)
        x2, y3 = over_x(after(q2, x1, y0, *tails)), over_y(after(q3, x1, y0, *tails))
        x3, y2 = over_x(after(q3, fy0, fx1)), over_y(after(q2, fy0, fx1))
        query_a, within_a, state = first_call(
            places,
            (0, 1, 2, 3),
            [(tokens,), (x0, x1), (y0, y1), (fy0, fx1)],
            w_qkv,
            along,
            inside,
            2 * quarter,
            quarter,
            size,
            group,
        )
        fy2, fx3 = over_y(after(x2, state)), over_x(after(y3, state))
        acc = part_call(
            places, (1, 2), [(x2, x3), (y2, y3)], w_qkv, 2 * quarter, 0, cols, before=acc
        )
        far = (fy2, fx3)
        k, v, mid, state, sent = state_call(
            places, far, w_qkv, acc, inside, state, quarter, group
        )
        query_b, within_b = later_call(
            places, far, w_qkv, acc, k, v, along, inside, mid, group
        )
    else:
        gathered = lax.all_gather(tokens, "head", axis=1, tiled=True)
        query, within, state = first_call(
            places,
            (),
            [(gathered,)],
            w_qkv,
            along,
            inside,
            rows,
            quarter,
            size,
            group,
        )
        sent = state.astype(BF16)

    other = swap(sent).astype(F32)
    first = jnp.where(core == 0, state, other)
    second = jnp.where(core == 0, other, state)
    tail_first = jnp.where(core == 0, tail, tail_other)
    tail_second = jnp.where(core == 0, tail_other, tail)
    share = heads // 2

    def mine(x):
        return lax.dynamic_slice_in_dim(x, core * share, share, 0)

    chip_state = (
        jnp.exp(-mine(tail_second))[:, None, None] * mine(first) + mine(second)
    ).astype(BF16)
    gap = jnp.zeros((share,), F32)
    chip_entering = jnp.zeros((share, size, size), F32)
    shifted = [later(chip_state, s) for s in range(1, n_chips)]
    if square:
        shifted = lax.optimization_barrier((*shifted, query_b, within_b))[: n_chips - 1]
    for s in range(1, n_chips):
        chip_entering += jnp.exp(-gap)[:, None, None] * shifted[s - 1].astype(F32)
        gap += mine(tails[s - 1])
    chip_entering += jnp.exp(-gap)[:, None, None] * mine(prior_state)
    there = swap(chip_entering.astype(BF16)).astype(F32)
    entering = jnp.concatenate(
        [jnp.where(core == 0, chip_entering, there), jnp.where(core == 0, there, chip_entering)]
    )
    entering = jnp.where(
        core == 0, entering, jnp.exp(-tail_first)[:, None, None] * entering + first
    ).astype(BF16)

    if not square:
        normed = head_call(places, 0, query, within, entering, down, w_out, width, quarter)[0]
        partial = dot(normed, w_out).astype(BF16)
        return lax.psum_scatter(partial, "head", scatter_dimension=1, tiled=True)

    na, far0, far1 = head_call(
        places, 3, query_a, within_a, entering, down, w_out, width, quarter
    )
    far0, far1 = over_x(far0), over_y(far1)
    nb, far2, far3, near_x, near_y = near_call(
        places, query_b, within_b, entering, down, na, w_out, width
    )
    far2, far3 = over_x(far2), over_y(far3)
    near_x, near_y = over_x(after(near_x, far0, far1)), over_y(after(near_y, far0, far1))

    def out(block, *parts, arrived=()):
        return out_call(places, block, parts, quarter, w_out, width, arrived)

    n0, n1, n2, n3 = (na, 0), (na, 1), (nb, 0), (nb, 1)
    sum_x1 = over_x(out(1, n1, arrived=[(far1, (0,))]))
    sum_y0 = over_y(out(2, n0, arrived=[(far0, (0,))]))
    sum_x3 = over_x(out(1, n3, arrived=[(far3, (0,))]))
    sum_y2 = over_y(out(2, n2, arrived=[(far2, (0,))]))
    kept = out(0, n0, n1, n2, n3, arrived=[(near_x, (0, 2)), (near_y, (1, 3))])
    kept = last_call(kept, sum_y0, sum_x1, 0)
    return last_call(kept, sum_y2, sum_x3, 1)


def solution(mesh):
    in_specs = (
        P("seq", "head"),
        P(None, None, "head"),
        P("head", None),
        P("head", "seq"),
        P("head", None, None),
    )
    body = functools.partial(local, mesh.shape["head"], mesh.shape["seq"])
    return jax.shard_map(
        body, mesh=mesh, in_specs=in_specs, out_specs=P("seq", "head"), check_vma=False
    )
```

time: 304 us -> 203 us (0.67)
  waiting for transfers between devices: 193 us -> 39.9 us
  Pallas kernels: 0 us -> 92.9 us
  matrix products: 68 us -> 0 us
  starting transfers between devices: 0.08 us -> 46.8 us
  between operations: 13.8 us -> 0.54 us
  blocking collectives: 13.1 us -> 0 us
  local copies, waits for them, and re-layouts: 4.75 us -> 16.7 us
  other arithmetic: 8.95 us -> 2.2 us
    all_gather x2 -> x0, waiting for transfers between devices: 100 us -> none  [the longest x1 87.1 us: local(): lax.all_gather(tokens, 'head', axis=1, tiled=True)]
    pallas_call x0 -> x15, Pallas kernels: none -> 92.9 us  [call(): pl.pallas_call(kernel, out_shape=tuple(outs), grid_spec=pltpu.PrefetchSca...]
    reduce_scatter x1 -> x0, waiting for transfers between devices: 91.6 us -> none  [local(): lax.psum_scatter(partial_value.astype(jnp.bfloat16), 'head', scatter_dime...]
    dot_general x5 -> x0, matrix products: 68 us -> none  [the longest x1 32 us: local(): jnp.einsum('tr,cre->cte', lax.all_gather(tokens, 'head', axis=1, tiled=Tr...]
    ppermute x0 -> x31, starting transfers between devices: none -> 46.8 us  [the longest x6 22 us: later(): lax.ppermute(x, 'seq', perm=[(i, i + 2 * step) for i in range(n_seq - 2 *...]
    ppermute x0 -> x31, waiting for transfers between devices: none -> 39.9 us  [the longest x2 21.8 us: local(): far2, far3 = (over_x(far2), over_y(far3))]
    unnamed x1 -> x0, blocking collectives: 13.1 us -> none
    unnamed x13 -> x52, local copies, waits for them, and re-layouts: 2.92 us -> 14.1 us
  transfers between devices with their start and end apart: 3 -> 31, of which waited for: 3 -> 11; matrix products, arithmetic and copies ran while one was open for 2% -> 0% of each run, Pallas kernels for 0% -> 39%
where the time goes in v2:
time: 203 us; the launch traced here: 199 us
  Pallas kernels  92.9 us (46%)
  starting transfers between devices  46.8 us (23%)
  waiting for transfers between devices  39.9 us (20%)
  local copies, waits for them, and re-layouts  16.7 us (8%)
  other arithmetic  2.2 us (1%)
    pallas_call x15, Pallas kernels, call(): pl.pallas_call(kernel, out_shape=tuple(outs), grid_spec=pltpu.PrefetchSca...  92.9 us
    ppermute x6, starting transfers between devices, later(): lax.ppermute(x, 'seq', perm=[(i, i + 2 * step) for i in range(n_seq - 2 *...  22 us
    ppermute x2, waiting for transfers between devices, local(): far2, far3 = (over_x(far2), over_y(far3))  21.8 us
    unnamed x52, local copies, waits for them, and re-layouts  14.1 us
    ppermute x1, waiting for transfers between devices, local(): sum_y2 = over_y(out(2, n2, arrived=[(far2, (0,))]))  4.93 us
    ppermute x6, waiting for transfers between devices, later(): lax.ppermute(x, 'seq', perm=[(i, i + 2 * step) for i in range(n_seq - 2 *...  4.79 us
  transfers between devices with their start and end apart: 31, of which 11 were waited for; matrix products, arithmetic and copies ran while one was open for 0% of the time, Pallas kernels for 39%

profile of v2, /device:TPU:8, one launch (start us, length us, event | category | flops | bytes accessed | tf_op | source)
XLA Modules:
  0.0 199.0 jit_solution(4445925640481542984)
XLA Ops:
  0.0 2.4 %fusion.6 = (bf16[256,1024]{1,0:T(8,128)(2,1)}, bf16[256,1024]{1,0:T(8,128)(2,1)}) fusion(bf16[1024,1024]{1,0:T(8,128)(2,1)} %refs_0_.3), kind=kLoop, calls=%fused_computation.22 | loop fusion | bytes 2097152 | tf_op jit(solution)/shard_map/slice | solution.py:561
  2.4 1.5 collective-permute-start.3
  5.5 6.9 %part.2.refs_6_ = f32[3,512,1024]{2,1,0:T(8,128)S(1)} custom-call(s32[4]{0:T(128)S(1)} %pad_add_fusion._, bf16[1024,1024]{1,0:T(8,128)(2,1)S(1)} %copy-done.4, bf16[3,4096,1024]{2,1,0:T(8,128)(2,1)} %refs_2_.3), custom_call_target="tpu_custom_call" | custom-call | flops 3221225472 | bytes 33554432 | tf_op jit(solution)/shard_map/part/pallas_call | solution.py:34
  12.4 2.6 %copy-done.1 = f32[3,512,1024]{2,1,0:T(8,128)} copy-done((f32[3,512,1024]{2,1,0:T(8,128)}, f32[3,512,1024]{2,1,0:T(8,128)S(1)}, u32[]{:S(2)}) %copy-start.1) | copy-done | bytes 6291480
  19.3 1.5 collective-permute-start.4
  22.8 11.0 %collective-permute-start.8 = (f32[8]{0:T(128)S(1)}, f32[8]{0:T(128)S(1)}, u32[]{:S(2)}, u32[]{:S(2)}) collective-permute-start(f32[8]{0:T(128)S(1)} %get-tuple-element.86), channel_id=1, source_target_pairs={{0,16},{4,20},{8,24},{12,28},{1,17},{5,21},{9,25},{13,29},{2,18},{... | collective-permute-start | bytes 104 | tf_op jit(solution)/shard_map/ppermute | solution.py:554
  35.1 1.9 collective-permute-start.7
  37.1 3.5 %collective-permute-done.7 = f32[8]{0:T(128)S(1)} collective-permute-done((f32[8]{0:T(128)S(1)}, f32[8]{0:T(128)S(1)}, u32[]{:S(2)}, u32[]{:S(2)}) %collective-permute-start.7) | collective-permute-done | bytes 64 | tf_op jit(solution)/shard_map/ppermute | solution.py:554
  44.6 24.1 %first.1 = (bf16[512,1024]{1,0:T(8,128)(2,1)S(1)}, f32[512,1024]{1,0:T(8,128)S(1)}, f32[8,128,128]{2,1,0:T(8,128)S(1)}) custom-call(s32[4]{0:T(128)S(1)} %pad_add_fusion._, bf16[1024,1024]{1,0:T(8,128)(2,1)S(1)} %copy-done.4, bf16[256,1024]{1,0:T(8,128)(2,1)} %collective-permute-done.refs_1_, bf16[256,1024]{1,0:T(8,128)(2,1)} %collective-permute-done.1.refs_2_, ...), custom_call_target="tpu_custom_call" | custom-call | flops 12884901888 | bytes 109641728 | tf_op jit(solution)/shard_map/first/pallas_call | solution.py:34
  70.5 10.7 %part.3.refs_4_.refs_5_.refs_3_ = f32[3,512,1024]{2,1,0:T(8,128)S(1)} custom-call(s32[4]{0:T(128)S(1)} %pad_add_fusion._, bf16[256,1024]{1,0:T(8,128)(2,1)S(1)} %collective-permute-done.10.refs_0_, bf16[256,1024]{1,0:T(8,128)(2,1)S(1)} %collective-permute-done.14.refs_1_, ...), custom_call_target="tpu_custom_call", output_to_operand_aliasing={{}: (7, {})} | custom-call | flops 6442450944 | bytes 65011712 | tf_op jit(solution)/shard_map/part/pallas_call | solution.py:34
  81.2 7.2 %states.1 = (bf16[512,1024]{1,0:T(8,128)(2,1)S(1)}, bf16[512,1024]{1,0:T(8,128)(2,1)S(1)}, f32[2,8,128,128]{3,2,1,0:T(8,128)S(1)}, f32[8,128,128]{2,1,0:T(8,128)S(1)}, bf16[8,128,128]{2,1,0:T(8,128)(2,1)S(1)}) custom-call(s32[4]{0:T(128)S(1)} %pad_add_fusion._, bf16[256,1024]{1,0:T(8,128)(2,1)S(1)} %collective-permute-done.11.refs_0_, ...), custom_call_target="tpu_custom_call" | custom-call | flops 2147483648 | bytes 68452352 | tf_op jit(solution)/shard_map/states/pallas_call | solution.py:34
  93.8 5.7 %collective-permute-start.18 = (bf16[4,128,128]{2,1,0:T(8,128)(2,1)S(1)}, bf16[4,128,128]{2,1,0:T(8,128)(2,1)S(1)}, u32[]{:S(2)}, u32[]{:S(2)}) collective-permute-start(bf16[4,128,128]{2,1,0:T(8,128)(2,1)S(1)} %fusion.1), channel_id=1, source_target_pairs={{0,16},{4,20},{8,24},{12,28},{1,17},{5,21},{9,25},{13,29},{2,18},{... | collective-permute-start | bytes 393224 | tf_op jit(solution)/shard_map/ppermute | solution.py:554
  99.5 2.1 %collective-permute-start.17 = (bf16[4,128,128]{2,1,0:T(8,128)(2,1)S(1)}, bf16[4,128,128]{2,1,0:T(8,128)(2,1)S(1)}, u32[]{:S(2)}, u32[]{:S(2)}) collective-permute-start(bf16[4,128,128]{2,1,0:T(8,128)(2,1)S(1)} %fusion.1), channel_id=1, source_target_pairs={{0,8},{4,12},{8,16},{12,20},{16,24},{20,28},{1,9},{5,13},{9,17},{1... | collective-permute-start | bytes 393224 | tf_op jit(solution)/shard_map/ppermute | solution.py:554
  101.6 2.9 %copy-done.3 = f32[3,512,1024]{2,1,0:T(8,128)S(1)} copy-done((f32[3,512,1024]{2,1,0:T(8,128)S(1)}, f32[3,512,1024]{2,1,0:T(8,128)}, u32[]{:S(2)}) %copy-start.3) | copy-done | bytes 6291480
  105.9 8.1 %later.1 = (bf16[512,1024]{1,0:T(8,128)(2,1)S(1)}, f32[512,1024]{1,0:T(8,128)S(1)}) custom-call(s32[4]{0:T(128)S(1)} %pad_add_fusion._, bf16[256,1024]{1,0:T(8,128)(2,1)S(1)} %collective-permute-done.11.refs_0_, bf16[256,1024]{1,0:T(8,128)(2,1)S(1)} %collective-permute-done.13.refs_1_, bf16[3,4096,1024]{2,1,0:T(8,128)(2,1)} %refs_2_.3, ...), custom_call_target="tpu_custom_call" | custom-call | flops 1879048192 | bytes 38862848 | tf_op jit(solution)/shard_map/later/pallas_call | solution.py:34
  114.1 1.6 fusion.4
  117.4 4.9 %heads.1 = (bf16[512,1024]{1,0:T(8,128)(2,1)S(1)}, bf16[256,1024]{1,0:T(8,128)(2,1)S(1)}, bf16[256,1024]{1,0:T(8,128)(2,1)S(1)}) custom-call(s32[4]{0:T(128)S(1)} %pad_add_fusion._, bf16[512,1024]{1,0:T(8,128)(2,1)S(1)} %copy-done.12, f32[512,1024]{1,0:T(8,128)S(1)} %copy-done.6, bf16[8,128,128]{2,1,0:T(8,128)(2,1)S(1)} %select_convert_fusion.entering_ref, ...), custom_call_target="tpu_custom_call" | custom-call | flops 1 | bytes 1 | tf_op jit(solution)/shard_map/heads/pallas_call | solution.py:34
  123.3 1.5 collective-permute-start.22
  124.8 9.2 %heads_near.1 = (bf16[512,1024]{1,0:T(8,128)(2,1)S(1)}, bf16[256,1024]{1,0:T(8,128)(2,1)S(1)}, bf16[256,1024]{1,0:T(8,128)(2,1)S(1)}, bf16[512,1024]{1,0:T(8,128)(2,1)S(1)}, bf16[512,1024]{1,0:T(8,128)(2,1)S(1)}) custom-call(s32[4]{0:T(128)S(1)} %pad_add_fusion._, bf16[512,1024]{1,0:T(8,128)(2,1)S(1)} %copy-done.20, f32[512,1024]{1,0:T(8,128)S(1)} %copy-done.8, ...), custom_call_target="tpu_custom_call" | custom-call | flops 1 | bytes 1 | tf_op jit(solution)/shard_map/heads_near/pallas_call | solution.py:34
  134.1 2.2 %collective-permute-done.21.refs_2_ = bf16[256,1024]{1,0:T(8,128)(2,1)S(1)} collective-permute-done((bf16[256,1024]{1,0:T(8,128)(2,1)S(1)}, bf16[256,1024]{1,0:T(8,128)(2,1)S(1)}, u32[]{:S(2)}, u32[]{:S(2)}) %collective-permute-start.21) | collective-permute-done | bytes 524320 | tf_op jit(solution)/shard_map/ppermute | solution.py:647
  141.1 3.4 %copy-done = bf16[1024,4096]{1,0:T(8,128)(2,1)S(1)} copy-done((bf16[1024,4096]{1,0:T(8,128)(2,1)S(1)}, bf16[1024,4096]{1,0:T(8,128)(2,1)}, u32[]{:S(2)}) %copy-start) | copy-done | bytes 8388632
  144.4 2.3 %project_out.6 = bf16[256,1024]{1,0:T(8,128)(2,1)S(1)} custom-call(s32[4]{0:T(128)S(1)} %pad_add_fusion._, bf16[512,1024]{1,0:T(8,128)(2,1)S(1)} %get-tuple-element.67.first_ref.refs_0_.refs_1_, bf16[1024,4096]{1,0:T(8,128)(2,1)S(1)} %copy-done, bf16[256,1024]{1,0:T(8,128)(2,1)S(1)} %collective-permute-done.21.refs_2_), custom_call_target="tpu_custom_call" | custom-call | flops 1 | bytes 1 | tf_op jit(solution)/shard_map/project_out/pallas_call | solution.py:34
  146.7 1.6 collective-permute-start.25
  148.3 2.3 %project_out.7 = bf16[256,1024]{1,0:T(8,128)(2,1)S(1)} custom-call(s32[4]{0:T(128)S(1)} %pad_add_fusion._, bf16[512,1024]{1,0:T(8,128)(2,1)S(1)} %get-tuple-element.67.first_ref.refs_0_.refs_1_, bf16[1024,4096]{1,0:T(8,128)(2,1)S(1)} %copy-done, bf16[256,1024]{1,0:T(8,128)(2,1)S(1)} %collective-permute-done.22.refs_2_), custom_call_target="tpu_custom_call" | custom-call | flops 1 | bytes 1 | tf_op jit(solution)/shard_map/project_out/pallas_call | solution.py:34
  150.6 21.8 %collective-permute-done.27.refs_2_ = bf16[256,1024]{1,0:T(8,128)(2,1)S(1)} collective-permute-done((bf16[256,1024]{1,0:T(8,128)(2,1)S(1)}, bf16[256,1024]{1,0:T(8,128)(2,1)S(1)}, u32[]{:S(2)}, u32[]{:S(2)}) %collective-permute-start.27) | collective-permute-done | bytes 524320 | tf_op jit(solution)/shard_map/ppermute | solution.py:651
  173.4 2.3 %project_out.8 = bf16[256,1024]{1,0:T(8,128)(2,1)S(1)} custom-call(s32[4]{0:T(128)S(1)} %pad_add_fusion._, bf16[512,1024]{1,0:T(8,128)(2,1)S(1)} %get-tuple-element.68.refs_2_.refs_3_.refs_0_, bf16[1024,4096]{1,0:T(8,128)(2,1)S(1)} %copy-done, bf16[256,1024]{1,0:T(8,128)(2,1)S(1)} %collective-permute-done.27.refs_2_), custom_call_target="tpu_custom_call" | custom-call | flops 1 | bytes 1 | tf_op jit(solution)/shard_map/project_out/pallas_call | solution.py:34
  176.8 2.3 %project_out.9 = bf16[256,1024]{1,0:T(8,128)(2,1)S(1)} custom-call(s32[4]{0:T(128)S(1)} %pad_add_fusion._, bf16[512,1024]{1,0:T(8,128)(2,1)S(1)} %get-tuple-element.68.refs_2_.refs_3_.refs_0_, bf16[1024,4096]{1,0:T(8,128)(2,1)S(1)} %copy-done, bf16[256,1024]{1,0:T(8,128)(2,1)S(1)} %collective-permute-done.29.refs_2_), custom_call_target="tpu_custom_call" | custom-call | flops 1 | bytes 1 | tf_op jit(solution)/shard_map/project_out/pallas_call | solution.py:34
  179.0 1.5 collective-permute-start.30
  180.5 4.9 %project_out.5.kept_ref = bf16[1024,1024]{1,0:T(8,128)(2,1)} custom-call(s32[4]{0:T(128)S(1)} %pad_add_fusion._, bf16[512,1024]{1,0:T(8,128)(2,1)S(1)} %get-tuple-element.67.first_ref.refs_0_.refs_1_, bf16[512,1024]{1,0:T(8,128)(2,1)S(1)} %get-tuple-element.67.first_ref.refs_0_.refs_1_, bf16[512,1024]{1,0:T(8,128)(2,1)S(1)} %get-tuple-element.68.refs_2_.refs_3_.refs_0_, ...), custom_call_target="tpu_custom_call" | custom-call | flops 1 | bytes 1 | tf_op jit(solution)/shard_map/project_out/pallas_call | solution.py:34
  187.2 3.4 %last_add.2.kept_ref = bf16[1024,1024]{1,0:T(8,128)(2,1)} custom-call(s32[1]{0:T(128)} %constant.10.clone.1._, bf16[1024,1024]{1,0:T(8,128)(2,1)} %project_out.5.kept_ref, bf16[256,1024]{1,0:T(8,128)(2,1)S(1)} %collective-permute-done.25.a_ref, bf16[256,1024]{1,0:T(8,128)(2,1)S(1)} %collective-permute-done.26.b_ref), custom_call_target="tpu_custom_call", output_to_operand_aliasing={{}: (1, {})} | custom-call | flops 1048576 | bytes 5242880 | tf_op jit(solution)/shard_map/last_add/pallas_call | solution.py:34
  190.6 4.9 %collective-permute-done.28.a_ref = bf16[256,1024]{1,0:T(8,128)(2,1)S(1)} collective-permute-done((bf16[256,1024]{1,0:T(8,128)(2,1)S(1)}, bf16[256,1024]{1,0:T(8,128)(2,1)S(1)}, u32[]{:S(2)}, u32[]{:S(2)}) %collective-permute-start.28) | collective-permute-done | bytes 524320 | tf_op jit(solution)/shard_map/ppermute | solution.py:661
  195.5 3.4 %last_add.3 = bf16[1024,1024]{1,0:T(8,128)(2,1)} custom-call(s32[1]{0:T(128)} %constant.10.clone.1._, bf16[1024,1024]{1,0:T(8,128)(2,1)} %last_add.2.kept_ref, bf16[256,1024]{1,0:T(8,128)(2,1)S(1)} %collective-permute-done.28.a_ref, bf16[256,1024]{1,0:T(8,128)(2,1)S(1)} %collective-permute-done.30.b_ref), custom_call_target="tpu_custom_call", output_to_operand_aliasing={{}: (1, {})} | custom-call | flops 1048576 | bytes 5242880 | tf_op jit(solution)/shard_map/last_add/pallas_call | solution.py:34
  (112 shorter events, 32.9 us)
Async XLA Ops:
  2.4 15.5 %collective-permute-start.3 = (bf16[256,1024]{1,0:T(8,128)(2,1)}, bf16[256,1024]{1,0:T(8,128)(2,1)S(1)}, u32[]{:S(2)}, u32[]{:S(2)}) collective-permute-start(bf16[256,1024]{1,0:T(8,128)(2,1)} %get-tuple-element.41), channel_id=1, source_target_pairs={{0,2},{1,3},{2,0},{3,1},{4,6},{5,7},{6,4},{7,5},{8,10},{9,11},{10,... | collective-permute-start | bytes 1572872 | tf_op jit(solution)/shard_map/ppermute | solution.py:562
  3.9 15.4 %collective-permute-start = (bf16[256,1024]{1,0:T(8,128)(2,1)}, bf16[256,1024]{1,0:T(8,128)(2,1)}, u32[]{:S(2)}, u32[]{:S(2)}) collective-permute-start(bf16[256,1024]{1,0:T(8,128)(2,1)} %get-tuple-element.42), channel_id=1, source_target_pairs={{0,1},{1,0},{2,3},{3,2},{4,5},{5,4},{6,7},{7,6},{8,9},{9,8},{10,11... | collective-permute-start | bytes 1572872 | tf_op jit(solution)/shard_map/ppermute | solution.py:562
  15.0 25.6 %collective-permute-start.1 = (bf16[256,1024]{1,0:T(8,128)(2,1)}, bf16[256,1024]{1,0:T(8,128)(2,1)}, u32[]{:S(2)}, u32[]{:S(2)}) collective-permute-start(bf16[256,1024]{1,0:T(8,128)(2,1)} %get-tuple-element.41), channel_id=1, source_target_pairs={{0,1},{1,0},{2,3},{3,2},{4,5},{5,4},{6,7},{7,6},{8,9},{9,8},{10,11... | collective-permute-start | bytes 1572872 | tf_op jit(solution)/shard_map/ppermute | solution.py:566
  15.5 25.0 %collective-permute-start.2 = (bf16[256,1024]{1,0:T(8,128)(2,1)}, bf16[256,1024]{1,0:T(8,128)(2,1)}, u32[]{:S(2)}, u32[]{:S(2)}) collective-permute-start(bf16[256,1024]{1,0:T(8,128)(2,1)} %get-tuple-element.42), channel_id=1, source_target_pairs={{0,2},{1,3},{2,0},{3,1},{4,6},{5,7},{6,4},{7,5},{8,10},{9,11},{10,... | collective-permute-start | bytes 1572872 | tf_op jit(solution)/shard_map/ppermute | solution.py:566
  17.8 24.3 %collective-permute-start.5 = (bf16[256,1024]{1,0:T(8,128)(2,1)S(1)}, bf16[256,1024]{1,0:T(8,128)(2,1)}, u32[]{:S(2)}, u32[]{:S(2)}) collective-permute-start(bf16[256,1024]{1,0:T(8,128)(2,1)S(1)} %collective-permute-done.3.refs_4_), channel_id=1, source_target_pairs={{0,1},{1,0},{2,3},{3,2},{4,5},{5,4},{6,7},{7,6},{8,9},{9,8},{10,11... | collective-permute-start | bytes 1572872 | tf_op jit(solution)/shard_map/ppermute | solution.py:567
  19.3 22.8 %collective-permute-start.4 = (bf16[256,1024]{1,0:T(8,128)(2,1)}, bf16[256,1024]{1,0:T(8,128)(2,1)}, u32[]{:S(2)}, u32[]{:S(2)}) collective-permute-start(bf16[256,1024]{1,0:T(8,128)(2,1)} %collective-permute-done.refs_1_), channel_id=1, source_target_pairs={{0,2},{1,3},{2,0},{3,1},{4,6},{5,7},{6,4},{7,5},{8,10},{9,11},{10,... | collective-permute-start | bytes 1572872 | tf_op jit(solution)/shard_map/ppermute | solution.py:567
  21.0 1.2 collective-permute-start.6
  22.1 0.7 collective-permute-start.9
  22.8 12.3 %collective-permute-start.8 = (f32[8]{0:T(128)S(1)}, f32[8]{0:T(128)S(1)}, u32[]{:S(2)}, u32[]{:S(2)}) collective-permute-start(f32[8]{0:T(128)S(1)} %get-tuple-element.86), channel_id=1, source_target_pairs={{0,16},{4,20},{8,24},{12,28},{1,17},{5,21},{9,25},{13,29},{2,18},{... | collective-permute-start | bytes 104 | tf_op jit(solution)/shard_map/ppermute | solution.py:554
  35.1 5.4 %collective-permute-start.7 = (f32[8]{0:T(128)S(1)}, f32[8]{0:T(128)S(1)}, u32[]{:S(2)}, u32[]{:S(2)}) collective-permute-start(f32[8]{0:T(128)S(1)} %get-tuple-element.86), channel_id=1, source_target_pairs={{0,8},{4,12},{8,16},{12,20},{16,24},{20,28},{1,9},{5,13},{9,17},{1... | collective-permute-start | bytes 104 | tf_op jit(solution)/shard_map/ppermute | solution.py:554
  40.6 28.2 %collective-permute-start.10 = (bf16[256,1024]{1,0:T(8,128)(2,1)S(1)}, bf16[256,1024]{1,0:T(8,128)(2,1)S(1)}, u32[]{:S(2)}, u32[]{:S(2)}) collective-permute-start(bf16[256,1024]{1,0:T(8,128)(2,1)S(1)} %get-tuple-element.55), channel_id=1, source_target_pairs={{0,1},{1,0},{2,3},{3,2},{4,5},{5,4},{6,7},{7,6},{8,9},{9,8},{10,11... | collective-permute-start | bytes 1572872 | tf_op jit(solution)/shard_map/ppermute | solution.py:568
  41.1 27.7 %collective-permute-start.12 = (bf16[256,1024]{1,0:T(8,128)(2,1)S(1)}, bf16[256,1024]{1,0:T(8,128)(2,1)S(1)}, u32[]{:S(2)}, u32[]{:S(2)}) collective-permute-start(bf16[256,1024]{1,0:T(8,128)(2,1)S(1)} %get-tuple-element.54), channel_id=1, source_target_pairs={{0,2},{1,3},{2,0},{3,1},{4,6},{5,7},{6,4},{7,5},{8,10},{9,11},{10,... | collective-permute-start | bytes 1572872 | tf_op jit(solution)/shard_map/ppermute | solution.py:568
  42.1 28.3 %collective-permute-start.15 = (bf16[256,1024]{1,0:T(8,128)(2,1)S(1)}, bf16[256,1024]{1,0:T(8,128)(2,1)S(1)}, u32[]{:S(2)}, u32[]{:S(2)}) collective-permute-start(bf16[256,1024]{1,0:T(8,128)(2,1)S(1)} %get-tuple-element.55), channel_id=1, source_target_pairs={{0,2},{1,3},{2,0},{3,1},{4,6},{5,7},{6,4},{7,5},{8,10},{9,11},{10,... | collective-permute-start | bytes 1572872 | tf_op jit(solution)/shard_map/ppermute | solution.py:569
  43.1 27.3 %collective-permute-start.14 = (bf16[256,1024]{1,0:T(8,128)(2,1)S(1)}, bf16[256,1024]{1,0:T(8,128)(2,1)S(1)}, u32[]{:S(2)}, u32[]{:S(2)}) collective-permute-start(bf16[256,1024]{1,0:T(8,128)(2,1)S(1)} %get-tuple-element.54), channel_id=1, source_target_pairs={{0,1},{1,0},{2,3},{3,2},{4,5},{5,4},{6,7},{7,6},{8,9},{9,8},{10,11... | collective-permute-start | bytes 1572872 | tf_op jit(solution)/shard_map/ppermute | solution.py:569
  44.6 25.8 %slice-start.3 = ((s8[6291456]{0:T(1024)(128)(4,1)}), s8[2097152]{0:T(1024)(128)(4,1)S(1)}, s32[]{:S(2)}) async-start(s8[6291456]{0:T(1024)(128)(4,1)} %bitcast.6), calls=%async_computation.3 | async-start | bytes 4194304
  68.8 12.3 %collective-permute-start.11 = (bf16[256,1024]{1,0:T(8,128)(2,1)S(1)}, bf16[256,1024]{1,0:T(8,128)(2,1)S(1)}, u32[]{:S(2)}, u32[]{:S(2)}) collective-permute-start(bf16[256,1024]{1,0:T(8,128)(2,1)S(1)} %collective-permute-done.10.refs_0_), channel_id=1, source_target_pairs={{0,2},{1,3},{2,0},{3,1},{4,6},{5,7},{6,4},{7,5},{8,10},{9,11},{10,... | collective-permute-start | bytes 1572872 | tf_op jit(solution)/shard_map/ppermute | solution.py:582
  69.4 11.8 %collective-permute-start.13 = (bf16[256,1024]{1,0:T(8,128)(2,1)S(1)}, bf16[256,1024]{1,0:T(8,128)(2,1)S(1)}, u32[]{:S(2)}, u32[]{:S(2)}) collective-permute-start(bf16[256,1024]{1,0:T(8,128)(2,1)S(1)} %collective-permute-done.12.refs_3_), channel_id=1, source_target_pairs={{0,1},{1,0},{2,3},{3,2},{4,5},{5,4},{6,7},{7,6},{8,9},{9,8},{10,11... | collective-permute-start | bytes 1572872 | tf_op jit(solution)/shard_map/ppermute | solution.py:582
  91.4 1.5 collective-permute-start.16
  93.1 20.9 %collective-permute-start.19 = (bf16[4,128,128]{2,1,0:T(8,128)(2,1)S(1)}, bf16[4,128,128]{2,1,0:T(8,128)(2,1)S(1)}, u32[]{:S(2)}, u32[]{:S(2)}) collective-permute-start(bf16[4,128,128]{2,1,0:T(8,128)(2,1)S(1)} %fusion.1), channel_id=1, source_target_pairs={{0,24},{4,28},{1,25},{5,29},{2,26},{6,30},{3,27},{7,31}} | collective-permute-start | bytes 393224 | tf_op jit(solution)/shard_map/ppermute | solution.py:554
  93.8 20.3 %collective-permute-start.18 = (bf16[4,128,128]{2,1,0:T(8,128)(2,1)S(1)}, bf16[4,128,128]{2,1,0:T(8,128)(2,1)S(1)}, u32[]{:S(2)}, u32[]{:S(2)}) collective-permute-start(bf16[4,128,128]{2,1,0:T(8,128)(2,1)S(1)} %fusion.1), channel_id=1, source_target_pairs={{0,16},{4,20},{8,24},{12,28},{1,17},{5,21},{9,25},{13,29},{2,18},{... | collective-permute-start | bytes 393224 | tf_op jit(solution)/shard_map/ppermute | solution.py:554
  99.5 14.6 %collective-permute-start.17 = (bf16[4,128,128]{2,1,0:T(8,128)(2,1)S(1)}, bf16[4,128,128]{2,1,0:T(8,128)(2,1)S(1)}, u32[]{:S(2)}, u32[]{:S(2)}) collective-permute-start(bf16[4,128,128]{2,1,0:T(8,128)(2,1)S(1)} %fusion.1), channel_id=1, source_target_pairs={{0,8},{4,12},{8,16},{12,20},{16,24},{20,28},{1,9},{5,13},{9,17},{1... | collective-permute-start | bytes 393224 | tf_op jit(solution)/shard_map/ppermute | solution.py:554
  115.7 1.4 collective-permute-start.20
  122.3 14.0 %collective-permute-start.21 = (bf16[256,1024]{1,0:T(8,128)(2,1)S(1)}, bf16[256,1024]{1,0:T(8,128)(2,1)S(1)}, u32[]{:S(2)}, u32[]{:S(2)}) collective-permute-start(bf16[256,1024]{1,0:T(8,128)(2,1)S(1)} %get-tuple-element.70), channel_id=1, source_target_pairs={{0,1},{1,0},{2,3},{3,2},{4,5},{5,4},{6,7},{7,6},{8,9},{9,8},{10,11... | collective-permute-start | bytes 1572872 | tf_op jit(solution)/shard_map/ppermute | solution.py:647
  123.3 13.7 %collective-permute-start.22 = (bf16[256,1024]{1,0:T(8,128)(2,1)S(1)}, bf16[256,1024]{1,0:T(8,128)(2,1)S(1)}, u32[]{:S(2)}, u32[]{:S(2)}) collective-permute-start(bf16[256,1024]{1,0:T(8,128)(2,1)S(1)} %get-tuple-element.71), channel_id=1, source_target_pairs={{0,2},{1,3},{2,0},{3,1},{4,6},{5,7},{6,4},{7,5},{8,10},{9,11},{10,... | collective-permute-start | bytes 1572872 | tf_op jit(solution)/shard_map/ppermute | solution.py:647
  137.0 42.0 %collective-permute-start.23 = (bf16[512,1024]{1,0:T(8,128)(2,1)S(1)}, bf16[512,1024]{1,0:T(8,128)(2,1)S(1)}, u32[]{:S(2)}, u32[]{:S(2)}) collective-permute-start(bf16[512,1024]{1,0:T(8,128)(2,1)S(1)} %get-tuple-element.72), channel_id=1, source_target_pairs={{0,1},{1,0},{2,3},{3,2},{4,5},{5,4},{6,7},{7,6},{8,9},{9,8},{10,11... | collective-permute-start | bytes 3145736 | tf_op jit(solution)/shard_map/ppermute | solution.py:652
  138.1 42.5 %collective-permute-start.24 = (bf16[512,1024]{1,0:T(8,128)(2,1)S(1)}, bf16[512,1024]{1,0:T(8,128)(2,1)S(1)}, u32[]{:S(2)}, u32[]{:S(2)}) collective-permute-start(bf16[512,1024]{1,0:T(8,128)(2,1)S(1)} %get-tuple-element.74), channel_id=1, source_target_pairs={{0,2},{1,3},{2,0},{3,1},{4,6},{5,7},{6,4},{7,5},{8,10},{9,11},{10,... | collective-permute-start | bytes 3145736 | tf_op jit(solution)/shard_map/ppermute | solution.py:652
  139.1 33.2 %collective-permute-start.27 = (bf16[256,1024]{1,0:T(8,128)(2,1)S(1)}, bf16[256,1024]{1,0:T(8,128)(2,1)S(1)}, u32[]{:S(2)}, u32[]{:S(2)}) collective-permute-start(bf16[256,1024]{1,0:T(8,128)(2,1)S(1)} %get-tuple-element.75), channel_id=1, source_target_pairs={{0,1},{1,0},{2,3},{3,2},{4,5},{5,4},{6,7},{7,6},{8,9},{9,8},{10,11... | collective-permute-start | bytes 1572872 | tf_op jit(solution)/shard_map/ppermute | solution.py:651
  140.5 35.1 %collective-permute-start.29 = (bf16[256,1024]{1,0:T(8,128)(2,1)S(1)}, bf16[256,1024]{1,0:T(8,128)(2,1)S(1)}, u32[]{:S(2)}, u32[]{:S(2)}) collective-permute-start(bf16[256,1024]{1,0:T(8,128)(2,1)S(1)} %get-tuple-element.76), channel_id=1, source_target_pairs={{0,2},{1,3},{2,0},{3,1},{4,6},{5,7},{6,4},{7,5},{8,10},{9,11},{10,... | collective-permute-start | bytes 1572872 | tf_op jit(solution)/shard_map/ppermute | solution.py:651
  146.7 39.9 %collective-permute-start.25 = (bf16[256,1024]{1,0:T(8,128)(2,1)S(1)}, bf16[256,1024]{1,0:T(8,128)(2,1)S(1)}, u32[]{:S(2)}, u32[]{:S(2)}) collective-permute-start(bf16[256,1024]{1,0:T(8,128)(2,1)S(1)} %project_out.6), channel_id=1, source_target_pairs={{0,2},{1,3},{2,0},{3,1},{4,6},{5,7},{6,4},{7,5},{8,10},{9,11},{10,... | collective-permute-start | bytes 1572872 | tf_op jit(solution)/shard_map/ppermute | solution.py:659
  172.3 14.9 %collective-permute-start.26 = (bf16[256,1024]{1,0:T(8,128)(2,1)S(1)}, bf16[256,1024]{1,0:T(8,128)(2,1)S(1)}, u32[]{:S(2)}, u32[]{:S(2)}) collective-permute-start(bf16[256,1024]{1,0:T(8,128)(2,1)S(1)} %project_out.7), channel_id=1, source_target_pairs={{0,1},{1,0},{2,3},{3,2},{4,5},{5,4},{6,7},{7,6},{8,9},{9,8},{10,11... | collective-permute-start | bytes 1572872 | tf_op jit(solution)/shard_map/ppermute | solution.py:658
  175.6 19.9 %collective-permute-start.28 = (bf16[256,1024]{1,0:T(8,128)(2,1)S(1)}, bf16[256,1024]{1,0:T(8,128)(2,1)S(1)}, u32[]{:S(2)}, u32[]{:S(2)}) collective-permute-start(bf16[256,1024]{1,0:T(8,128)(2,1)S(1)} %project_out.8), channel_id=1, source_target_pairs={{0,2},{1,3},{2,0},{3,1},{4,6},{5,7},{6,4},{7,5},{8,10},{9,11},{10,... | collective-permute-start | bytes 1572872 | tf_op jit(solution)/shard_map/ppermute | solution.py:661
  179.0 16.5 %collective-permute-start.30 = (bf16[256,1024]{1,0:T(8,128)(2,1)S(1)}, bf16[256,1024]{1,0:T(8,128)(2,1)S(1)}, u32[]{:S(2)}, u32[]{:S(2)}) collective-permute-start(bf16[256,1024]{1,0:T(8,128)(2,1)S(1)} %project_out.9), channel_id=1, source_target_pairs={{0,1},{1,0},{2,3},{3,2},{4,5},{5,4},{6,7},{7,6},{8,9},{9,8},{10,11... | collective-permute-start | bytes 1572872 | tf_op jit(solution)/shard_map/ppermute | solution.py:660
  (25 other events, 174.9 us)

commit v3 on v2

--- a/solution.py
+++ b/solution.py
@@ -8,7 +8,7 @@
 from jax.sharding import PartitionSpec as P
 
 BF16, F32 = jnp.bfloat16, jnp.float32
-PARAMS = pltpu.CompilerParams(vmem_limit_bytes=40 * 1024 * 1024)
+PARAMS = pltpu.CompilerParams(vmem_limit_bytes=60 * 1024 * 1024)
 
 
 def dot(a, b, contract=((1,), (0,))):
@@ -48,6 +48,32 @@
         ),
         name=name,
     )(scalars, *ins)
+
+
+def cut_kernel(first, x_ref, a_ref, b_ref, sems):
+    tall = a_ref.shape[0]
+    copies = [
+        pltpu.make_async_copy(x_ref.at[pl.ds((first + i) * tall, tall)], out, sems.at[i])
+        for i, out in enumerate((a_ref, b_ref))
+    ]
+    for copy in copies:
+        copy.start()
+    for copy in copies:
+        copy.wait()
+
+
+def cut_call(x, first):
+    rows, width = x.shape
+    half = struct((rows // 4, width), x.dtype)
+    return pl.pallas_call(
+        functools.partial(cut_kernel, first),
+        out_shape=(half, half),
+        in_specs=[pl.BlockSpec(memory_space=pl.ANY)],
+        out_specs=[pl.BlockSpec(memory_space=pl.ANY)] * 2,
+        scratch_shapes=[pltpu.SemaphoreType.DMA((2,))],
+        cost_estimate=pl.CostEstimate(flops=0, bytes_accessed=x.size * 2, transcendentals=0),
+        name="cut",
+    )(x)
 
 
 def decay_kernel(chunk, _, rate_ref, along_ref, inside_ref, down_ref, tail_ref):
@@ -112,12 +138,12 @@
     return jnp.exp(-last) * state + dot(scaled, v, ((0,), (0,)))
 
 
-def first_kernel(layout, chunk, group, size, _, *refs):
+def first_kernel(layout, added, chunk, group, size, _, *refs):
     count = sum(layout)
     x_refs, w_refs, refs = refs[:count], refs[count : count + len(layout)], refs[count + len(layout) :]
-    along_ref, inside_ref, q_ref, within_ref, state_ref, held = refs
+    along_ref, inside_ref, q_ref, within_ref, state_ref, held = refs[-6:]
     j = pl.program_id(0)
-    rows, depth = held.shape[1], held.shape[2]
+    rows = held.shape[1]
 
     @pl.when(j == 0)
     def _():
@@ -132,6 +158,8 @@
         total = dot(held[0], w_refs[0][c])
         for i in range(1, len(layout)):
             total = total + dot(held[i], w_refs[i][c])
+        if added:
+            total = total + refs[0][c]
         return total.astype(BF16)
 
     q_all, k_all, v_all = project(0), project(1), project(2)
@@ -150,7 +178,7 @@
         state_ref[a] = state
 
 
-def first_call(places, blocks, pieces, w_qkv, along, inside, rows, chunk, size, group):
+def first_call(places, blocks, pieces, before, w_qkv, along, inside, rows, chunk, size, group):
     heads = along.shape[0]
     cols = group * size
     flat = [p for piece in pieces for p in piece]
@@ -161,17 +189,20 @@
 
     wide = pl.BlockSpec((rows, cols), lambda j, o: (0, j))
     return call(
-        functools.partial(first_kernel, tuple(len(p) for p in pieces), chunk, group, size),
+        functools.partial(
+            first_kernel, tuple(len(p) for p in pieces), bool(before), chunk, group, size
+        ),
         "first",
         heads // group,
         places,
-        (*flat, *[w_qkv] * len(pieces), along, inside),
+        (*flat, *[w_qkv] * len(pieces), *before, along, inside),
         [
             pl.BlockSpec((rows // len(piece), depth), lambda j, o: (0, 0))
             for piece in pieces
             for _ in piece
         ]
         + [block(i) for i in range(len(pieces))]
+        + [pl.BlockSpec((3, rows, cols), lambda j, o: (0, 0, j)) for _ in before]
         + [fixed((heads, rows)), fixed((rows, heads))],
         (
             struct((rows, heads * size), BF16),
@@ -179,7 +210,7 @@
             struct((heads, size, size), F32),
         ),
         [wide, wide, pl.BlockSpec((group, size, size), lambda j, o: (j, 0, 0))],
-        2 * rows * w_qkv.size,
+        2 * rows * 3 * heads * size * depth * len(pieces),
         scratch=[pltpu.VMEM((len(pieces), rows, depth), BF16)],
     )
 
@@ -208,7 +239,7 @@
         out_ref[c] = total
 
 
-def part_call(places, blocks, pieces, w_qkv, rows, row_block, cols, before=None):
+def part_call(places, blocks, pieces, w_qkv, rows, cols, before=None, at=0):
     flat = [p for piece in pieces for p in piece]
     depth = flat[0].shape[1]
     width = w_qkv.shape[2]
@@ -216,17 +247,14 @@
     def block(i):
         return pl.BlockSpec((3, depth, cols), lambda j, o: (0, o[blocks[i]], j))
 
-    acc = pl.BlockSpec((3, rows, cols), lambda j, o: (0, 0, j))
     ins = [*flat, *[w_qkv] * len(pieces)]
     specs = [
-        pl.BlockSpec((rows // len(piece), depth), lambda j, o: (row_block, 0))
-        for piece in pieces
-        for _ in piece
+        pl.BlockSpec((rows // len(piece), depth), lambda j, o: (0, 0)) for piece in pieces for _ in piece
     ] + [block(i) for i in range(len(pieces))]
     if before is not None:
         ins.append(before)
-        specs.append(acc)
-    (out,) = call(
+        specs.append(pl.BlockSpec((3, rows, cols), lambda j, o: (0, at, j)))
+    return call(
         functools.partial(part_kernel, tuple(len(p) for p in pieces), before is not None),
         "part",
         width // cols,
@@ -234,12 +262,10 @@
         ins,
         specs,
         (struct((3, rows, width), F32),),
-        [acc],
+        [pl.BlockSpec((3, rows, cols), lambda j, o: (0, 0, j))],
         2 * rows * depth * len(pieces) * width * 3,
         scratch=[pltpu.VMEM((len(pieces), rows, depth), BF16)],
-        aliases=None if before is None else {len(ins): 0},
-    )
-    return out
+    )[0]
 
 
 def state_kernel(chunk, group, size, _, *refs):
@@ -366,82 +392,73 @@
     )
 
 
-def normalise(rows, q_ref, within_ref, entering_ref, down_ref, normed_ref):
+def head_kernel(_, q_ref, within_ref, entering_ref, down_ref, w_ref, normed_ref, *out_refs):
     heads, size = entering_ref.shape[0], entering_ref.shape[1]
-    fade = jnp.exp(-down_ref[...])
-    for a in range(heads):
-        lanes = slice(a * size, (a + 1) * size)
-        combined = within_ref[:, lanes] + dot(q_ref[:, lanes], entering_ref[a]) * fade[:, a : a + 1]
-        power = jnp.mean(combined * combined, axis=1, keepdims=True)
-        normed_ref[rows, lanes] = (combined * lax.rsqrt(power + 1e-06)).astype(BF16)
-
-
-def head_kernel(_, q_ref, within_ref, entering_ref, down_ref, w_ref, normed_ref, *parts):
     tall = q_ref.shape[0]
-    for p, part in enumerate(parts):
+    for p, out_ref in enumerate(out_refs):
+        rows = slice(p * tall, (p + 1) * tall)
 
         @pl.when(pl.program_id(0) == p)
-        def _(p=p, part=part):
-            rows = slice(p * tall, (p + 1) * tall)
-            normalise(rows, q_ref, within_ref, entering_ref, down_ref, normed_ref)
-            part[...] = dot(normed_ref[rows, :], w_ref[...]).astype(BF16)
-
-
-def head_call(places, block, q, within, entering, down, w_out, width, tile):
+        def _(rows=rows, out_ref=out_ref):
+            fade = jnp.exp(-down_ref[...])
+            for a in range(heads):
+                lanes = slice(a * size, (a + 1) * size)
+                seen = dot(q_ref[:, lanes], entering_ref[a]) * fade[:, a : a + 1]
+                combined = within_ref[:, lanes] + seen
+                power = jnp.mean(combined * combined, axis=1, keepdims=True)
+                normed_ref[rows, lanes] = (combined * lax.rsqrt(power + 1e-06)).astype(BF16)
+            out_ref[...] = dot(normed_ref[rows, :], w_ref[...]).astype(BF16)
+
+
+def head_call(places, block, q, within, entering, down, w_out, width, at):
     rows, cols = q.shape
+    tall = rows // 2
     heads = entering.shape[0]
-    parts = rows // tile
-    part = pl.BlockSpec((tile, cols), lambda i, o: (i, 0))
+    part = pl.BlockSpec((tall, cols), lambda i, o: (i, 0))
     return call(
         head_kernel,
         "heads",
-        parts,
+        2,
         places,
         (q, within, entering, down, w_out),
         [
             part,
             part,
             fixed(entering.shape),
-            pl.BlockSpec((tile, heads), lambda i, o: (i, 0)),
+            pl.BlockSpec((tall, heads), lambda i, o: (2 * at + i, 0)),
             pl.BlockSpec((cols, width), lambda i, o: (0, o[block])),
         ],
-        (struct((rows, cols), BF16), *[struct((tile, width), BF16)] * parts),
-        [fixed((rows, cols))] + [fixed((tile, width))] * parts,
+        (struct((rows, cols), BF16), *[struct((tall, width), BF16)] * 2),
+        [fixed((rows, cols))] + [fixed((tall, width))] * 2,
         2 * rows * cols * (width + 128),
         light=True,
     )
 
 
-def near_kernel(
-    _, q_ref, within_ref, entering_ref, down_ref, first_ref, w_ref, normed_ref, *out_refs
-):
-    far_refs, near_refs = out_refs[:2], out_refs[2:]
+def heads_near_kernel(_, q_ref, within_ref, entering_ref, down_ref, first_ref, w_ref, normed_ref, *out_refs):
     tall = q_ref.shape[0]
-    for p in range(2):
+    head_kernel(_, q_ref, within_ref, entering_ref, down_ref, w_ref, normed_ref, *out_refs[:2])
+    for p, out_ref in enumerate(out_refs[2:]):
         rows = slice(p * tall, (p + 1) * tall)
 
-        @pl.when(pl.program_id(0) == p)
-        def _(p=p, rows=rows):
-            normalise(rows, q_ref, within_ref, entering_ref, down_ref, normed_ref)
-            far_refs[p][...] = dot(normed_ref[rows, :], w_ref[...]).astype(BF16)
-
         @pl.when(pl.program_id(0) == 2 + p)
-        def _(p=p, rows=rows):
-            near_refs[p][:tall, :] = dot(first_ref[rows, :], w_ref[...]).astype(BF16)
-            near_refs[p][tall:, :] = dot(normed_ref[rows, :], w_ref[...]).astype(BF16)
-
-
-def near_call(places, q, within, entering, down, first, w_out, width):
+        def _(rows=rows, out_ref=out_ref):
+            out_ref[:tall, :] = dot(first_ref[rows, :], w_ref[...]).astype(BF16)
+            out_ref[tall:, :] = dot(normed_ref[rows, :], w_ref[...]).astype(BF16)
+
+
+def heads_near_call(places, q, within, entering, down, normed_a, w_out, width):
     rows, cols = q.shape
     tall = rows // 2
     heads = entering.shape[0]
     part = pl.BlockSpec((tall, cols), lambda i, o: (jnp.minimum(i, 1), 0))
-    return call(
-        near_kernel,
+    quarter, half = (tall, width), (rows, width)
+    return call(
+        heads_near_kernel,
         "heads_near",
         4,
         places,
-        (q, within, entering, down, first, w_out),
+        (q, within, entering, down, normed_a, w_out),
         [
             part,
             part,
@@ -450,81 +467,110 @@
             fixed((rows, cols)),
             pl.BlockSpec((cols, width), lambda i, o: (0, o[jnp.where(i < 2, 3, i - 1)])),
         ],
-        (
-            struct((rows, cols), BF16),
-            struct((tall, width), BF16),
-            struct((tall, width), BF16),
-            struct((rows, width), BF16),
-            struct((rows, width), BF16),
-        ),
+        (struct((rows, cols), BF16), *[struct(quarter, BF16)] * 2, *[struct(half, BF16)] * 2),
+        [fixed((rows, cols)), fixed(quarter), fixed(quarter), fixed(half), fixed(half)],
+        2 * rows * cols * (3 * width + 128),
+        light=True,
+    )
+
+
+def pair_kernel(_, normed_ref, x_ref, y_ref, w_ref, out_x_ref, out_y_ref):
+    tall = x_ref.shape[0]
+
+    @pl.when(pl.program_id(0) == 0)
+    def _():
+        out_x_ref[...] = (dot(normed_ref[tall:, :], w_ref[...]) + x_ref[...].astype(F32)).astype(BF16)
+
+    @pl.when(pl.program_id(0) == 1)
+    def _():
+        out_y_ref[...] = (dot(normed_ref[:tall, :], w_ref[...]) + y_ref[...].astype(F32)).astype(BF16)
+
+
+def pair_call(places, normed, for_x, for_y, w_out, width):
+    rows, cols = normed.shape
+    quarter = (rows // 2, width)
+    return call(
+        pair_kernel,
+        "sum_pair",
+        2,
+        places,
+        (normed, for_x, for_y, w_out),
         [
             fixed((rows, cols)),
-            fixed((tall, width)),
-            fixed((tall, width)),
-            fixed((rows, width)),
-            fixed((rows, width)),
+            fixed(quarter),
+            fixed(quarter),
+            pl.BlockSpec((cols, width), lambda i, o: (0, o[1 + i])),
         ],
-        2 * rows * cols * (3 * width + 128),
+        (struct(quarter, BF16),) * 2,
+        [fixed(quarter)] * 2,
+        2 * rows * cols * width,
         light=True,
     )
 
 
-def out_kernel(count, kept, _, *refs):
-    w_ref, out_ref = refs[count], refs[-1]
-    arrived = refs[count + 1 : -1]
-    tall = refs[0].shape[0]
-    for i in range(count):
-        total = dot(refs[i][...], w_ref[...])
-        for ref, which in zip(arrived, kept, strict=True):
-            if i in which:
-                at = which.index(i) * tall
-                total = total + ref[at : at + tall, :].astype(F32)
-        out_ref[i * tall : (i + 1) * tall, :] = total.astype(BF16)
-
-
-def out_call(places, block, normed, tall, w_out, width, arrived=()):
-    cols = normed[0][0].shape[1]
-    rows = tall * len(normed)
-    tile = min(width, 256)
-    per = width // tile
-    return call(
-        functools.partial(out_kernel, len(normed), tuple(w for _, w in arrived)),
-        "project_out",
-        per,
+def own_kernel(_, normed_ref, w_ref, *refs):
+    out_ref = refs[-1]
+    tall = out_ref.shape[0]
+    each = len(refs) // 2
+    for p in range(2):
+        rows = slice(p * tall, (p + 1) * tall)
+
+        @pl.when(pl.program_id(0) == p)
+        def _(p=p, rows=rows):
+            total = dot(normed_ref[rows, :], w_ref[...])
+            for ref in refs[p * each : (p + 1) * each]:
+                total = total + ref[...].astype(F32)
+            out_ref[...] = total.astype(BF16)
+
+
+def own_call(places, normed, first, second, w_out, width, height):
+    rows, cols = normed.shape
+    quarter = (rows // 2, width)
+    return call(
+        own_kernel,
+        "own_block",
+        2,
         places,
-        (*[n for n, _ in normed], w_out, *[a for a, _ in arrived]),
-        [pl.BlockSpec((tall, cols), lambda j, o, at=at: (at, 0)) for _, at in normed]
-        + [pl.BlockSpec((cols, tile), lambda j, o: (0, o[block] * per + j))]
-        + [pl.BlockSpec((a.shape[0], tile), lambda j, o: (0, j)) for a, _ in arrived],
-        (struct((rows, width), BF16),),
-        [pl.BlockSpec((rows, tile), lambda j, o: (0, j))],
+        (normed, w_out, *[a for a, _ in (*first, *second)]),
+        [fixed((rows, cols)), pl.BlockSpec((cols, width), lambda i, o: (0, o[0]))]
+        + [pl.BlockSpec(quarter, lambda i, o, at=at: (at, 0)) for _, at in (*first, *second)],
+        (struct((rows * height, width), BF16),),
+        [pl.BlockSpec(quarter, lambda i, o: (i, 0))],
         2 * rows * cols * width,
         light=True,
     )[0]
 
 
-def last_kernel(_, kept_ref, a_ref, b_ref, out_ref):
-    tall = a_ref.shape[0]
-    out_ref[:tall, :] = (kept_ref[:tall, :].astype(F32) + a_ref[...].astype(F32)).astype(BF16)
-    out_ref[tall:, :] = (kept_ref[tall:, :].astype(F32) + b_ref[...].astype(F32)).astype(BF16)
-
-
-def last_call(kept, a, b, half):
-    rows, width = kept.shape
-    tile = min(width, 256)
-    pair = pl.BlockSpec((rows // 2, tile), lambda j, o: (half, j))
-    quarter = pl.BlockSpec((rows // 4, tile), lambda j, o: (0, j))
+def last_kernel(_, kept_ref, a_ref, b_ref, above_ref, out_ref):
+    del above_ref
+
+    @pl.when(pl.program_id(0) == 0)
+    def _():
+        out_ref[...] = (kept_ref[...].astype(F32) + a_ref[...].astype(F32)).astype(BF16)
+
+    @pl.when(pl.program_id(0) == 1)
+    def _():
+        out_ref[...] = (kept_ref[...].astype(F32) + b_ref[...].astype(F32)).astype(BF16)
+
+
+def last_call(kept, a, b, above):
+    tall, width = a.shape
     return call(
         last_kernel,
         "last_add",
-        width // tile,
+        2,
         jnp.zeros((1,), jnp.int32),
-        (kept, a, b),
-        [pair, quarter, quarter],
-        (struct(kept.shape, BF16),),
-        [pair],
-        rows * width,
-        aliases={1: 0},
+        (kept, a, b, above),
+        [
+            pl.BlockSpec((tall, width), lambda j, o: (j, 0)),
+            fixed((tall, width)),
+            fixed((tall, width)),
+            pl.BlockSpec(memory_space=pl.ANY),
+        ],
+        (struct(above.shape, BF16),),
+        [pl.BlockSpec((tall, width), lambda j, o: (2 + j, 0))],
+        tall * width,
+        aliases={4: 0},
     )[0]
 
 
@@ -546,31 +592,26 @@
     along, inside, down, tail = decay_call(decay_rate, quarter)
     tail = tail[:, 0]
     pos = lax.axis_index("seq")
-    core = pos % 2
-    n_chips = n_seq // 2
+    core, chip = pos % 2, pos // 2
     swap = functools.partial(lax.ppermute, axis_name="seq", perm=[(i, i ^ 1) for i in range(n_seq)])
-
-    def later(x, step):
-        return lax.ppermute(x, "seq", perm=[(i, i + 2 * step) for i in range(n_seq - 2 * step)])
-
     tail_other = swap(tail)
-    tail_chip = tail + tail_other
-    tails = [later(tail_chip, s) for s in range(1, n_chips)]
 
     if square:
-        q0, q1 = tokens[:quarter], tokens[quarter : 2 * quarter]
-        x0, y1 = over_x(q0), over_y(q1)
-        acc = part_call(places, (0,), [(tokens,)], w_qkv, 2 * quarter, 1, cols)
-        rest = after(tokens, acc)
-        q2, q3 = rest[2 * quarter : 3 * quarter], rest[3 * quarter :]
-        x1, y0 = over_x(after(q1, acc)), over_y(after(q0, acc))
+        q0, q1 = cut_call(tokens, 0)
+        x0, y1, x1, y0 = over_x(q0), over_y(q1), over_x(q1), over_y(q0)
+        acc = part_call(places, (0,), [(tokens,)], w_qkv, rows, cols)
+        q2, q3 = cut_call(after(tokens, acc), 2)
         fy0, fx1 = over_y(x0), over_x(y1)
-        x2, y3 = over_x(after(q2, x1, y0, *tails)), over_y(after(q3, x1, y0, *tails))
-        x3, y2 = over_x(after(q3, fy0, fx1)), over_y(after(q2, fy0, fx1))
+        x2, y3 = over_x(after(q2, x1, y0)), over_y(after(q3, x1, y0))
+        acc_a = part_call(
+            places, (1, 2), [(x0, x1), (y0, y1)], w_qkv, 2 * quarter, cols, before=acc, at=0
+        )
+        x3, y2 = over_x(after(q3, fy0, fx1, acc_a)), over_y(after(q2, fy0, fx1, acc_a))
         query_a, within_a, state = first_call(
             places,
-            (0, 1, 2, 3),
-            [(tokens,), (x0, x1), (y0, y1), (fy0, fx1)],
+            (3,),
+            [(fy0, fx1)],
+            (acc_a,),
             w_qkv,
             along,
             inside,
@@ -580,29 +621,17 @@
             group,
         )
         fy2, fx3 = over_y(after(x2, state)), over_x(after(y3, state))
-        acc = part_call(
-            places, (1, 2), [(x2, x3), (y2, y3)], w_qkv, 2 * quarter, 0, cols, before=acc
+        acc_b = part_call(
+            places, (1, 2), [(x2, x3), (y2, y3)], w_qkv, 2 * quarter, cols, before=acc, at=1
         )
         far = (fy2, fx3)
         k, v, mid, state, sent = state_call(
-            places, far, w_qkv, acc, inside, state, quarter, group
-        )
-        query_b, within_b = later_call(
-            places, far, w_qkv, acc, k, v, along, inside, mid, group
+            places, far, w_qkv, acc_b, inside, state, quarter, group
         )
     else:
         gathered = lax.all_gather(tokens, "head", axis=1, tiled=True)
         query, within, state = first_call(
-            places,
-            (),
-            [(gathered,)],
-            w_qkv,
-            along,
-            inside,
-            rows,
-            quarter,
-            size,
-            group,
+            places, (), [(gathered,)], (), w_qkv, along, inside, rows, quarter, size, group
         )
         sent = state.astype(BF16)
 
@@ -616,18 +645,21 @@
     def mine(x):
         return lax.dynamic_slice_in_dim(x, core * share, share, 0)
 
-    chip_state = (
-        jnp.exp(-mine(tail_second))[:, None, None] * mine(first) + mine(second)
-    ).astype(BF16)
-    gap = jnp.zeros((share,), F32)
-    chip_entering = jnp.zeros((share, size, size), F32)
-    shifted = [later(chip_state, s) for s in range(1, n_chips)]
-    if square:
-        shifted = lax.optimization_barrier((*shifted, query_b, within_b))[: n_chips - 1]
-    for s in range(1, n_chips):
-        chip_entering += jnp.exp(-gap)[:, None, None] * shifted[s - 1].astype(F32)
-        gap += mine(tails[s - 1])
-    chip_entering += jnp.exp(-gap)[:, None, None] * mine(prior_state)
+    chip_state = jnp.exp(-mine(tail_second))[:, None, None] * mine(first) + mine(second)
+    chip_decay = jnp.exp(-mine(tail + tail_other))[:, None, None]
+    chip_entering = mine(prior_state)
+    hops = n_seq // 2 - 1
+    for hop in range(hops):
+        leaving = (chip_decay * chip_entering + chip_state).astype(BF16)
+        arriving = lax.ppermute(
+            leaving, "seq", perm=[(2 * hop + c, 2 * hop + 2 + c) for c in range(2)]
+        )
+        if square and hop == hops // 2:
+            query_b, within_b = later_call(
+                places, far, w_qkv, acc_b, k, v, along, inside, after(mid, leaving), group
+            )
+            arriving = after(arriving, query_b, within_b)
+        chip_entering = jnp.where(chip == hop + 1, arriving.astype(F32), chip_entering)
     there = swap(chip_entering.astype(BF16)).astype(F32)
     entering = jnp.concatenate(
         [jnp.where(core == 0, chip_entering, there), jnp.where(core == 0, there, chip_entering)]
@@ -637,31 +669,40 @@
     ).astype(BF16)
 
     if not square:
-        normed = head_call(places, 0, query, within, entering, down, w_out, width, quarter)[0]
-        partial = dot(normed, w_out).astype(BF16)
+        halves = [
+            head_call(
+                places,
+                0,
+                query[r * rows // 2 : (r + 1) * rows // 2],
+                within[r * rows // 2 : (r + 1) * rows // 2],
+                entering,
+                down,
+                w_out,
+                width,
+                r,
+            )[0]
+            for r in range(2)
+        ]
+        partial = dot(jnp.concatenate(halves), w_out).astype(BF16)
         return lax.psum_scatter(partial, "head", scatter_dimension=1, tiled=True)
 
-    na, far0, far1 = head_call(
-        places, 3, query_a, within_a, entering, down, w_out, width, quarter
-    )
+    na, far0, far1 = head_call(places, 3, query_a, within_a, entering, down, w_out, width, 0)
     far0, far1 = over_x(far0), over_y(far1)
-    nb, far2, far3, near_x, near_y = near_call(
+    nb, far2, far3, near_x, near_y = heads_near_call(
         places, query_b, within_b, entering, down, na, w_out, width
     )
+    near_x, near_y = over_x(after(near_x, far0, far1)), over_y(after(near_y, far0, far1))
     far2, far3 = over_x(far2), over_y(far3)
-    near_x, near_y = over_x(after(near_x, far0, far1)), over_y(after(near_y, far0, far1))
-
-    def out(block, *parts, arrived=()):
-        return out_call(places, block, parts, quarter, w_out, width, arrived)
-
-    n0, n1, n2, n3 = (na, 0), (na, 1), (nb, 0), (nb, 1)
-    sum_x1 = over_x(out(1, n1, arrived=[(far1, (0,))]))
-    sum_y0 = over_y(out(2, n0, arrived=[(far0, (0,))]))
-    sum_x3 = over_x(out(1, n3, arrived=[(far3, (0,))]))
-    sum_y2 = over_y(out(2, n2, arrived=[(far2, (0,))]))
-    kept = out(0, n0, n1, n2, n3, arrived=[(near_x, (0, 2)), (near_y, (1, 3))])
-    kept = last_call(kept, sum_y0, sum_x1, 0)
-    return last_call(kept, sum_y2, sum_x3, 1)
+    sum1, sum0 = pair_call(places, after(na, near_x, near_y), far1, far0, w_out, width)
+    far2, far3 = after(far2, sum1), after(far3, sum1)
+    sum1, sum0 = over_x(sum1), over_y(sum0)
+    sum3, sum2 = pair_call(places, nb, far3, far2, w_out, width)
+    sum3, sum2 = over_x(sum3), over_y(sum2)
+    below = own_call(places, nb, ((near_x, 1),), ((near_y, 1),), w_out, width, 1)
+    above = own_call(
+        places, na, ((near_x, 0), (sum0, 0)), ((near_y, 0), (sum1, 0)), w_out, width, 2
+    )
+    return last_call(below, sum2, sum3, above)
 
 
 def solution(mesh):

time: 203 us -> 267 us (1.32); the launches traced: 199 us -> 266 us
  Pallas kernels: 92.9 us -> 184 us
  starting transfers between devices: 46.8 us -> 25.6 us
  local copies, waits for them, and re-layouts: 16.7 us -> 7.81 us
  waiting for transfers between devices: 39.9 us -> 44.1 us
    pallas_call x0 -> x2, Pallas kernels: none -> 65.8 us  [cut_call(): pl.pallas_call(functools.partial(cut_kernel, first), out_shape=(half, hal...]
    pallas_call x15 -> x14, Pallas kernels: 92.9 us -> 118 us  [call(): pl.pallas_call(kernel, out_shape=tuple(outs), grid_spec=pltpu.PrefetchSca...]
    ppermute x1, waiting for transfers between devices: 0.01 us -> 22.3 us  [local(): over_y(after(near_y, far0, far1))]
    ppermute x18 -> x15, starting transfers between devices: 35.4 us -> 16.2 us  [the longest x4 4.12 us: local(): x0, y1, x1, y0 = (over_x(q0), over_y(q1), over_x(q1), over_y(q0))]
    ppermute x2, waiting for transfers between devices: 21.8 us -> 4.3 us  [local(): far2, far3 = (over_x(far2), over_y(far3))]
    ppermute x2, waiting for transfers between devices: 0.01 us -> 7.18 us  [local(): fy0, fx1 = (over_y(x0), over_x(y1))]
    unnamed x52 -> x42, local copies, waits for them, and re-layouts: 14.1 us -> 7 us
    ppermute x18 -> x15, waiting for transfers between devices: 11.5 us -> 6.06 us  [the longest x3 5.55 us: local(): lax.ppermute(leaving, 'seq', perm=[(2 * hop + c, 2 * hop + 2 + c) for c i...]
  transfers between devices with their start and end apart: 31 -> 28, of which waited for: 11 -> 10; matrix products, arithmetic and copies ran while one was open for 0% -> 1% of each run, Pallas kernels for 39% -> 53%
where the time goes in v3:
time: 267 us; the launch traced here: 266 us
  Pallas kernels  184 us (69%)
  waiting for transfers between devices  44.1 us (17%)
  starting transfers between devices  25.6 us (10%)
  local copies, waits for them, and re-layouts  7.81 us (3%)
  other arithmetic  4.12 us (2%)
    pallas_call x14, Pallas kernels, call(): pl.pallas_call(kernel, out_shape=tuple(outs), grid_spec=pltpu.PrefetchSca...  118 us
    pallas_call x2, Pallas kernels, cut_call(): pl.pallas_call(functools.partial(cut_kernel, first), out_shape=(half, hal...  65.8 us
    ppermute x1, waiting for transfers between devices, local(): over_y(after(near_y, far0, far1))  22.3 us
    ppermute x2, waiting for transfers between devices, local(): fy0, fx1 = (over_y(x0), over_x(y1))  7.18 us
    unnamed x42, local copies, waits for them, and re-layouts  7 us
    ppermute x3, waiting for transfers between devices, local(): lax.ppermute(leaving, 'seq', perm=[(2 * hop + c, 2 * hop + 2 + c) for c i...  5.55 us
  transfers between devices with their start and end apart: 28, of which 10 were waited for; matrix products, arithmetic and copies ran while one was open for 1% of the time, Pallas kernels for 53%

profile of v3, /device:TPU:8, one launch (start us, length us, event | category | flops | bytes accessed | tf_op | source)
XLA Modules:
  0.0 265.9 jit_solution(11709805087021591985)
XLA Ops:
  0.0 32.9 %cut.3 = (bf16[256,1024]{1,0:T(8,128)(2,1)}, bf16[256,1024]{1,0:T(8,128)(2,1)}) custom-call(bf16[1024,1024]{1,0:T(8,128)(2,1)} %x_ref.2), custom_call_target="tpu_custom_call" | custom-call | bytes 2097152 | tf_op jit(solution)/shard_map/cut/pallas_call | solution.py:68
  32.9 1.6 collective-permute-start.1
  34.5 1.5 collective-permute-start.3
  37.6 12.7 %part.3.refs_6_ = f32[3,1024,1024]{2,1,0:T(8,128)} custom-call(s32[4]{0:T(128)} %pad_add_fusion._, bf16[1024,1024]{1,0:T(8,128)(2,1)} %x_ref.2, bf16[3,4096,1024]{2,1,0:T(8,128)(2,1)} %refs_2_.5), custom_call_target="tpu_custom_call" | custom-call | flops 6442450944 | bytes 39845888 | tf_op jit(solution)/shard_map/part/pallas_call | solution.py:34
  50.3 32.9 %cut.2 = (bf16[256,1024]{1,0:T(8,128)(2,1)}, bf16[256,1024]{1,0:T(8,128)(2,1)}) custom-call(bf16[1024,1024]{1,0:T(8,128)(2,1)} %x_ref.2), custom_call_target="tpu_custom_call" | custom-call | bytes 2097152 | tf_op jit(solution)/shard_map/cut/pallas_call | solution.py:68
  83.3 1.6 collective-permute-start.8
  84.9 1.5 collective-permute-start.2
  87.7 13.8 %part.4.refs_3_ = f32[3,512,1024]{2,1,0:T(8,128)} custom-call(s32[4]{0:T(128)} %pad_add_fusion._, bf16[256,1024]{1,0:T(8,128)(2,1)} %copy-done.10, bf16[256,1024]{1,0:T(8,128)(2,1)} %copy-done.12, bf16[256,1024]{1,0:T(8,128)(2,1)} %copy-done.9, bf16[256,1024]{1,0:T(8,128)(2,1)} %copy-done.11, bf16[3,4096,1024]{2,1,0:T(8,128)(2,1)} %refs_2_.5, ...), custom_call_target="tpu_custom_call" | custom-call | flops 6442450944 | bytes 71303168 | tf_op jit(solution)/shard_map/part/pallas_call | solution.py:34
  101.5 5.8 %collective-permute-done.4.refs_0_ = bf16[256,1024]{1,0:T(8,128)(2,1)S(1)} collective-permute-done((bf16[256,1024]{1,0:T(8,128)(2,1)S(1)}, bf16[256,1024]{1,0:T(8,128)(2,1)S(1)}, u32[]{:S(2)}, u32[]{:S(2)}) %collective-permute-start.4) | collective-permute-done | bytes 524320 | tf_op jit(solution)/shard_map/ppermute | solution.py:604
  107.3 1.3 collective-permute-done.6.refs_1_
  109.7 1.5 collective-permute-start.10
  111.1 2.5 decay.1
  114.6 12.0 %first.1 = (bf16[512,1024]{1,0:T(8,128)(2,1)}, f32[512,1024]{1,0:T(8,128)}, f32[8,128,128]{2,1,0:T(8,128)}) custom-call(s32[4]{0:T(128)} %pad_add_fusion._, bf16[256,1024]{1,0:T(8,128)(2,1)} %copy-done.20, bf16[256,1024]{1,0:T(8,128)(2,1)} %collective-permute-done.6.refs_1_, bf16[3,4096,1024]{2,1,0:T(8,128)(2,1)} %refs_2_.5, f32[3,512,1024]{2,1,0:T(8,128)} %part.4.refs_3_, ...), custom_call_target="tpu_custom_call" | custom-call | flops 3221225472 | bytes 36241408 | tf_op jit(solution)/shard_map/first/pallas_call | solution.py:34
  129.9 13.8 %part.5.refs_4_.refs_5_.refs_3_ = f32[3,512,1024]{2,1,0:T(8,128)} custom-call(s32[4]{0:T(128)} %pad_add_fusion._, bf16[256,1024]{1,0:T(8,128)(2,1)} %copy-done.6, bf16[256,1024]{1,0:T(8,128)(2,1)} %copy-done.8, bf16[256,1024]{1,0:T(8,128)(2,1)} %copy-done.7, bf16[256,1024]{1,0:T(8,128)(2,1)} %copy-done.5, bf16[3,4096,1024]{2,1,0:T(8,128)(2,1)} %refs_2_.5, ...), custom_call_target="tpu_custom_call" | custom-call | flops 6442450944 | bytes 71303168 | tf_op jit(solution)/shard_map/part/pallas_call | solution.py:34
  145.3 8.8 %states.1 = (bf16[512,1024]{1,0:T(8,128)(2,1)}, bf16[512,1024]{1,0:T(8,128)(2,1)}, f32[2,8,128,128]{3,2,1,0:T(8,128)}, f32[8,128,128]{2,1,0:T(8,128)}, bf16[8,128,128]{2,1,0:T(8,128)(2,1)}) custom-call(s32[4]{0:T(128)} %pad_add_fusion._, bf16[256,1024]{1,0:T(8,128)(2,1)} %copy-done.3, bf16[256,1024]{1,0:T(8,128)(2,1)} %copy-done.2, ...), custom_call_target="tpu_custom_call" | custom-call | flops 2147483648 | bytes 68452352 | tf_op jit(solution)/shard_map/states/pallas_call | solution.py:34
  154.2 1.6 collective-permute-done.13
  158.1 1.3 collective-permute-start.14
  159.4 5.5 %collective-permute-done.14 = bf16[4,128,128]{2,1,0:T(8,128)(2,1)S(1)} collective-permute-done((bf16[4,128,128]{2,1,0:T(8,128)(2,1)S(1)}, bf16[4,128,128]{2,1,0:T(8,128)(2,1)S(1)}, u32[]{:S(2)}, u32[]{:S(2)}) %collective-permute-start.14) | collective-permute-done | bytes 131104 | tf_op jit(solution)/shard_map/ppermute | solution.py:654
  165.1 1.3 collective-permute-start.15
  166.4 9.4 %later.1 = (bf16[512,1024]{1,0:T(8,128)(2,1)}, f32[512,1024]{1,0:T(8,128)}) custom-call(s32[4]{0:T(128)} %pad_add_fusion._, bf16[256,1024]{1,0:T(8,128)(2,1)} %copy-done.3, bf16[256,1024]{1,0:T(8,128)(2,1)} %copy-done.2, bf16[3,4096,1024]{2,1,0:T(8,128)(2,1)} %refs_2_.5, f32[3,512,1024]{2,1,0:T(8,128)} %part.5.refs_4_.refs_5_.refs_3_, ...), custom_call_target="tpu_custom_call" | custom-call | flops 1879048192 | bytes 38862848 | tf_op jit(solution)/shard_map/later/pallas_call | solution.py:34
  176.8 1.3 collective-permute-done.17
  179.0 8.9 %heads.1 = (bf16[512,1024]{1,0:T(8,128)(2,1)}, bf16[256,1024]{1,0:T(8,128)(2,1)}, bf16[256,1024]{1,0:T(8,128)(2,1)}) custom-call(s32[4]{0:T(128)} %pad_add_fusion._, bf16[512,1024]{1,0:T(8,128)(2,1)} %get-tuple-element.74.q_ref, f32[512,1024]{1,0:T(8,128)} %get-tuple-element.75.within_ref, bf16[8,128,128]{2,1,0:T(8,128)(2,1)} %select_convert_fusion.entering_ref, ...), custom_call_target="tpu_custom_call" | custom-call | flops 1 | bytes 1 | tf_op jit(solution)/shard_map/heads/pallas_call | solution.py:34
  187.9 1.4 collective-permute-start.18
  190.3 12.6 %heads_near.1 = (bf16[512,1024]{1,0:T(8,128)(2,1)}, bf16[256,1024]{1,0:T(8,128)(2,1)}, bf16[256,1024]{1,0:T(8,128)(2,1)}, bf16[512,1024]{1,0:T(8,128)(2,1)}, bf16[512,1024]{1,0:T(8,128)(2,1)}) custom-call(s32[4]{0:T(128)} %pad_add_fusion._, bf16[512,1024]{1,0:T(8,128)(2,1)} %get-tuple-element.70.q_ref, f32[512,1024]{1,0:T(8,128)} %get-tuple-element.71.within_ref, ...), custom_call_target="tpu_custom_call" | custom-call | flops 1 | bytes 1 | tf_op jit(solution)/shard_map/heads_near/pallas_call | solution.py:34
  204.8 1.5 collective-permute-start.23
  207.3 22.3 %collective-permute-done.21.refs_1_.refs_2_ = bf16[512,1024]{1,0:T(8,128)(2,1)S(1)} collective-permute-done((bf16[512,1024]{1,0:T(8,128)(2,1)}, bf16[512,1024]{1,0:T(8,128)(2,1)S(1)}, u32[]{:S(2)}, u32[]{:S(2)}) %collective-permute-start.21) | collective-permute-done | bytes 1048608 | tf_op jit(solution)/shard_map/ppermute | solution.py:694
  230.5 5.3 %sum_pair.2 = (bf16[256,1024]{1,0:T(8,128)(2,1)}, bf16[256,1024]{1,0:T(8,128)(2,1)}) custom-call(s32[4]{0:T(128)} %pad_add_fusion._, bf16[512,1024]{1,0:T(8,128)(2,1)} %get-tuple-element.85.first_ref.normed_ref, bf16[256,1024]{1,0:T(8,128)(2,1)} %copy-done.18, bf16[256,1024]{1,0:T(8,128)(2,1)} %copy-done.17, bf16[1024,4096]{1,0:T(8,128)(2,1)} %w_ref.11), custom_call_target="tpu_custom_call" | custom-call | flops 1 | bytes 1 | tf_op jit(solution)/shard_map/sum_pair/pallas_call | solution.py:34
  237.5 4.3 %collective-permute-done.23.y_ref = bf16[256,1024]{1,0:T(8,128)(2,1)S(1)} collective-permute-done((bf16[256,1024]{1,0:T(8,128)(2,1)}, bf16[256,1024]{1,0:T(8,128)(2,1)S(1)}, u32[]{:S(2)}, u32[]{:S(2)}) %collective-permute-start.23) | collective-permute-done | bytes 524320 | tf_op jit(solution)/shard_map/ppermute | solution.py:695
  242.6 5.3 %sum_pair.3 = (bf16[256,1024]{1,0:T(8,128)(2,1)}, bf16[256,1024]{1,0:T(8,128)(2,1)}) custom-call(s32[4]{0:T(128)} %pad_add_fusion._, bf16[512,1024]{1,0:T(8,128)(2,1)} %get-tuple-element.77.normed_ref, bf16[256,1024]{1,0:T(8,128)(2,1)} %collective-permute-done.22.x_ref, bf16[256,1024]{1,0:T(8,128)(2,1)} %copy-done.19, bf16[1024,4096]{1,0:T(8,128)(2,1)} %w_ref.11), custom_call_target="tpu_custom_call" | custom-call | flops 1 | bytes 1 | tf_op jit(solution)/shard_map/sum_pair/pallas_call | solution.py:34
  249.6 5.1 %own_block.2.kept_ref = bf16[512,1024]{1,0:T(8,128)(2,1)} custom-call(s32[4]{0:T(128)} %pad_add_fusion._, bf16[512,1024]{1,0:T(8,128)(2,1)} %get-tuple-element.77.normed_ref, bf16[1024,4096]{1,0:T(8,128)(2,1)} %w_ref.11, bf16[512,1024]{1,0:T(8,128)(2,1)} %copy-done.1, bf16[512,1024]{1,0:T(8,128)(2,1)} %copy-done), custom_call_target="tpu_custom_call" | custom-call | flops 1 | bytes 1 | tf_op jit(solution)/shard_map/own_block/pallas_call | solution.py:34
  256.3 5.5 %own_block.3.above_ref = bf16[1024,1024]{1,0:T(8,128)(2,1)} custom-call(s32[4]{0:T(128)} %pad_add_fusion._, bf16[512,1024]{1,0:T(8,128)(2,1)} %get-tuple-element.85.first_ref.normed_ref, bf16[1024,4096]{1,0:T(8,128)(2,1)} %w_ref.11, bf16[512,1024]{1,0:T(8,128)(2,1)} %copy-done.1, bf16[256,1024]{1,0:T(8,128)(2,1)} %copy-done.13, bf16[512,1024]{1,0:T(8,128)(2,1)} %copy-done, ...), custom_call_target="tpu_custom_call" | custom-call | flops 1 | bytes 1 | tf_op jit(solution)/shard_map/own_block/pallas_call | solution.py:34
  263.4 2.4 last_add.1
  (94 shorter events, 26.2 us)
Async XLA Ops:
  32.9 50.4 %collective-permute-start.1 = (bf16[256,1024]{1,0:T(8,128)(2,1)}, bf16[256,1024]{1,0:T(8,128)(2,1)S(1)}, u32[]{:S(2)}, u32[]{:S(2)}) collective-permute-start(bf16[256,1024]{1,0:T(8,128)(2,1)} %get-tuple-element.52), channel_id=1, source_target_pairs={{0,2},{1,3},{2,0},{3,1},{4,6},{5,7},{6,4},{7,5},{8,10},{9,11},{10,... | collective-permute-start | bytes 1572872 | tf_op jit(solution)/shard_map/ppermute | solution.py:601
  34.5 51.9 %collective-permute-start.3 = (bf16[256,1024]{1,0:T(8,128)(2,1)}, bf16[256,1024]{1,0:T(8,128)(2,1)S(1)}, u32[]{:S(2)}, u32[]{:S(2)}) collective-permute-start(bf16[256,1024]{1,0:T(8,128)(2,1)} %get-tuple-element.52), channel_id=1, source_target_pairs={{0,1},{1,0},{2,3},{3,2},{4,5},{5,4},{6,7},{7,6},{8,9},{9,8},{10,11... | collective-permute-start | bytes 1572872 | tf_op jit(solution)/shard_map/ppermute | solution.py:601
  36.0 47.3 %collective-permute-start = (bf16[256,1024]{1,0:T(8,128)(2,1)}, bf16[256,1024]{1,0:T(8,128)(2,1)S(1)}, u32[]{:S(2)}, u32[]{:S(2)}) collective-permute-start(bf16[256,1024]{1,0:T(8,128)(2,1)} %get-tuple-element.51), channel_id=1, source_target_pairs={{0,1},{1,0},{2,3},{3,2},{4,5},{5,4},{6,7},{7,6},{8,9},{9,8},{10,11... | collective-permute-start | bytes 1572872 | tf_op jit(solution)/shard_map/ppermute | solution.py:601
  36.5 50.4 %collective-permute-start.5 = (bf16[256,1024]{1,0:T(8,128)(2,1)}, bf16[256,1024]{1,0:T(8,128)(2,1)S(1)}, u32[]{:S(2)}, u32[]{:S(2)}) collective-permute-start(bf16[256,1024]{1,0:T(8,128)(2,1)} %get-tuple-element.51), channel_id=1, source_target_pairs={{0,2},{1,3},{2,0},{3,1},{4,6},{5,7},{6,4},{7,5},{8,10},{9,11},{10,... | collective-permute-start | bytes 1572872 | tf_op jit(solution)/shard_map/ppermute | solution.py:601
  83.3 43.3 %collective-permute-start.8 = (bf16[256,1024]{1,0:T(8,128)(2,1)}, bf16[256,1024]{1,0:T(8,128)(2,1)S(1)}, u32[]{:S(2)}, u32[]{:S(2)}) collective-permute-start(bf16[256,1024]{1,0:T(8,128)(2,1)} %get-tuple-element.61), channel_id=1, source_target_pairs={{0,2},{1,3},{2,0},{3,1},{4,6},{5,7},{6,4},{7,5},{8,10},{9,11},{10,... | collective-permute-start | bytes 1572872 | tf_op jit(solution)/shard_map/ppermute | solution.py:605
  84.9 42.3 %collective-permute-start.2 = (bf16[256,1024]{1,0:T(8,128)(2,1)}, bf16[256,1024]{1,0:T(8,128)(2,1)S(1)}, u32[]{:S(2)}, u32[]{:S(2)}) collective-permute-start(bf16[256,1024]{1,0:T(8,128)(2,1)} %get-tuple-element.62), channel_id=1, source_target_pairs={{0,1},{1,0},{2,3},{3,2},{4,5},{5,4},{6,7},{7,6},{8,9},{9,8},{10,11... | collective-permute-start | bytes 1572872 | tf_op jit(solution)/shard_map/ppermute | solution.py:605
  86.4 21.0 %collective-permute-start.4 = (bf16[256,1024]{1,0:T(8,128)(2,1)S(1)}, bf16[256,1024]{1,0:T(8,128)(2,1)S(1)}, u32[]{:S(2)}, u32[]{:S(2)}) collective-permute-start(bf16[256,1024]{1,0:T(8,128)(2,1)S(1)} %collective-permute-done.3.refs_0_), channel_id=1, source_target_pairs={{0,2},{1,3},{2,0},{3,1},{4,6},{5,7},{6,4},{7,5},{8,10},{9,11},{10,... | collective-permute-start | bytes 1572872 | tf_op jit(solution)/shard_map/ppermute | solution.py:604
  86.9 21.8 %collective-permute-start.6 = (bf16[256,1024]{1,0:T(8,128)(2,1)S(1)}, bf16[256,1024]{1,0:T(8,128)(2,1)}, u32[]{:S(2)}, u32[]{:S(2)}) collective-permute-start(bf16[256,1024]{1,0:T(8,128)(2,1)S(1)} %collective-permute-done.5.refs_3_), channel_id=1, source_target_pairs={{0,1},{1,0},{2,3},{3,2},{4,5},{5,4},{6,7},{7,6},{8,9},{9,8},{10,11... | collective-permute-start | bytes 1572872 | tf_op jit(solution)/shard_map/ppermute | solution.py:604
  108.7 19.6 %collective-permute-start.11 = (bf16[256,1024]{1,0:T(8,128)(2,1)}, bf16[256,1024]{1,0:T(8,128)(2,1)S(1)}, u32[]{:S(2)}, u32[]{:S(2)}) collective-permute-start(bf16[256,1024]{1,0:T(8,128)(2,1)} %get-tuple-element.62), channel_id=1, source_target_pairs={{0,2},{1,3},{2,0},{3,1},{4,6},{5,7},{6,4},{7,5},{8,10},{9,11},{10,... | collective-permute-start | bytes 1572872 | tf_op jit(solution)/shard_map/ppermute | solution.py:609
  109.7 18.6 %collective-permute-start.10 = (bf16[256,1024]{1,0:T(8,128)(2,1)}, bf16[256,1024]{1,0:T(8,128)(2,1)S(1)}, u32[]{:S(2)}, u32[]{:S(2)}) collective-permute-start(bf16[256,1024]{1,0:T(8,128)(2,1)} %get-tuple-element.61), channel_id=1, source_target_pairs={{0,1},{1,0},{2,3},{3,2},{4,5},{5,4},{6,7},{7,6},{8,9},{9,8},{10,11... | collective-permute-start | bytes 1572872 | tf_op jit(solution)/shard_map/ppermute | solution.py:609
  114.5 39.7 %collective-permute-start.12 = (f32[8]{0:T(128)S(1)}, f32[8]{0:T(128)S(1)}, u32[]{:S(2)}, u32[]{:S(2)}) collective-permute-start(f32[8]{0:T(128)S(1)} %slice_reduce_fusion), channel_id=1, source_target_pairs={{0,4},{4,0},{8,12},{12,8},{16,20},{20,16},{24,28},{28,24},{1,5},{5... | collective-permute-start | bytes 104 | tf_op jit(solution)/shard_map/ppermute | solution.py:597
  126.6 17.1 %collective-permute-start.9 = (bf16[256,1024]{1,0:T(8,128)(2,1)S(1)}, bf16[256,1024]{1,0:T(8,128)(2,1)S(1)}, u32[]{:S(2)}, u32[]{:S(2)}) collective-permute-start(bf16[256,1024]{1,0:T(8,128)(2,1)S(1)} %collective-permute-done.8.refs_3_), channel_id=1, source_target_pairs={{0,1},{1,0},{2,3},{3,2},{4,5},{5,4},{6,7},{7,6},{8,9},{9,8},{10,11... | collective-permute-start | bytes 1572872 | tf_op jit(solution)/shard_map/ppermute | solution.py:623
  127.2 16.5 %collective-permute-start.7 = (bf16[256,1024]{1,0:T(8,128)(2,1)S(1)}, bf16[256,1024]{1,0:T(8,128)(2,1)S(1)}, u32[]{:S(2)}, u32[]{:S(2)}) collective-permute-start(bf16[256,1024]{1,0:T(8,128)(2,1)S(1)} %collective-permute-done.2.refs_0_), channel_id=1, source_target_pairs={{0,2},{1,3},{2,0},{3,1},{4,6},{5,7},{6,4},{7,5},{8,10},{9,11},{10,... | collective-permute-start | bytes 1572872 | tf_op jit(solution)/shard_map/ppermute | solution.py:623
  154.1 1.8 collective-permute-start.13
  158.1 6.9 %collective-permute-start.14 = (bf16[4,128,128]{2,1,0:T(8,128)(2,1)S(1)}, bf16[4,128,128]{2,1,0:T(8,128)(2,1)S(1)}, u32[]{:S(2)}, u32[]{:S(2)}) collective-permute-start(bf16[4,128,128]{2,1,0:T(8,128)(2,1)S(1)} %get-tuple-element.95), channel_id=1, source_target_pairs={{0,8},{4,12},{1,9},{5,13},{2,10},{6,14},{3,11},{7,15}} | collective-permute-start | bytes 393224 | tf_op jit(solution)/shard_map/ppermute | solution.py:654
  165.1 10.7 %collective-permute-start.15 = (bf16[4,128,128]{2,1,0:T(8,128)(2,1)S(1)}, bf16[4,128,128]{2,1,0:T(8,128)(2,1)S(1)}, u32[]{:S(2)}, u32[]{:S(2)}) collective-permute-start(bf16[4,128,128]{2,1,0:T(8,128)(2,1)S(1)} %add_convert_fusion.1), channel_id=1, source_target_pairs={{8,16},{12,20},{9,17},{13,21},{10,18},{14,22},{11,19},{15,23}} | collective-permute-start | bytes 393224 | tf_op jit(solution)/shard_map/ppermute | solution.py:654
  175.9 0.7 collective-permute-start.16
  176.7 1.4 collective-permute-start.17
  187.9 15.0 %collective-permute-start.18 = (bf16[256,1024]{1,0:T(8,128)(2,1)}, bf16[256,1024]{1,0:T(8,128)(2,1)S(1)}, u32[]{:S(2)}, u32[]{:S(2)}) collective-permute-start(bf16[256,1024]{1,0:T(8,128)(2,1)} %get-tuple-element.79), channel_id=1, source_target_pairs={{0,1},{1,0},{2,3},{3,2},{4,5},{5,4},{6,7},{7,6},{8,9},{9,8},{10,11... | collective-permute-start | bytes 1572872 | tf_op jit(solution)/shard_map/ppermute | solution.py:690
  189.3 13.9 %collective-permute-start.19 = (bf16[256,1024]{1,0:T(8,128)(2,1)}, bf16[256,1024]{1,0:T(8,128)(2,1)S(1)}, u32[]{:S(2)}, u32[]{:S(2)}) collective-permute-start(bf16[256,1024]{1,0:T(8,128)(2,1)} %get-tuple-element.80), channel_id=1, source_target_pairs={{0,2},{1,3},{2,0},{3,1},{4,6},{5,7},{6,4},{7,5},{8,10},{9,11},{10,... | collective-permute-start | bytes 1572872 | tf_op jit(solution)/shard_map/ppermute | solution.py:690
  202.9 27.7 %copy-start.17 = (bf16[256,1024]{1,0:T(8,128)(2,1)}, bf16[256,1024]{1,0:T(8,128)(2,1)S(1)}, u32[]{:S(2)}) copy-start(bf16[256,1024]{1,0:T(8,128)(2,1)S(1)} %collective-permute-done.18.y_ref) | copy-start | bytes 1572868
  203.2 27.3 %copy-start.18 = (bf16[256,1024]{1,0:T(8,128)(2,1)}, bf16[256,1024]{1,0:T(8,128)(2,1)S(1)}, u32[]{:S(2)}) copy-start(bf16[256,1024]{1,0:T(8,128)(2,1)S(1)} %collective-permute-done.19.x_ref) | copy-start | bytes 1572868
  203.2 26.3 %collective-permute-start.21 = (bf16[512,1024]{1,0:T(8,128)(2,1)}, bf16[512,1024]{1,0:T(8,128)(2,1)S(1)}, u32[]{:S(2)}, u32[]{:S(2)}) collective-permute-start(bf16[512,1024]{1,0:T(8,128)(2,1)} %get-tuple-element.83), channel_id=1, source_target_pairs={{0,2},{1,3},{2,0},{3,1},{4,6},{5,7},{6,4},{7,5},{8,10},{9,11},{10,... | collective-permute-start | bytes 3145736 | tf_op jit(solution)/shard_map/ppermute | solution.py:694
  204.2 26.3 %collective-permute-start.20 = (bf16[512,1024]{1,0:T(8,128)(2,1)}, bf16[512,1024]{1,0:T(8,128)(2,1)S(1)}, u32[]{:S(2)}, u32[]{:S(2)}) collective-permute-start(bf16[512,1024]{1,0:T(8,128)(2,1)} %get-tuple-element.81), channel_id=1, source_target_pairs={{0,1},{1,0},{2,3},{3,2},{4,5},{5,4},{6,7},{7,6},{8,9},{9,8},{10,11... | collective-permute-start | bytes 3145736 | tf_op jit(solution)/shard_map/ppermute | solution.py:694
  204.8 37.0 %collective-permute-start.23 = (bf16[256,1024]{1,0:T(8,128)(2,1)}, bf16[256,1024]{1,0:T(8,128)(2,1)S(1)}, u32[]{:S(2)}, u32[]{:S(2)}) collective-permute-start(bf16[256,1024]{1,0:T(8,128)(2,1)} %get-tuple-element.88), channel_id=1, source_target_pairs={{0,1},{1,0},{2,3},{3,2},{4,5},{5,4},{6,7},{7,6},{8,9},{9,8},{10,11... | collective-permute-start | bytes 1572872 | tf_op jit(solution)/shard_map/ppermute | solution.py:695
  206.2 35.5 %collective-permute-start.22 = (bf16[256,1024]{1,0:T(8,128)(2,1)}, bf16[256,1024]{1,0:T(8,128)(2,1)}, u32[]{:S(2)}, u32[]{:S(2)}) collective-permute-start(bf16[256,1024]{1,0:T(8,128)(2,1)} %get-tuple-element.84), channel_id=1, source_target_pairs={{0,2},{1,3},{2,0},{3,1},{4,6},{5,7},{6,4},{7,5},{8,10},{9,11},{10,... | collective-permute-start | bytes 1572872 | tf_op jit(solution)/shard_map/ppermute | solution.py:695
  229.6 18.3 %copy-start = (bf16[512,1024]{1,0:T(8,128)(2,1)}, bf16[512,1024]{1,0:T(8,128)(2,1)S(1)}, u32[]{:S(2)}) copy-start(bf16[512,1024]{1,0:T(8,128)(2,1)S(1)} %collective-permute-done.21.refs_1_.refs_2_) | copy-start | bytes 3145732
  230.5 17.3 %copy-start.1 = (bf16[512,1024]{1,0:T(8,128)(2,1)}, bf16[512,1024]{1,0:T(8,128)(2,1)S(1)}, u32[]{:S(2)}) copy-start(bf16[512,1024]{1,0:T(8,128)(2,1)S(1)} %collective-permute-done.20.refs_0_) | copy-start | bytes 3145732
  235.8 18.9 %collective-permute-start.26 = (bf16[256,1024]{1,0:T(8,128)(2,1)}, bf16[256,1024]{1,0:T(8,128)(2,1)S(1)}, u32[]{:S(2)}, u32[]{:S(2)}) collective-permute-start(bf16[256,1024]{1,0:T(8,128)(2,1)} %get-tuple-element.92), channel_id=1, source_target_pairs={{0,2},{1,3},{2,0},{3,1},{4,6},{5,7},{6,4},{7,5},{8,10},{9,11},{10,... | collective-permute-start | bytes 1572872 | tf_op jit(solution)/shard_map/ppermute | solution.py:698
  236.9 17.8 %collective-permute-start.27 = (bf16[256,1024]{1,0:T(8,128)(2,1)}, bf16[256,1024]{1,0:T(8,128)(2,1)S(1)}, u32[]{:S(2)}, u32[]{:S(2)}) collective-permute-start(bf16[256,1024]{1,0:T(8,128)(2,1)} %get-tuple-element.86), channel_id=1, source_target_pairs={{0,1},{1,0},{2,3},{3,2},{4,5},{5,4},{6,7},{7,6},{8,9},{9,8},{10,11... | collective-permute-start | bytes 1572872 | tf_op jit(solution)/shard_map/ppermute | solution.py:698
  247.9 13.9 %collective-permute-start.24 = (bf16[256,1024]{1,0:T(8,128)(2,1)}, bf16[256,1024]{1,0:T(8,128)(2,1)S(1)}, u32[]{:S(2)}, u32[]{:S(2)}) collective-permute-start(bf16[256,1024]{1,0:T(8,128)(2,1)} %get-tuple-element.90), channel_id=1, source_target_pairs={{0,2},{1,3},{2,0},{3,1},{4,6},{5,7},{6,4},{7,5},{8,10},{9,11},{10,... | collective-permute-start | bytes 1572872 | tf_op jit(solution)/shard_map/ppermute | solution.py:700
  249.0 13.3 %collective-permute-start.25 = (bf16[256,1024]{1,0:T(8,128)(2,1)}, bf16[256,1024]{1,0:T(8,128)(2,1)S(1)}, u32[]{:S(2)}, u32[]{:S(2)}) collective-permute-start(bf16[256,1024]{1,0:T(8,128)(2,1)} %get-tuple-element.91), channel_id=1, source_target_pairs={{0,1},{1,0},{2,3},{3,2},{4,5},{5,4},{6,7},{7,6},{8,9},{9,8},{10,11... | collective-permute-start | bytes 1572872 | tf_op jit(solution)/shard_map/ppermute | solution.py:700
  (17 other events, 34.9 us)

commit v4 on v3

--- a/solution.py
+++ b/solution.py
@@ -1,4 +1,5 @@
 import functools
+import math
 
 import jax
 import jax.numpy as jnp
@@ -8,7 +9,7 @@
 from jax.sharding import PartitionSpec as P
 
 BF16, F32 = jnp.bfloat16, jnp.float32
-PARAMS = pltpu.CompilerParams(vmem_limit_bytes=60 * 1024 * 1024)
+MIB = 1024 * 1024
 
 
 def dot(a, b, contract=((1,), (0,))):
@@ -29,7 +30,7 @@
 
 def call(kernel, name, steps, scalars, ins, in_specs, outs, out_specs, flops, scratch=(), aliases=None, light=False):
     moved = sum(a.size * a.dtype.itemsize for a in ins) + sum(
-        o.size * jnp.dtype(o.dtype).itemsize for o in outs
+        math.prod(o.shape) * jnp.dtype(o.dtype).itemsize for o in outs
     )
     return pl.pallas_call(
         kernel,
@@ -42,7 +43,7 @@
             scratch_shapes=list(scratch),
         ),
         input_output_aliases=aliases or {},
-        compiler_params=PARAMS,
+        compiler_params=pltpu.CompilerParams(vmem_limit_bytes=(24 if light else 32) * MIB),
         cost_estimate=pl.CostEstimate(
             flops=1 if light else flops, bytes_accessed=1 if light else moved, transcendentals=0
         ),
@@ -50,30 +51,26 @@
     )(scalars, *ins)
 
 
-def cut_kernel(first, x_ref, a_ref, b_ref, sems):
+def cut_kernel(_, x_ref, a_ref, b_ref):
     tall = a_ref.shape[0]
-    copies = [
-        pltpu.make_async_copy(x_ref.at[pl.ds((first + i) * tall, tall)], out, sems.at[i])
-        for i, out in enumerate((a_ref, b_ref))
-    ]
-    for copy in copies:
-        copy.start()
-    for copy in copies:
-        copy.wait()
-
-
-def cut_call(x, first):
+    a_ref[...] = x_ref[:tall, :]
+    b_ref[...] = x_ref[tall:, :]
+
+
+def cut_call(x):
     rows, width = x.shape
-    half = struct((rows // 4, width), x.dtype)
-    return pl.pallas_call(
-        functools.partial(cut_kernel, first),
-        out_shape=(half, half),
-        in_specs=[pl.BlockSpec(memory_space=pl.ANY)],
-        out_specs=[pl.BlockSpec(memory_space=pl.ANY)] * 2,
-        scratch_shapes=[pltpu.SemaphoreType.DMA((2,))],
-        cost_estimate=pl.CostEstimate(flops=0, bytes_accessed=x.size * 2, transcendentals=0),
-        name="cut",
-    )(x)
+    quarter = (rows // 4, width)
+    return call(
+        cut_kernel,
+        "cut",
+        1,
+        jnp.zeros((1,), jnp.int32),
+        (x,),
+        [fixed((rows // 2, width))],
+        (struct(quarter, x.dtype),) * 2,
+        [fixed(quarter)] * 2,
+        1,
+    )
 
 
 def decay_kernel(chunk, _, rate_ref, along_ref, inside_ref, down_ref, tail_ref):
@@ -205,13 +202,43 @@
         + [pl.BlockSpec((3, rows, cols), lambda j, o: (0, 0, j)) for _ in before]
         + [fixed((heads, rows)), fixed((rows, heads))],
         (
-            struct((rows, heads * size), BF16),
-            struct((rows, heads * size), F32),
+            pltpu.HBM((rows, heads * size), BF16),
+            pltpu.HBM((rows, heads * size), F32),
             struct((heads, size, size), F32),
         ),
         [wide, wide, pl.BlockSpec((group, size, size), lambda j, o: (j, 0, 0))],
         2 * rows * 3 * heads * size * depth * len(pieces),
         scratch=[pltpu.VMEM((len(pieces), rows, depth), BF16)],
+    )
+
+
+def own_part_kernel(_, x_ref, w_ref, out_ref, c_ref, d_ref):
+    rows = x_ref.shape[0]
+    tall = c_ref.shape[0]
+
+    @pl.when(pl.program_id(0) == 0)
+    def _():
+        c_ref[...] = x_ref[rows - 2 * tall : rows - tall, :]
+        d_ref[...] = x_ref[rows - tall :, :]
+
+    for c in range(3):
+        out_ref[c] = dot(x_ref[...], w_ref[c])
+
+
+def own_part_call(places, tokens, w_qkv, cols):
+    rows, depth = tokens.shape
+    width = w_qkv.shape[2]
+    quarter = (rows // 4, depth)
+    return call(
+        own_part_kernel,
+        "own_part",
+        width // cols,
+        places,
+        (tokens, w_qkv),
+        [fixed((rows, depth)), pl.BlockSpec((3, depth, cols), lambda j, o: (0, o[0], j))],
+        (pltpu.HBM((3, rows, width), F32), struct(quarter, BF16), struct(quarter, BF16)),
+        [pl.BlockSpec((3, rows, cols), lambda j, o: (0, 0, j)), fixed(quarter), fixed(quarter)],
+        2 * rows * depth * width * 3,
     )
 
 
@@ -316,9 +343,9 @@
         + [pl.BlockSpec((1, rows, cols), lambda j, o, c=c: (c, 0, j)) for c in (1, 2)]
         + [pl.BlockSpec((rows, heads), lambda j, o: (1, 0)), small],
         (
-            struct((rows, width), BF16),
-            struct((rows, width), BF16),
-            struct((chunks, heads, size, size), F32),
+            pltpu.HBM((rows, width), BF16),
+            pltpu.HBM((rows, width), BF16),
+            pltpu.HBM((chunks, heads, size, size), F32),
             struct(state.shape, F32),
             struct(state.shape, BF16),
         ),
@@ -593,18 +620,34 @@
     tail = tail[:, 0]
     pos = lax.axis_index("seq")
     core, chip = pos % 2, pos // 2
+    n_chips = n_seq // 2
     swap = functools.partial(lax.ppermute, axis_name="seq", perm=[(i, i ^ 1) for i in range(n_seq)])
+
+    def hop(x, *pairs):
+        return lax.ppermute(
+            x, "seq", perm=[(2 * a + c, 2 * b + c) for a, b in pairs for c in range(2)]
+        )
+
     tail_other = swap(tail)
+    tail_chip = tail + tail_other
+    tail_below = hop(tail_chip, (2, 3)) if n_chips == 4 else tail_chip
 
     if square:
-        q0, q1 = cut_call(tokens, 0)
+        q0, q1 = cut_call(tokens)
         x0, y1, x1, y0 = over_x(q0), over_y(q1), over_x(q1), over_y(q0)
-        acc = part_call(places, (0,), [(tokens,)], w_qkv, rows, cols)
-        q2, q3 = cut_call(after(tokens, acc), 2)
+        acc, q2, q3 = own_part_call(places, tokens, w_qkv, cols)
         fy0, fx1 = over_y(x0), over_x(y1)
-        x2, y3 = over_x(after(q2, x1, y0)), over_y(after(q3, x1, y0))
+        x2 = over_x(after(q2, x1, y0, tail_below, inside))
+        y3 = over_y(after(q3, x1, y0, tail_below, inside))
         acc_a = part_call(
-            places, (1, 2), [(x0, x1), (y0, y1)], w_qkv, 2 * quarter, cols, before=acc, at=0
+            places,
+            (1, 2),
+            [(x0, x1), (y0, y1)],
+            w_qkv,
+            2 * quarter,
+            cols,
+            before=acc,
+            at=0,
         )
         x3, y2 = over_x(after(q3, fy0, fx1, acc_a)), over_y(after(q2, fy0, fx1, acc_a))
         query_a, within_a, state = first_call(
@@ -622,7 +665,14 @@
         )
         fy2, fx3 = over_y(after(x2, state)), over_x(after(y3, state))
         acc_b = part_call(
-            places, (1, 2), [(x2, x3), (y2, y3)], w_qkv, 2 * quarter, cols, before=acc, at=1
+            places,
+            (1, 2),
+            [(x2, x3), (y2, y3)],
+            w_qkv,
+            2 * quarter,
+            cols,
+            before=acc,
+            at=1,
         )
         far = (fy2, fx3)
         k, v, mid, state, sent = state_call(
@@ -646,20 +696,33 @@
         return lax.dynamic_slice_in_dim(x, core * share, share, 0)
 
     chip_state = jnp.exp(-mine(tail_second))[:, None, None] * mine(first) + mine(second)
-    chip_decay = jnp.exp(-mine(tail + tail_other))[:, None, None]
+    chip_decay = jnp.exp(-mine(tail_chip))[:, None, None]
     chip_entering = mine(prior_state)
-    hops = n_seq // 2 - 1
-    for hop in range(hops):
-        leaving = (chip_decay * chip_entering + chip_state).astype(BF16)
-        arriving = lax.ppermute(
-            leaving, "seq", perm=[(2 * hop + c, 2 * hop + 2 + c) for c in range(2)]
-        )
-        if square and hop == hops // 2:
+
+    def leaving():
+        return (chip_decay * chip_entering + chip_state).astype(BF16)
+
+    if n_chips == 4:
+        arriving = hop(jnp.where(chip == 2, chip_state.astype(BF16), leaving()), (0, 1), (2, 3))
+        chip_entering = jnp.where(chip == 1, arriving.astype(F32), chip_entering)
+        sum_first = leaving()
+        to_third, to_second = hop(sum_first, (1, 3)), hop(sum_first, (1, 2))
+        if square:
             query_b, within_b = later_call(
-                places, far, w_qkv, acc_b, k, v, along, inside, after(mid, leaving), group
+                places, far, w_qkv, acc_b, k, v, along, inside, after(mid, sum_first), group
             )
-            arriving = after(arriving, query_b, within_b)
-        chip_entering = jnp.where(chip == hop + 1, arriving.astype(F32), chip_entering)
+            to_third, to_second, _ = lax.optimization_barrier((to_third, to_second, query_b))
+        third = jnp.exp(-mine(tail_below))[:, None, None] * to_third.astype(F32)
+        chip_entering = jnp.where(chip == 2, to_second.astype(F32), chip_entering)
+        chip_entering = jnp.where(chip == 3, third + arriving.astype(F32), chip_entering)
+    else:
+        for step in range(n_chips - 1):
+            arriving = hop(leaving(), (step, step + 1))
+            chip_entering = jnp.where(chip == step + 1, arriving.astype(F32), chip_entering)
+        if square:
+            query_b, within_b = later_call(
+                places, far, w_qkv, acc_b, k, v, along, inside, mid, group
+            )
     there = swap(chip_entering.astype(BF16)).astype(F32)
     entering = jnp.concatenate(
         [jnp.where(core == 0, chip_entering, there), jnp.where(core == 0, there, chip_entering)]

time: 267 us -> 209 us (0.78)
  Pallas kernels: 184 us -> 86.2 us
  waiting for transfers between devices: 44.1 us -> 64.9 us
  local copies, waits for them, and re-layouts: 7.81 us -> 21.6 us
  starting transfers between devices: 25.6 us -> 31.7 us
    pallas_call x2 -> x0, Pallas kernels: 65.8 us -> none  [cut_call(): pl.pallas_call(functools.partial(cut_kernel, first), out_shape=(half, hal...]
    pallas_call x14 -> x15, Pallas kernels: 118 us -> 86.2 us  [call(): pl.pallas_call(kernel, out_shape=tuple(outs), grid_spec=pltpu.PrefetchSca...]
    ppermute x1, waiting for transfers between devices: 0.97 us -> 22 us  [local(): over_x(after(near_x, far0, far1))]
    ppermute x1, waiting for transfers between devices: 22.3 us -> 1.49 us  [local(): over_y(after(near_y, far0, far1))]
    unnamed x42 -> x38, local copies, waits for them, and re-layouts: 7 us -> 21.5 us
    ppermute x2, waiting for transfers between devices: 0.01 us -> 6.51 us  [local(): sum1, sum0 = (over_x(sum1), over_y(sum0))]
    ppermute x5 -> x6, starting transfers between devices: 6.33 us -> 11.3 us  [the longest x4 9.29 us: hop(): lax.ppermute(x, 'seq', perm=[(2 * a + c, 2 * b + c) for a, b in pairs for...]
    ppermute x4, waiting for transfers between devices: 0.01 us -> 4.38 us  [local(): x0, y1, x1, y0 = (over_x(q0), over_y(q1), over_x(q1), over_y(q0))]
  transfers between devices with their start and end apart: 28 -> 29, of which waited for: 10 -> 13; matrix products, arithmetic and copies ran while one was open for 1% -> 0% of each run, Pallas kernels for 53% -> 34%
where the time goes in v4:
time: 209 us; the launch traced here: 208 us
  Pallas kernels  86.2 us (41%)
  waiting for transfers between devices  64.9 us (31%)
  starting transfers between devices  31.7 us (15%)
  local copies, waits for them, and re-layouts  21.6 us (10%)
  other arithmetic  3.44 us (2%)
    pallas_call x15, Pallas kernels, call(): pl.pallas_call(kernel, out_shape=tuple(outs), grid_spec=pltpu.PrefetchSca...  86.2 us
    ppermute x1, waiting for transfers between devices, local(): over_x(after(near_x, far0, far1))  22 us
    unnamed x38, local copies, waits for them, and re-layouts  21.5 us
    ppermute x4, starting transfers between devices, hop(): lax.ppermute(x, 'seq', perm=[(2 * a + c, 2 * b + c) for a, b in pairs for...  9.29 us
    ppermute x2, waiting for transfers between devices, local(): far2, far3 = (over_x(far2), over_y(far3))  6.79 us
    ppermute x2, waiting for transfers between devices, local(): sum1, sum0 = (over_x(sum1), over_y(sum0))  6.51 us
    ppermute x4, waiting for transfers between devices, hop(): lax.ppermute(x, 'seq', perm=[(2 * a + c, 2 * b + c) for a, b in pairs for...  6.26 us
    ppermute x2, waiting for transfers between devices, local(): fy0, fx1 = (over_y(x0), over_x(y1))  5.84 us
  transfers between devices with their start and end apart: 29, of which 13 were waited for; matrix products, arithmetic and copies ran while one was open for 0% of the time, Pallas kernels for 34%

profile of v4, /device:TPU:8, one launch (start us, length us, event | category | flops | bytes accessed | tf_op | source)
XLA Modules:
  0.0 208.2 jit_solution(10723697502596031085)
XLA Ops:
  0.0 1.6 copy-done.4
  2.6 1.5 collective-permute-start.1
  8.7 1.6 copy-done.5
  10.3 12.0 %own_part.1 = (f32[3,1024,1024]{2,1,0:T(8,128)}, bf16[256,1024]{1,0:T(8,128)(2,1)S(1)}, bf16[256,1024]{1,0:T(8,128)(2,1)S(1)}) custom-call(s32[4]{0:T(128)S(1)} %pad_add_fusion._, bf16[1024,1024]{1,0:T(8,128)(2,1)S(1)} %copy-done.5, bf16[3,4096,1024]{2,1,0:T(8,128)(2,1)} %refs_2_.5), custom_call_target="tpu_custom_call" | custom-call | flops 6442450944 | bytes 40894464 | tf_op jit(solution)/shard_map/own_part/pallas_call | solution.py:35
  24.6 4.4 %collective-permute-done.refs_1_ = bf16[256,1024]{1,0:T(8,128)(2,1)S(1)} collective-permute-done((bf16[256,1024]{1,0:T(8,128)(2,1)}, bf16[256,1024]{1,0:T(8,128)(2,1)S(1)}, u32[]{:S(2)}, u32[]{:S(2)}) %collective-permute-start) | collective-permute-done | bytes 524320 | tf_op jit(solution)/shard_map/ppermute | solution.py:637
  29.0 1.5 collective-permute-start.4
  31.0 1.5 collective-permute-start.6
  33.0 4.6 %copy-done.2 = f32[3,1024,1024]{2,1,0:T(8,128)S(1)} copy-done((f32[3,1024,1024]{2,1,0:T(8,128)S(1)}, f32[3,1024,1024]{2,1,0:T(8,128)}, u32[]{:S(2)}) %copy-start.2) | copy-done | bytes 12582936
  37.6 10.6 %part.2.refs_3_ = f32[3,512,1024]{2,1,0:T(8,128)S(1)} custom-call(s32[4]{0:T(128)S(1)} %pad_add_fusion._, bf16[256,1024]{1,0:T(8,128)(2,1)S(1)} %collective-permute-done.5.refs_0_, bf16[256,1024]{1,0:T(8,128)(2,1)S(1)} %collective-permute-done.refs_1_, bf16[256,1024]{1,0:T(8,128)(2,1)S(1)} %collective-permute-done.1.refs_2_, ...), custom_call_target="tpu_custom_call" | custom-call | flops 6442450944 | bytes 71303168 | tf_op jit(solution)/shard_map/part/pallas_call | solution.py:35
  48.3 5.8 %collective-permute-done.6.refs_0_ = bf16[256,1024]{1,0:T(8,128)(2,1)S(1)} collective-permute-done((bf16[256,1024]{1,0:T(8,128)(2,1)S(1)}, bf16[256,1024]{1,0:T(8,128)(2,1)S(1)}, u32[]{:S(2)}, u32[]{:S(2)}) %collective-permute-start.6) | collective-permute-done | bytes 524320 | tf_op jit(solution)/shard_map/ppermute | solution.py:639
  55.2 11.1 %first.1 = (bf16[512,1024]{1,0:T(8,128)(2,1)}, f32[512,1024]{1,0:T(8,128)}, f32[8,128,128]{2,1,0:T(8,128)S(1)}) custom-call(s32[4]{0:T(128)S(1)} %pad_add_fusion._, bf16[256,1024]{1,0:T(8,128)(2,1)S(1)} %collective-permute-done.6.refs_0_, bf16[256,1024]{1,0:T(8,128)(2,1)S(1)} %collective-permute-done.8.refs_1_, bf16[3,4096,1024]{2,1,0:T(8,128)(2,1)} %refs_2_.5, ...), custom_call_target="tpu_custom_call" | custom-call | flops 3221225472 | bytes 36241408 | tf_op jit(solution)/shard_map/first/pallas_call | solution.py:35
  66.3 1.5 collective-permute-start.9
  67.8 1.5 collective-permute-start.11
  69.3 4.6 %copy-done.3 = f32[3,1024,1024]{2,1,0:T(8,128)S(1)} copy-done((f32[3,1024,1024]{2,1,0:T(8,128)S(1)}, f32[3,1024,1024]{2,1,0:T(8,128)}, u32[]{:S(2)}) %copy-start.3) | copy-done | bytes 12582936
  73.9 10.6 %part.3.refs_4_.refs_5_.refs_3_ = f32[3,512,1024]{2,1,0:T(8,128)S(1)} custom-call(s32[4]{0:T(128)S(1)} %pad_add_fusion._, bf16[256,1024]{1,0:T(8,128)(2,1)S(1)} %collective-permute-done.4.refs_0_, bf16[256,1024]{1,0:T(8,128)(2,1)S(1)} %collective-permute-done.12.refs_1_, bf16[256,1024]{1,0:T(8,128)(2,1)S(1)} %collective-permute-done.13.refs_2_, ...), custom_call_target="tpu_custom_call" | custom-call | flops 6442450944 | bytes 71303168 | tf_op jit(solution)/shard_map/part/pallas_call | solution.py:35
  84.6 7.8 %states.1 = (bf16[512,1024]{1,0:T(8,128)(2,1)}, bf16[512,1024]{1,0:T(8,128)(2,1)}, f32[2,8,128,128]{3,2,1,0:T(8,128)}, f32[8,128,128]{2,1,0:T(8,128)S(1)}, bf16[8,128,128]{2,1,0:T(8,128)(2,1)S(1)}) custom-call(s32[4]{0:T(128)S(1)} %pad_add_fusion._, bf16[256,1024]{1,0:T(8,128)(2,1)S(1)} %collective-permute-done.9.refs_0_, ...), custom_call_target="tpu_custom_call" | custom-call | flops 2147483648 | bytes 68452352 | tf_op jit(solution)/shard_map/states/pallas_call | solution.py:35
  94.0 1.7 fusion.2
  97.1 6.3 %collective-permute-done.15 = bf16[4,128,128]{2,1,0:T(8,128)(2,1)S(1)} collective-permute-done((bf16[4,128,128]{2,1,0:T(8,128)(2,1)}, bf16[4,128,128]{2,1,0:T(8,128)(2,1)S(1)}, u32[]{:S(2)}, u32[]{:S(2)}) %collective-permute-start.15) | collective-permute-done | bytes 131104 | tf_op jit(solution)/shard_map/ppermute | solution.py:627
  104.4 5.9 %collective-permute-start.16 = (bf16[4,128,128]{2,1,0:T(8,128)(2,1)S(1)}, bf16[4,128,128]{2,1,0:T(8,128)(2,1)S(1)}, u32[]{:S(2)}, u32[]{:S(2)}) collective-permute-start(bf16[4,128,128]{2,1,0:T(8,128)(2,1)S(1)} %add_convert_fusion), channel_id=1, source_target_pairs={{8,24},{12,28},{9,25},{13,29},{10,26},{14,30},{11,27},{15,31}} | collective-permute-start | bytes 393224 | tf_op jit(solution)/shard_map/ppermute | solution.py:627
  111.8 2.9 %copy-done.1 = f32[3,512,1024]{2,1,0:T(8,128)S(1)} copy-done((f32[3,512,1024]{2,1,0:T(8,128)S(1)}, f32[3,512,1024]{2,1,0:T(8,128)}, u32[]{:S(2)}) %copy-start.1) | copy-done | bytes 6291480
  118.6 8.1 %later.1 = (bf16[512,1024]{1,0:T(8,128)(2,1)S(1)}, f32[512,1024]{1,0:T(8,128)S(1)}) custom-call(s32[4]{0:T(128)S(1)} %pad_add_fusion._, bf16[256,1024]{1,0:T(8,128)(2,1)S(1)} %collective-permute-done.9.refs_0_, bf16[256,1024]{1,0:T(8,128)(2,1)S(1)} %collective-permute-done.11.refs_1_, bf16[3,4096,1024]{2,1,0:T(8,128)(2,1)} %refs_2_.5, ...), custom_call_target="tpu_custom_call" | custom-call | flops 1879048192 | bytes 38862848 | tf_op jit(solution)/shard_map/later/pallas_call | solution.py:35
  128.5 4.9 %heads.1 = (bf16[512,1024]{1,0:T(8,128)(2,1)S(1)}, bf16[256,1024]{1,0:T(8,128)(2,1)S(1)}, bf16[256,1024]{1,0:T(8,128)(2,1)S(1)}) custom-call(s32[4]{0:T(128)S(1)} %pad_add_fusion._, bf16[512,1024]{1,0:T(8,128)(2,1)S(1)} %copy-done.7, f32[512,1024]{1,0:T(8,128)S(1)} %copy-done.6, bf16[8,128,128]{2,1,0:T(8,128)(2,1)S(1)} %select_convert_fusion.entering_ref, ...), custom_call_target="tpu_custom_call" | custom-call | flops 1 | bytes 1 | tf_op jit(solution)/shard_map/heads/pallas_call | solution.py:35
  135.2 7.8 %heads_near.1 = (bf16[512,1024]{1,0:T(8,128)(2,1)S(1)}, bf16[256,1024]{1,0:T(8,128)(2,1)S(1)}, bf16[256,1024]{1,0:T(8,128)(2,1)S(1)}, bf16[512,1024]{1,0:T(8,128)(2,1)S(1)}, bf16[512,1024]{1,0:T(8,128)(2,1)S(1)}) custom-call(s32[4]{0:T(128)S(1)} %pad_add_fusion._, bf16[512,1024]{1,0:T(8,128)(2,1)S(1)} %get-tuple-element.71.q_ref, ...), custom_call_target="tpu_custom_call" | custom-call | flops 1 | bytes 1 | tf_op jit(solution)/shard_map/heads_near/pallas_call | solution.py:35
  143.0 4.4 %collective-permute-done.19.y_ref = bf16[256,1024]{1,0:T(8,128)(2,1)S(1)} collective-permute-done((bf16[256,1024]{1,0:T(8,128)(2,1)S(1)}, bf16[256,1024]{1,0:T(8,128)(2,1)S(1)}, u32[]{:S(2)}, u32[]{:S(2)}) %collective-permute-start.19) | collective-permute-done | bytes 524320 | tf_op jit(solution)/shard_map/ppermute | solution.py:753
  151.8 22.0 %collective-permute-done.21.refs_0_ = bf16[512,1024]{1,0:T(8,128)(2,1)S(1)} collective-permute-done((bf16[512,1024]{1,0:T(8,128)(2,1)S(1)}, bf16[512,1024]{1,0:T(8,128)(2,1)S(1)}, u32[]{:S(2)}, u32[]{:S(2)}) %collective-permute-start.21) | collective-permute-done | bytes 1048608 | tf_op jit(solution)/shard_map/ppermute | solution.py:757
  175.3 2.3 %sum_pair.2 = (bf16[256,1024]{1,0:T(8,128)(2,1)S(1)}, bf16[256,1024]{1,0:T(8,128)(2,1)S(1)}) custom-call(s32[4]{0:T(128)S(1)} %pad_add_fusion._, bf16[512,1024]{1,0:T(8,128)(2,1)S(1)} %get-tuple-element.87.first_ref.normed_ref, bf16[256,1024]{1,0:T(8,128)(2,1)S(1)} %collective-permute-done.20.x_ref, bf16[256,1024]{1,0:T(8,128)(2,1)S(1)} %collective-permute-done.19.y_ref, ...), custom_call_target="tpu_custom_call" | custom-call | flops 1 | bytes 1 | tf_op jit(solution)/shard_map/sum_pair/pallas_call | solution.py:35
  178.2 6.0 %collective-permute-done.23.x_ref = bf16[256,1024]{1,0:T(8,128)(2,1)S(1)} collective-permute-done((bf16[256,1024]{1,0:T(8,128)(2,1)S(1)}, bf16[256,1024]{1,0:T(8,128)(2,1)S(1)}, u32[]{:S(2)}, u32[]{:S(2)}) %collective-permute-start.23) | collective-permute-done | bytes 524320 | tf_op jit(solution)/shard_map/ppermute | solution.py:758
  186.3 2.3 %sum_pair.3 = (bf16[256,1024]{1,0:T(8,128)(2,1)S(1)}, bf16[256,1024]{1,0:T(8,128)(2,1)S(1)}) custom-call(s32[4]{0:T(128)S(1)} %pad_add_fusion._, bf16[512,1024]{1,0:T(8,128)(2,1)S(1)} %get-tuple-element.79.normed_ref, bf16[256,1024]{1,0:T(8,128)(2,1)S(1)} %collective-permute-done.23.x_ref, bf16[256,1024]{1,0:T(8,128)(2,1)S(1)} %collective-permute-done.24.y_ref, ...), custom_call_target="tpu_custom_call" | custom-call | flops 1 | bytes 1 | tf_op jit(solution)/shard_map/sum_pair/pallas_call | solution.py:35
  191.0 2.4 %own_block.2.kept_ref = bf16[512,1024]{1,0:T(8,128)(2,1)S(1)} custom-call(s32[4]{0:T(128)S(1)} %pad_add_fusion._, bf16[512,1024]{1,0:T(8,128)(2,1)S(1)} %get-tuple-element.79.normed_ref, bf16[1024,4096]{1,0:T(8,128)(2,1)S(1)} %bitcast.5, bf16[512,1024]{1,0:T(8,128)(2,1)S(1)} %collective-permute-done.21.refs_0_, ...), custom_call_target="tpu_custom_call" | custom-call | flops 1 | bytes 1 | tf_op jit(solution)/shard_map/own_block/pallas_call | solution.py:35
  193.4 6.5 %collective-permute-done.27.refs_1_ = bf16[256,1024]{1,0:T(8,128)(2,1)S(1)} collective-permute-done((bf16[256,1024]{1,0:T(8,128)(2,1)S(1)}, bf16[256,1024]{1,0:T(8,128)(2,1)S(1)}, u32[]{:S(2)}, u32[]{:S(2)}) %collective-permute-start.27) | collective-permute-done | bytes 524320 | tf_op jit(solution)/shard_map/ppermute | solution.py:761
  199.9 3.1 %own_block.3.above_ref = bf16[1024,1024]{1,0:T(8,128)(2,1)} custom-call(s32[4]{0:T(128)S(1)} %pad_add_fusion._, bf16[512,1024]{1,0:T(8,128)(2,1)S(1)} %get-tuple-element.87.first_ref.normed_ref, bf16[1024,4096]{1,0:T(8,128)(2,1)S(1)} %bitcast.5, bf16[512,1024]{1,0:T(8,128)(2,1)S(1)} %collective-permute-done.21.refs_0_, ...), custom_call_target="tpu_custom_call" | custom-call | flops 1 | bytes 1 | tf_op jit(solution)/shard_map/own_block/pallas_call | solution.py:35
  203.0 4.1 %collective-permute-done.25.a_ref = bf16[256,1024]{1,0:T(8,128)(2,1)S(1)} collective-permute-done((bf16[256,1024]{1,0:T(8,128)(2,1)S(1)}, bf16[256,1024]{1,0:T(8,128)(2,1)S(1)}, u32[]{:S(2)}, u32[]{:S(2)}) %collective-permute-start.25) | collective-permute-done | bytes 524320 | tf_op jit(solution)/shard_map/ppermute | solution.py:763
  (92 shorter events, 34.7 us)
Async XLA Ops:
  2.6 26.4 %collective-permute-start.1 = (bf16[256,1024]{1,0:T(8,128)(2,1)}, bf16[256,1024]{1,0:T(8,128)(2,1)S(1)}, u32[]{:S(2)}, u32[]{:S(2)}) collective-permute-start(bf16[256,1024]{1,0:T(8,128)(2,1)} %get-tuple-element.52), channel_id=1, source_target_pairs={{0,2},{1,3},{2,0},{3,1},{4,6},{5,7},{6,4},{7,5},{8,10},{9,11},{10,... | collective-permute-start | bytes 1572872 | tf_op jit(solution)/shard_map/ppermute | solution.py:637
  4.1 26.8 %collective-permute-start.5 = (bf16[256,1024]{1,0:T(8,128)(2,1)}, bf16[256,1024]{1,0:T(8,128)(2,1)S(1)}, u32[]{:S(2)}, u32[]{:S(2)}) collective-permute-start(bf16[256,1024]{1,0:T(8,128)(2,1)} %get-tuple-element.52), channel_id=1, source_target_pairs={{0,1},{1,0},{2,3},{3,2},{4,5},{5,4},{6,7},{7,6},{8,9},{9,8},{10,11... | collective-permute-start | bytes 1572872 | tf_op jit(solution)/shard_map/ppermute | solution.py:637
  5.6 23.3 %collective-permute-start = (bf16[256,1024]{1,0:T(8,128)(2,1)}, bf16[256,1024]{1,0:T(8,128)(2,1)S(1)}, u32[]{:S(2)}, u32[]{:S(2)}) collective-permute-start(bf16[256,1024]{1,0:T(8,128)(2,1)} %get-tuple-element.51), channel_id=1, source_target_pairs={{0,1},{1,0},{2,3},{3,2},{4,5},{5,4},{6,7},{7,6},{8,9},{9,8},{10,11... | collective-permute-start | bytes 1572872 | tf_op jit(solution)/shard_map/ppermute | solution.py:637
  6.2 26.3 %collective-permute-start.7 = (bf16[256,1024]{1,0:T(8,128)(2,1)}, bf16[256,1024]{1,0:T(8,128)(2,1)S(1)}, u32[]{:S(2)}, u32[]{:S(2)}) collective-permute-start(bf16[256,1024]{1,0:T(8,128)(2,1)} %get-tuple-element.51), channel_id=1, source_target_pairs={{0,2},{1,3},{2,0},{3,1},{4,6},{5,7},{6,4},{7,5},{8,10},{9,11},{10,... | collective-permute-start | bytes 1572872 | tf_op jit(solution)/shard_map/ppermute | solution.py:637
  8.5 15.4 %collective-permute-start.2 = (f32[8]{0:T(128)S(1)}, f32[8]{0:T(128)S(1)}, u32[]{:S(2)}, u32[]{:S(2)}) collective-permute-start(f32[8]{0:T(128)S(1)} %slice_reduce_fusion), channel_id=1, source_target_pairs={{0,4},{4,0},{8,12},{12,8},{16,20},{20,16},{24,28},{28,24},{1,5},{5... | collective-permute-start | bytes 104 | tf_op jit(solution)/shard_map/ppermute | solution.py:631
  23.9 0.7 collective-permute-start.3
  29.0 37.3 %collective-permute-start.4 = (bf16[256,1024]{1,0:T(8,128)(2,1)}, bf16[256,1024]{1,0:T(8,128)(2,1)S(1)}, u32[]{:S(2)}, u32[]{:S(2)}) collective-permute-start(bf16[256,1024]{1,0:T(8,128)(2,1)} %copy-done.12), channel_id=1, source_target_pairs={{0,1},{1,0},{2,3},{3,2},{4,5},{5,4},{6,7},{7,6},{8,9},{9,8},{10,11... | collective-permute-start | bytes 1572872 | tf_op jit(solution)/shard_map/ppermute | solution.py:640
  30.5 37.4 %collective-permute-start.10 = (bf16[256,1024]{1,0:T(8,128)(2,1)}, bf16[256,1024]{1,0:T(8,128)(2,1)S(1)}, u32[]{:S(2)}, u32[]{:S(2)}) collective-permute-start(bf16[256,1024]{1,0:T(8,128)(2,1)} %copy-done.14), channel_id=1, source_target_pairs={{0,2},{1,3},{2,0},{3,1},{4,6},{5,7},{6,4},{7,5},{8,10},{9,11},{10,... | collective-permute-start | bytes 1572872 | tf_op jit(solution)/shard_map/ppermute | solution.py:641
  31.0 23.1 %collective-permute-start.6 = (bf16[256,1024]{1,0:T(8,128)(2,1)S(1)}, bf16[256,1024]{1,0:T(8,128)(2,1)S(1)}, u32[]{:S(2)}, u32[]{:S(2)}) collective-permute-start(bf16[256,1024]{1,0:T(8,128)(2,1)S(1)} %collective-permute-done.5.refs_0_), channel_id=1, source_target_pairs={{0,2},{1,3},{2,0},{3,1},{4,6},{5,7},{6,4},{7,5},{8,10},{9,11},{10,... | collective-permute-start | bytes 1572872 | tf_op jit(solution)/shard_map/ppermute | solution.py:639
  32.5 21.6 %collective-permute-start.8 = (bf16[256,1024]{1,0:T(8,128)(2,1)S(1)}, bf16[256,1024]{1,0:T(8,128)(2,1)S(1)}, u32[]{:S(2)}, u32[]{:S(2)}) collective-permute-start(bf16[256,1024]{1,0:T(8,128)(2,1)S(1)} %collective-permute-done.7.refs_3_), channel_id=1, source_target_pairs={{0,1},{1,0},{2,3},{3,2},{4,5},{5,4},{6,7},{7,6},{8,9},{9,8},{10,11... | collective-permute-start | bytes 1572872 | tf_op jit(solution)/shard_map/ppermute | solution.py:639
  37.6 16.5 %copy-start.15 = (bf16[256,1024]{1,0:T(8,128)(2,1)S(1)}, bf16[256,1024]{1,0:T(8,128)(2,1)}, u32[]{:S(2)}) copy-start(bf16[256,1024]{1,0:T(8,128)(2,1)} %copy-done.14) | copy-start | bytes 1572868
  37.6 17.0 %copy-start.13 = (bf16[256,1024]{1,0:T(8,128)(2,1)S(1)}, bf16[256,1024]{1,0:T(8,128)(2,1)}, u32[]{:S(2)}) copy-start(bf16[256,1024]{1,0:T(8,128)(2,1)} %copy-done.12) | copy-start | bytes 1572868
  54.1 15.2 %collective-permute-start.12 = (bf16[256,1024]{1,0:T(8,128)(2,1)S(1)}, bf16[256,1024]{1,0:T(8,128)(2,1)S(1)}, u32[]{:S(2)}, u32[]{:S(2)}) collective-permute-start(bf16[256,1024]{1,0:T(8,128)(2,1)S(1)} %copy-done.15), channel_id=1, source_target_pairs={{0,1},{1,0},{2,3},{3,2},{4,5},{5,4},{6,7},{7,6},{8,9},{9,8},{10,11... | collective-permute-start | bytes 1572872 | tf_op jit(solution)/shard_map/ppermute | solution.py:652
  54.7 14.7 %collective-permute-start.13 = (bf16[256,1024]{1,0:T(8,128)(2,1)S(1)}, bf16[256,1024]{1,0:T(8,128)(2,1)S(1)}, u32[]{:S(2)}, u32[]{:S(2)}) collective-permute-start(bf16[256,1024]{1,0:T(8,128)(2,1)S(1)} %copy-done.13), channel_id=1, source_target_pairs={{0,2},{1,3},{2,0},{3,1},{4,6},{5,7},{6,4},{7,5},{8,10},{9,11},{10,... | collective-permute-start | bytes 1572872 | tf_op jit(solution)/shard_map/ppermute | solution.py:652
  66.3 18.3 %collective-permute-start.9 = (bf16[256,1024]{1,0:T(8,128)(2,1)S(1)}, bf16[256,1024]{1,0:T(8,128)(2,1)S(1)}, u32[]{:S(2)}, u32[]{:S(2)}) collective-permute-start(bf16[256,1024]{1,0:T(8,128)(2,1)S(1)} %collective-permute-done.4.refs_0_), channel_id=1, source_target_pairs={{0,2},{1,3},{2,0},{3,1},{4,6},{5,7},{6,4},{7,5},{8,10},{9,11},{10,... | collective-permute-start | bytes 1572872 | tf_op jit(solution)/shard_map/ppermute | solution.py:666
  67.8 16.8 %collective-permute-start.11 = (bf16[256,1024]{1,0:T(8,128)(2,1)S(1)}, bf16[256,1024]{1,0:T(8,128)(2,1)S(1)}, u32[]{:S(2)}, u32[]{:S(2)}) collective-permute-start(bf16[256,1024]{1,0:T(8,128)(2,1)S(1)} %collective-permute-done.10.refs_3_), channel_id=1, source_target_pairs={{0,1},{1,0},{2,3},{3,2},{4,5},{5,4},{6,7},{7,6},{8,9},{9,8},{10,11... | collective-permute-start | bytes 1572872 | tf_op jit(solution)/shard_map/ppermute | solution.py:666
  92.4 1.5 collective-permute-start.14
  95.8 7.6 %collective-permute-start.15 = (bf16[4,128,128]{2,1,0:T(8,128)(2,1)}, bf16[4,128,128]{2,1,0:T(8,128)(2,1)S(1)}, u32[]{:S(2)}, u32[]{:S(2)}) collective-permute-start(bf16[4,128,128]{2,1,0:T(8,128)(2,1)} %get-tuple-element.97), channel_id=1, source_target_pairs={{0,8},{4,12},{16,24},{20,28},{1,9},{5,13},{17,25},{21,29},{2,10},{... | collective-permute-start | bytes 393224 | tf_op jit(solution)/shard_map/ppermute | solution.py:627
  104.4 22.3 %collective-permute-start.16 = (bf16[4,128,128]{2,1,0:T(8,128)(2,1)S(1)}, bf16[4,128,128]{2,1,0:T(8,128)(2,1)S(1)}, u32[]{:S(2)}, u32[]{:S(2)}) collective-permute-start(bf16[4,128,128]{2,1,0:T(8,128)(2,1)S(1)} %add_convert_fusion), channel_id=1, source_target_pairs={{8,24},{12,28},{9,25},{13,29},{10,26},{14,30},{11,27},{15,31}} | collective-permute-start | bytes 393224 | tf_op jit(solution)/shard_map/ppermute | solution.py:627
  110.3 16.4 %collective-permute-start.17 = (bf16[4,128,128]{2,1,0:T(8,128)(2,1)S(1)}, bf16[4,128,128]{2,1,0:T(8,128)(2,1)S(1)}, u32[]{:S(2)}, u32[]{:S(2)}) collective-permute-start(bf16[4,128,128]{2,1,0:T(8,128)(2,1)S(1)} %add_convert_fusion), channel_id=1, source_target_pairs={{8,16},{12,20},{9,17},{13,21},{10,18},{14,22},{11,19},{15,23}} | collective-permute-start | bytes 393224 | tf_op jit(solution)/shard_map/ppermute | solution.py:627
  111.8 16.7 %slice-start = ((s8[8388608]{0:T(1024)(128)(4,1)}), s8[4194304]{0:T(1024)(128)(4,1)S(1)}, s32[]{:S(2)}) async-start(s8[8388608]{0:T(1024)(128)(4,1)} %bitcast.4), calls=%async_computation | async-start | bytes 8388608
  126.9 1.4 collective-permute-start.18
  133.4 14.0 %collective-permute-start.19 = (bf16[256,1024]{1,0:T(8,128)(2,1)S(1)}, bf16[256,1024]{1,0:T(8,128)(2,1)S(1)}, u32[]{:S(2)}, u32[]{:S(2)}) collective-permute-start(bf16[256,1024]{1,0:T(8,128)(2,1)S(1)} %get-tuple-element.81), channel_id=1, source_target_pairs={{0,1},{1,0},{2,3},{3,2},{4,5},{5,4},{6,7},{7,6},{8,9},{9,8},{10,11... | collective-permute-start | bytes 1572872 | tf_op jit(solution)/shard_map/ppermute | solution.py:753
  134.0 13.7 %collective-permute-start.20 = (bf16[256,1024]{1,0:T(8,128)(2,1)S(1)}, bf16[256,1024]{1,0:T(8,128)(2,1)S(1)}, u32[]{:S(2)}, u32[]{:S(2)}) collective-permute-start(bf16[256,1024]{1,0:T(8,128)(2,1)S(1)} %get-tuple-element.82), channel_id=1, source_target_pairs={{0,2},{1,3},{2,0},{3,1},{4,6},{5,7},{6,4},{7,5},{8,10},{9,11},{10,... | collective-permute-start | bytes 1572872 | tf_op jit(solution)/shard_map/ppermute | solution.py:753
  147.7 26.1 %collective-permute-start.21 = (bf16[512,1024]{1,0:T(8,128)(2,1)S(1)}, bf16[512,1024]{1,0:T(8,128)(2,1)S(1)}, u32[]{:S(2)}, u32[]{:S(2)}) collective-permute-start(bf16[512,1024]{1,0:T(8,128)(2,1)S(1)} %get-tuple-element.83), channel_id=1, source_target_pairs={{0,1},{1,0},{2,3},{3,2},{4,5},{5,4},{6,7},{7,6},{8,9},{9,8},{10,11... | collective-permute-start | bytes 3145736 | tf_op jit(solution)/shard_map/ppermute | solution.py:757
  149.2 26.1 %collective-permute-start.22 = (bf16[512,1024]{1,0:T(8,128)(2,1)S(1)}, bf16[512,1024]{1,0:T(8,128)(2,1)S(1)}, u32[]{:S(2)}, u32[]{:S(2)}) collective-permute-start(bf16[512,1024]{1,0:T(8,128)(2,1)S(1)} %get-tuple-element.85), channel_id=1, source_target_pairs={{0,2},{1,3},{2,0},{3,1},{4,6},{5,7},{6,4},{7,5},{8,10},{9,11},{10,... | collective-permute-start | bytes 3145736 | tf_op jit(solution)/shard_map/ppermute | solution.py:757
  150.4 33.8 %collective-permute-start.23 = (bf16[256,1024]{1,0:T(8,128)(2,1)S(1)}, bf16[256,1024]{1,0:T(8,128)(2,1)S(1)}, u32[]{:S(2)}, u32[]{:S(2)}) collective-permute-start(bf16[256,1024]{1,0:T(8,128)(2,1)S(1)} %get-tuple-element.86), channel_id=1, source_target_pairs={{0,2},{1,3},{2,0},{3,1},{4,6},{5,7},{6,4},{7,5},{8,10},{9,11},{10,... | collective-permute-start | bytes 1572872 | tf_op jit(solution)/shard_map/ppermute | solution.py:758
  151.2 33.8 %collective-permute-start.24 = (bf16[256,1024]{1,0:T(8,128)(2,1)S(1)}, bf16[256,1024]{1,0:T(8,128)(2,1)S(1)}, u32[]{:S(2)}, u32[]{:S(2)}) collective-permute-start(bf16[256,1024]{1,0:T(8,128)(2,1)S(1)} %get-tuple-element.90), channel_id=1, source_target_pairs={{0,1},{1,0},{2,3},{3,2},{4,5},{5,4},{6,7},{7,6},{8,9},{9,8},{10,11... | collective-permute-start | bytes 1572872 | tf_op jit(solution)/shard_map/ppermute | solution.py:758
  177.6 22.3 %collective-permute-start.28 = (bf16[256,1024]{1,0:T(8,128)(2,1)S(1)}, bf16[256,1024]{1,0:T(8,128)(2,1)S(1)}, u32[]{:S(2)}, u32[]{:S(2)}) collective-permute-start(bf16[256,1024]{1,0:T(8,128)(2,1)S(1)} %get-tuple-element.88), channel_id=1, source_target_pairs={{0,1},{1,0},{2,3},{3,2},{4,5},{5,4},{6,7},{7,6},{8,9},{9,8},{10,11... | collective-permute-start | bytes 1572872 | tf_op jit(solution)/shard_map/ppermute | solution.py:761
  185.0 14.9 %collective-permute-start.27 = (bf16[256,1024]{1,0:T(8,128)(2,1)S(1)}, bf16[256,1024]{1,0:T(8,128)(2,1)S(1)}, u32[]{:S(2)}, u32[]{:S(2)}) collective-permute-start(bf16[256,1024]{1,0:T(8,128)(2,1)S(1)} %get-tuple-element.94), channel_id=1, source_target_pairs={{0,2},{1,3},{2,0},{3,1},{4,6},{5,7},{6,4},{7,5},{8,10},{9,11},{10,... | collective-permute-start | bytes 1572872 | tf_op jit(solution)/shard_map/ppermute | solution.py:761
  188.6 18.5 %collective-permute-start.25 = (bf16[256,1024]{1,0:T(8,128)(2,1)S(1)}, bf16[256,1024]{1,0:T(8,128)(2,1)S(1)}, u32[]{:S(2)}, u32[]{:S(2)}) collective-permute-start(bf16[256,1024]{1,0:T(8,128)(2,1)S(1)} %get-tuple-element.92), channel_id=1, source_target_pairs={{0,2},{1,3},{2,0},{3,1},{4,6},{5,7},{6,4},{7,5},{8,10},{9,11},{10,... | collective-permute-start | bytes 1572872 | tf_op jit(solution)/shard_map/ppermute | solution.py:763
  189.5 17.6 %collective-permute-start.26 = (bf16[256,1024]{1,0:T(8,128)(2,1)S(1)}, bf16[256,1024]{1,0:T(8,128)(2,1)S(1)}, u32[]{:S(2)}, u32[]{:S(2)}) collective-permute-start(bf16[256,1024]{1,0:T(8,128)(2,1)S(1)} %get-tuple-element.93), channel_id=1, source_target_pairs={{0,1},{1,0},{2,3},{3,2},{4,5},{5,4},{6,7},{7,6},{8,9},{9,8},{10,11... | collective-permute-start | bytes 1572872 | tf_op jit(solution)/shard_map/ppermute | solution.py:763
  (16 other events, 67.2 us)

commit v5 on v4

--- a/solution.py
+++ b/solution.py
@@ -22,6 +22,10 @@
 
 def struct(shape, dtype):
     return jax.ShapeDtypeStruct(shape, dtype)
+
+
+def stay(x):
+    return pltpu.with_memory_space_constraint(x, pltpu.HBM)
 
 
 def fixed(shape):
@@ -242,10 +246,11 @@
     )
 
 
-def part_kernel(layout, added, _, *refs):
+def part_kernel(layout, outs, _, *refs):
     count = sum(layout)
     x_refs, w_refs = refs[:count], refs[count : count + len(layout)]
-    out_ref, held = refs[-2], refs[-1]
+    before_ref, out_refs, held = refs[-2 - outs], refs[-1 - outs : -1], refs[-1]
+    targets = [(ref, c) for ref in out_refs for c in range(ref.shape[0])]
     rows = held.shape[1]
 
     @pl.when(pl.program_id(0) == 0)
@@ -261,12 +266,11 @@
         total = dot(held[0], w_refs[0][c])
         for i in range(1, len(layout)):
             total = total + dot(held[i], w_refs[i][c])
-        if added:
-            total = total + refs[-3][c]
-        out_ref[c] = total
-
-
-def part_call(places, blocks, pieces, w_qkv, rows, cols, before=None, at=0):
+        ref, at = targets[c]
+        ref[at] = total + before_ref[c]
+
+
+def part_call(places, blocks, pieces, w_qkv, rows, cols, before, at, apart=False):
     flat = [p for piece in pieces for p in piece]
     depth = flat[0].shape[1]
     width = w_qkv.shape[2]
@@ -278,21 +282,24 @@
     specs = [
         pl.BlockSpec((rows // len(piece), depth), lambda j, o: (0, 0)) for piece in pieces for _ in piece
     ] + [block(i) for i in range(len(pieces))]
-    if before is not None:
-        ins.append(before)
-        specs.append(pl.BlockSpec((3, rows, cols), lambda j, o: (0, at, j)))
-    return call(
-        functools.partial(part_kernel, tuple(len(p) for p in pieces), before is not None),
+    ins.append(before)
+    specs.append(pl.BlockSpec((3, rows, cols), lambda j, o: (0, at, j)))
+    outs = [struct((3, rows, width), F32)]
+    if apart:
+        outs = [pltpu.HBM((1, rows, width), F32), struct((2, rows, width), F32)]
+    out = call(
+        functools.partial(part_kernel, tuple(len(p) for p in pieces), len(outs)),
         "part",
         width // cols,
         places,
         ins,
         specs,
-        (struct((3, rows, width), F32),),
-        [pl.BlockSpec((3, rows, cols), lambda j, o: (0, 0, j))],
+        outs,
+        [pl.BlockSpec((o.shape[0], rows, cols), lambda j, o: (0, 0, j)) for o in outs],
         2 * rows * depth * len(pieces) * width * 3,
         scratch=[pltpu.VMEM((len(pieces), rows, depth), BF16)],
-    )[0]
+    )
+    return out if apart else out[0]
 
 
 def state_kernel(chunk, group, size, _, *refs):
@@ -340,7 +347,7 @@
         (*far, w_qkv, w_qkv, acc, acc, inside, state),
         [fixed(far[0].shape), fixed(far[1].shape)]
         + [pl.BlockSpec((1, depth, cols), lambda j, o, c=c: (c, o[3], j)) for c in (1, 2)]
-        + [pl.BlockSpec((1, rows, cols), lambda j, o, c=c: (c, 0, j)) for c in (1, 2)]
+        + [pl.BlockSpec((1, rows, cols), lambda j, o, c=c: (c, 0, j)) for c in (0, 1)]
         + [pl.BlockSpec((rows, heads), lambda j, o: (1, 0)), small],
         (
             pltpu.HBM((rows, width), BF16),
@@ -434,69 +441,38 @@
                 combined = within_ref[:, lanes] + seen
                 power = jnp.mean(combined * combined, axis=1, keepdims=True)
                 normed_ref[rows, lanes] = (combined * lax.rsqrt(power + 1e-06)).astype(BF16)
-            out_ref[...] = dot(normed_ref[rows, :], w_ref[...]).astype(BF16)
-
-
-def head_call(places, block, q, within, entering, down, w_out, width, at):
+            out_ref[:tall, :] = dot(normed_ref[rows, :], w_ref[...]).astype(BF16)
+
+        @pl.when(pl.program_id(0) == 2 + p)
+        def _(rows=rows, out_ref=out_ref):
+            out_ref[tall:, :] = dot(normed_ref[rows, :], w_ref[...]).astype(BF16)
+
+
+def head_call(places, blocks, q, within, entering, down, w_out, width, at):
     rows, cols = q.shape
     tall = rows // 2
     heads = entering.shape[0]
-    part = pl.BlockSpec((tall, cols), lambda i, o: (i, 0))
+    part = pl.BlockSpec((tall, cols), lambda i, o: (jnp.minimum(i, 1), 0))
+    far, x, y = blocks
     return call(
         head_kernel,
         "heads",
-        2,
+        4,
         places,
         (q, within, entering, down, w_out),
         [
             part,
             part,
             fixed(entering.shape),
-            pl.BlockSpec((tall, heads), lambda i, o: (2 * at + i, 0)),
-            pl.BlockSpec((cols, width), lambda i, o: (0, o[block])),
+            pl.BlockSpec((tall, heads), lambda i, o: (2 * at + jnp.minimum(i, 1), 0)),
+            pl.BlockSpec(
+                (cols, width),
+                lambda i, o: (0, o[jnp.where(i < 2, far, jnp.where(i == 2, x, y))]),
+            ),
         ],
-        (struct((rows, cols), BF16), *[struct((tall, width), BF16)] * 2),
-        [fixed((rows, cols))] + [fixed((tall, width))] * 2,
-        2 * rows * cols * (width + 128),
-        light=True,
-    )
-
-
-def heads_near_kernel(_, q_ref, within_ref, entering_ref, down_ref, first_ref, w_ref, normed_ref, *out_refs):
-    tall = q_ref.shape[0]
-    head_kernel(_, q_ref, within_ref, entering_ref, down_ref, w_ref, normed_ref, *out_refs[:2])
-    for p, out_ref in enumerate(out_refs[2:]):
-        rows = slice(p * tall, (p + 1) * tall)
-
-        @pl.when(pl.program_id(0) == 2 + p)
-        def _(rows=rows, out_ref=out_ref):
-            out_ref[:tall, :] = dot(first_ref[rows, :], w_ref[...]).astype(BF16)
-            out_ref[tall:, :] = dot(normed_ref[rows, :], w_ref[...]).astype(BF16)
-
-
-def heads_near_call(places, q, within, entering, down, normed_a, w_out, width):
-    rows, cols = q.shape
-    tall = rows // 2
-    heads = entering.shape[0]
-    part = pl.BlockSpec((tall, cols), lambda i, o: (jnp.minimum(i, 1), 0))
-    quarter, half = (tall, width), (rows, width)
-    return call(
-        heads_near_kernel,
-        "heads_near",
-        4,
-        places,
-        (q, within, entering, down, normed_a, w_out),
-        [
-            part,
-            part,
-            fixed(entering.shape),
-            pl.BlockSpec((tall, heads), lambda i, o: (2 + jnp.minimum(i, 1), 0)),
-            fixed((rows, cols)),
-            pl.BlockSpec((cols, width), lambda i, o: (0, o[jnp.where(i < 2, 3, i - 1)])),
-        ],
-        (struct((rows, cols), BF16), *[struct(quarter, BF16)] * 2, *[struct(half, BF16)] * 2),
-        [fixed((rows, cols)), fixed(quarter), fixed(quarter), fixed(half), fixed(half)],
-        2 * rows * cols * (3 * width + 128),
+        (struct((rows, cols), BF16), *[struct((rows, width), BF16)] * 2),
+        [fixed((rows, cols))] + [fixed((rows, width))] * 2,
+        2 * rows * cols * (2 * width + 128),
         light=True,
     )
 
@@ -628,17 +604,20 @@
             x, "seq", perm=[(2 * a + c, 2 * b + c) for a, b in pairs for c in range(2)]
         )
 
-    tail_other = swap(tail)
-    tail_chip = tail + tail_other
-    tail_below = hop(tail_chip, (2, 3)) if n_chips == 4 else tail_chip
+    def chip_tails(tail):
+        other = swap(tail)
+        return other, tail + other, hop(tail + other, (2, 3)) if n_chips == 4 else None
 
     if square:
+        tokens = stay(tokens)
         q0, q1 = cut_call(tokens)
         x0, y1, x1, y0 = over_x(q0), over_y(q1), over_x(q1), over_y(q0)
         acc, q2, q3 = own_part_call(places, tokens, w_qkv, cols)
+        acc = stay(acc)
         fy0, fx1 = over_y(x0), over_x(y1)
-        x2 = over_x(after(q2, x1, y0, tail_below, inside))
-        y3 = over_y(after(q3, x1, y0, tail_below, inside))
+        tail_other, tail_chip, tail_below = chip_tails(after(tail, x0, y1))
+        x2 = over_x(after(q2, x1, y0, tail_chip))
+        y3 = over_y(after(q3, x1, y0, tail_chip))
         acc_a = part_call(
             places,
             (1, 2),
@@ -646,10 +625,11 @@
             w_qkv,
             2 * quarter,
             cols,
-            before=acc,
+            before=stay(after(acc, tail_chip)),
             at=0,
         )
-        x3, y2 = over_x(after(q3, fy0, fx1, acc_a)), over_y(after(q2, fy0, fx1, acc_a))
+        earlier = (fy0, fx1, acc_a) if tail_below is None else (fy0, fx1, acc_a, tail_below)
+        x3, y2 = over_x(after(q3, *earlier)), over_y(after(q2, *earlier))
         query_a, within_a, state = first_call(
             places,
             (3,),
@@ -664,7 +644,7 @@
             group,
         )
         fy2, fx3 = over_y(after(x2, state)), over_x(after(y3, state))
-        acc_b = part_call(
+        acc_q, acc_kv = part_call(
             places,
             (1, 2),
             [(x2, x3), (y2, y3)],
@@ -673,12 +653,14 @@
             cols,
             before=acc,
             at=1,
+            apart=True,
         )
         far = (fy2, fx3)
         k, v, mid, state, sent = state_call(
-            places, far, w_qkv, acc_b, inside, state, quarter, group
+            places, far, w_qkv, acc_kv, inside, state, quarter, group
         )
     else:
+        tail_other, tail_chip, tail_below = chip_tails(tail)
         gathered = lax.all_gather(tokens, "head", axis=1, tiled=True)
         query, within, state = first_call(
             places, (), [(gathered,)], (), w_qkv, along, inside, rows, quarter, size, group
@@ -707,11 +689,6 @@
         chip_entering = jnp.where(chip == 1, arriving.astype(F32), chip_entering)
         sum_first = leaving()
         to_third, to_second = hop(sum_first, (1, 3)), hop(sum_first, (1, 2))
-        if square:
-            query_b, within_b = later_call(
-                places, far, w_qkv, acc_b, k, v, along, inside, after(mid, sum_first), group
-            )
-            to_third, to_second, _ = lax.optimization_barrier((to_third, to_second, query_b))
         third = jnp.exp(-mine(tail_below))[:, None, None] * to_third.astype(F32)
         chip_entering = jnp.where(chip == 2, to_second.astype(F32), chip_entering)
         chip_entering = jnp.where(chip == 3, third + arriving.astype(F32), chip_entering)
@@ -719,10 +696,6 @@
         for step in range(n_chips - 1):
             arriving = hop(leaving(), (step, step + 1))
             chip_entering = jnp.where(chip == step + 1, arriving.astype(F32), chip_entering)
-        if square:
-            query_b, within_b = later_call(
-                places, far, w_qkv, acc_b, k, v, along, inside, mid, group
-            )
     there = swap(chip_entering.astype(BF16)).astype(F32)
     entering = jnp.concatenate(
         [jnp.where(core == 0, chip_entering, there), jnp.where(core == 0, there, chip_entering)]
@@ -735,7 +708,7 @@
         halves = [
             head_call(
                 places,
-                0,
+                (0, 0, 0),
                 query[r * rows // 2 : (r + 1) * rows // 2],
                 within[r * rows // 2 : (r + 1) * rows // 2],
                 entering,
@@ -749,21 +722,25 @@
         partial = dot(jnp.concatenate(halves), w_out).astype(BF16)
         return lax.psum_scatter(partial, "head", scatter_dimension=1, tiled=True)
 
-    na, far0, far1 = head_call(places, 3, query_a, within_a, entering, down, w_out, width, 0)
-    far0, far1 = over_x(far0), over_y(far1)
-    nb, far2, far3, near_x, near_y = heads_near_call(
-        places, query_b, within_b, entering, down, na, w_out, width
-    )
-    near_x, near_y = over_x(after(near_x, far0, far1)), over_y(after(near_y, far0, far1))
-    far2, far3 = over_x(far2), over_y(far3)
-    sum1, sum0 = pair_call(places, after(na, near_x, near_y), far1, far0, w_out, width)
-    far2, far3 = after(far2, sum1), after(far3, sum1)
+    na, by_x, by_y = head_call(
+        places, (3, 1, 2), query_a, within_a, entering, down, w_out, width, 0
+    )
+    by_x, by_y = over_x(by_x), over_y(by_y)
+    query_b, within_b = later_call(
+        places, far, w_qkv, stay(acc_q), stay(k), stay(v), along, inside, stay(after(mid, na)), group
+    )
+    nb, by_x2, by_y2 = head_call(
+        places, (3, 1, 2), query_b, within_b, entering, down, w_out, width, 1
+    )
+    by_x2, by_y2 = over_x(by_x2), over_y(by_y2)
+    sum1, sum0 = pair_call(places, after(na, nb), by_y, by_x, w_out, width)
+    by_x2, by_y2 = after(by_x2, sum1), after(by_y2, sum1)
     sum1, sum0 = over_x(sum1), over_y(sum0)
-    sum3, sum2 = pair_call(places, nb, far3, far2, w_out, width)
+    sum3, sum2 = pair_call(places, nb, by_y2, by_x2, w_out, width)
     sum3, sum2 = over_x(sum3), over_y(sum2)
-    below = own_call(places, nb, ((near_x, 1),), ((near_y, 1),), w_out, width, 1)
+    below = own_call(places, after(nb, sum1, sum0), ((by_x2, 1),), ((by_y2, 1),), w_out, width, 1)
     above = own_call(
-        places, na, ((near_x, 0), (sum0, 0)), ((near_y, 0), (sum1, 0)), w_out, width, 2
+        places, na, ((by_x, 1), (sum0, 0)), ((by_y, 1), (sum1, 0)), w_out, width, 2
     )
     return last_call(below, sum2, sum3, above)
 

time: 209 us -> 193 us (0.923)
  local copies, waits for them, and re-layouts: 21.6 us -> 5.11 us
  waiting for transfers between devices: 64.9 us -> 58.6 us
  Pallas kernels: 86.2 us -> 90 us
  other arithmetic: 3.44 us -> 6.69 us
    unnamed x38 -> x24, local copies, waits for them, and re-layouts: 21.5 us -> 5 us
    ppermute x2, waiting for transfers between devices: 5.84 us -> 0.01 us  [local(): fy0, fx1 = (over_y(x0), over_x(y1))]
    pallas_call x15, Pallas kernels: 86.2 us -> 90 us  [call(): pl.pallas_call(kernel, out_shape=tuple(outs), grid_spec=pltpu.PrefetchSca...]
    ppermute x11 -> x9, waiting for transfers between devices: 35 us -> 31.5 us  [the longest x2 17 us: local(): by_x2, by_y2 = (over_x(by_x2), over_y(by_y2))]
    ppermute x11 -> x9, starting transfers between devices: 9 us -> 8.37 us  [the longest x2 3.01 us: local(): x3, y2 = (over_x(after(q3, *earlier)), over_y(after(q2, *earlier)))]
  transfers between devices with their start and end apart: 29 -> 27, of which waited for: 13 -> 12; matrix products, arithmetic and copies ran while one was open for 0% -> 0% of each run, Pallas kernels for 34% -> 38%
where the time goes in v5:
time: 193 us; the launch traced here: 192 us
  Pallas kernels  90 us (47%)
  waiting for transfers between devices  58.6 us (30%)
  starting transfers between devices  31.3 us (16%)
  other arithmetic  6.69 us (3%)
  local copies, waits for them, and re-layouts  5.11 us (3%)
    pallas_call x15, Pallas kernels, call(): pl.pallas_call(kernel, out_shape=tuple(outs), grid_spec=pltpu.PrefetchSca...  90 us
    ppermute x2, waiting for transfers between devices, local(): by_x2, by_y2 = (over_x(by_x2), over_y(by_y2))  17 us
    ppermute x4, starting transfers between devices, hop(): lax.ppermute(x, 'seq', perm=[(2 * a + c, 2 * b + c) for a, b in pairs for...  8.56 us
    ppermute x4, waiting for transfers between devices, hop(): lax.ppermute(x, 'seq', perm=[(2 * a + c, 2 * b + c) for a, b in pairs for...  8.1 us
    ppermute x2, waiting for transfers between devices, local(): by_x, by_y = (over_x(by_x), over_y(by_y))  7.38 us
    ppermute x2, waiting for transfers between devices, local(): x3, y2 = (over_x(after(q3, *earlier)), over_y(after(q2, *earlier)))  7.05 us
    ppermute x2, waiting for transfers between devices, local(): sum1, sum0 = (over_x(sum1), over_y(sum0))  5.8 us
    ppermute x4, waiting for transfers between devices, local(): x0, y1, x1, y0 = (over_x(q0), over_y(q1), over_x(q1), over_y(q0))  5.69 us
  transfers between devices with their start and end apart: 27, of which 12 were waited for; matrix products, arithmetic and copies ran while one was open for 0% of the time, Pallas kernels for 38%

profile of v5, /device:TPU:8, one launch (start us, length us, event | category | flops | bytes accessed | tf_op | source)
XLA Modules:
  0.0 192.0 jit_solution(5404029313086951874)
XLA Ops:
  0.0 2.2 %cut.1 = (bf16[256,1024]{1,0:T(8,128)(2,1)}, bf16[256,1024]{1,0:T(8,128)(2,1)}) custom-call(s32[1]{0:T(128)} %constant.32.clone.1._, bf16[1024,1024]{1,0:T(8,128)(2,1)} %x_ref.3), custom_call_target="tpu_custom_call" | custom-call | flops 1 | bytes 3145728 | tf_op jit(solution)/shard_map/cut/pallas_call | solution.py:39
  2.2 1.5 collective-permute-start.1
  6.4 12.6 %own_part.1 = (f32[3,1024,1024]{2,1,0:T(8,128)}, bf16[256,1024]{1,0:T(8,128)(2,1)S(1)}, bf16[256,1024]{1,0:T(8,128)(2,1)S(1)}) custom-call(s32[4]{0:T(128)S(1)} %pad_add_fusion._, bf16[1024,1024]{1,0:T(8,128)(2,1)} %x_ref.3, bf16[3,4096,1024]{2,1,0:T(8,128)(2,1)} %refs_2_.5), custom_call_target="tpu_custom_call" | custom-call | flops 6442450944 | bytes 40894464 | tf_op jit(solution)/shard_map/own_part/pallas_call | solution.py:39
  21.7 5.7 %collective-permute-done.3.refs_3_ = bf16[256,1024]{1,0:T(8,128)(2,1)S(1)} collective-permute-done((bf16[256,1024]{1,0:T(8,128)(2,1)}, bf16[256,1024]{1,0:T(8,128)(2,1)S(1)}, u32[]{:S(2)}, u32[]{:S(2)}) %collective-permute-start.3) | collective-permute-done | bytes 524320 | tf_op jit(solution)/shard_map/ppermute | solution.py:614
  27.3 1.5 collective-permute-start.6
  32.2 11.5 %part.2.refs_3_ = f32[3,512,1024]{2,1,0:T(8,128)S(1)} custom-call(s32[4]{0:T(128)S(1)} %pad_add_fusion._, bf16[256,1024]{1,0:T(8,128)(2,1)S(1)} %collective-permute-done.2.refs_0_, bf16[256,1024]{1,0:T(8,128)(2,1)S(1)} %collective-permute-done.refs_1_, bf16[256,1024]{1,0:T(8,128)(2,1)S(1)} %collective-permute-done.1.refs_2_, ...), custom_call_target="tpu_custom_call" | custom-call | flops 6442450944 | bytes 71303168 | tf_op jit(solution)/shard_map/part/pallas_call | solution.py:39
  45.2 1.5 collective-permute-start.13
  46.8 11.2 %first.1 = (bf16[512,1024]{1,0:T(8,128)(2,1)}, f32[512,1024]{1,0:T(8,128)}, f32[8,128,128]{2,1,0:T(8,128)S(1)}) custom-call(s32[4]{0:T(128)S(1)} %pad_add_fusion._, bf16[256,1024]{1,0:T(8,128)(2,1)S(1)} %collective-permute-done.6.refs_0_, bf16[256,1024]{1,0:T(8,128)(2,1)S(1)} %collective-permute-done.7.refs_1_, bf16[3,4096,1024]{2,1,0:T(8,128)(2,1)} %refs_2_.5, ...), custom_call_target="tpu_custom_call" | custom-call | flops 3221225472 | bytes 36241408 | tf_op jit(solution)/shard_map/first/pallas_call | solution.py:39
  59.0 7.0 %collective-permute-done.12.refs_1_ = bf16[256,1024]{1,0:T(8,128)(2,1)S(1)} collective-permute-done((bf16[256,1024]{1,0:T(8,128)(2,1)S(1)}, bf16[256,1024]{1,0:T(8,128)(2,1)S(1)}, u32[]{:S(2)}, u32[]{:S(2)}) %collective-permute-start.12) | collective-permute-done | bytes 524320 | tf_op jit(solution)/shard_map/ppermute | solution.py:632
  66.1 11.7 %part.3 = (f32[1,512,1024]{2,1,0:T(8,128)}, f32[2,512,1024]{2,1,0:T(8,128)S(1)}) custom-call(s32[4]{0:T(128)S(1)} %pad_add_fusion._, bf16[256,1024]{1,0:T(8,128)(2,1)S(1)} %collective-permute-done.5.refs_0_, bf16[256,1024]{1,0:T(8,128)(2,1)S(1)} %collective-permute-done.12.refs_1_, bf16[256,1024]{1,0:T(8,128)(2,1)S(1)} %collective-permute-done.13.refs_2_, ...), custom_call_target="tpu_custom_call" | custom-call | flops 6442450944 | bytes 71303168 | tf_op jit(solution)/shard_map/part/pallas_call | solution.py:39
  77.8 6.9 %states.1 = (bf16[512,1024]{1,0:T(8,128)(2,1)}, bf16[512,1024]{1,0:T(8,128)(2,1)}, f32[2,8,128,128]{3,2,1,0:T(8,128)}, f32[8,128,128]{2,1,0:T(8,128)S(1)}, bf16[8,128,128]{2,1,0:T(8,128)(2,1)S(1)}) custom-call(s32[4]{0:T(128)S(1)} %pad_add_fusion._, bf16[256,1024]{1,0:T(8,128)(2,1)S(1)} %collective-permute-done.8.refs_0_, ...), custom_call_target="tpu_custom_call" | custom-call | flops 2147483648 | bytes 64258048 | tf_op jit(solution)/shard_map/states/pallas_call | solution.py:39
  84.9 1.6 collective-permute-done.14
  90.8 6.3 %collective-permute-done.15 = bf16[4,128,128]{2,1,0:T(8,128)(2,1)S(1)} collective-permute-done((bf16[4,128,128]{2,1,0:T(8,128)(2,1)}, bf16[4,128,128]{2,1,0:T(8,128)(2,1)S(1)}, u32[]{:S(2)}, u32[]{:S(2)}) %collective-permute-start.15) | collective-permute-done | bytes 131104 | tf_op jit(solution)/shard_map/ppermute | solution.py:603
  98.3 3.4 %collective-permute-start.17 = (bf16[4,128,128]{2,1,0:T(8,128)(2,1)S(1)}, bf16[4,128,128]{2,1,0:T(8,128)(2,1)}, u32[]{:S(2)}, u32[]{:S(2)}) collective-permute-start(bf16[4,128,128]{2,1,0:T(8,128)(2,1)S(1)} %add_convert_fusion), channel_id=1, source_target_pairs={{8,16},{12,20},{9,17},{13,21},{10,18},{14,22},{11,19},{15,23}} | collective-permute-start | bytes 393224 | tf_op jit(solution)/shard_map/ppermute | solution.py:603
  101.6 3.1 %collective-permute-start.16 = (bf16[4,128,128]{2,1,0:T(8,128)(2,1)S(1)}, bf16[4,128,128]{2,1,0:T(8,128)(2,1)}, u32[]{:S(2)}, u32[]{:S(2)}) collective-permute-start(bf16[4,128,128]{2,1,0:T(8,128)(2,1)S(1)} %add_convert_fusion), channel_id=1, source_target_pairs={{8,24},{12,28},{9,25},{13,29},{10,26},{14,30},{11,27},{15,31}} | collective-permute-start | bytes 393224 | tf_op jit(solution)/shard_map/ppermute | solution.py:603
  104.8 1.8 collective-permute-done.16
  110.4 3.4 %copy-done = bf16[1024,4096]{1,0:T(8,128)(2,1)S(1)} copy-done((bf16[1024,4096]{1,0:T(8,128)(2,1)S(1)}, bf16[1024,4096]{1,0:T(8,128)(2,1)}, u32[]{:S(2)}) %copy-start) | copy-done | bytes 8388632
  113.8 6.7 %heads.2 = (bf16[512,1024]{1,0:T(8,128)(2,1)S(1)}, bf16[512,1024]{1,0:T(8,128)(2,1)S(1)}, bf16[512,1024]{1,0:T(8,128)(2,1)S(1)}) custom-call(s32[4]{0:T(128)S(1)} %pad_add_fusion._, bf16[512,1024]{1,0:T(8,128)(2,1)S(1)} %copy-done.2, f32[512,1024]{1,0:T(8,128)S(1)} %copy-done.1, bf16[8,128,128]{2,1,0:T(8,128)(2,1)S(1)} %select_convert_fusion.entering_ref, ...), custom_call_target="tpu_custom_call" | custom-call | flops 1 | bytes 1 | tf_op jit(solution)/shard_map/heads/pallas_call | solution.py:39
  122.6 8.3 %later.1 = (bf16[512,1024]{1,0:T(8,128)(2,1)S(1)}, f32[512,1024]{1,0:T(8,128)S(1)}) custom-call(s32[4]{0:T(128)S(1)} %pad_add_fusion._, bf16[256,1024]{1,0:T(8,128)(2,1)S(1)} %collective-permute-done.8.refs_0_, bf16[256,1024]{1,0:T(8,128)(2,1)S(1)} %collective-permute-done.10.refs_1_, bf16[3,4096,1024]{2,1,0:T(8,128)(2,1)} %refs_2_.5, ...), custom_call_target="tpu_custom_call" | custom-call | flops 1879048192 | bytes 34668544 | tf_op jit(solution)/shard_map/later/pallas_call | solution.py:39
  130.9 6.7 %heads.3 = (bf16[512,1024]{1,0:T(8,128)(2,1)S(1)}, bf16[512,1024]{1,0:T(8,128)(2,1)S(1)}, bf16[512,1024]{1,0:T(8,128)(2,1)S(1)}) custom-call(s32[4]{0:T(128)S(1)} %pad_add_fusion._, bf16[512,1024]{1,0:T(8,128)(2,1)S(1)} %get-tuple-element.78.q_ref, f32[512,1024]{1,0:T(8,128)S(1)} %get-tuple-element.79.within_ref, ...), custom_call_target="tpu_custom_call" | custom-call | flops 1 | bytes 1 | tf_op jit(solution)/shard_map/heads/pallas_call | solution.py:39
  138.2 1.5 collective-permute-start.24
  139.7 6.8 %collective-permute-done.19.x_ref.refs_2_ = bf16[512,1024]{1,0:T(8,128)(2,1)S(1)} collective-permute-done((bf16[512,1024]{1,0:T(8,128)(2,1)S(1)}, bf16[512,1024]{1,0:T(8,128)(2,1)S(1)}, u32[]{:S(2)}, u32[]{:S(2)}) %collective-permute-start.19) | collective-permute-done | bytes 1048608 | tf_op jit(solution)/shard_map/ppermute | solution.py:728
  147.1 2.3 %sum_pair.2 = (bf16[256,1024]{1,0:T(8,128)(2,1)S(1)}, bf16[256,1024]{1,0:T(8,128)(2,1)S(1)}) custom-call(s32[4]{0:T(128)S(1)} %pad_add_fusion._, bf16[512,1024]{1,0:T(8,128)(2,1)S(1)} %get-tuple-element.81.normed_ref, bf16[512,1024]{1,0:T(8,128)(2,1)S(1)} %collective-permute-done.19.x_ref.refs_2_, ...), custom_call_target="tpu_custom_call" | custom-call | flops 1 | bytes 1 | tf_op jit(solution)/shard_map/sum_pair/pallas_call | solution.py:39
  149.5 1.6 collective-permute-start.21
  151.0 1.5 collective-permute-start.22
  152.5 17.0 %collective-permute-done.23.refs_0_.y_ref = bf16[512,1024]{1,0:T(8,128)(2,1)S(1)} collective-permute-done((bf16[512,1024]{1,0:T(8,128)(2,1)S(1)}, bf16[512,1024]{1,0:T(8,128)(2,1)S(1)}, u32[]{:S(2)}, u32[]{:S(2)}) %collective-permute-start.23) | collective-permute-done | bytes 1048608 | tf_op jit(solution)/shard_map/ppermute | solution.py:735
  169.6 2.3 %sum_pair.3 = (bf16[256,1024]{1,0:T(8,128)(2,1)S(1)}, bf16[256,1024]{1,0:T(8,128)(2,1)S(1)}) custom-call(s32[4]{0:T(128)S(1)} %pad_add_fusion._, bf16[512,1024]{1,0:T(8,128)(2,1)S(1)} %get-tuple-element.86.normed_ref, bf16[512,1024]{1,0:T(8,128)(2,1)S(1)} %collective-permute-done.24.refs_1_.x_ref, ...), custom_call_target="tpu_custom_call" | custom-call | flops 1 | bytes 1 | tf_op jit(solution)/shard_map/sum_pair/pallas_call | solution.py:39
  171.9 1.6 collective-permute-start.25
  175.0 5.8 %collective-permute-done.21.refs_3_ = bf16[256,1024]{1,0:T(8,128)(2,1)S(1)} collective-permute-done((bf16[256,1024]{1,0:T(8,128)(2,1)S(1)}, bf16[256,1024]{1,0:T(8,128)(2,1)S(1)}, u32[]{:S(2)}, u32[]{:S(2)}) %collective-permute-start.21) | collective-permute-done | bytes 524320 | tf_op jit(solution)/shard_map/ppermute | solution.py:738
  180.8 2.4 %own_block.2.kept_ref = bf16[512,1024]{1,0:T(8,128)(2,1)S(1)} custom-call(s32[4]{0:T(128)S(1)} %pad_add_fusion._, bf16[512,1024]{1,0:T(8,128)(2,1)S(1)} %get-tuple-element.86.normed_ref, bf16[1024,4096]{1,0:T(8,128)(2,1)S(1)} %bitcast.5, bf16[512,1024]{1,0:T(8,128)(2,1)S(1)} %collective-permute-done.23.refs_0_.y_ref, ...), custom_call_target="tpu_custom_call" | custom-call | flops 1 | bytes 1 | tf_op jit(solution)/shard_map/own_block/pallas_call | solution.py:39
  183.2 3.1 %own_block.3.above_ref = bf16[1024,1024]{1,0:T(8,128)(2,1)} custom-call(s32[4]{0:T(128)S(1)} %pad_add_fusion._, bf16[512,1024]{1,0:T(8,128)(2,1)S(1)} %get-tuple-element.81.normed_ref, bf16[1024,4096]{1,0:T(8,128)(2,1)S(1)} %bitcast.5, bf16[512,1024]{1,0:T(8,128)(2,1)S(1)} %collective-permute-done.20.y_ref.refs_0_, ...), custom_call_target="tpu_custom_call" | custom-call | flops 1 | bytes 1 | tf_op jit(solution)/shard_map/own_block/pallas_call | solution.py:39
  186.3 4.4 %collective-permute-done.25.a_ref = bf16[256,1024]{1,0:T(8,128)(2,1)S(1)} collective-permute-done((bf16[256,1024]{1,0:T(8,128)(2,1)S(1)}, bf16[256,1024]{1,0:T(8,128)(2,1)S(1)}, u32[]{:S(2)}, u32[]{:S(2)}) %collective-permute-start.25) | collective-permute-done | bytes 524320 | tf_op jit(solution)/shard_map/ppermute | solution.py:740
  (74 shorter events, 26.8 us)
Async XLA Ops:
  2.2 28.8 %collective-permute-start.1 = (bf16[256,1024]{1,0:T(8,128)(2,1)}, bf16[256,1024]{1,0:T(8,128)(2,1)S(1)}, u32[]{:S(2)}, u32[]{:S(2)}) collective-permute-start(bf16[256,1024]{1,0:T(8,128)(2,1)} %get-tuple-element.51), channel_id=1, source_target_pairs={{0,2},{1,3},{2,0},{3,1},{4,6},{5,7},{6,4},{7,5},{8,10},{9,11},{10,... | collective-permute-start | bytes 1572872 | tf_op jit(solution)/shard_map/ppermute | solution.py:614
  3.8 17.9 %collective-permute-start.2 = (bf16[256,1024]{1,0:T(8,128)(2,1)}, bf16[256,1024]{1,0:T(8,128)(2,1)S(1)}, u32[]{:S(2)}, u32[]{:S(2)}) collective-permute-start(bf16[256,1024]{1,0:T(8,128)(2,1)} %get-tuple-element.51), channel_id=1, source_target_pairs={{0,1},{1,0},{2,3},{3,2},{4,5},{5,4},{6,7},{7,6},{8,9},{9,8},{10,11... | collective-permute-start | bytes 1572872 | tf_op jit(solution)/shard_map/ppermute | solution.py:614
  5.2 25.8 %collective-permute-start = (bf16[256,1024]{1,0:T(8,128)(2,1)}, bf16[256,1024]{1,0:T(8,128)(2,1)S(1)}, u32[]{:S(2)}, u32[]{:S(2)}) collective-permute-start(bf16[256,1024]{1,0:T(8,128)(2,1)} %get-tuple-element.50), channel_id=1, source_target_pairs={{0,1},{1,0},{2,3},{3,2},{4,5},{5,4},{6,7},{7,6},{8,9},{9,8},{10,11... | collective-permute-start | bytes 1572872 | tf_op jit(solution)/shard_map/ppermute | solution.py:614
  5.8 21.6 %collective-permute-start.3 = (bf16[256,1024]{1,0:T(8,128)(2,1)}, bf16[256,1024]{1,0:T(8,128)(2,1)S(1)}, u32[]{:S(2)}, u32[]{:S(2)}) collective-permute-start(bf16[256,1024]{1,0:T(8,128)(2,1)} %get-tuple-element.50), channel_id=1, source_target_pairs={{0,2},{1,3},{2,0},{3,1},{4,6},{5,7},{6,4},{7,5},{8,10},{9,11},{10,... | collective-permute-start | bytes 1572872 | tf_op jit(solution)/shard_map/ppermute | solution.py:614
  6.4 14.2 %copy-start.3 = (f32[8,1024]{1,0:T(8,128)S(1)}, f32[8,1024]{1,0:T(8,128)}, u32[]{:S(2)}) copy-start(f32[8,1024]{1,0:T(8,128)} %rate_ref.1) | copy-start | bytes 98308
  27.3 3.0 %collective-permute-start.4 = (f32[8]{0:T(128)S(1)}, f32[8]{0:T(128)S(1)}, u32[]{:S(2)}, u32[]{:S(2)}) collective-permute-start(f32[8]{0:T(128)S(1)} %slice_reduce_fusion), channel_id=1, source_target_pairs={{0,4},{4,0},{8,12},{12,8},{16,20},{20,16},{24,28},{28,24},{1,5},{5... | collective-permute-start | bytes 104 | tf_op jit(solution)/shard_map/ppermute | solution.py:608
  27.3 16.4 %collective-permute-start.6 = (bf16[256,1024]{1,0:T(8,128)(2,1)S(1)}, bf16[256,1024]{1,0:T(8,128)(2,1)S(1)}, u32[]{:S(2)}, u32[]{:S(2)}) collective-permute-start(bf16[256,1024]{1,0:T(8,128)(2,1)S(1)} %collective-permute-done.2.refs_0_), channel_id=1, source_target_pairs={{0,2},{1,3},{2,0},{3,1},{4,6},{5,7},{6,4},{7,5},{8,10},{9,11},{10,... | collective-permute-start | bytes 1572872 | tf_op jit(solution)/shard_map/ppermute | solution.py:617
  28.9 14.9 %collective-permute-start.7 = (bf16[256,1024]{1,0:T(8,128)(2,1)S(1)}, bf16[256,1024]{1,0:T(8,128)(2,1)S(1)}, u32[]{:S(2)}, u32[]{:S(2)}) collective-permute-start(bf16[256,1024]{1,0:T(8,128)(2,1)S(1)} %collective-permute-done.3.refs_3_), channel_id=1, source_target_pairs={{0,1},{1,0},{2,3},{3,2},{4,5},{5,4},{6,7},{7,6},{8,9},{9,8},{10,11... | collective-permute-start | bytes 1572872 | tf_op jit(solution)/shard_map/ppermute | solution.py:617
  30.4 13.3 %collective-permute-start.11 = (f32[8]{0:T(128)S(1)}, f32[8]{0:T(128)S(1)}, u32[]{:S(2)}, u32[]{:S(2)}) collective-permute-start(f32[8]{0:T(128)S(1)} %get-tuple-element.101), channel_id=1, source_target_pairs={{16,24},{20,28},{17,25},{21,29},{18,26},{22,30},{19,27},{23,31}} | collective-permute-start | bytes 104 | tf_op jit(solution)/shard_map/ppermute | solution.py:603
  31.1 26.9 %collective-permute-start.5 = (bf16[256,1024]{1,0:T(8,128)(2,1)}, bf16[256,1024]{1,0:T(8,128)(2,1)S(1)}, u32[]{:S(2)}, u32[]{:S(2)}) collective-permute-start(bf16[256,1024]{1,0:T(8,128)(2,1)} %copy-done.4), channel_id=1, source_target_pairs={{0,1},{1,0},{2,3},{3,2},{4,5},{5,4},{6,7},{7,6},{8,9},{9,8},{10,11... | collective-permute-start | bytes 1572872 | tf_op jit(solution)/shard_map/ppermute | solution.py:619
  31.7 12.1 %copy-start.7 = (bf16[256,1024]{1,0:T(8,128)(2,1)S(1)}, bf16[256,1024]{1,0:T(8,128)(2,1)}, u32[]{:S(2)}) copy-start(bf16[256,1024]{1,0:T(8,128)(2,1)} %copy-done.6) | copy-start | bytes 1572868
  31.7 13.6 %copy-start.5 = (bf16[256,1024]{1,0:T(8,128)(2,1)S(1)}, bf16[256,1024]{1,0:T(8,128)(2,1)}, u32[]{:S(2)}) copy-start(bf16[256,1024]{1,0:T(8,128)(2,1)} %copy-done.4) | copy-start | bytes 1572868
  31.7 26.8 %collective-permute-start.9 = (bf16[256,1024]{1,0:T(8,128)(2,1)}, bf16[256,1024]{1,0:T(8,128)(2,1)S(1)}, u32[]{:S(2)}, u32[]{:S(2)}) collective-permute-start(bf16[256,1024]{1,0:T(8,128)(2,1)} %copy-done.6), channel_id=1, source_target_pairs={{0,2},{1,3},{2,0},{3,1},{4,6},{5,7},{6,4},{7,5},{8,10},{9,11},{10,... | collective-permute-start | bytes 1572872 | tf_op jit(solution)/shard_map/ppermute | solution.py:620
  43.7 22.4 %collective-permute-start.12 = (bf16[256,1024]{1,0:T(8,128)(2,1)S(1)}, bf16[256,1024]{1,0:T(8,128)(2,1)S(1)}, u32[]{:S(2)}, u32[]{:S(2)}) collective-permute-start(bf16[256,1024]{1,0:T(8,128)(2,1)S(1)} %copy-done.7), channel_id=1, source_target_pairs={{0,1},{1,0},{2,3},{3,2},{4,5},{5,4},{6,7},{7,6},{8,9},{9,8},{10,11... | collective-permute-start | bytes 1572872 | tf_op jit(solution)/shard_map/ppermute | solution.py:632
  45.2 20.9 %collective-permute-start.13 = (bf16[256,1024]{1,0:T(8,128)(2,1)S(1)}, bf16[256,1024]{1,0:T(8,128)(2,1)S(1)}, u32[]{:S(2)}, u32[]{:S(2)}) collective-permute-start(bf16[256,1024]{1,0:T(8,128)(2,1)S(1)} %copy-done.5), channel_id=1, source_target_pairs={{0,2},{1,3},{2,0},{3,1},{4,6},{5,7},{6,4},{7,5},{8,10},{9,11},{10,... | collective-permute-start | bytes 1572872 | tf_op jit(solution)/shard_map/ppermute | solution.py:632
  57.9 19.9 %collective-permute-start.8 = (bf16[256,1024]{1,0:T(8,128)(2,1)S(1)}, bf16[256,1024]{1,0:T(8,128)(2,1)S(1)}, u32[]{:S(2)}, u32[]{:S(2)}) collective-permute-start(bf16[256,1024]{1,0:T(8,128)(2,1)S(1)} %collective-permute-done.5.refs_0_), channel_id=1, source_target_pairs={{0,2},{1,3},{2,0},{3,1},{4,6},{5,7},{6,4},{7,5},{8,10},{9,11},{10,... | collective-permute-start | bytes 1572872 | tf_op jit(solution)/shard_map/ppermute | solution.py:646
  58.4 19.3 %collective-permute-start.10 = (bf16[256,1024]{1,0:T(8,128)(2,1)S(1)}, bf16[256,1024]{1,0:T(8,128)(2,1)S(1)}, u32[]{:S(2)}, u32[]{:S(2)}) collective-permute-start(bf16[256,1024]{1,0:T(8,128)(2,1)S(1)} %collective-permute-done.9.refs_3_), channel_id=1, source_target_pairs={{0,1},{1,0},{2,3},{3,2},{4,5},{5,4},{6,7},{7,6},{8,9},{9,8},{10,11... | collective-permute-start | bytes 1572872 | tf_op jit(solution)/shard_map/ppermute | solution.py:646
  84.7 1.7 collective-permute-start.14
  89.4 21.1 %copy-start.2 = (bf16[512,1024]{1,0:T(8,128)(2,1)S(1)}, bf16[512,1024]{1,0:T(8,128)(2,1)}, u32[]{:S(2)}) copy-start(bf16[512,1024]{1,0:T(8,128)(2,1)} %get-tuple-element.71.q_ref) | copy-start | bytes 3145732
  89.4 7.8 %collective-permute-start.15 = (bf16[4,128,128]{2,1,0:T(8,128)(2,1)}, bf16[4,128,128]{2,1,0:T(8,128)(2,1)S(1)}, u32[]{:S(2)}, u32[]{:S(2)}) collective-permute-start(bf16[4,128,128]{2,1,0:T(8,128)(2,1)} %get-tuple-element.95), channel_id=1, source_target_pairs={{0,8},{4,12},{16,24},{20,28},{1,9},{5,13},{17,25},{21,29},{2,10},{... | collective-permute-start | bytes 393224 | tf_op jit(solution)/shard_map/ppermute | solution.py:603
  98.3 6.6 %collective-permute-start.17 = (bf16[4,128,128]{2,1,0:T(8,128)(2,1)S(1)}, bf16[4,128,128]{2,1,0:T(8,128)(2,1)}, u32[]{:S(2)}, u32[]{:S(2)}) collective-permute-start(bf16[4,128,128]{2,1,0:T(8,128)(2,1)S(1)} %add_convert_fusion), channel_id=1, source_target_pairs={{8,16},{12,20},{9,17},{13,21},{10,18},{14,22},{11,19},{15,23}} | collective-permute-start | bytes 393224 | tf_op jit(solution)/shard_map/ppermute | solution.py:603
  101.6 5.0 %collective-permute-start.16 = (bf16[4,128,128]{2,1,0:T(8,128)(2,1)S(1)}, bf16[4,128,128]{2,1,0:T(8,128)(2,1)}, u32[]{:S(2)}, u32[]{:S(2)}) collective-permute-start(bf16[4,128,128]{2,1,0:T(8,128)(2,1)S(1)} %add_convert_fusion), channel_id=1, source_target_pairs={{8,24},{12,28},{9,25},{13,29},{10,26},{14,30},{11,27},{15,31}} | collective-permute-start | bytes 393224 | tf_op jit(solution)/shard_map/ppermute | solution.py:603
  107.8 1.4 collective-permute-start.18
  120.5 26.1 %collective-permute-start.19 = (bf16[512,1024]{1,0:T(8,128)(2,1)S(1)}, bf16[512,1024]{1,0:T(8,128)(2,1)S(1)}, u32[]{:S(2)}, u32[]{:S(2)}) collective-permute-start(bf16[512,1024]{1,0:T(8,128)(2,1)S(1)} %get-tuple-element.82), channel_id=1, source_target_pairs={{0,2},{1,3},{2,0},{3,1},{4,6},{5,7},{6,4},{7,5},{8,10},{9,11},{10,... | collective-permute-start | bytes 3145736 | tf_op jit(solution)/shard_map/ppermute | solution.py:728
  121.1 26.0 %collective-permute-start.20 = (bf16[512,1024]{1,0:T(8,128)(2,1)S(1)}, bf16[512,1024]{1,0:T(8,128)(2,1)S(1)}, u32[]{:S(2)}, u32[]{:S(2)}) collective-permute-start(bf16[512,1024]{1,0:T(8,128)(2,1)S(1)} %get-tuple-element.83), channel_id=1, source_target_pairs={{0,1},{1,0},{2,3},{3,2},{4,5},{5,4},{6,7},{7,6},{8,9},{9,8},{10,11... | collective-permute-start | bytes 3145736 | tf_op jit(solution)/shard_map/ppermute | solution.py:728
  122.6 8.3 %slice-start.1 = ((s8[8388608]{0:T(1024)(128)(4,1)}), s8[4194304]{0:T(1024)(128)(4,1)S(1)}, s32[]{:S(2)}) async-start(s8[8388608]{0:T(1024)(128)(4,1)} %bitcast.4), calls=%async_computation.1 | async-start | bytes 8388608
  137.6 32.0 %collective-permute-start.23 = (bf16[512,1024]{1,0:T(8,128)(2,1)S(1)}, bf16[512,1024]{1,0:T(8,128)(2,1)S(1)}, u32[]{:S(2)}, u32[]{:S(2)}) collective-permute-start(bf16[512,1024]{1,0:T(8,128)(2,1)S(1)} %get-tuple-element.87), channel_id=1, source_target_pairs={{0,1},{1,0},{2,3},{3,2},{4,5},{5,4},{6,7},{7,6},{8,9},{9,8},{10,11... | collective-permute-start | bytes 3145736 | tf_op jit(solution)/shard_map/ppermute | solution.py:735
  138.2 31.4 %collective-permute-start.24 = (bf16[512,1024]{1,0:T(8,128)(2,1)S(1)}, bf16[512,1024]{1,0:T(8,128)(2,1)S(1)}, u32[]{:S(2)}, u32[]{:S(2)}) collective-permute-start(bf16[512,1024]{1,0:T(8,128)(2,1)S(1)} %get-tuple-element.89), channel_id=1, source_target_pairs={{0,2},{1,3},{2,0},{3,1},{4,6},{5,7},{6,4},{7,5},{8,10},{9,11},{10,... | collective-permute-start | bytes 3145736 | tf_op jit(solution)/shard_map/ppermute | solution.py:735
  149.5 31.4 %collective-permute-start.21 = (bf16[256,1024]{1,0:T(8,128)(2,1)S(1)}, bf16[256,1024]{1,0:T(8,128)(2,1)S(1)}, u32[]{:S(2)}, u32[]{:S(2)}) collective-permute-start(bf16[256,1024]{1,0:T(8,128)(2,1)S(1)} %get-tuple-element.84), channel_id=1, source_target_pairs={{0,1},{1,0},{2,3},{3,2},{4,5},{5,4},{6,7},{7,6},{8,9},{9,8},{10,11... | collective-permute-start | bytes 1572872 | tf_op jit(solution)/shard_map/ppermute | solution.py:738
  151.0 29.8 %collective-permute-start.22 = (bf16[256,1024]{1,0:T(8,128)(2,1)S(1)}, bf16[256,1024]{1,0:T(8,128)(2,1)S(1)}, u32[]{:S(2)}, u32[]{:S(2)}) collective-permute-start(bf16[256,1024]{1,0:T(8,128)(2,1)S(1)} %get-tuple-element.85), channel_id=1, source_target_pairs={{0,2},{1,3},{2,0},{3,1},{4,6},{5,7},{6,4},{7,5},{8,10},{9,11},{10,... | collective-permute-start | bytes 1572872 | tf_op jit(solution)/shard_map/ppermute | solution.py:738
  171.9 18.8 %collective-permute-start.25 = (bf16[256,1024]{1,0:T(8,128)(2,1)S(1)}, bf16[256,1024]{1,0:T(8,128)(2,1)S(1)}, u32[]{:S(2)}, u32[]{:S(2)}) collective-permute-start(bf16[256,1024]{1,0:T(8,128)(2,1)S(1)} %get-tuple-element.91), channel_id=1, source_target_pairs={{0,2},{1,3},{2,0},{3,1},{4,6},{5,7},{6,4},{7,5},{8,10},{9,11},{10,... | collective-permute-start | bytes 1572872 | tf_op jit(solution)/shard_map/ppermute | solution.py:740
  173.5 17.4 %collective-permute-start.26 = (bf16[256,1024]{1,0:T(8,128)(2,1)S(1)}, bf16[256,1024]{1,0:T(8,128)(2,1)S(1)}, u32[]{:S(2)}, u32[]{:S(2)}) collective-permute-start(bf16[256,1024]{1,0:T(8,128)(2,1)S(1)} %get-tuple-element.92), channel_id=1, source_target_pairs={{0,1},{1,0},{2,3},{3,2},{4,5},{5,4},{6,7},{7,6},{8,9},{9,8},{10,11... | collective-permute-start | bytes 1572872 | tf_op jit(solution)/shard_map/ppermute | solution.py:740
  (7 other events, 23.6 us)

commit v6 on v5

--- a/solution.py
+++ b/solution.py
@@ -26,6 +26,10 @@
 
 def stay(x):
     return pltpu.with_memory_space_constraint(x, pltpu.HBM)
+
+
+def near(x):
+    return pltpu.with_memory_space_constraint(x, pltpu.VMEM)
 
 
 def fixed(shape):
@@ -240,7 +244,7 @@
         places,
         (tokens, w_qkv),
         [fixed((rows, depth)), pl.BlockSpec((3, depth, cols), lambda j, o: (0, o[0], j))],
-        (pltpu.HBM((3, rows, width), F32), struct(quarter, BF16), struct(quarter, BF16)),
+        (pltpu.HBM((3, rows, width), F32), pltpu.HBM(quarter, BF16), pltpu.HBM(quarter, BF16)),
         [pl.BlockSpec((3, rows, cols), lambda j, o: (0, 0, j)), fixed(quarter), fixed(quarter)],
         2 * rows * depth * width * 3,
     )
@@ -302,7 +306,7 @@
     return out if apart else out[0]
 
 
-def state_kernel(chunk, group, size, _, *refs):
+def state_kernel(chunk, group, size, places, *refs):
     xa, xb, wk, wv, acc_k, acc_v, inside_ref, state_ref = refs[:8]
     k_ref, v_ref, mid_ref, end_ref, sent_ref, held = refs[8:]
     j = pl.program_id(0)
@@ -317,6 +321,7 @@
     v_all = (acc_v[0] + dot(held[...], wv[0])).astype(BF16)
     k_ref[...] = k_all
     v_ref[...] = v_all
+    ends = []
     for a in range(group):
         head = j * group + a
         lanes = slice(a * size, (a + 1) * size)
@@ -328,7 +333,14 @@
                 k_all[here, lanes], v_all[here, lanes], column(inside_ref[here, :], head), state
             )
         end_ref[a] = state
-        sent_ref[a] = state.astype(BF16)
+        ends.append(state.astype(BF16))
+    core = places[4]
+    half = pl.num_programs(0) // 2
+
+    @pl.when(jnp.where(core == 0, j >= half, j < half))
+    def _():
+        for a in range(group):
+            sent_ref[a] = ends[a]
 
 
 def state_call(places, far, w_qkv, acc, inside, state, chunk, group):
@@ -339,6 +351,11 @@
     wide = pl.BlockSpec((rows, cols), lambda j, o: (0, j))
     small = pl.BlockSpec((group, size, size), lambda j, o: (j, 0, 0))
     chunks = rows // chunk
+    half = heads // group // 2
+
+    def sent_block(j, o):
+        return jnp.where(o[4] == 0, jnp.maximum(j - half, 0), jnp.minimum(j, half - 1)), 0, 0
+
     return call(
         functools.partial(state_kernel, chunk, group, size),
         "states",
@@ -354,14 +371,14 @@
             pltpu.HBM((rows, width), BF16),
             pltpu.HBM((chunks, heads, size, size), F32),
             struct(state.shape, F32),
-            struct(state.shape, BF16),
+            struct((heads // 2, size, size), BF16),
         ),
         [
             wide,
             wide,
             pl.BlockSpec((chunks, group, size, size), lambda j, o: (0, j, 0, 0)),
             small,
-            small,
+            pl.BlockSpec((group, size, size), sent_block),
         ],
         4 * rows * depth * width,
         scratch=[pltpu.VMEM((rows, depth), BF16)],
@@ -426,8 +443,83 @@
     )
 
 
-def head_kernel(_, q_ref, within_ref, entering_ref, down_ref, w_ref, normed_ref, *out_refs):
-    heads, size = entering_ref.shape[0], entering_ref.shape[1]
+def fades(tail_ref, other_ref, place, head):
+    own, other = tail_ref[pl.ds(head, 1), :], other_ref[pl.ds(head, 1), :]
+    first = jnp.where(place == 0, own, other)
+    return jnp.exp(-first), jnp.exp(first - (own + other)), jnp.exp(-(own + other))
+
+
+def chip_kernel(places, state_ref, come_ref, tail_ref, other_ref, prior_ref, *out_refs):
+    leaving_ref, chip_ref, first_ref = out_refs
+    core, chip = places[4], places[5]
+    share = come_ref.shape[0]
+    for i in range(share):
+        head = core * share + i
+        _, second_fade, fade = fades(tail_ref, other_ref, core, head)
+        ours, come = state_ref[head], come_ref[i].astype(F32)
+        first, second = jnp.where(core == 0, ours, come), jnp.where(core == 0, come, ours)
+        total = second_fade * first + second
+        first_ref[i] = first
+        chip_ref[i] = total
+        leaving_ref[i] = jnp.where(chip == 2, total, fade * prior_ref[head] + total).astype(BF16)
+
+
+def pass_kernel(places, come_ref, chip_ref, tail_ref, other_ref, leaving_ref):
+    share = come_ref.shape[0]
+    for i in range(share):
+        fade = fades(tail_ref, other_ref, places[4], places[4] * share + i)[2]
+        leaving_ref[i] = (fade * come_ref[i].astype(F32) + chip_ref[i]).astype(BF16)
+
+
+def enter_kernel(
+    places, come_ref, second_ref, third_ref, first_ref, tail_ref, other_ref, below_ref, prior_ref, *out_refs
+):
+    here_ref, passed_ref = out_refs
+    core, chip = places[4], places[5]
+    share = come_ref.shape[0]
+    for i in range(share):
+        head = core * share + i
+        come = come_ref[i].astype(F32)
+        below = jnp.exp(-below_ref[pl.ds(head, 1), :])
+        state = jnp.where(chip == 0, prior_ref[head], come)
+        state = jnp.where(chip == 2, second_ref[i].astype(F32), state)
+        state = jnp.where(chip == 3, below * third_ref[i].astype(F32) + come, state)
+        later = fades(tail_ref, other_ref, core, head)[0] * state + first_ref[i]
+        here_ref[i] = jnp.where(core == 0, state, later).astype(BF16)
+        passed_ref[i] = jnp.where(core == 0, later, state).astype(BF16)
+
+
+def small_call(kernel, name, places, ins, outs):
+    whole = pl.BlockSpec(memory_space=pltpu.VMEM)
+    return pl.pallas_call(
+        kernel,
+        out_shape=tuple(outs),
+        in_specs=[pl.BlockSpec(memory_space=pltpu.SMEM)] + [whole] * len(ins),
+        out_specs=[whole] * len(outs),
+        compiler_params=pltpu.CompilerParams(vmem_limit_bytes=4 * MIB),
+        cost_estimate=pl.CostEstimate(flops=1, bytes_accessed=1, transcendentals=0),
+        name=name,
+    )(places, *ins)
+
+
+def chip_call(places, state, come, tails, prior):
+    outs = (struct(come.shape, BF16), struct(come.shape, F32), struct(come.shape, F32))
+    return small_call(chip_kernel, "chip_state", places, (state, come, *tails, prior), outs)
+
+
+def pass_call(places, come, chip_state, tails):
+    outs = (struct(come.shape, BF16),)
+    return small_call(pass_kernel, "pass_on", places, (come, chip_state, *tails), outs)[0]
+
+
+def enter_call(places, come, second, third, first, tails, below, prior):
+    outs = (struct(come.shape, BF16),) * 2
+    ins = (come, second, third, first, *tails, below, prior)
+    return small_call(enter_kernel, "enter", places, ins, outs)
+
+
+def head_kernel(places, q_ref, within_ref, here_ref, there_ref, down_ref, w_ref, normed_ref, *out_refs):
+    share, size = here_ref.shape[0], here_ref.shape[1]
     tall = q_ref.shape[0]
     for p, out_ref in enumerate(out_refs):
         rows = slice(p * tall, (p + 1) * tall)
@@ -435,9 +527,11 @@
         @pl.when(pl.program_id(0) == p)
         def _(rows=rows, out_ref=out_ref):
             fade = jnp.exp(-down_ref[...])
-            for a in range(heads):
+            for a in range(2 * share):
                 lanes = slice(a * size, (a + 1) * size)
-                seen = dot(q_ref[:, lanes], entering_ref[a]) * fade[:, a : a + 1]
+                ours = places[4] == a // share
+                entering = jnp.where(ours, here_ref[a % share], there_ref[a % share])
+                seen = dot(q_ref[:, lanes], entering) * fade[:, a : a + 1]
                 combined = within_ref[:, lanes] + seen
                 power = jnp.mean(combined * combined, axis=1, keepdims=True)
                 normed_ref[rows, lanes] = (combined * lax.rsqrt(power + 1e-06)).astype(BF16)
@@ -451,7 +545,7 @@
 def head_call(places, blocks, q, within, entering, down, w_out, width, at):
     rows, cols = q.shape
     tall = rows // 2
-    heads = entering.shape[0]
+    heads = down.shape[1]
     part = pl.BlockSpec((tall, cols), lambda i, o: (jnp.minimum(i, 1), 0))
     far, x, y = blocks
     return call(
@@ -459,11 +553,12 @@
         "heads",
         4,
         places,
-        (q, within, entering, down, w_out),
+        (q, within, *entering, down, w_out),
         [
             part,
             part,
-            fixed(entering.shape),
+            fixed(entering[0].shape),
+            fixed(entering[1].shape),
             pl.BlockSpec((tall, heads), lambda i, o: (2 * at + jnp.minimum(i, 1), 0)),
             pl.BlockSpec(
                 (cols, width),
@@ -589,20 +684,18 @@
     over_x = functools.partial(lax.ppermute, axis_name="head", perm=[(i, i ^ 1) for i in range(n_head)])
     over_y = functools.partial(lax.ppermute, axis_name="head", perm=[(i, i ^ 2) for i in range(n_head)])
 
-    flips = (0, 1, 2, 3) if square else (0,)
-    places = jnp.stack([place ^ f for f in flips])
+    pos = lax.axis_index("seq").astype(jnp.int32)
+    core, chip = pos % 2, pos // 2
+    flips = (0, 1, 2, 3) if square else (0, 0, 0, 0)
+    places = jnp.stack([*[place ^ f for f in flips], core, chip])
 
     along, inside, down, tail = decay_call(decay_rate, quarter)
-    tail = tail[:, 0]
-    pos = lax.axis_index("seq")
-    core, chip = pos % 2, pos // 2
     n_chips = n_seq // 2
     swap = functools.partial(lax.ppermute, axis_name="seq", perm=[(i, i ^ 1) for i in range(n_seq)])
 
     def hop(x, *pairs):
-        return lax.ppermute(
-            x, "seq", perm=[(2 * a + c, 2 * b + c) for a, b in pairs for c in range(2)]
-        )
+        perm = [(2 * a + c, 2 * b + c) for a, b in pairs for c in range(2)]
+        return lax.ppermute(x, "seq", perm=perm)
 
     def chip_tails(tail):
         other = swap(tail)
@@ -611,11 +704,12 @@
     if square:
         tokens = stay(tokens)
         q0, q1 = cut_call(tokens)
-        x0, y1, x1, y0 = over_x(q0), over_y(q1), over_x(q1), over_y(q0)
-        acc, q2, q3 = own_part_call(places, tokens, w_qkv, cols)
+        x0, y1 = over_x(q0), over_y(q1)
+        x1, y0 = over_x(after(q1, inside)), over_y(after(q0, inside))
+        acc, q2, q3 = own_part_call(places, after(tokens, inside), w_qkv, cols)
         acc = stay(acc)
         fy0, fx1 = over_y(x0), over_x(y1)
-        tail_other, tail_chip, tail_below = chip_tails(after(tail, x0, y1))
+        tail_other, tail_chip, tail_below = chip_tails(after(tail, x0, y1, acc))
         x2 = over_x(after(q2, x1, y0, tail_chip))
         y3 = over_y(after(q3, x1, y0, tail_chip))
         acc_a = part_call(
@@ -665,44 +759,39 @@
         query, within, state = first_call(
             places, (), [(gathered,)], (), w_qkv, along, inside, rows, quarter, size, group
         )
-        sent = state.astype(BF16)
-
-    other = swap(sent).astype(F32)
-    first = jnp.where(core == 0, state, other)
-    second = jnp.where(core == 0, other, state)
-    tail_first = jnp.where(core == 0, tail, tail_other)
-    tail_second = jnp.where(core == 0, tail_other, tail)
-    share = heads // 2
-
-    def mine(x):
-        return lax.dynamic_slice_in_dim(x, core * share, share, 0)
-
-    chip_state = jnp.exp(-mine(tail_second))[:, None, None] * mine(first) + mine(second)
-    chip_decay = jnp.exp(-mine(tail_chip))[:, None, None]
-    chip_entering = mine(prior_state)
-
-    def leaving():
-        return (chip_decay * chip_entering + chip_state).astype(BF16)
-
-    if n_chips == 4:
-        arriving = hop(jnp.where(chip == 2, chip_state.astype(BF16), leaving()), (0, 1), (2, 3))
-        chip_entering = jnp.where(chip == 1, arriving.astype(F32), chip_entering)
-        sum_first = leaving()
-        to_third, to_second = hop(sum_first, (1, 3)), hop(sum_first, (1, 2))
-        third = jnp.exp(-mine(tail_below))[:, None, None] * to_third.astype(F32)
-        chip_entering = jnp.where(chip == 2, to_second.astype(F32), chip_entering)
-        chip_entering = jnp.where(chip == 3, third + arriving.astype(F32), chip_entering)
+
+    tails = (tail, tail_other)
+    if square and n_chips == 4:
+        leaving, chip_state, first = chip_call(places, state, near(swap(sent)), tails, prior_state)
+        arriving = near(hop(leaving, (0, 1), (2, 3)))
+        leaving = pass_call(places, arriving, chip_state, tails)
+        to_third, to_second = near(hop(leaving, (1, 3))), near(hop(leaving, (1, 2)))
+        here, passed = enter_call(
+            places, arriving, to_second, to_third, first, tails, tail_below, prior_state
+        )
     else:
+        share = heads // 2
+
+        def mine(x, core=core):
+            return lax.dynamic_slice_in_dim(x, core * share, share, 0)
+
+        def decay(tail):
+            return jnp.exp(-mine(tail)[:, :1, None])
+
+        ours = mine(state)
+        other = swap(mine(state, 1 - core).astype(BF16)).astype(F32)
+        first = jnp.where(core == 0, ours, other)
+        second = jnp.where(core == 0, other, ours)
+        chip_state = decay(jnp.where(core == 0, tail_other, tail)) * first + second
+        chip_entering = mine(prior_state)
         for step in range(n_chips - 1):
-            arriving = hop(leaving(), (step, step + 1))
+            leaving = (decay(tail_chip) * chip_entering + chip_state).astype(BF16)
+            arriving = hop(leaving, (step, step + 1))
             chip_entering = jnp.where(chip == step + 1, arriving.astype(F32), chip_entering)
-    there = swap(chip_entering.astype(BF16)).astype(F32)
-    entering = jnp.concatenate(
-        [jnp.where(core == 0, chip_entering, there), jnp.where(core == 0, there, chip_entering)]
-    )
-    entering = jnp.where(
-        core == 0, entering, jnp.exp(-tail_first)[:, None, None] * entering + first
-    ).astype(BF16)
+        other = decay(jnp.where(core == 0, tail, tail_other)) * chip_entering + first
+        here = jnp.where(core == 0, chip_entering, other).astype(BF16)
+        passed = jnp.where(core == 0, other, chip_entering).astype(BF16)
+    entering = (here, swap(passed))
 
     if not square:
         halves = [
@@ -723,7 +812,7 @@
         return lax.psum_scatter(partial, "head", scatter_dimension=1, tiled=True)
 
     na, by_x, by_y = head_call(
-        places, (3, 1, 2), query_a, within_a, entering, down, w_out, width, 0
+        places, (3, 1, 2), stay(query_a), stay(within_a), entering, down, w_out, width, 0
     )
     by_x, by_y = over_x(by_x), over_y(by_y)
     query_b, within_b = later_call(

time: 193 us -> 188 us (0.974)
  waiting for transfers between devices: 58.6 us -> 65.4 us
  other arithmetic: 6.69 us -> 0.01 us
  local copies, waits for them, and re-layouts: 5.11 us -> 0.11 us
  Pallas kernels: 90 us -> 93.5 us
  starting transfers between devices: 31.3 us -> 28 us
    unnamed x24 -> x12, local copies, waits for them, and re-layouts: 5 us -> 0.03 us
    convert_element_type x4 -> x0, other arithmetic: 4.48 us -> none  [the longest x1 1.2 us: local(): entering = jnp.where(core == 0, entering, jnp.exp(-tail_first)[:, None, N...]
    ppermute x10, waiting for transfers between devices: 16.7 us -> 21 us  [the longest x2 9.66 us: local(): x0, y1 = (over_x(q0), over_y(q1))]
    select_n x3 -> x0, other arithmetic: 1.97 us -> none  [the longest x1 1.01 us: local(): first = jnp.where(core == 0, state, other)]
  transfers between devices with their start and end apart: 27 -> 27, of which waited for: 12 -> 13; matrix products, arithmetic and copies ran while one was open for 0% -> 0% of each run, Pallas kernels for 38% -> 39%
where the time goes in v6:
time: 188 us; the launch traced here: 187 us
  Pallas kernels  93.5 us (50%)
  waiting for transfers between devices  65.4 us (35%)
  starting transfers between devices  28 us (15%)
    pallas_call x15, Pallas kernels, call(): pl.pallas_call(kernel, out_shape=tuple(outs), grid_spec=pltpu.PrefetchSca...  91.6 us
    ppermute x2, waiting for transfers between devices, local(): by_x2, by_y2 = (over_x(by_x2), over_y(by_y2))  18.1 us
    ppermute x2, waiting for transfers between devices, local(): x0, y1 = (over_x(q0), over_y(q1))  9.66 us
    ppermute x2, waiting for transfers between devices, local(): by_x, by_y = (over_x(by_x), over_y(by_y))  8.7 us
    ppermute x4, waiting for transfers between devices, hop(): return lax.ppermute(x, 'seq', perm=perm)  8.64 us
    ppermute x4, starting transfers between devices, hop(): return lax.ppermute(x, 'seq', perm=perm)  7.29 us
    ppermute x2, waiting for transfers between devices, local(): sum1, sum0 = (over_x(sum1), over_y(sum0))  6.84 us
    ppermute x2, waiting for transfers between devices, local(): x3, y2 = (over_x(after(q3, *earlier)), over_y(after(q2, *earlier)))  6.13 us
  transfers between devices with their start and end apart: 27, of which 13 were waited for; matrix products, arithmetic and copies ran while one was open for 0% of the time, Pallas kernels for 39%

profile of v6, /device:TPU:8, one launch (start us, length us, event | category | flops | bytes accessed | tf_op | source)
XLA Modules:
  0.0 187.3 jit_solution(13115506685491155850)
XLA Ops:
  0.0 2.2 %cut.1 = (bf16[256,1024]{1,0:T(8,128)(2,1)}, bf16[256,1024]{1,0:T(8,128)(2,1)}) custom-call(s32[1]{0:T(128)} %constant.29.clone.1._, bf16[1024,1024]{1,0:T(8,128)(2,1)} %x_ref.2), custom_call_target="tpu_custom_call" | custom-call | flops 1 | bytes 3145728 | tf_op jit(solution)/shard_map/cut/pallas_call | solution.py:43
  2.2 1.5 collective-permute-start.3
  4.7 1.5 collective-permute-start
  7.4 12.5 %own_part.1 = (f32[3,1024,1024]{2,1,0:T(8,128)}, bf16[256,1024]{1,0:T(8,128)(2,1)}, bf16[256,1024]{1,0:T(8,128)(2,1)}) custom-call(s32[6]{0:T(128)S(1)} %stack.27._.places, bf16[1024,1024]{1,0:T(8,128)(2,1)} %x_ref.2, bf16[3,4096,1024]{2,1,0:T(8,128)(2,1)} %refs_2_.5), custom_call_target="tpu_custom_call" | custom-call | flops 6442450944 | bytes 40894464 | tf_op jit(solution)/shard_map/own_part/pallas_call | solution.py:43
  20.0 9.7 %collective-permute-done.2.refs_0_ = bf16[256,1024]{1,0:T(8,128)(2,1)S(1)} collective-permute-done((bf16[256,1024]{1,0:T(8,128)(2,1)}, bf16[256,1024]{1,0:T(8,128)(2,1)S(1)}, u32[]{:S(2)}, u32[]{:S(2)}) %collective-permute-start.2) | collective-permute-done | bytes 524320 | tf_op jit(solution)/shard_map/ppermute | solution.py:707
  30.1 1.5 collective-permute-start.7
  34.4 11.5 %part.2.refs_3_ = f32[3,512,1024]{2,1,0:T(8,128)S(1)} custom-call(s32[6]{0:T(128)S(1)} %stack.27._.places, bf16[256,1024]{1,0:T(8,128)(2,1)S(1)} %collective-permute-done.2.refs_0_, bf16[256,1024]{1,0:T(8,128)(2,1)S(1)} %collective-permute-done.refs_1_, bf16[256,1024]{1,0:T(8,128)(2,1)S(1)} %collective-permute-done.1.refs_2_, ...), custom_call_target="tpu_custom_call" | custom-call | flops 6442450944 | bytes 71303168 | tf_op jit(solution)/shard_map/part/pallas_call | solution.py:43
  46.0 1.6 collective-permute-start.12
  48.0 11.2 %first.1 = (bf16[512,1024]{1,0:T(8,128)(2,1)}, f32[512,1024]{1,0:T(8,128)}, f32[8,128,128]{2,1,0:T(8,128)S(1)}) custom-call(s32[6]{0:T(128)S(1)} %stack.27._.places, bf16[256,1024]{1,0:T(8,128)(2,1)S(1)} %collective-permute-done.6.refs_0_, bf16[256,1024]{1,0:T(8,128)(2,1)S(1)} %collective-permute-done.7.refs_1_, bf16[3,4096,1024]{2,1,0:T(8,128)(2,1)} %refs_2_.5, ...), custom_call_target="tpu_custom_call" | custom-call | flops 3221225472 | bytes 36241408 | tf_op jit(solution)/shard_map/first/pallas_call | solution.py:43
  59.2 1.5 collective-permute-start.8
  61.2 6.1 %collective-permute-done.12.refs_1_ = bf16[256,1024]{1,0:T(8,128)(2,1)S(1)} collective-permute-done((bf16[256,1024]{1,0:T(8,128)(2,1)S(1)}, bf16[256,1024]{1,0:T(8,128)(2,1)S(1)}, u32[]{:S(2)}, u32[]{:S(2)}) %collective-permute-start.12) | collective-permute-done | bytes 524320 | tf_op jit(solution)/shard_map/ppermute | solution.py:726
  67.4 11.7 %part.3 = (f32[1,512,1024]{2,1,0:T(8,128)}, f32[2,512,1024]{2,1,0:T(8,128)S(1)}) custom-call(s32[6]{0:T(128)S(1)} %stack.27._.places, bf16[256,1024]{1,0:T(8,128)(2,1)S(1)} %collective-permute-done.5.refs_0_, bf16[256,1024]{1,0:T(8,128)(2,1)S(1)} %collective-permute-done.12.refs_1_, bf16[256,1024]{1,0:T(8,128)(2,1)S(1)} %collective-permute-done.13.refs_2_, ...), custom_call_target="tpu_custom_call" | custom-call | flops 6442450944 | bytes 71303168 | tf_op jit(solution)/shard_map/part/pallas_call | solution.py:43
  79.1 7.7 %states.1 = (bf16[512,1024]{1,0:T(8,128)(2,1)}, bf16[512,1024]{1,0:T(8,128)(2,1)}, f32[2,8,128,128]{3,2,1,0:T(8,128)}, f32[8,128,128]{2,1,0:T(8,128)S(1)}, bf16[4,128,128]{2,1,0:T(8,128)(2,1)S(1)}) custom-call(s32[6]{0:T(128)S(1)} %stack.27._.places, bf16[256,1024]{1,0:T(8,128)(2,1)S(1)} %collective-permute-done.8.refs_0_, ...), custom_call_target="tpu_custom_call" | custom-call | flops 2147483648 | bytes 64126976 | tf_op jit(solution)/shard_map/states/pallas_call | solution.py:43
  90.1 6.1 %collective-permute-done.15.come_ref = bf16[4,128,128]{2,1,0:T(8,128)(2,1)S(1)} collective-permute-done((bf16[4,128,128]{2,1,0:T(8,128)(2,1)S(1)}, bf16[4,128,128]{2,1,0:T(8,128)(2,1)S(1)}, u32[]{:S(2)}, u32[]{:S(2)}) %collective-permute-start.15) | collective-permute-done | bytes 131104 | tf_op jit(solution)/shard_map/ppermute | solution.py:698
  96.8 2.6 %collective-permute-start.16 = (bf16[4,128,128]{2,1,0:T(8,128)(2,1)S(1)}, bf16[4,128,128]{2,1,0:T(8,128)(2,1)S(1)}, u32[]{:S(2)}, u32[]{:S(2)}) collective-permute-start(bf16[4,128,128]{2,1,0:T(8,128)(2,1)S(1)} %pass_on.1), channel_id=1, source_target_pairs={{8,16},{12,20},{9,17},{13,21},{10,18},{14,22},{11,19},{15,23}} | collective-permute-start | bytes 393224 | tf_op jit(solution)/shard_map/ppermute | solution.py:698
  99.4 2.8 %collective-permute-start.17 = (bf16[4,128,128]{2,1,0:T(8,128)(2,1)S(1)}, bf16[4,128,128]{2,1,0:T(8,128)(2,1)S(1)}, u32[]{:S(2)}, u32[]{:S(2)}) collective-permute-start(bf16[4,128,128]{2,1,0:T(8,128)(2,1)S(1)} %pass_on.1), channel_id=1, source_target_pairs={{8,24},{12,28},{9,25},{13,29},{10,26},{14,30},{11,27},{15,31}} | collective-permute-start | bytes 393224 | tf_op jit(solution)/shard_map/ppermute | solution.py:698
  102.3 2.3 %collective-permute-done.17.third_ref = bf16[4,128,128]{2,1,0:T(8,128)(2,1)S(1)} collective-permute-done((bf16[4,128,128]{2,1,0:T(8,128)(2,1)S(1)}, bf16[4,128,128]{2,1,0:T(8,128)(2,1)S(1)}, u32[]{:S(2)}, u32[]{:S(2)}) %collective-permute-start.17) | collective-permute-done | bytes 131104 | tf_op jit(solution)/shard_map/ppermute | solution.py:698
  106.8 8.0 %heads.2 = (bf16[512,1024]{1,0:T(8,128)(2,1)S(1)}, bf16[512,1024]{1,0:T(8,128)(2,1)S(1)}, bf16[512,1024]{1,0:T(8,128)(2,1)S(1)}) custom-call(s32[6]{0:T(128)S(1)} %stack.27._.places, bf16[512,1024]{1,0:T(8,128)(2,1)} %get-tuple-element.82.q_ref, f32[512,1024]{1,0:T(8,128)} %get-tuple-element.83.within_ref, ...), custom_call_target="tpu_custom_call" | custom-call | flops 1 | bytes 1 | tf_op jit(solution)/shard_map/heads/pallas_call | solution.py:43
  114.7 1.6 collective-permute-start.19
  117.8 8.0 %later.1 = (bf16[512,1024]{1,0:T(8,128)(2,1)S(1)}, f32[512,1024]{1,0:T(8,128)S(1)}) custom-call(s32[6]{0:T(128)S(1)} %stack.27._.places, bf16[256,1024]{1,0:T(8,128)(2,1)S(1)} %collective-permute-done.8.refs_0_, bf16[256,1024]{1,0:T(8,128)(2,1)S(1)} %collective-permute-done.10.refs_1_, bf16[3,4096,1024]{2,1,0:T(8,128)(2,1)} %refs_2_.5, ...), custom_call_target="tpu_custom_call" | custom-call | flops 1879048192 | bytes 34668544 | tf_op jit(solution)/shard_map/later/pallas_call | solution.py:43
  125.9 6.7 %heads.3 = (bf16[512,1024]{1,0:T(8,128)(2,1)S(1)}, bf16[512,1024]{1,0:T(8,128)(2,1)S(1)}, bf16[512,1024]{1,0:T(8,128)(2,1)S(1)}) custom-call(s32[6]{0:T(128)S(1)} %stack.27._.places, bf16[512,1024]{1,0:T(8,128)(2,1)S(1)} %get-tuple-element.94.q_ref, f32[512,1024]{1,0:T(8,128)S(1)} %get-tuple-element.95.within_ref, ...), custom_call_target="tpu_custom_call" | custom-call | flops 1 | bytes 1 | tf_op jit(solution)/shard_map/heads/pallas_call | solution.py:43
  133.7 7.1 %collective-permute-done.19.x_ref.refs_2_ = bf16[512,1024]{1,0:T(8,128)(2,1)S(1)} collective-permute-done((bf16[512,1024]{1,0:T(8,128)(2,1)S(1)}, bf16[512,1024]{1,0:T(8,128)(2,1)S(1)}, u32[]{:S(2)}, u32[]{:S(2)}) %collective-permute-start.19) | collective-permute-done | bytes 1048608 | tf_op jit(solution)/shard_map/ppermute | solution.py:817
  140.8 1.6 collective-permute-done.20.y_ref.refs_0_
  142.4 2.3 %sum_pair.2 = (bf16[256,1024]{1,0:T(8,128)(2,1)S(1)}, bf16[256,1024]{1,0:T(8,128)(2,1)S(1)}) custom-call(s32[6]{0:T(128)S(1)} %stack.27._.places, bf16[512,1024]{1,0:T(8,128)(2,1)S(1)} %get-tuple-element.97.normed_ref, bf16[512,1024]{1,0:T(8,128)(2,1)S(1)} %collective-permute-done.19.x_ref.refs_2_, ...), custom_call_target="tpu_custom_call" | custom-call | flops 1 | bytes 1 | tf_op jit(solution)/shard_map/sum_pair/pallas_call | solution.py:43
  144.7 1.6 collective-permute-start.21
  146.8 18.1 %collective-permute-done.23.refs_0_.y_ref = bf16[512,1024]{1,0:T(8,128)(2,1)S(1)} collective-permute-done((bf16[512,1024]{1,0:T(8,128)(2,1)S(1)}, bf16[512,1024]{1,0:T(8,128)(2,1)S(1)}, u32[]{:S(2)}, u32[]{:S(2)}) %collective-permute-start.23) | collective-permute-done | bytes 1048608 | tf_op jit(solution)/shard_map/ppermute | solution.py:824
  164.8 2.3 %sum_pair.3 = (bf16[256,1024]{1,0:T(8,128)(2,1)S(1)}, bf16[256,1024]{1,0:T(8,128)(2,1)S(1)}) custom-call(s32[6]{0:T(128)S(1)} %stack.27._.places, bf16[512,1024]{1,0:T(8,128)(2,1)S(1)} %get-tuple-element.102.normed_ref, bf16[512,1024]{1,0:T(8,128)(2,1)S(1)} %collective-permute-done.24.refs_1_.x_ref, ...), custom_call_target="tpu_custom_call" | custom-call | flops 1 | bytes 1 | tf_op jit(solution)/shard_map/sum_pair/pallas_call | solution.py:43
  167.7 1.5 collective-permute-start.26
  169.2 6.8 %collective-permute-done.21.refs_3_ = bf16[256,1024]{1,0:T(8,128)(2,1)S(1)} collective-permute-done((bf16[256,1024]{1,0:T(8,128)(2,1)S(1)}, bf16[256,1024]{1,0:T(8,128)(2,1)S(1)}, u32[]{:S(2)}, u32[]{:S(2)}) %collective-permute-start.21) | collective-permute-done | bytes 524320 | tf_op jit(solution)/shard_map/ppermute | solution.py:827
  176.1 2.4 %own_block.2.kept_ref = bf16[512,1024]{1,0:T(8,128)(2,1)S(1)} custom-call(s32[6]{0:T(128)S(1)} %stack.27._.places, bf16[512,1024]{1,0:T(8,128)(2,1)S(1)} %get-tuple-element.102.normed_ref, bf16[1024,4096]{1,0:T(8,128)(2,1)S(1)} %bitcast.7, bf16[512,1024]{1,0:T(8,128)(2,1)S(1)} %collective-permute-done.23.refs_0_.y_ref, ...), custom_call_target="tpu_custom_call" | custom-call | flops 1 | bytes 1 | tf_op jit(solution)/shard_map/own_block/pallas_call | solution.py:43
  178.5 3.0 %own_block.3.above_ref = bf16[1024,1024]{1,0:T(8,128)(2,1)} custom-call(s32[6]{0:T(128)S(1)} %stack.27._.places, bf16[512,1024]{1,0:T(8,128)(2,1)S(1)} %get-tuple-element.97.normed_ref, bf16[1024,4096]{1,0:T(8,128)(2,1)S(1)} %bitcast.7, bf16[512,1024]{1,0:T(8,128)(2,1)S(1)} %collective-permute-done.20.y_ref.refs_0_, ...), custom_call_target="tpu_custom_call" | custom-call | flops 1 | bytes 1 | tf_op jit(solution)/shard_map/own_block/pallas_call | solution.py:43
  181.5 3.4 %collective-permute-done.25.a_ref = bf16[256,1024]{1,0:T(8,128)(2,1)S(1)} collective-permute-done((bf16[256,1024]{1,0:T(8,128)(2,1)S(1)}, bf16[256,1024]{1,0:T(8,128)(2,1)S(1)}, u32[]{:S(2)}, u32[]{:S(2)}) %collective-permute-start.25) | collective-permute-done | bytes 524320 | tf_op jit(solution)/shard_map/ppermute | solution.py:829
  (55 shorter events, 18.6 us)
Async XLA Ops:
  2.2 27.4 %collective-permute-start.3 = (bf16[256,1024]{1,0:T(8,128)(2,1)}, bf16[256,1024]{1,0:T(8,128)(2,1)S(1)}, u32[]{:S(2)}, u32[]{:S(2)}) collective-permute-start(bf16[256,1024]{1,0:T(8,128)(2,1)} %get-tuple-element.61), channel_id=1, source_target_pairs={{0,2},{1,3},{2,0},{3,1},{4,6},{5,7},{6,4},{7,5},{8,10},{9,11},{10,... | collective-permute-start | bytes 1572872 | tf_op jit(solution)/shard_map/ppermute | solution.py:707
  4.7 27.6 %collective-permute-start = (bf16[256,1024]{1,0:T(8,128)(2,1)}, bf16[256,1024]{1,0:T(8,128)(2,1)S(1)}, u32[]{:S(2)}, u32[]{:S(2)}) collective-permute-start(bf16[256,1024]{1,0:T(8,128)(2,1)} %get-tuple-element.61), channel_id=1, source_target_pairs={{0,1},{1,0},{2,3},{3,2},{4,5},{5,4},{6,7},{7,6},{8,9},{9,8},{10,11... | collective-permute-start | bytes 1572872 | tf_op jit(solution)/shard_map/ppermute | solution.py:708
  6.3 23.3 %collective-permute-start.2 = (bf16[256,1024]{1,0:T(8,128)(2,1)}, bf16[256,1024]{1,0:T(8,128)(2,1)S(1)}, u32[]{:S(2)}, u32[]{:S(2)}) collective-permute-start(bf16[256,1024]{1,0:T(8,128)(2,1)} %get-tuple-element.63), channel_id=1, source_target_pairs={{0,1},{1,0},{2,3},{3,2},{4,5},{5,4},{6,7},{7,6},{8,9},{9,8},{10,11... | collective-permute-start | bytes 1572872 | tf_op jit(solution)/shard_map/ppermute | solution.py:707
  6.8 25.5 %collective-permute-start.1 = (bf16[256,1024]{1,0:T(8,128)(2,1)}, bf16[256,1024]{1,0:T(8,128)(2,1)S(1)}, u32[]{:S(2)}, u32[]{:S(2)}) collective-permute-start(bf16[256,1024]{1,0:T(8,128)(2,1)} %get-tuple-element.63), channel_id=1, source_target_pairs={{0,2},{1,3},{2,0},{3,1},{4,6},{5,7},{6,4},{7,5},{8,10},{9,11},{10,... | collective-permute-start | bytes 1572872 | tf_op jit(solution)/shard_map/ppermute | solution.py:708
  29.6 2.0 %collective-permute-start.4 = (f32[8,128]{1,0:T(8,128)S(1)}, f32[8,128]{1,0:T(8,128)S(1)}, u32[]{:S(2)}, u32[]{:S(2)}) collective-permute-start(f32[8,128]{1,0:T(8,128)S(1)} %get-tuple-element.66.tail_ref), channel_id=1, source_target_pairs={{0,4},{4,0},{8,12},{12,8},{16,20},{20,16},{24,28},{28,24},{1,5},{5... | collective-permute-start | bytes 12296 | tf_op jit(solution)/shard_map/ppermute | solution.py:701
  29.6 16.3 %collective-permute-start.6 = (bf16[256,1024]{1,0:T(8,128)(2,1)S(1)}, bf16[256,1024]{1,0:T(8,128)(2,1)S(1)}, u32[]{:S(2)}, u32[]{:S(2)}) collective-permute-start(bf16[256,1024]{1,0:T(8,128)(2,1)S(1)} %collective-permute-done.2.refs_0_), channel_id=1, source_target_pairs={{0,2},{1,3},{2,0},{3,1},{4,6},{5,7},{6,4},{7,5},{8,10},{9,11},{10,... | collective-permute-start | bytes 1572872 | tf_op jit(solution)/shard_map/ppermute | solution.py:711
  30.1 15.8 %collective-permute-start.7 = (bf16[256,1024]{1,0:T(8,128)(2,1)S(1)}, bf16[256,1024]{1,0:T(8,128)(2,1)S(1)}, u32[]{:S(2)}, u32[]{:S(2)}) collective-permute-start(bf16[256,1024]{1,0:T(8,128)(2,1)S(1)} %collective-permute-done.3.refs_3_), channel_id=1, source_target_pairs={{0,1},{1,0},{2,3},{3,2},{4,5},{5,4},{6,7},{7,6},{8,9},{9,8},{10,11... | collective-permute-start | bytes 1572872 | tf_op jit(solution)/shard_map/ppermute | solution.py:711
  31.6 14.3 %collective-permute-start.11 = (f32[8,128]{1,0:T(8,128)S(1)}, f32[8,128]{1,0:T(8,128)S(1)}, u32[]{:S(2)}, u32[]{:S(2)}) collective-permute-start(f32[8,128]{1,0:T(8,128)S(1)} %add.10), channel_id=1, source_target_pairs={{16,24},{20,28},{17,25},{21,29},{18,26},{22,30},{19,27},{23,31}} | collective-permute-start | bytes 12296 | tf_op jit(solution)/shard_map/ppermute | solution.py:698
  32.3 26.9 %collective-permute-start.5 = (bf16[256,1024]{1,0:T(8,128)(2,1)}, bf16[256,1024]{1,0:T(8,128)(2,1)S(1)}, u32[]{:S(2)}, u32[]{:S(2)}) collective-permute-start(bf16[256,1024]{1,0:T(8,128)(2,1)} %get-tuple-element.76), channel_id=1, source_target_pairs={{0,1},{1,0},{2,3},{3,2},{4,5},{5,4},{6,7},{7,6},{8,9},{9,8},{10,11... | collective-permute-start | bytes 1572872 | tf_op jit(solution)/shard_map/ppermute | solution.py:713
  33.0 12.9 %copy-start.3 = (bf16[256,1024]{1,0:T(8,128)(2,1)S(1)}, bf16[256,1024]{1,0:T(8,128)(2,1)}, u32[]{:S(2)}) copy-start(bf16[256,1024]{1,0:T(8,128)(2,1)} %get-tuple-element.75) | copy-start | bytes 1572868
  33.0 14.5 %copy-start.2 = (bf16[256,1024]{1,0:T(8,128)(2,1)S(1)}, bf16[256,1024]{1,0:T(8,128)(2,1)}, u32[]{:S(2)}) copy-start(bf16[256,1024]{1,0:T(8,128)(2,1)} %get-tuple-element.76) | copy-start | bytes 1572868
  33.0 27.7 %collective-permute-start.9 = (bf16[256,1024]{1,0:T(8,128)(2,1)}, bf16[256,1024]{1,0:T(8,128)(2,1)S(1)}, u32[]{:S(2)}, u32[]{:S(2)}) collective-permute-start(bf16[256,1024]{1,0:T(8,128)(2,1)} %get-tuple-element.75), channel_id=1, source_target_pairs={{0,2},{1,3},{2,0},{3,1},{4,6},{5,7},{6,4},{7,5},{8,10},{9,11},{10,... | collective-permute-start | bytes 1572872 | tf_op jit(solution)/shard_map/ppermute | solution.py:714
  46.0 21.4 %collective-permute-start.12 = (bf16[256,1024]{1,0:T(8,128)(2,1)S(1)}, bf16[256,1024]{1,0:T(8,128)(2,1)S(1)}, u32[]{:S(2)}, u32[]{:S(2)}) collective-permute-start(bf16[256,1024]{1,0:T(8,128)(2,1)S(1)} %copy-done.3), channel_id=1, source_target_pairs={{0,1},{1,0},{2,3},{3,2},{4,5},{5,4},{6,7},{7,6},{8,9},{9,8},{10,11... | collective-permute-start | bytes 1572872 | tf_op jit(solution)/shard_map/ppermute | solution.py:726
  47.5 19.9 %collective-permute-start.13 = (bf16[256,1024]{1,0:T(8,128)(2,1)S(1)}, bf16[256,1024]{1,0:T(8,128)(2,1)S(1)}, u32[]{:S(2)}, u32[]{:S(2)}) collective-permute-start(bf16[256,1024]{1,0:T(8,128)(2,1)S(1)} %copy-done.2), channel_id=1, source_target_pairs={{0,2},{1,3},{2,0},{3,1},{4,6},{5,7},{6,4},{7,5},{8,10},{9,11},{10,... | collective-permute-start | bytes 1572872 | tf_op jit(solution)/shard_map/ppermute | solution.py:726
  59.2 19.9 %collective-permute-start.8 = (bf16[256,1024]{1,0:T(8,128)(2,1)S(1)}, bf16[256,1024]{1,0:T(8,128)(2,1)S(1)}, u32[]{:S(2)}, u32[]{:S(2)}) collective-permute-start(bf16[256,1024]{1,0:T(8,128)(2,1)S(1)} %collective-permute-done.5.refs_0_), channel_id=1, source_target_pairs={{0,2},{1,3},{2,0},{3,1},{4,6},{5,7},{6,4},{7,5},{8,10},{9,11},{10,... | collective-permute-start | bytes 1572872 | tf_op jit(solution)/shard_map/ppermute | solution.py:740
  60.7 18.4 %collective-permute-start.10 = (bf16[256,1024]{1,0:T(8,128)(2,1)S(1)}, bf16[256,1024]{1,0:T(8,128)(2,1)S(1)}, u32[]{:S(2)}, u32[]{:S(2)}) collective-permute-start(bf16[256,1024]{1,0:T(8,128)(2,1)S(1)} %collective-permute-done.9.refs_3_), channel_id=1, source_target_pairs={{0,1},{1,0},{2,3},{3,2},{4,5},{5,4},{6,7},{7,6},{8,9},{9,8},{10,11... | collective-permute-start | bytes 1572872 | tf_op jit(solution)/shard_map/ppermute | solution.py:740
  79.1 27.7 %slice-start = ((s8[8388608]{0:T(1024)(128)(4,1)}), s8[4194304]{0:T(1024)(128)(4,1)S(1)}, s32[]{:S(2)}) async-start(s8[8388608]{0:T(1024)(128)(4,1)} %bitcast.6), calls=%async_computation | async-start | bytes 8388608
  79.1 9.1 %copy-start = (f32[8,128,128]{2,1,0:T(8,128)S(1)}, f32[8,128,128]{2,1,0:T(8,128)}, u32[]{:S(2)}) copy-start(f32[8,128,128]{2,1,0:T(8,128)} %prior_ref.3) | copy-start | bytes 1572868
  79.1 27.7 %slice-start.1 = ((s8[8388608]{0:T(1024)(128)(4,1)}), s8[4194304]{0:T(1024)(128)(4,1)S(1)}, s32[]{:S(2)}) async-start(s8[8388608]{0:T(1024)(128)(4,1)} %bitcast.6), calls=%async_computation.1 | async-start | bytes 8388608
  86.8 1.3 collective-permute-start.14
  88.8 7.4 %collective-permute-start.15 = (bf16[4,128,128]{2,1,0:T(8,128)(2,1)S(1)}, bf16[4,128,128]{2,1,0:T(8,128)(2,1)S(1)}, u32[]{:S(2)}, u32[]{:S(2)}) collective-permute-start(bf16[4,128,128]{2,1,0:T(8,128)(2,1)S(1)} %get-tuple-element.86), channel_id=1, source_target_pairs={{0,8},{4,12},{16,24},{20,28},{1,9},{5,13},{17,25},{21,29},{2,10},{... | collective-permute-start | bytes 393224 | tf_op jit(solution)/shard_map/ppermute | solution.py:698
  96.8 5.5 %collective-permute-start.16 = (bf16[4,128,128]{2,1,0:T(8,128)(2,1)S(1)}, bf16[4,128,128]{2,1,0:T(8,128)(2,1)S(1)}, u32[]{:S(2)}, u32[]{:S(2)}) collective-permute-start(bf16[4,128,128]{2,1,0:T(8,128)(2,1)S(1)} %pass_on.1), channel_id=1, source_target_pairs={{8,16},{12,20},{9,17},{13,21},{10,18},{14,22},{11,19},{15,23}} | collective-permute-start | bytes 393224 | tf_op jit(solution)/shard_map/ppermute | solution.py:698
  99.4 5.3 %collective-permute-start.17 = (bf16[4,128,128]{2,1,0:T(8,128)(2,1)S(1)}, bf16[4,128,128]{2,1,0:T(8,128)(2,1)S(1)}, u32[]{:S(2)}, u32[]{:S(2)}) collective-permute-start(bf16[4,128,128]{2,1,0:T(8,128)(2,1)S(1)} %pass_on.1), channel_id=1, source_target_pairs={{8,24},{12,28},{9,25},{13,29},{10,26},{14,30},{11,27},{15,31}} | collective-permute-start | bytes 393224 | tf_op jit(solution)/shard_map/ppermute | solution.py:698
  105.3 1.4 collective-permute-start.18
  114.7 26.1 %collective-permute-start.19 = (bf16[512,1024]{1,0:T(8,128)(2,1)S(1)}, bf16[512,1024]{1,0:T(8,128)(2,1)S(1)}, u32[]{:S(2)}, u32[]{:S(2)}) collective-permute-start(bf16[512,1024]{1,0:T(8,128)(2,1)S(1)} %get-tuple-element.98), channel_id=1, source_target_pairs={{0,2},{1,3},{2,0},{3,1},{4,6},{5,7},{6,4},{7,5},{8,10},{9,11},{10,... | collective-permute-start | bytes 3145736 | tf_op jit(solution)/shard_map/ppermute | solution.py:817
  116.3 26.0 %collective-permute-start.20 = (bf16[512,1024]{1,0:T(8,128)(2,1)S(1)}, bf16[512,1024]{1,0:T(8,128)(2,1)S(1)}, u32[]{:S(2)}, u32[]{:S(2)}) collective-permute-start(bf16[512,1024]{1,0:T(8,128)(2,1)S(1)} %get-tuple-element.99), channel_id=1, source_target_pairs={{0,1},{1,0},{2,3},{3,2},{4,5},{5,4},{6,7},{7,6},{8,9},{9,8},{10,11... | collective-permute-start | bytes 3145736 | tf_op jit(solution)/shard_map/ppermute | solution.py:817
  132.6 32.3 %collective-permute-start.23 = (bf16[512,1024]{1,0:T(8,128)(2,1)S(1)}, bf16[512,1024]{1,0:T(8,128)(2,1)S(1)}, u32[]{:S(2)}, u32[]{:S(2)}) collective-permute-start(bf16[512,1024]{1,0:T(8,128)(2,1)S(1)} %get-tuple-element.103), channel_id=1, source_target_pairs={{0,1},{1,0},{2,3},{3,2},{4,5},{5,4},{6,7},{7,6},{8,9},{9,8},{10,11... | collective-permute-start | bytes 3145736 | tf_op jit(solution)/shard_map/ppermute | solution.py:824
  133.2 31.7 %collective-permute-start.24 = (bf16[512,1024]{1,0:T(8,128)(2,1)S(1)}, bf16[512,1024]{1,0:T(8,128)(2,1)S(1)}, u32[]{:S(2)}, u32[]{:S(2)}) collective-permute-start(bf16[512,1024]{1,0:T(8,128)(2,1)S(1)} %get-tuple-element.105), channel_id=1, source_target_pairs={{0,2},{1,3},{2,0},{3,1},{4,6},{5,7},{6,4},{7,5},{8,10},{9,11},{10,... | collective-permute-start | bytes 3145736 | tf_op jit(solution)/shard_map/ppermute | solution.py:824
  144.7 31.4 %collective-permute-start.21 = (bf16[256,1024]{1,0:T(8,128)(2,1)S(1)}, bf16[256,1024]{1,0:T(8,128)(2,1)S(1)}, u32[]{:S(2)}, u32[]{:S(2)}) collective-permute-start(bf16[256,1024]{1,0:T(8,128)(2,1)S(1)} %get-tuple-element.100), channel_id=1, source_target_pairs={{0,1},{1,0},{2,3},{3,2},{4,5},{5,4},{6,7},{7,6},{8,9},{9,8},{10,11... | collective-permute-start | bytes 1572872 | tf_op jit(solution)/shard_map/ppermute | solution.py:827
  146.2 29.8 %collective-permute-start.22 = (bf16[256,1024]{1,0:T(8,128)(2,1)S(1)}, bf16[256,1024]{1,0:T(8,128)(2,1)S(1)}, u32[]{:S(2)}, u32[]{:S(2)}) collective-permute-start(bf16[256,1024]{1,0:T(8,128)(2,1)S(1)} %get-tuple-element.101), channel_id=1, source_target_pairs={{0,2},{1,3},{2,0},{3,1},{4,6},{5,7},{6,4},{7,5},{8,10},{9,11},{10,... | collective-permute-start | bytes 1572872 | tf_op jit(solution)/shard_map/ppermute | solution.py:827
  167.2 17.8 %collective-permute-start.25 = (bf16[256,1024]{1,0:T(8,128)(2,1)S(1)}, bf16[256,1024]{1,0:T(8,128)(2,1)S(1)}, u32[]{:S(2)}, u32[]{:S(2)}) collective-permute-start(bf16[256,1024]{1,0:T(8,128)(2,1)S(1)} %get-tuple-element.107), channel_id=1, source_target_pairs={{0,2},{1,3},{2,0},{3,1},{4,6},{5,7},{6,4},{7,5},{8,10},{9,11},{10,... | collective-permute-start | bytes 1572872 | tf_op jit(solution)/shard_map/ppermute | solution.py:829
  167.7 18.5 %collective-permute-start.26 = (bf16[256,1024]{1,0:T(8,128)(2,1)S(1)}, bf16[256,1024]{1,0:T(8,128)(2,1)S(1)}, u32[]{:S(2)}, u32[]{:S(2)}) collective-permute-start(bf16[256,1024]{1,0:T(8,128)(2,1)S(1)} %get-tuple-element.108), channel_id=1, source_target_pairs={{0,1},{1,0},{2,3},{3,2},{4,5},{5,4},{6,7},{7,6},{8,9},{9,8},{10,11... | collective-permute-start | bytes 1572872 | tf_op jit(solution)/shard_map/ppermute | solution.py:829
  (1 other events, 3.8 us)

commit v7 on v6

--- a/solution.py
+++ b/solution.py
@@ -81,7 +81,7 @@
     )
 
 
-def decay_kernel(chunk, _, rate_ref, along_ref, inside_ref, down_ref, tail_ref):
+def decay_kernel(chunk, _, rate_ref, along_ref, inside_ref, down_ref, tail_ref, end_ref, half_ref):
     heads, rows = rate_ref.shape
     lane = lax.broadcasted_iota(jnp.int32, (heads, chunk), 1)
     base = jnp.zeros((heads, 1), F32)
@@ -95,11 +95,13 @@
         insides.append(x)
         wholes.append(x + base)
         base = base + x[:, chunk - 1 :]
-    inside = jnp.concatenate(insides, axis=1)
+    inside, whole = jnp.concatenate(insides, axis=1), jnp.concatenate(wholes, axis=1)
     along_ref[...] = inside
     inside_ref[...] = inside.T
-    down_ref[...] = jnp.concatenate(wholes, axis=1).T
+    down_ref[...] = whole.T
     tail_ref[...] = jnp.broadcast_to(base, tail_ref.shape)
+    end_ref[...] = jnp.exp(whole - base)
+    half_ref[...] = jnp.broadcast_to(jnp.exp(whole[:, rows // 2 - 1 : rows // 2] - base), half_ref.shape)
 
 
 def decay_call(rate, chunk):
@@ -116,8 +118,17 @@
             struct((rows, heads), F32),
             struct((rows, heads), F32),
             struct((heads, 128), F32),
+            struct((heads, rows), F32),
+            struct((heads, 128), F32),
         ),
-        [fixed((heads, rows)), fixed((rows, heads)), fixed((rows, heads)), fixed((heads, 128))],
+        [
+            fixed((heads, rows)),
+            fixed((rows, heads)),
+            fixed((rows, heads)),
+            fixed((heads, 128)),
+            fixed((heads, rows)),
+            fixed((heads, 128)),
+        ],
         heads * rows * 16,
     )
 
@@ -220,32 +231,33 @@
     )
 
 
-def own_part_kernel(_, x_ref, w_ref, out_ref, c_ref, d_ref):
-    rows = x_ref.shape[0]
-    tall = c_ref.shape[0]
-
+def own_part_kernel(_, x_ref, w_ref, out_ref, *cut_refs):
     @pl.when(pl.program_id(0) == 0)
     def _():
-        c_ref[...] = x_ref[rows - 2 * tall : rows - tall, :]
-        d_ref[...] = x_ref[rows - tall :, :]
+        for i, ref in enumerate(cut_refs):
+            tall = ref.shape[0]
+            ref[...] = x_ref[i * tall : (i + 1) * tall, :]
 
     for c in range(3):
         out_ref[c] = dot(x_ref[...], w_ref[c])
 
 
-def own_part_call(places, tokens, w_qkv, cols):
-    rows, depth = tokens.shape
+def own_part_call(places, tokens, w_qkv, cols, half, cuts):
+    rows, depth = tokens.shape[0] // 2, tokens.shape[1]
     width = w_qkv.shape[2]
-    quarter = (rows // 4, depth)
+    quarter = (rows // 2, depth)
     return call(
         own_part_kernel,
         "own_part",
         width // cols,
         places,
         (tokens, w_qkv),
-        [fixed((rows, depth)), pl.BlockSpec((3, depth, cols), lambda j, o: (0, o[0], j))],
-        (pltpu.HBM((3, rows, width), F32), pltpu.HBM(quarter, BF16), pltpu.HBM(quarter, BF16)),
-        [pl.BlockSpec((3, rows, cols), lambda j, o: (0, 0, j)), fixed(quarter), fixed(quarter)],
+        [
+            pl.BlockSpec((rows, depth), lambda j, o: (half, 0)),
+            pl.BlockSpec((3, depth, cols), lambda j, o: (0, o[0], j)),
+        ],
+        (pltpu.HBM((3, rows, width), F32), *[pltpu.HBM(quarter, BF16)] * cuts),
+        [pl.BlockSpec((3, rows, cols), lambda j, o: (0, 0, j))] + [fixed(quarter)] * cuts,
         2 * rows * depth * width * 3,
     )
 
@@ -274,7 +286,7 @@
         ref[at] = total + before_ref[c]
 
 
-def part_call(places, blocks, pieces, w_qkv, rows, cols, before, at, apart=False):
+def part_call(places, blocks, pieces, w_qkv, rows, cols, before, apart=False):
     flat = [p for piece in pieces for p in piece]
     depth = flat[0].shape[1]
     width = w_qkv.shape[2]
@@ -287,7 +299,7 @@
         pl.BlockSpec((rows // len(piece), depth), lambda j, o: (0, 0)) for piece in pieces for _ in piece
     ] + [block(i) for i in range(len(pieces))]
     ins.append(before)
-    specs.append(pl.BlockSpec((3, rows, cols), lambda j, o: (0, at, j)))
+    specs.append(pl.BlockSpec((3, rows, cols), lambda j, o: (0, 0, j)))
     outs = [struct((3, rows, width), F32)]
     if apart:
         outs = [pltpu.HBM((1, rows, width), F32), struct((2, rows, width), F32)]
@@ -306,9 +318,9 @@
     return out if apart else out[0]
 
 
-def state_kernel(chunk, group, size, places, *refs):
-    xa, xb, wk, wv, acc_k, acc_v, inside_ref, state_ref = refs[:8]
-    k_ref, v_ref, mid_ref, end_ref, sent_ref, held = refs[8:]
+def state_kernel(group, size, places, *refs):
+    xa, xb, wk, wv, acc_k, acc_v, end_ref, half_ref, state_ref = refs[:9]
+    k_ref, v_ref, out_ref, sent_ref, held = refs[9:]
     j = pl.program_id(0)
     rows = held.shape[0]
 
@@ -323,70 +335,56 @@
     v_ref[...] = v_all
     ends = []
     for a in range(group):
-        head = j * group + a
+        head = pl.ds(j * group + a, 1)
         lanes = slice(a * size, (a + 1) * size)
-        state = state_ref[a]
-        for c in range(rows // chunk):
-            here = slice(c * chunk, (c + 1) * chunk)
-            mid_ref[c, a] = state
-            state = advance(
-                k_all[here, lanes], v_all[here, lanes], column(inside_ref[here, :], head), state
-            )
-        end_ref[a] = state
-        ends.append(state.astype(BF16))
-    core = places[4]
+        scaled = (k_all[:, lanes].astype(F32).T * end_ref[head, :]).astype(BF16)
+        end = half_ref[head, :] * state_ref[a] + dot(scaled, v_all[:, lanes])
+        out_ref[a] = end
+        ends.append(end.astype(BF16))
     half = pl.num_programs(0) // 2
 
-    @pl.when(jnp.where(core == 0, j >= half, j < half))
+    @pl.when(jnp.where(places[4] == 0, j >= half, j < half))
     def _():
         for a in range(group):
             sent_ref[a] = ends[a]
 
 
-def state_call(places, far, w_qkv, acc, inside, state, chunk, group):
+def state_call(places, far, w_qkv, acc, to_end, half_fade, state, group):
     _, rows, width = acc.shape
     heads, size = state.shape[0], state.shape[1]
     depth = far[0].shape[1]
     cols = group * size
     wide = pl.BlockSpec((rows, cols), lambda j, o: (0, j))
     small = pl.BlockSpec((group, size, size), lambda j, o: (j, 0, 0))
-    chunks = rows // chunk
     half = heads // group // 2
 
     def sent_block(j, o):
         return jnp.where(o[4] == 0, jnp.maximum(j - half, 0), jnp.minimum(j, half - 1)), 0, 0
 
     return call(
-        functools.partial(state_kernel, chunk, group, size),
+        functools.partial(state_kernel, group, size),
         "states",
         heads // group,
         places,
-        (*far, w_qkv, w_qkv, acc, acc, inside, state),
+        (*far, w_qkv, w_qkv, acc, acc, to_end, half_fade, state),
         [fixed(far[0].shape), fixed(far[1].shape)]
         + [pl.BlockSpec((1, depth, cols), lambda j, o, c=c: (c, o[3], j)) for c in (1, 2)]
         + [pl.BlockSpec((1, rows, cols), lambda j, o, c=c: (c, 0, j)) for c in (0, 1)]
-        + [pl.BlockSpec((rows, heads), lambda j, o: (1, 0)), small],
+        + [pl.BlockSpec((heads, rows), lambda j, o: (0, 1)), fixed(half_fade.shape), small],
         (
             pltpu.HBM((rows, width), BF16),
             pltpu.HBM((rows, width), BF16),
-            pltpu.HBM((chunks, heads, size, size), F32),
             struct(state.shape, F32),
             struct((heads // 2, size, size), BF16),
         ),
-        [
-            wide,
-            wide,
-            pl.BlockSpec((chunks, group, size, size), lambda j, o: (0, j, 0, 0)),
-            small,
-            pl.BlockSpec((group, size, size), sent_block),
-        ],
+        [wide, wide, small, pl.BlockSpec((group, size, size), sent_block)],
         4 * rows * depth * width,
         scratch=[pltpu.VMEM((rows, depth), BF16)],
     )
 
 
 def later_kernel(chunk, group, size, _, *refs):
-    xa, xb, wq, acc_q, k_ref, v_ref, along_ref, inside_ref, mid_ref, q_ref, within_ref, held = refs
+    xa, xb, wq, acc_q, k_ref, v_ref, along_ref, inside_ref, state_ref, q_ref, within_ref, held = refs
     j = pl.program_id(0)
     rows = held.shape[0]
 
@@ -400,22 +398,19 @@
     for a in range(group):
         head = j * group + a
         lanes = slice(a * size, (a + 1) * size)
+        state = state_ref[a]
         for c in range(rows // chunk):
             here = slice(c * chunk, (c + 1) * chunk)
-            within_ref[here, lanes] = scores(
-                q_all[here, lanes],
-                k_ref[here, lanes],
-                v_ref[here, lanes],
-                along_ref[pl.ds(head, 1), here],
-                column(inside_ref[here, :], head),
-                mid_ref[c, a],
-            )
-
-
-def later_call(places, far, w_qkv, acc, k, v, along, inside, mid, group):
+            q, k, v = q_all[here, lanes], k_ref[here, lanes], v_ref[here, lanes]
+            along, down = along_ref[pl.ds(head, 1), here], column(inside_ref[here, :], head)
+            within_ref[here, lanes] = scores(q, k, v, along, down, state)
+            if c + 1 < rows // chunk:
+                state = advance(k, v, down, state)
+
+
+def later_call(places, far, w_qkv, acc, k, v, along, inside, state, chunk, group):
     _, rows, width = acc.shape
-    chunks, heads, size = mid.shape[0], mid.shape[1], mid.shape[2]
-    chunk = rows // chunks
+    heads, size = state.shape[0], state.shape[1]
     depth = far[0].shape[1]
     cols = group * size
     wide = pl.BlockSpec((rows, cols), lambda j, o: (0, j))
@@ -424,7 +419,7 @@
         "later",
         heads // group,
         places,
-        (*far, w_qkv, acc, k, v, along, inside, mid),
+        (*far, w_qkv, acc, k, v, along, inside, state),
         [
             fixed(far[0].shape),
             fixed(far[1].shape),
@@ -434,7 +429,7 @@
             wide,
             pl.BlockSpec((heads, rows), lambda j, o: (0, 1)),
             pl.BlockSpec((rows, heads), lambda j, o: (1, 0)),
-            pl.BlockSpec((chunks, group, size, size), lambda j, o: (0, j, 0, 0)),
+            pl.BlockSpec((group, size, size), lambda j, o: (j, 0, 0)),
         ],
         (struct((rows, width), BF16), struct((rows, width), F32)),
         [wide, wide],
@@ -537,9 +532,11 @@
                 normed_ref[rows, lanes] = (combined * lax.rsqrt(power + 1e-06)).astype(BF16)
             out_ref[:tall, :] = dot(normed_ref[rows, :], w_ref[...]).astype(BF16)
 
-        @pl.when(pl.program_id(0) == 2 + p)
-        def _(rows=rows, out_ref=out_ref):
-            out_ref[tall:, :] = dot(normed_ref[rows, :], w_ref[...]).astype(BF16)
+        if out_ref.shape[0] > tall:
+
+            @pl.when(pl.program_id(0) == 2 + p)
+            def _(rows=rows, out_ref=out_ref):
+                out_ref[tall:, :] = dot(normed_ref[rows, :], w_ref[...]).astype(BF16)
 
 
 def head_call(places, blocks, q, within, entering, down, w_out, width, at):
@@ -547,11 +544,18 @@
     tall = rows // 2
     heads = down.shape[1]
     part = pl.BlockSpec((tall, cols), lambda i, o: (jnp.minimum(i, 1), 0))
-    far, x, y = blocks
+    near = len(blocks) > 1
+    out = (tall * (2 if near else 1), width)
+
+    def columns(i, o):
+        if not near:
+            return 0, o[blocks[0]]
+        return 0, o[jnp.where(i < 2, blocks[0], jnp.where(i == 2, blocks[1], blocks[2]))]
+
     return call(
         head_kernel,
         "heads",
-        4,
+        4 if near else 2,
         places,
         (q, within, *entering, down, w_out),
         [
@@ -560,13 +564,10 @@
             fixed(entering[0].shape),
             fixed(entering[1].shape),
             pl.BlockSpec((tall, heads), lambda i, o: (2 * at + jnp.minimum(i, 1), 0)),
-            pl.BlockSpec(
-                (cols, width),
-                lambda i, o: (0, o[jnp.where(i < 2, far, jnp.where(i == 2, x, y))]),
-            ),
+            pl.BlockSpec((cols, width), columns),
         ],
-        (struct((rows, cols), BF16), *[struct((rows, width), BF16)] * 2),
-        [fixed((rows, cols))] + [fixed((rows, width))] * 2,
+        (struct((rows, cols), BF16), *[struct(out, BF16)] * 2),
+        [fixed((rows, cols))] + [fixed(out)] * 2,
         2 * rows * cols * (2 * width + 128),
         light=True,
     )
@@ -689,7 +690,7 @@
     flips = (0, 1, 2, 3) if square else (0, 0, 0, 0)
     places = jnp.stack([*[place ^ f for f in flips], core, chip])
 
-    along, inside, down, tail = decay_call(decay_rate, quarter)
+    along, inside, down, tail, to_end, half_fade = decay_call(decay_rate, quarter)
     n_chips = n_seq // 2
     swap = functools.partial(lax.ppermute, axis_name="seq", perm=[(i, i ^ 1) for i in range(n_seq)])
 
@@ -704,12 +705,11 @@
     if square:
         tokens = stay(tokens)
         q0, q1 = cut_call(tokens)
-        x0, y1 = over_x(q0), over_y(q1)
-        x1, y0 = over_x(after(q1, inside)), over_y(after(q0, inside))
-        acc, q2, q3 = own_part_call(places, after(tokens, inside), w_qkv, cols)
-        acc = stay(acc)
+        x0, y1, x1, y0 = over_x(q0), over_y(q1), over_x(q1), over_y(q0)
+        (acc_a,) = own_part_call(places, tokens, w_qkv, cols, 0, 0)
+        acc_b, q2, q3 = own_part_call(places, stay(after(tokens, acc_a, x0, y1)), w_qkv, cols, 1, 2)
         fy0, fx1 = over_y(x0), over_x(y1)
-        tail_other, tail_chip, tail_below = chip_tails(after(tail, x0, y1, acc))
+        tail_other, tail_chip, tail_below = chip_tails(after(tail, acc_a, x0, y1))
         x2 = over_x(after(q2, x1, y0, tail_chip))
         y3 = over_y(after(q3, x1, y0, tail_chip))
         acc_a = part_call(
@@ -719,8 +719,7 @@
             w_qkv,
             2 * quarter,
             cols,
-            before=stay(after(acc, tail_chip)),
-            at=0,
+            before=stay(after(acc_a, tail_chip, acc_b)),
         )
         earlier = (fy0, fx1, acc_a) if tail_below is None else (fy0, fx1, acc_a, tail_below)
         x3, y2 = over_x(after(q3, *earlier)), over_y(after(q2, *earlier))
@@ -745,13 +744,13 @@
             w_qkv,
             2 * quarter,
             cols,
-            before=acc,
-            at=1,
+            before=stay(acc_b),
             apart=True,
         )
         far = (fy2, fx3)
-        k, v, mid, state, sent = state_call(
-            places, far, w_qkv, acc_kv, inside, state, quarter, group
+        middle = state
+        k, v, state, sent = state_call(
+            places, far, w_qkv, acc_kv, to_end, half_fade, middle, group
         )
     else:
         tail_other, tail_chip, tail_below = chip_tails(tail)
@@ -797,7 +796,7 @@
         halves = [
             head_call(
                 places,
-                (0, 0, 0),
+                (0,),
                 query[r * rows // 2 : (r + 1) * rows // 2],
                 within[r * rows // 2 : (r + 1) * rows // 2],
                 entering,
@@ -814,9 +813,10 @@
     na, by_x, by_y = head_call(
         places, (3, 1, 2), stay(query_a), stay(within_a), entering, down, w_out, width, 0
     )
+    middle = stay(after(middle, na))
     by_x, by_y = over_x(by_x), over_y(by_y)
     query_b, within_b = later_call(
-        places, far, w_qkv, stay(acc_q), stay(k), stay(v), along, inside, stay(after(mid, na)), group
+        places, far, w_qkv, stay(acc_q), stay(k), stay(v), along, inside, middle, quarter, group
     )
     nb, by_x2, by_y2 = head_call(
         places, (3, 1, 2), query_b, within_b, entering, down, w_out, width, 1

time: 188 us -> 186 us (0.989)
  waiting for transfers between devices: 65.4 us -> 57.4 us
  Pallas kernels: 93.5 us -> 98.3 us
    ppermute x4, waiting for transfers between devices: 9.67 us -> 1.99 us  [local(): x0, y1, x1, y0 = (over_x(q0), over_y(q1), over_x(q1), over_y(q0))]
    pallas_call x15 -> x16, Pallas kernels: 91.6 us -> 96.4 us  [call(): pl.pallas_call(kernel, out_shape=tuple(outs), grid_spec=pltpu.PrefetchSca...]
    ppermute x2, starting transfers between devices: 1.09 us -> 3.06 us  [local(): by_x2, by_y2 = (over_x(by_x2), over_y(by_y2))]
    ppermute x2, starting transfers between devices: 3.09 us -> 1.14 us  [local(): by_x, by_y = (over_x(by_x), over_y(by_y))]
  transfers between devices with their start and end apart: 27 -> 27, of which waited for: 13 -> 16; matrix products, arithmetic and copies ran while one was open for 0% -> 0% of each run, Pallas kernels for 39% -> 42%
where the time goes in v7:
time: 186 us; the launch traced here: 185 us
  Pallas kernels  98.3 us (53%)
  waiting for transfers between devices  57.4 us (31%)
  starting transfers between devices  28.1 us (15%)
    pallas_call x16, Pallas kernels, call(): pl.pallas_call(kernel, out_shape=tuple(outs), grid_spec=pltpu.PrefetchSca...  96.4 us
    ppermute x2, waiting for transfers between devices, local(): by_x2, by_y2 = (over_x(by_x2), over_y(by_y2))  18 us
    ppermute x4, waiting for transfers between devices, hop(): return lax.ppermute(x, 'seq', perm=perm)  8.64 us
    ppermute x2, waiting for transfers between devices, local(): by_x, by_y = (over_x(by_x), over_y(by_y))  7.45 us
    ppermute x4, starting transfers between devices, hop(): return lax.ppermute(x, 'seq', perm=perm)  7.29 us
    ppermute x2, waiting for transfers between devices, local(): x3, y2 = (over_x(after(q3, *earlier)), over_y(after(q2, *earlier)))  7.07 us
    ppermute x2, waiting for transfers between devices, local(): sum1, sum0 = (over_x(sum1), over_y(sum0))  6.79 us
    ppermute x2, waiting for transfers between devices, local(): sum3, sum2 = (over_x(sum3), over_y(sum2))  4.67 us
  transfers between devices with their start and end apart: 27, of which 16 were waited for; matrix products, arithmetic and copies ran while one was open for 0% of the time, Pallas kernels for 42%

profile of v7, /device:TPU:8, one launch (start us, length us, event | category | flops | bytes accessed | tf_op | source)
XLA Modules:
  0.0 184.9 jit_solution(10756354871141732816)
XLA Ops:
  0.0 2.2 %cut.1 = (bf16[256,1024]{1,0:T(8,128)(2,1)}, bf16[256,1024]{1,0:T(8,128)(2,1)}) custom-call(s32[1]{0:T(128)} %constant.29.clone.1._, bf16[1024,1024]{1,0:T(8,128)(2,1)} %x_ref.4), custom_call_target="tpu_custom_call" | custom-call | flops 1 | bytes 3145728 | tf_op jit(solution)/shard_map/cut/pallas_call | solution.py:43
  3.7 1.5 collective-permute-start.1
  8.1 8.6 %own_part.2.refs_6_ = f32[3,512,1024]{2,1,0:T(8,128)} custom-call(s32[6]{0:T(128)S(1)} %stack.27._.places, bf16[1024,1024]{1,0:T(8,128)(2,1)} %x_ref.4, bf16[3,4096,1024]{2,1,0:T(8,128)(2,1)} %refs_2_.5), custom_call_target="tpu_custom_call" | custom-call | flops 3221225472 | bytes 33554432 | tf_op jit(solution)/shard_map/own_part/pallas_call | solution.py:43
  17.2 1.5 collective-permute-done.1.refs_3_
  18.8 8.7 %own_part.3 = (f32[3,512,1024]{2,1,0:T(8,128)}, bf16[256,1024]{1,0:T(8,128)(2,1)}, bf16[256,1024]{1,0:T(8,128)(2,1)}) custom-call(s32[6]{0:T(128)S(1)} %stack.27._.places, bf16[1024,1024]{1,0:T(8,128)(2,1)} %x_ref.4, bf16[3,4096,1024]{2,1,0:T(8,128)(2,1)} %refs_2_.5), custom_call_target="tpu_custom_call" | custom-call | flops 3221225472 | bytes 34603008 | tf_op jit(solution)/shard_map/own_part/pallas_call | solution.py:43
  27.5 1.5 collective-permute-start.6
  32.3 11.4 %part.2.refs_3_ = f32[3,512,1024]{2,1,0:T(8,128)S(1)} custom-call(s32[6]{0:T(128)S(1)} %stack.27._.places, bf16[256,1024]{1,0:T(8,128)(2,1)S(1)} %collective-permute-done.refs_0_, bf16[256,1024]{1,0:T(8,128)(2,1)S(1)} %collective-permute-done.2.refs_1_, bf16[256,1024]{1,0:T(8,128)(2,1)S(1)} %collective-permute-done.3.refs_2_, ...), custom_call_target="tpu_custom_call" | custom-call | flops 6442450944 | bytes 65011712 | tf_op jit(solution)/shard_map/part/pallas_call | solution.py:43
  43.8 1.6 collective-permute-start.13
  45.9 11.2 %first.1 = (bf16[512,1024]{1,0:T(8,128)(2,1)}, f32[512,1024]{1,0:T(8,128)}, f32[8,128,128]{2,1,0:T(8,128)S(1)}) custom-call(s32[6]{0:T(128)S(1)} %stack.27._.places, bf16[256,1024]{1,0:T(8,128)(2,1)S(1)} %collective-permute-done.6.refs_0_, bf16[256,1024]{1,0:T(8,128)(2,1)S(1)} %collective-permute-done.7.refs_1_, bf16[3,4096,1024]{2,1,0:T(8,128)(2,1)} %refs_2_.5, ...), custom_call_target="tpu_custom_call" | custom-call | flops 3221225472 | bytes 36241408 | tf_op jit(solution)/shard_map/first/pallas_call | solution.py:43
  57.1 1.6 collective-permute-start.10
  59.2 5.5 %collective-permute-done.13.refs_2_ = bf16[256,1024]{1,0:T(8,128)(2,1)S(1)} collective-permute-done((bf16[256,1024]{1,0:T(8,128)(2,1)S(1)}, bf16[256,1024]{1,0:T(8,128)(2,1)S(1)}, u32[]{:S(2)}, u32[]{:S(2)}) %collective-permute-start.13) | collective-permute-done | bytes 524320 | tf_op jit(solution)/shard_map/ppermute | solution.py:725
  64.7 1.6 collective-permute-done.12.refs_1_
  66.3 11.6 %part.3 = (f32[1,512,1024]{2,1,0:T(8,128)}, f32[2,512,1024]{2,1,0:T(8,128)S(1)}) custom-call(s32[6]{0:T(128)S(1)} %stack.27._.places, bf16[256,1024]{1,0:T(8,128)(2,1)S(1)} %collective-permute-done.5.refs_0_, bf16[256,1024]{1,0:T(8,128)(2,1)S(1)} %collective-permute-done.12.refs_1_, bf16[256,1024]{1,0:T(8,128)(2,1)S(1)} %collective-permute-done.13.refs_2_, ...), custom_call_target="tpu_custom_call" | custom-call | flops 6442450944 | bytes 65011712 | tf_op jit(solution)/shard_map/part/pallas_call | solution.py:43
  77.9 7.5 %states.1 = (bf16[512,1024]{1,0:T(8,128)(2,1)}, bf16[512,1024]{1,0:T(8,128)(2,1)}, f32[8,128,128]{2,1,0:T(8,128)S(1)}, bf16[4,128,128]{2,1,0:T(8,128)(2,1)S(1)}) custom-call(s32[6]{0:T(128)S(1)} %stack.27._.places, bf16[256,1024]{1,0:T(8,128)(2,1)S(1)} %collective-permute-done.8.refs_0_, bf16[256,1024]{1,0:T(8,128)(2,1)S(1)} %collective-permute-done.10.refs_1_, ...), custom_call_target="tpu_custom_call" | custom-call | flops 2147483648 | bytes 63082496 | tf_op jit(solution)/shard_map/states/pallas_call | solution.py:43
  88.7 6.1 %collective-permute-done.15.come_ref = bf16[4,128,128]{2,1,0:T(8,128)(2,1)S(1)} collective-permute-done((bf16[4,128,128]{2,1,0:T(8,128)(2,1)S(1)}, bf16[4,128,128]{2,1,0:T(8,128)(2,1)S(1)}, u32[]{:S(2)}, u32[]{:S(2)}) %collective-permute-start.15) | collective-permute-done | bytes 131104 | tf_op jit(solution)/shard_map/ppermute | solution.py:699
  95.5 2.6 %collective-permute-start.16 = (bf16[4,128,128]{2,1,0:T(8,128)(2,1)S(1)}, bf16[4,128,128]{2,1,0:T(8,128)(2,1)S(1)}, u32[]{:S(2)}, u32[]{:S(2)}) collective-permute-start(bf16[4,128,128]{2,1,0:T(8,128)(2,1)S(1)} %pass_on.1), channel_id=1, source_target_pairs={{8,16},{12,20},{9,17},{13,21},{10,18},{14,22},{11,19},{15,23}} | collective-permute-start | bytes 393224 | tf_op jit(solution)/shard_map/ppermute | solution.py:699
  98.1 2.8 %collective-permute-start.17 = (bf16[4,128,128]{2,1,0:T(8,128)(2,1)S(1)}, bf16[4,128,128]{2,1,0:T(8,128)(2,1)S(1)}, u32[]{:S(2)}, u32[]{:S(2)}) collective-permute-start(bf16[4,128,128]{2,1,0:T(8,128)(2,1)S(1)} %pass_on.1), channel_id=1, source_target_pairs={{8,24},{12,28},{9,25},{13,29},{10,26},{14,30},{11,27},{15,31}} | collective-permute-start | bytes 393224 | tf_op jit(solution)/shard_map/ppermute | solution.py:699
  101.0 2.3 %collective-permute-done.17.third_ref = bf16[4,128,128]{2,1,0:T(8,128)(2,1)S(1)} collective-permute-done((bf16[4,128,128]{2,1,0:T(8,128)(2,1)S(1)}, bf16[4,128,128]{2,1,0:T(8,128)(2,1)S(1)}, u32[]{:S(2)}, u32[]{:S(2)}) %collective-permute-start.17) | collective-permute-done | bytes 131104 | tf_op jit(solution)/shard_map/ppermute | solution.py:699
  105.4 7.9 %heads.2 = (bf16[512,1024]{1,0:T(8,128)(2,1)S(1)}, bf16[512,1024]{1,0:T(8,128)(2,1)S(1)}, bf16[512,1024]{1,0:T(8,128)(2,1)S(1)}) custom-call(s32[6]{0:T(128)S(1)} %stack.27._.places, bf16[512,1024]{1,0:T(8,128)(2,1)} %get-tuple-element.80.q_ref, f32[512,1024]{1,0:T(8,128)} %get-tuple-element.81.within_ref, ...), custom_call_target="tpu_custom_call" | custom-call | flops 1 | bytes 1 | tf_op jit(solution)/shard_map/heads/pallas_call | solution.py:43
  114.5 8.3 %later.1 = (bf16[512,1024]{1,0:T(8,128)(2,1)S(1)}, f32[512,1024]{1,0:T(8,128)S(1)}) custom-call(s32[6]{0:T(128)S(1)} %stack.27._.places, bf16[256,1024]{1,0:T(8,128)(2,1)S(1)} %collective-permute-done.8.refs_0_, bf16[256,1024]{1,0:T(8,128)(2,1)S(1)} %collective-permute-done.10.refs_1_, bf16[3,4096,1024]{2,1,0:T(8,128)(2,1)} %refs_2_.5, ...), custom_call_target="tpu_custom_call" | custom-call | flops 1879048192 | bytes 34144256 | tf_op jit(solution)/shard_map/later/pallas_call | solution.py:43
  122.8 6.7 %heads.3 = (bf16[512,1024]{1,0:T(8,128)(2,1)S(1)}, bf16[512,1024]{1,0:T(8,128)(2,1)S(1)}, bf16[512,1024]{1,0:T(8,128)(2,1)S(1)}) custom-call(s32[6]{0:T(128)S(1)} %stack.27._.places, bf16[512,1024]{1,0:T(8,128)(2,1)S(1)} %get-tuple-element.92.q_ref, f32[512,1024]{1,0:T(8,128)S(1)} %get-tuple-element.93.within_ref, ...), custom_call_target="tpu_custom_call" | custom-call | flops 1 | bytes 1 | tf_op jit(solution)/shard_map/heads/pallas_call | solution.py:43
  129.5 1.6 collective-permute-start.24
  131.0 1.5 collective-permute-start.23
  132.5 6.9 %collective-permute-done.19.x_ref.refs_2_ = bf16[512,1024]{1,0:T(8,128)(2,1)S(1)} collective-permute-done((bf16[512,1024]{1,0:T(8,128)(2,1)S(1)}, bf16[512,1024]{1,0:T(8,128)(2,1)S(1)}, u32[]{:S(2)}, u32[]{:S(2)}) %collective-permute-start.19) | collective-permute-done | bytes 1048608 | tf_op jit(solution)/shard_map/ppermute | solution.py:817
  140.0 2.3 %sum_pair.2 = (bf16[256,1024]{1,0:T(8,128)(2,1)S(1)}, bf16[256,1024]{1,0:T(8,128)(2,1)S(1)}) custom-call(s32[6]{0:T(128)S(1)} %stack.27._.places, bf16[512,1024]{1,0:T(8,128)(2,1)S(1)} %get-tuple-element.95.normed_ref, bf16[512,1024]{1,0:T(8,128)(2,1)S(1)} %collective-permute-done.19.x_ref.refs_2_, ...), custom_call_target="tpu_custom_call" | custom-call | flops 1 | bytes 1 | tf_op jit(solution)/shard_map/sum_pair/pallas_call | solution.py:43
  144.4 17.5 %collective-permute-done.24.refs_1_.x_ref = bf16[512,1024]{1,0:T(8,128)(2,1)S(1)} collective-permute-done((bf16[512,1024]{1,0:T(8,128)(2,1)S(1)}, bf16[512,1024]{1,0:T(8,128)(2,1)S(1)}, u32[]{:S(2)}, u32[]{:S(2)}) %collective-permute-start.24) | collective-permute-done | bytes 1048608 | tf_op jit(solution)/shard_map/ppermute | solution.py:824
  162.4 2.3 %sum_pair.3 = (bf16[256,1024]{1,0:T(8,128)(2,1)S(1)}, bf16[256,1024]{1,0:T(8,128)(2,1)S(1)}) custom-call(s32[6]{0:T(128)S(1)} %stack.27._.places, bf16[512,1024]{1,0:T(8,128)(2,1)S(1)} %get-tuple-element.100.normed_ref, bf16[512,1024]{1,0:T(8,128)(2,1)S(1)} %collective-permute-done.24.refs_1_.x_ref, ...), custom_call_target="tpu_custom_call" | custom-call | flops 1 | bytes 1 | tf_op jit(solution)/shard_map/sum_pair/pallas_call | solution.py:43
  164.8 1.6 collective-permute-start.25
  166.9 6.8 %collective-permute-done.21.refs_3_ = bf16[256,1024]{1,0:T(8,128)(2,1)S(1)} collective-permute-done((bf16[256,1024]{1,0:T(8,128)(2,1)S(1)}, bf16[256,1024]{1,0:T(8,128)(2,1)S(1)}, u32[]{:S(2)}, u32[]{:S(2)}) %collective-permute-start.21) | collective-permute-done | bytes 524320 | tf_op jit(solution)/shard_map/ppermute | solution.py:827
  173.7 2.4 %own_block.2.kept_ref = bf16[512,1024]{1,0:T(8,128)(2,1)S(1)} custom-call(s32[6]{0:T(128)S(1)} %stack.27._.places, bf16[512,1024]{1,0:T(8,128)(2,1)S(1)} %get-tuple-element.100.normed_ref, bf16[1024,4096]{1,0:T(8,128)(2,1)S(1)} %bitcast.7, bf16[512,1024]{1,0:T(8,128)(2,1)S(1)} %collective-permute-done.23.refs_0_.y_ref, ...), custom_call_target="tpu_custom_call" | custom-call | flops 1 | bytes 1 | tf_op jit(solution)/shard_map/own_block/pallas_call | solution.py:43
  176.1 3.0 %own_block.3.above_ref = bf16[1024,1024]{1,0:T(8,128)(2,1)} custom-call(s32[6]{0:T(128)S(1)} %stack.27._.places, bf16[512,1024]{1,0:T(8,128)(2,1)S(1)} %get-tuple-element.95.normed_ref, bf16[1024,4096]{1,0:T(8,128)(2,1)S(1)} %bitcast.7, bf16[512,1024]{1,0:T(8,128)(2,1)S(1)} %collective-permute-done.20.y_ref.refs_0_, ...), custom_call_target="tpu_custom_call" | custom-call | flops 1 | bytes 1 | tf_op jit(solution)/shard_map/own_block/pallas_call | solution.py:43
  179.1 4.4 %collective-permute-done.25.a_ref = bf16[256,1024]{1,0:T(8,128)(2,1)S(1)} collective-permute-done((bf16[256,1024]{1,0:T(8,128)(2,1)S(1)}, bf16[256,1024]{1,0:T(8,128)(2,1)S(1)}, u32[]{:S(2)}, u32[]{:S(2)}) %collective-permute-start.25) | collective-permute-done | bytes 524320 | tf_op jit(solution)/shard_map/ppermute | solution.py:829
  (58 shorter events, 21.5 us)
Async XLA Ops:
  2.2 15.0 %collective-permute-start = (bf16[256,1024]{1,0:T(8,128)(2,1)}, bf16[256,1024]{1,0:T(8,128)(2,1)S(1)}, u32[]{:S(2)}, u32[]{:S(2)}) collective-permute-start(bf16[256,1024]{1,0:T(8,128)(2,1)} %get-tuple-element.56), channel_id=1, source_target_pairs={{0,1},{1,0},{2,3},{3,2},{4,5},{5,4},{6,7},{7,6},{8,9},{9,8},{10,11... | collective-permute-start | bytes 1572872 | tf_op jit(solution)/shard_map/ppermute | solution.py:708
  3.7 15.1 %collective-permute-start.1 = (bf16[256,1024]{1,0:T(8,128)(2,1)}, bf16[256,1024]{1,0:T(8,128)(2,1)S(1)}, u32[]{:S(2)}, u32[]{:S(2)}) collective-permute-start(bf16[256,1024]{1,0:T(8,128)(2,1)} %get-tuple-element.57), channel_id=1, source_target_pairs={{0,2},{1,3},{2,0},{3,1},{4,6},{5,7},{6,4},{7,5},{8,10},{9,11},{10,... | collective-permute-start | bytes 1572872 | tf_op jit(solution)/shard_map/ppermute | solution.py:708
  5.2 25.0 %collective-permute-start.2 = (bf16[256,1024]{1,0:T(8,128)(2,1)}, bf16[256,1024]{1,0:T(8,128)(2,1)S(1)}, u32[]{:S(2)}, u32[]{:S(2)}) collective-permute-start(bf16[256,1024]{1,0:T(8,128)(2,1)} %get-tuple-element.57), channel_id=1, source_target_pairs={{0,1},{1,0},{2,3},{3,2},{4,5},{5,4},{6,7},{7,6},{8,9},{9,8},{10,11... | collective-permute-start | bytes 1572872 | tf_op jit(solution)/shard_map/ppermute | solution.py:708
  5.8 24.5 %collective-permute-start.3 = (bf16[256,1024]{1,0:T(8,128)(2,1)}, bf16[256,1024]{1,0:T(8,128)(2,1)S(1)}, u32[]{:S(2)}, u32[]{:S(2)}) collective-permute-start(bf16[256,1024]{1,0:T(8,128)(2,1)} %get-tuple-element.56), channel_id=1, source_target_pairs={{0,2},{1,3},{2,0},{3,1},{4,6},{5,7},{6,4},{7,5},{8,10},{9,11},{10,... | collective-permute-start | bytes 1572872 | tf_op jit(solution)/shard_map/ppermute | solution.py:708
  18.8 10.8 %collective-permute-start.4 = (f32[8,128]{1,0:T(8,128)S(1)}, f32[8,128]{1,0:T(8,128)S(1)}, u32[]{:S(2)}, u32[]{:S(2)}) collective-permute-start(f32[8,128]{1,0:T(8,128)S(1)} %get-tuple-element.61.tail_ref), channel_id=1, source_target_pairs={{0,4},{4,0},{8,12},{12,8},{16,20},{20,16},{24,28},{28,24},{1,5},{5... | collective-permute-start | bytes 12296 | tf_op jit(solution)/shard_map/ppermute | solution.py:702
  27.5 16.2 %collective-permute-start.6 = (bf16[256,1024]{1,0:T(8,128)(2,1)S(1)}, bf16[256,1024]{1,0:T(8,128)(2,1)S(1)}, u32[]{:S(2)}, u32[]{:S(2)}) collective-permute-start(bf16[256,1024]{1,0:T(8,128)(2,1)S(1)} %collective-permute-done.refs_0_), channel_id=1, source_target_pairs={{0,2},{1,3},{2,0},{3,1},{4,6},{5,7},{6,4},{7,5},{8,10},{9,11},{10,... | collective-permute-start | bytes 1572872 | tf_op jit(solution)/shard_map/ppermute | solution.py:711
  29.0 14.8 %collective-permute-start.7 = (bf16[256,1024]{1,0:T(8,128)(2,1)S(1)}, bf16[256,1024]{1,0:T(8,128)(2,1)S(1)}, u32[]{:S(2)}, u32[]{:S(2)}) collective-permute-start(bf16[256,1024]{1,0:T(8,128)(2,1)S(1)} %collective-permute-done.1.refs_3_), channel_id=1, source_target_pairs={{0,1},{1,0},{2,3},{3,2},{4,5},{5,4},{6,7},{7,6},{8,9},{9,8},{10,11... | collective-permute-start | bytes 1572872 | tf_op jit(solution)/shard_map/ppermute | solution.py:711
  29.6 14.2 %collective-permute-start.11 = (f32[8,128]{1,0:T(8,128)S(1)}, f32[8,128]{1,0:T(8,128)S(1)}, u32[]{:S(2)}, u32[]{:S(2)}) collective-permute-start(f32[8,128]{1,0:T(8,128)S(1)} %add.10), channel_id=1, source_target_pairs={{16,24},{20,28},{17,25},{21,29},{18,26},{22,30},{19,27},{23,31}} | collective-permute-start | bytes 12296 | tf_op jit(solution)/shard_map/ppermute | solution.py:699
  30.2 26.9 %collective-permute-start.9 = (bf16[256,1024]{1,0:T(8,128)(2,1)}, bf16[256,1024]{1,0:T(8,128)(2,1)S(1)}, u32[]{:S(2)}, u32[]{:S(2)}) collective-permute-start(bf16[256,1024]{1,0:T(8,128)(2,1)} %get-tuple-element.72), channel_id=1, source_target_pairs={{0,2},{1,3},{2,0},{3,1},{4,6},{5,7},{6,4},{7,5},{8,10},{9,11},{10,... | collective-permute-start | bytes 1572872 | tf_op jit(solution)/shard_map/ppermute | solution.py:714
  30.8 13.0 %copy-start.4 = (bf16[256,1024]{1,0:T(8,128)(2,1)S(1)}, bf16[256,1024]{1,0:T(8,128)(2,1)}, u32[]{:S(2)}) copy-start(bf16[256,1024]{1,0:T(8,128)(2,1)} %get-tuple-element.73) | copy-start | bytes 1572868
  30.8 14.5 %copy-start.3 = (bf16[256,1024]{1,0:T(8,128)(2,1)S(1)}, bf16[256,1024]{1,0:T(8,128)(2,1)}, u32[]{:S(2)}) copy-start(bf16[256,1024]{1,0:T(8,128)(2,1)} %get-tuple-element.72) | copy-start | bytes 1572868
  30.8 27.9 %collective-permute-start.5 = (bf16[256,1024]{1,0:T(8,128)(2,1)}, bf16[256,1024]{1,0:T(8,128)(2,1)S(1)}, u32[]{:S(2)}, u32[]{:S(2)}) collective-permute-start(bf16[256,1024]{1,0:T(8,128)(2,1)} %get-tuple-element.73), channel_id=1, source_target_pairs={{0,1},{1,0},{2,3},{3,2},{4,5},{5,4},{6,7},{7,6},{8,9},{9,8},{10,11... | collective-permute-start | bytes 1572872 | tf_op jit(solution)/shard_map/ppermute | solution.py:713
  43.8 20.9 %collective-permute-start.13 = (bf16[256,1024]{1,0:T(8,128)(2,1)S(1)}, bf16[256,1024]{1,0:T(8,128)(2,1)S(1)}, u32[]{:S(2)}, u32[]{:S(2)}) collective-permute-start(bf16[256,1024]{1,0:T(8,128)(2,1)S(1)} %copy-done.4), channel_id=1, source_target_pairs={{0,2},{1,3},{2,0},{3,1},{4,6},{5,7},{6,4},{7,5},{8,10},{9,11},{10,... | collective-permute-start | bytes 1572872 | tf_op jit(solution)/shard_map/ppermute | solution.py:725
  45.3 20.9 %collective-permute-start.12 = (bf16[256,1024]{1,0:T(8,128)(2,1)S(1)}, bf16[256,1024]{1,0:T(8,128)(2,1)S(1)}, u32[]{:S(2)}, u32[]{:S(2)}) collective-permute-start(bf16[256,1024]{1,0:T(8,128)(2,1)S(1)} %copy-done.3), channel_id=1, source_target_pairs={{0,1},{1,0},{2,3},{3,2},{4,5},{5,4},{6,7},{7,6},{8,9},{9,8},{10,11... | collective-permute-start | bytes 1572872 | tf_op jit(solution)/shard_map/ppermute | solution.py:725
  57.1 20.8 %copy-start = (f32[8,128,128]{2,1,0:T(8,128)}, f32[8,128,128]{2,1,0:T(8,128)S(1)}, u32[]{:S(2)}) copy-start(f32[8,128,128]{2,1,0:T(8,128)S(1)} %get-tuple-element.91.refs_8_) | copy-start | bytes 1572868
  57.1 20.8 %collective-permute-start.10 = (bf16[256,1024]{1,0:T(8,128)(2,1)S(1)}, bf16[256,1024]{1,0:T(8,128)(2,1)S(1)}, u32[]{:S(2)}, u32[]{:S(2)}) collective-permute-start(bf16[256,1024]{1,0:T(8,128)(2,1)S(1)} %collective-permute-done.9.refs_3_), channel_id=1, source_target_pairs={{0,1},{1,0},{2,3},{3,2},{4,5},{5,4},{6,7},{7,6},{8,9},{9,8},{10,11... | collective-permute-start | bytes 1572872 | tf_op jit(solution)/shard_map/ppermute | solution.py:739
  58.7 19.2 %collective-permute-start.8 = (bf16[256,1024]{1,0:T(8,128)(2,1)S(1)}, bf16[256,1024]{1,0:T(8,128)(2,1)S(1)}, u32[]{:S(2)}, u32[]{:S(2)}) collective-permute-start(bf16[256,1024]{1,0:T(8,128)(2,1)S(1)} %collective-permute-done.5.refs_0_), channel_id=1, source_target_pairs={{0,2},{1,3},{2,0},{3,1},{4,6},{5,7},{6,4},{7,5},{8,10},{9,11},{10,... | collective-permute-start | bytes 1572872 | tf_op jit(solution)/shard_map/ppermute | solution.py:739
  77.9 27.5 %slice-start = ((s8[8388608]{0:T(1024)(128)(4,1)}), s8[4194304]{0:T(1024)(128)(4,1)S(1)}, s32[]{:S(2)}) async-start(s8[8388608]{0:T(1024)(128)(4,1)} %bitcast.6), calls=%async_computation | async-start | bytes 8388608
  77.9 27.5 %slice-start.1 = ((s8[8388608]{0:T(1024)(128)(4,1)}), s8[4194304]{0:T(1024)(128)(4,1)S(1)}, s32[]{:S(2)}) async-start(s8[8388608]{0:T(1024)(128)(4,1)} %bitcast.6), calls=%async_computation.1 | async-start | bytes 8388608
  85.5 1.3 collective-permute-start.14
  87.4 7.4 %collective-permute-start.15 = (bf16[4,128,128]{2,1,0:T(8,128)(2,1)S(1)}, bf16[4,128,128]{2,1,0:T(8,128)(2,1)S(1)}, u32[]{:S(2)}, u32[]{:S(2)}) collective-permute-start(bf16[4,128,128]{2,1,0:T(8,128)(2,1)S(1)} %get-tuple-element.84), channel_id=1, source_target_pairs={{0,8},{4,12},{16,24},{20,28},{1,9},{5,13},{17,25},{21,29},{2,10},{... | collective-permute-start | bytes 393224 | tf_op jit(solution)/shard_map/ppermute | solution.py:699
  95.5 5.5 %collective-permute-start.16 = (bf16[4,128,128]{2,1,0:T(8,128)(2,1)S(1)}, bf16[4,128,128]{2,1,0:T(8,128)(2,1)S(1)}, u32[]{:S(2)}, u32[]{:S(2)}) collective-permute-start(bf16[4,128,128]{2,1,0:T(8,128)(2,1)S(1)} %pass_on.1), channel_id=1, source_target_pairs={{8,16},{12,20},{9,17},{13,21},{10,18},{14,22},{11,19},{15,23}} | collective-permute-start | bytes 393224 | tf_op jit(solution)/shard_map/ppermute | solution.py:699
  98.1 5.3 %collective-permute-start.17 = (bf16[4,128,128]{2,1,0:T(8,128)(2,1)S(1)}, bf16[4,128,128]{2,1,0:T(8,128)(2,1)S(1)}, u32[]{:S(2)}, u32[]{:S(2)}) collective-permute-start(bf16[4,128,128]{2,1,0:T(8,128)(2,1)S(1)} %pass_on.1), channel_id=1, source_target_pairs={{8,24},{12,28},{9,25},{13,29},{10,26},{14,30},{11,27},{15,31}} | collective-permute-start | bytes 393224 | tf_op jit(solution)/shard_map/ppermute | solution.py:699
  104.0 1.4 collective-permute-start.18
  113.4 26.1 %collective-permute-start.19 = (bf16[512,1024]{1,0:T(8,128)(2,1)S(1)}, bf16[512,1024]{1,0:T(8,128)(2,1)S(1)}, u32[]{:S(2)}, u32[]{:S(2)}) collective-permute-start(bf16[512,1024]{1,0:T(8,128)(2,1)S(1)} %get-tuple-element.96), channel_id=1, source_target_pairs={{0,2},{1,3},{2,0},{3,1},{4,6},{5,7},{6,4},{7,5},{8,10},{9,11},{10,... | collective-permute-start | bytes 3145736 | tf_op jit(solution)/shard_map/ppermute | solution.py:817
  113.9 26.0 %collective-permute-start.20 = (bf16[512,1024]{1,0:T(8,128)(2,1)S(1)}, bf16[512,1024]{1,0:T(8,128)(2,1)S(1)}, u32[]{:S(2)}, u32[]{:S(2)}) collective-permute-start(bf16[512,1024]{1,0:T(8,128)(2,1)S(1)} %get-tuple-element.97), channel_id=1, source_target_pairs={{0,1},{1,0},{2,3},{3,2},{4,5},{5,4},{6,7},{7,6},{8,9},{9,8},{10,11... | collective-permute-start | bytes 3145736 | tf_op jit(solution)/shard_map/ppermute | solution.py:817
  129.5 32.4 %collective-permute-start.24 = (bf16[512,1024]{1,0:T(8,128)(2,1)S(1)}, bf16[512,1024]{1,0:T(8,128)(2,1)S(1)}, u32[]{:S(2)}, u32[]{:S(2)}) collective-permute-start(bf16[512,1024]{1,0:T(8,128)(2,1)S(1)} %get-tuple-element.103), channel_id=1, source_target_pairs={{0,2},{1,3},{2,0},{3,1},{4,6},{5,7},{6,4},{7,5},{8,10},{9,11},{10,... | collective-permute-start | bytes 3145736 | tf_op jit(solution)/shard_map/ppermute | solution.py:824
  131.0 31.4 %collective-permute-start.23 = (bf16[512,1024]{1,0:T(8,128)(2,1)S(1)}, bf16[512,1024]{1,0:T(8,128)(2,1)S(1)}, u32[]{:S(2)}, u32[]{:S(2)}) collective-permute-start(bf16[512,1024]{1,0:T(8,128)(2,1)S(1)} %get-tuple-element.101), channel_id=1, source_target_pairs={{0,1},{1,0},{2,3},{3,2},{4,5},{5,4},{6,7},{7,6},{8,9},{9,8},{10,11... | collective-permute-start | bytes 3145736 | tf_op jit(solution)/shard_map/ppermute | solution.py:824
  142.3 31.4 %collective-permute-start.21 = (bf16[256,1024]{1,0:T(8,128)(2,1)S(1)}, bf16[256,1024]{1,0:T(8,128)(2,1)S(1)}, u32[]{:S(2)}, u32[]{:S(2)}) collective-permute-start(bf16[256,1024]{1,0:T(8,128)(2,1)S(1)} %get-tuple-element.98), channel_id=1, source_target_pairs={{0,1},{1,0},{2,3},{3,2},{4,5},{5,4},{6,7},{7,6},{8,9},{9,8},{10,11... | collective-permute-start | bytes 1572872 | tf_op jit(solution)/shard_map/ppermute | solution.py:827
  142.9 30.8 %collective-permute-start.22 = (bf16[256,1024]{1,0:T(8,128)(2,1)S(1)}, bf16[256,1024]{1,0:T(8,128)(2,1)S(1)}, u32[]{:S(2)}, u32[]{:S(2)}) collective-permute-start(bf16[256,1024]{1,0:T(8,128)(2,1)S(1)} %get-tuple-element.99), channel_id=1, source_target_pairs={{0,2},{1,3},{2,0},{3,1},{4,6},{5,7},{6,4},{7,5},{8,10},{9,11},{10,... | collective-permute-start | bytes 1572872 | tf_op jit(solution)/shard_map/ppermute | solution.py:827
  164.8 18.8 %collective-permute-start.25 = (bf16[256,1024]{1,0:T(8,128)(2,1)S(1)}, bf16[256,1024]{1,0:T(8,128)(2,1)S(1)}, u32[]{:S(2)}, u32[]{:S(2)}) collective-permute-start(bf16[256,1024]{1,0:T(8,128)(2,1)S(1)} %get-tuple-element.105), channel_id=1, source_target_pairs={{0,2},{1,3},{2,0},{3,1},{4,6},{5,7},{6,4},{7,5},{8,10},{9,11},{10,... | collective-permute-start | bytes 1572872 | tf_op jit(solution)/shard_map/ppermute | solution.py:829
  166.4 17.4 %collective-permute-start.26 = (bf16[256,1024]{1,0:T(8,128)(2,1)S(1)}, bf16[256,1024]{1,0:T(8,128)(2,1)S(1)}, u32[]{:S(2)}, u32[]{:S(2)}) collective-permute-start(bf16[256,1024]{1,0:T(8,128)(2,1)S(1)} %get-tuple-element.106), channel_id=1, source_target_pairs={{0,1},{1,0},{2,3},{3,2},{4,5},{5,4},{6,7},{7,6},{8,9},{9,8},{10,11... | collective-permute-start | bytes 1572872 | tf_op jit(solution)/shard_map/ppermute | solution.py:829
  (2 other events, 9.6 us)

commit v8 on v7

--- a/solution.py
+++ b/solution.py
@@ -59,26 +59,31 @@
     )(scalars, *ins)
 
 
-def cut_kernel(_, x_ref, a_ref, b_ref):
+def cut_kernel(x_ref, a_ref, b_ref, sems):
     tall = a_ref.shape[0]
-    a_ref[...] = x_ref[:tall, :]
-    b_ref[...] = x_ref[tall:, :]
+    copies = [
+        pltpu.make_async_copy(x_ref.at[pl.ds(i * tall, tall)], out_ref, sems.at[i])
+        for i, out_ref in enumerate((a_ref, b_ref))
+    ]
+    for copy in copies:
+        copy.start()
+    for copy in copies:
+        copy.wait()
 
 
 def cut_call(x):
     rows, width = x.shape
-    quarter = (rows // 4, width)
-    return call(
+    quarter = struct((rows // 4, width), x.dtype)
+    return pl.pallas_call(
         cut_kernel,
-        "cut",
-        1,
-        jnp.zeros((1,), jnp.int32),
-        (x,),
-        [fixed((rows // 2, width))],
-        (struct(quarter, x.dtype),) * 2,
-        [fixed(quarter)] * 2,
-        1,
-    )
+        out_shape=(quarter, quarter),
+        in_specs=[pl.BlockSpec(memory_space=pl.ANY)],
+        out_specs=[pl.BlockSpec(memory_space=pltpu.VMEM)] * 2,
+        scratch_shapes=[pltpu.SemaphoreType.DMA((2,))],
+        compiler_params=pltpu.CompilerParams(vmem_limit_bytes=4 * MIB),
+        cost_estimate=pl.CostEstimate(flops=1, bytes_accessed=x.size * 2, transcendentals=0),
+        name="cut",
+    )(x)
 
 
 def decay_kernel(chunk, _, rate_ref, along_ref, inside_ref, down_ref, tail_ref, end_ref, half_ref):
@@ -238,146 +243,151 @@
             tall = ref.shape[0]
             ref[...] = x_ref[i * tall : (i + 1) * tall, :]
 
-    for c in range(3):
-        out_ref[c] = dot(x_ref[...], w_ref[c])
-
-
-def own_part_call(places, tokens, w_qkv, cols, half, cuts):
+    out_ref[0] = dot(x_ref[...], w_ref[0])
+
+
+def own_part_call(places, tokens, w_qkv, half, cuts):
     rows, depth = tokens.shape[0] // 2, tokens.shape[1]
     width = w_qkv.shape[2]
     quarter = (rows // 2, depth)
     return call(
         own_part_kernel,
         "own_part",
-        width // cols,
+        3,
         places,
         (tokens, w_qkv),
         [
-            pl.BlockSpec((rows, depth), lambda j, o: (half, 0)),
-            pl.BlockSpec((3, depth, cols), lambda j, o: (0, o[0], j)),
+            pl.BlockSpec((rows, depth), lambda c, o: (half, 0)),
+            pl.BlockSpec((1, depth, width), lambda c, o: (c, o[0], 0)),
         ],
         (pltpu.HBM((3, rows, width), F32), *[pltpu.HBM(quarter, BF16)] * cuts),
-        [pl.BlockSpec((3, rows, cols), lambda j, o: (0, 0, j))] + [fixed(quarter)] * cuts,
+        [pl.BlockSpec((1, rows, width), lambda c, o: (c, 0, 0))] + [fixed(quarter)] * cuts,
         2 * rows * depth * width * 3,
     )
 
 
-def part_kernel(layout, outs, _, *refs):
-    count = sum(layout)
-    x_refs, w_refs = refs[:count], refs[count : count + len(layout)]
-    before_ref, out_refs, held = refs[-2 - outs], refs[-1 - outs : -1], refs[-1]
-    targets = [(ref, c) for ref in out_refs for c in range(ref.shape[0])]
-    rows = held.shape[1]
-
-    @pl.when(pl.program_id(0) == 0)
-    def _():
-        at = 0
-        for i, parts in enumerate(layout):
-            tall = rows // parts
-            for p in range(parts):
-                held[i, p * tall : (p + 1) * tall, :] = x_refs[at][...]
-                at += 1
-
-    for c in range(3):
-        total = dot(held[0], w_refs[0][c])
-        for i in range(1, len(layout)):
-            total = total + dot(held[i], w_refs[i][c])
-        ref, at = targets[c]
-        ref[at] = total + before_ref[c]
-
-
-def part_call(places, blocks, pieces, w_qkv, rows, cols, before, apart=False):
-    flat = [p for piece in pieces for p in piece]
-    depth = flat[0].shape[1]
-    width = w_qkv.shape[2]
-
-    def block(i):
-        return pl.BlockSpec((3, depth, cols), lambda j, o: (0, o[blocks[i]], j))
-
-    ins = [*flat, *[w_qkv] * len(pieces)]
-    specs = [
-        pl.BlockSpec((rows // len(piece), depth), lambda j, o: (0, 0)) for piece in pieces for _ in piece
-    ] + [block(i) for i in range(len(pieces))]
-    ins.append(before)
-    specs.append(pl.BlockSpec((3, rows, cols), lambda j, o: (0, 0, j)))
+def part_kernel(apart, _, xa, xb, ya, yb, w_ref, before_ref, *refs):
+    out_refs, held = refs[:-1], refs[-1]
+    j = pl.program_id(0)
+    tall = xa.shape[0]
+
+    @pl.when(j == 0)
+    def _():
+        held[0, :tall, :] = xa[...]
+        held[0, tall:, :] = xb[...]
+        held[1, :tall, :] = ya[...]
+        held[1, tall:, :] = yb[...]
+
+    def add(ref):
+        @pl.when(j % 2 == 0)
+        def _():
+            ref[0] = before_ref[0] + dot(held[0], w_ref[0])
+
+        @pl.when(j % 2 == 1)
+        def _():
+            ref[0] = ref[0] + dot(held[1], w_ref[0])
+
+    if not apart:
+        add(out_refs[0])
+        return
+
+    @pl.when(j < 2)
+    def _():
+        add(out_refs[0])
+
+    @pl.when(j >= 2)
+    def _():
+        add(out_refs[1])
+
+
+def part_call(places, pieces, w_qkv, before, apart=False):
+    tall, depth = pieces[0].shape
+    rows, width = 2 * tall, w_qkv.shape[2]
     outs = [struct((3, rows, width), F32)]
+    places_out = [lambda j, o: (j // 2, 0, 0)]
     if apart:
         outs = [pltpu.HBM((1, rows, width), F32), struct((2, rows, width), F32)]
+        places_out = [lambda j, o: (0, 0, 0), lambda j, o: (jnp.maximum(j // 2 - 1, 0), 0, 0)]
     out = call(
-        functools.partial(part_kernel, tuple(len(p) for p in pieces), len(outs)),
+        functools.partial(part_kernel, apart),
         "part",
-        width // cols,
+        6,
         places,
-        ins,
-        specs,
+        (*pieces, w_qkv, before),
+        [fixed((tall, depth))] * 4
+        + [
+            pl.BlockSpec((1, depth, width), lambda j, o: (j // 2, o[1 + j % 2], 0)),
+            pl.BlockSpec((1, rows, width), lambda j, o: (j // 2, 0, 0)),
+        ],
         outs,
-        [pl.BlockSpec((o.shape[0], rows, cols), lambda j, o: (0, 0, j)) for o in outs],
-        2 * rows * depth * len(pieces) * width * 3,
-        scratch=[pltpu.VMEM((len(pieces), rows, depth), BF16)],
+        [pl.BlockSpec((1, rows, width), place) for place in places_out],
+        2 * rows * depth * 2 * width * 3,
+        scratch=[pltpu.VMEM((2, rows, depth), BF16)],
     )
     return out if apart else out[0]
 
 
-def state_kernel(group, size, places, *refs):
-    xa, xb, wk, wv, acc_k, acc_v, end_ref, half_ref, state_ref = refs[:9]
-    k_ref, v_ref, out_ref, sent_ref, held = refs[9:]
+def state_kernel(size, places, *refs):
+    xa, xb, w_ref, acc_ref, end_ref, half_ref, state_ref, k_ref, v_ref, out_ref, sent_ref, held = refs
     j = pl.program_id(0)
-    rows = held.shape[0]
+    tall = xa.shape[0]
+    share = sent_ref.shape[0]
 
     @pl.when(j == 0)
     def _():
-        held[: rows // 2, :] = xa[...]
-        held[rows // 2 :, :] = xb[...]
-
-    k_all = (acc_k[0] + dot(held[...], wk[0])).astype(BF16)
-    v_all = (acc_v[0] + dot(held[...], wv[0])).astype(BF16)
-    k_ref[...] = k_all
-    v_ref[...] = v_all
-    ends = []
-    for a in range(group):
-        head = pl.ds(j * group + a, 1)
-        lanes = slice(a * size, (a + 1) * size)
-        scaled = (k_all[:, lanes].astype(F32).T * end_ref[head, :]).astype(BF16)
-        end = half_ref[head, :] * state_ref[a] + dot(scaled, v_all[:, lanes])
-        out_ref[a] = end
-        ends.append(end.astype(BF16))
-    half = pl.num_programs(0) // 2
-
-    @pl.when(jnp.where(places[4] == 0, j >= half, j < half))
-    def _():
-        for a in range(group):
-            sent_ref[a] = ends[a]
-
-
-def state_call(places, far, w_qkv, acc, to_end, half_fade, state, group):
+        held[:tall, :] = xa[...]
+        held[tall:, :] = xb[...]
+
+    total = (acc_ref[0] + dot(held[...], w_ref[0])).astype(BF16)
+
+    @pl.when(j % 2 == 0)
+    def _():
+        k_ref[...] = total
+
+    @pl.when(j % 2 == 1)
+    def _():
+        v_ref[...] = total
+        for a in range(share):
+            head = pl.ds((j // 2) * share + a, 1)
+            lanes = slice(a * size, (a + 1) * size)
+            scaled = (k_ref[:, lanes].astype(F32).T * end_ref[head, :]).astype(BF16)
+            end = half_ref[head, :] * state_ref[a] + dot(scaled, total[:, lanes])
+            out_ref[a] = end
+
+            @pl.when(j // 2 != places[4])
+            def _(a=a, end=end):
+                sent_ref[a] = end.astype(BF16)
+
+
+def state_call(places, far, w_qkv, acc, to_end, half_fade, state):
     _, rows, width = acc.shape
     heads, size = state.shape[0], state.shape[1]
     depth = far[0].shape[1]
-    cols = group * size
-    wide = pl.BlockSpec((rows, cols), lambda j, o: (0, j))
-    small = pl.BlockSpec((group, size, size), lambda j, o: (j, 0, 0))
-    half = heads // group // 2
-
-    def sent_block(j, o):
-        return jnp.where(o[4] == 0, jnp.maximum(j - half, 0), jnp.minimum(j, half - 1)), 0, 0
-
+    share, cols = heads // 2, width // 2
+    wide = pl.BlockSpec((rows, cols), lambda j, o: (0, j // 2))
+    small = pl.BlockSpec((share, size, size), lambda j, o: (j // 2, 0, 0))
     return call(
-        functools.partial(state_kernel, group, size),
+        functools.partial(state_kernel, size),
         "states",
-        heads // group,
+        4,
         places,
-        (*far, w_qkv, w_qkv, acc, acc, to_end, half_fade, state),
-        [fixed(far[0].shape), fixed(far[1].shape)]
-        + [pl.BlockSpec((1, depth, cols), lambda j, o, c=c: (c, o[3], j)) for c in (1, 2)]
-        + [pl.BlockSpec((1, rows, cols), lambda j, o, c=c: (c, 0, j)) for c in (0, 1)]
-        + [pl.BlockSpec((heads, rows), lambda j, o: (0, 1)), fixed(half_fade.shape), small],
+        (*far, w_qkv, acc, to_end, half_fade, state),
+        [
+            fixed(far[0].shape),
+            fixed(far[1].shape),
+            pl.BlockSpec((1, depth, cols), lambda j, o: (1 + j % 2, o[3], j // 2)),
+            pl.BlockSpec((1, rows, cols), lambda j, o: (j % 2, 0, j // 2)),
+            pl.BlockSpec((heads, rows), lambda j, o: (0, 1)),
+            fixed(half_fade.shape),
+            small,
+        ],
         (
             pltpu.HBM((rows, width), BF16),
             pltpu.HBM((rows, width), BF16),
             struct(state.shape, F32),
-            struct((heads // 2, size, size), BF16),
+            struct((share, size, size), BF16),
         ),
-        [wide, wide, small, pl.BlockSpec((group, size, size), sent_block)],
+        [wide, wide, small, fixed((share, size, size))],
         4 * rows * depth * width,
         scratch=[pltpu.VMEM((rows, depth), BF16)],
     )
@@ -680,7 +690,6 @@
     place = lax.axis_index("head").astype(jnp.int32)
     quarter = rows // 4
     group = 2 if heads % 2 == 0 else 1
-    cols = group * size
 
     over_x = functools.partial(lax.ppermute, axis_name="head", perm=[(i, i ^ 1) for i in range(n_head)])
     over_y = functools.partial(lax.ppermute, axis_name="head", perm=[(i, i ^ 2) for i in range(n_head)])
@@ -706,20 +715,14 @@
         tokens = stay(tokens)
         q0, q1 = cut_call(tokens)
         x0, y1, x1, y0 = over_x(q0), over_y(q1), over_x(q1), over_y(q0)
-        (acc_a,) = own_part_call(places, tokens, w_qkv, cols, 0, 0)
-        acc_b, q2, q3 = own_part_call(places, stay(after(tokens, acc_a, x0, y1)), w_qkv, cols, 1, 2)
+        (acc_a,) = own_part_call(places, tokens, w_qkv, 0, 0)
+        acc_b, q2, q3 = own_part_call(places, stay(after(tokens, acc_a, x0, y1)), w_qkv, 1, 2)
         fy0, fx1 = over_y(x0), over_x(y1)
         tail_other, tail_chip, tail_below = chip_tails(after(tail, acc_a, x0, y1))
         x2 = over_x(after(q2, x1, y0, tail_chip))
         y3 = over_y(after(q3, x1, y0, tail_chip))
         acc_a = part_call(
-            places,
-            (1, 2),
-            [(x0, x1), (y0, y1)],
-            w_qkv,
-            2 * quarter,
-            cols,
-            before=stay(after(acc_a, tail_chip, acc_b)),
+            places, (x0, x1, y0, y1), w_qkv, stay(after(acc_a, tail_chip, acc_b))
         )
         earlier = (fy0, fx1, acc_a) if tail_below is None else (fy0, fx1, acc_a, tail_below)
         x3, y2 = over_x(after(q3, *earlier)), over_y(after(q2, *earlier))
@@ -737,21 +740,10 @@
             group,
         )
         fy2, fx3 = over_y(after(x2, state)), over_x(after(y3, state))
-        acc_q, acc_kv = part_call(
-            places,
-            (1, 2),
-            [(x2, x3), (y2, y3)],
-            w_qkv,
-            2 * quarter,
-            cols,
-            before=stay(acc_b),
-            apart=True,
-        )
+        acc_q, acc_kv = part_call(places, (x2, x3, y2, y3), w_qkv, stay(acc_b), apart=True)
         far = (fy2, fx3)
         middle = state
-        k, v, state, sent = state_call(
-            places, far, w_qkv, acc_kv, to_end, half_fade, middle, group
-        )
+        k, v, state, sent = state_call(places, far, w_qkv, acc_kv, to_end, half_fade, middle)
     else:
         tail_other, tail_chip, tail_below = chip_tails(tail)
         gathered = lax.all_gather(tokens, "head", axis=1, tiled=True)

time: 186 us -> 190 us (1.022)
  Pallas kernels: 98.3 us -> 104 us
    pallas_call x16 -> x15, Pallas kernels: 96.4 us -> 99.8 us  [call(): pl.pallas_call(kernel, out_shape=tuple(outs), grid_spec=pltpu.PrefetchSca...]
    pallas_call x0 -> x1, Pallas kernels: none -> 2.18 us  [cut_call(): pl.pallas_call(cut_kernel, out_shape=(quarter, quarter), in_specs=[pl.Blo...]
  transfers between devices with their start and end apart: 27 -> 27, of which waited for: 16 -> 16; matrix products, arithmetic and copies ran while one was open for 0% -> 0% of each run, Pallas kernels for 42% -> 43%
where the time goes in v8:
time: 190 us; the launch traced here: 189 us
  Pallas kernels  104 us (55%)
  waiting for transfers between devices  55.8 us (29%)
  starting transfers between devices  28.2 us (15%)
    pallas_call x15, Pallas kernels, call(): pl.pallas_call(kernel, out_shape=tuple(outs), grid_spec=pltpu.PrefetchSca...  99.8 us
    ppermute x2, waiting for transfers between devices, local(): by_x2, by_y2 = (over_x(by_x2), over_y(by_y2))  18 us
    ppermute x4, waiting for transfers between devices, hop(): return lax.ppermute(x, 'seq', perm=perm)  8.64 us
    ppermute x2, waiting for transfers between devices, local(): by_x, by_y = (over_x(by_x), over_y(by_y))  7.45 us
    ppermute x4, starting transfers between devices, hop(): return lax.ppermute(x, 'seq', perm=perm)  7.29 us
    ppermute x2, waiting for transfers between devices, local(): sum1, sum0 = (over_x(sum1), over_y(sum0))  6.78 us
    ppermute x2, waiting for transfers between devices, local(): x3, y2 = (over_x(after(q3, *earlier)), over_y(after(q2, *earlier)))  5.91 us
    ppermute x2, waiting for transfers between devices, local(): sum3, sum2 = (over_x(sum3), over_y(sum2))  4.67 us
  transfers between devices with their start and end apart: 27, of which 16 were waited for; matrix products, arithmetic and copies ran while one was open for 0% of the time, Pallas kernels for 43%

profile of v8, /device:TPU:8, one launch (start us, length us, event | category | flops | bytes accessed | tf_op | source)
XLA Modules:
  0.0 189.0 jit_solution(952774928341566603)
XLA Ops:
  0.0 2.2 %cut.1 = (bf16[256,1024]{1,0:T(8,128)(2,1)}, bf16[256,1024]{1,0:T(8,128)(2,1)}) custom-call(bf16[1024,1024]{1,0:T(8,128)(2,1)} %x_ref.4), custom_call_target="tpu_custom_call" | custom-call | flops 1 | bytes 2097152 | tf_op jit(solution)/shard_map/cut/pallas_call | solution.py:77
  2.2 1.6 collective-permute-start
  3.7 1.5 collective-permute-start.1
  8.2 9.0 %own_part.2.before_ref = f32[3,512,1024]{2,1,0:T(8,128)} custom-call(s32[6]{0:T(128)S(1)} %stack.27._.places, bf16[1024,1024]{1,0:T(8,128)(2,1)} %x_ref.4, bf16[3,4096,1024]{2,1,0:T(8,128)(2,1)} %refs_2_.5), custom_call_target="tpu_custom_call" | custom-call | flops 3221225472 | bytes 33554432 | tf_op jit(solution)/shard_map/own_part/pallas_call | solution.py:43
  17.3 1.5 collective-permute-done.1.yb
  18.8 9.0 %own_part.3 = (f32[3,512,1024]{2,1,0:T(8,128)}, bf16[256,1024]{1,0:T(8,128)(2,1)}, bf16[256,1024]{1,0:T(8,128)(2,1)}) custom-call(s32[6]{0:T(128)S(1)} %stack.27._.places, bf16[1024,1024]{1,0:T(8,128)(2,1)} %x_ref.4, bf16[3,4096,1024]{2,1,0:T(8,128)(2,1)} %refs_2_.5), custom_call_target="tpu_custom_call" | custom-call | flops 3221225472 | bytes 34603008 | tf_op jit(solution)/shard_map/own_part/pallas_call | solution.py:43
  27.8 1.5 collective-permute-start.6
  32.6 12.6 %part.2.refs_3_ = f32[3,512,1024]{2,1,0:T(8,128)S(1)} custom-call(s32[6]{0:T(128)S(1)} %stack.27._.places, bf16[256,1024]{1,0:T(8,128)(2,1)S(1)} %collective-permute-done.xa, bf16[256,1024]{1,0:T(8,128)(2,1)S(1)} %collective-permute-done.2.xb, bf16[256,1024]{1,0:T(8,128)(2,1)S(1)} %collective-permute-done.3.ya, ...), custom_call_target="tpu_custom_call" | custom-call | flops 6442450944 | bytes 39845888 | tf_op jit(solution)/shard_map/part/pallas_call | solution.py:43
  45.2 1.6 collective-permute-start.13
  47.3 11.2 %first.1 = (bf16[512,1024]{1,0:T(8,128)(2,1)}, f32[512,1024]{1,0:T(8,128)}, f32[8,128,128]{2,1,0:T(8,128)S(1)}) custom-call(s32[6]{0:T(128)S(1)} %stack.27._.places, bf16[256,1024]{1,0:T(8,128)(2,1)S(1)} %collective-permute-done.6.refs_0_, bf16[256,1024]{1,0:T(8,128)(2,1)S(1)} %collective-permute-done.7.refs_1_, bf16[3,4096,1024]{2,1,0:T(8,128)(2,1)} %refs_2_.5, ...), custom_call_target="tpu_custom_call" | custom-call | flops 3221225472 | bytes 36241408 | tf_op jit(solution)/shard_map/first/pallas_call | solution.py:43
  58.6 1.6 collective-permute-start.10
  60.6 4.4 %collective-permute-done.13.ya = bf16[256,1024]{1,0:T(8,128)(2,1)S(1)} collective-permute-done((bf16[256,1024]{1,0:T(8,128)(2,1)S(1)}, bf16[256,1024]{1,0:T(8,128)(2,1)S(1)}, u32[]{:S(2)}, u32[]{:S(2)}) %collective-permute-start.13) | collective-permute-done | bytes 524320 | tf_op jit(solution)/shard_map/ppermute | solution.py:728
  65.0 1.6 collective-permute-done.12.xb
  66.6 13.9 %part.3 = (f32[1,512,1024]{2,1,0:T(8,128)}, f32[2,512,1024]{2,1,0:T(8,128)S(1)}) custom-call(s32[6]{0:T(128)S(1)} %stack.27._.places, bf16[256,1024]{1,0:T(8,128)(2,1)S(1)} %collective-permute-done.5.xa, bf16[256,1024]{1,0:T(8,128)(2,1)S(1)} %collective-permute-done.12.xb, bf16[256,1024]{1,0:T(8,128)(2,1)S(1)} %collective-permute-done.13.ya, ...), custom_call_target="tpu_custom_call" | custom-call | flops 6442450944 | bytes 39845888 | tf_op jit(solution)/shard_map/part/pallas_call | solution.py:43
  80.5 9.1 %states.1 = (bf16[512,1024]{1,0:T(8,128)(2,1)}, bf16[512,1024]{1,0:T(8,128)(2,1)}, f32[8,128,128]{2,1,0:T(8,128)S(1)}, bf16[4,128,128]{2,1,0:T(8,128)(2,1)S(1)}) custom-call(s32[6]{0:T(128)S(1)} %stack.27._.places, bf16[256,1024]{1,0:T(8,128)(2,1)S(1)} %collective-permute-done.8.refs_0_, bf16[256,1024]{1,0:T(8,128)(2,1)S(1)} %collective-permute-done.10.refs_1_, ...), custom_call_target="tpu_custom_call" | custom-call | flops 2147483648 | bytes 33722368 | tf_op jit(solution)/shard_map/states/pallas_call | solution.py:43
  92.9 6.1 %collective-permute-done.15.come_ref = bf16[4,128,128]{2,1,0:T(8,128)(2,1)S(1)} collective-permute-done((bf16[4,128,128]{2,1,0:T(8,128)(2,1)S(1)}, bf16[4,128,128]{2,1,0:T(8,128)(2,1)S(1)}, u32[]{:S(2)}, u32[]{:S(2)}) %collective-permute-start.15) | collective-permute-done | bytes 131104 | tf_op jit(solution)/shard_map/ppermute | solution.py:708
  99.6 2.6 %collective-permute-start.16 = (bf16[4,128,128]{2,1,0:T(8,128)(2,1)S(1)}, bf16[4,128,128]{2,1,0:T(8,128)(2,1)S(1)}, u32[]{:S(2)}, u32[]{:S(2)}) collective-permute-start(bf16[4,128,128]{2,1,0:T(8,128)(2,1)S(1)} %pass_on.1), channel_id=1, source_target_pairs={{8,16},{12,20},{9,17},{13,21},{10,18},{14,22},{11,19},{15,23}} | collective-permute-start | bytes 393224 | tf_op jit(solution)/shard_map/ppermute | solution.py:708
  102.2 2.8 %collective-permute-start.17 = (bf16[4,128,128]{2,1,0:T(8,128)(2,1)S(1)}, bf16[4,128,128]{2,1,0:T(8,128)(2,1)S(1)}, u32[]{:S(2)}, u32[]{:S(2)}) collective-permute-start(bf16[4,128,128]{2,1,0:T(8,128)(2,1)S(1)} %pass_on.1), channel_id=1, source_target_pairs={{8,24},{12,28},{9,25},{13,29},{10,26},{14,30},{11,27},{15,31}} | collective-permute-start | bytes 393224 | tf_op jit(solution)/shard_map/ppermute | solution.py:708
  105.1 2.3 %collective-permute-done.17.third_ref = bf16[4,128,128]{2,1,0:T(8,128)(2,1)S(1)} collective-permute-done((bf16[4,128,128]{2,1,0:T(8,128)(2,1)S(1)}, bf16[4,128,128]{2,1,0:T(8,128)(2,1)S(1)}, u32[]{:S(2)}, u32[]{:S(2)}) %collective-permute-start.17) | collective-permute-done | bytes 131104 | tf_op jit(solution)/shard_map/ppermute | solution.py:708
  109.6 7.9 %heads.2 = (bf16[512,1024]{1,0:T(8,128)(2,1)S(1)}, bf16[512,1024]{1,0:T(8,128)(2,1)S(1)}, bf16[512,1024]{1,0:T(8,128)(2,1)S(1)}) custom-call(s32[6]{0:T(128)S(1)} %stack.27._.places, bf16[512,1024]{1,0:T(8,128)(2,1)} %get-tuple-element.80.q_ref, f32[512,1024]{1,0:T(8,128)} %get-tuple-element.81.within_ref, ...), custom_call_target="tpu_custom_call" | custom-call | flops 1 | bytes 1 | tf_op jit(solution)/shard_map/heads/pallas_call | solution.py:43
  118.6 8.3 %later.1 = (bf16[512,1024]{1,0:T(8,128)(2,1)S(1)}, f32[512,1024]{1,0:T(8,128)S(1)}) custom-call(s32[6]{0:T(128)S(1)} %stack.27._.places, bf16[256,1024]{1,0:T(8,128)(2,1)S(1)} %collective-permute-done.8.refs_0_, bf16[256,1024]{1,0:T(8,128)(2,1)S(1)} %collective-permute-done.10.refs_1_, bf16[3,4096,1024]{2,1,0:T(8,128)(2,1)} %refs_2_.5, ...), custom_call_target="tpu_custom_call" | custom-call | flops 1879048192 | bytes 34144256 | tf_op jit(solution)/shard_map/later/pallas_call | solution.py:43
  126.9 6.7 %heads.3 = (bf16[512,1024]{1,0:T(8,128)(2,1)S(1)}, bf16[512,1024]{1,0:T(8,128)(2,1)S(1)}, bf16[512,1024]{1,0:T(8,128)(2,1)S(1)}) custom-call(s32[6]{0:T(128)S(1)} %stack.27._.places, bf16[512,1024]{1,0:T(8,128)(2,1)S(1)} %get-tuple-element.92.q_ref, f32[512,1024]{1,0:T(8,128)S(1)} %get-tuple-element.93.within_ref, ...), custom_call_target="tpu_custom_call" | custom-call | flops 1 | bytes 1 | tf_op jit(solution)/shard_map/heads/pallas_call | solution.py:43
  133.6 1.6 collective-permute-start.24
  136.7 6.9 %collective-permute-done.19.x_ref.refs_2_ = bf16[512,1024]{1,0:T(8,128)(2,1)S(1)} collective-permute-done((bf16[512,1024]{1,0:T(8,128)(2,1)S(1)}, bf16[512,1024]{1,0:T(8,128)(2,1)S(1)}, u32[]{:S(2)}, u32[]{:S(2)}) %collective-permute-start.19) | collective-permute-done | bytes 1048608 | tf_op jit(solution)/shard_map/ppermute | solution.py:809
  144.1 2.3 %sum_pair.2 = (bf16[256,1024]{1,0:T(8,128)(2,1)S(1)}, bf16[256,1024]{1,0:T(8,128)(2,1)S(1)}) custom-call(s32[6]{0:T(128)S(1)} %stack.27._.places, bf16[512,1024]{1,0:T(8,128)(2,1)S(1)} %get-tuple-element.95.normed_ref, bf16[512,1024]{1,0:T(8,128)(2,1)S(1)} %collective-permute-done.19.x_ref.refs_2_, ...), custom_call_target="tpu_custom_call" | custom-call | flops 1 | bytes 1 | tf_op jit(solution)/shard_map/sum_pair/pallas_call | solution.py:43
  148.6 17.5 %collective-permute-done.24.refs_1_.x_ref = bf16[512,1024]{1,0:T(8,128)(2,1)S(1)} collective-permute-done((bf16[512,1024]{1,0:T(8,128)(2,1)S(1)}, bf16[512,1024]{1,0:T(8,128)(2,1)S(1)}, u32[]{:S(2)}, u32[]{:S(2)}) %collective-permute-start.24) | collective-permute-done | bytes 1048608 | tf_op jit(solution)/shard_map/ppermute | solution.py:816
  166.6 2.3 %sum_pair.3 = (bf16[256,1024]{1,0:T(8,128)(2,1)S(1)}, bf16[256,1024]{1,0:T(8,128)(2,1)S(1)}) custom-call(s32[6]{0:T(128)S(1)} %stack.27._.places, bf16[512,1024]{1,0:T(8,128)(2,1)S(1)} %get-tuple-element.100.normed_ref, bf16[512,1024]{1,0:T(8,128)(2,1)S(1)} %collective-permute-done.24.refs_1_.x_ref, ...), custom_call_target="tpu_custom_call" | custom-call | flops 1 | bytes 1 | tf_op jit(solution)/shard_map/sum_pair/pallas_call | solution.py:43
  168.9 1.6 collective-permute-start.25
  171.0 6.8 %collective-permute-done.21.refs_3_ = bf16[256,1024]{1,0:T(8,128)(2,1)S(1)} collective-permute-done((bf16[256,1024]{1,0:T(8,128)(2,1)S(1)}, bf16[256,1024]{1,0:T(8,128)(2,1)S(1)}, u32[]{:S(2)}, u32[]{:S(2)}) %collective-permute-start.21) | collective-permute-done | bytes 524320 | tf_op jit(solution)/shard_map/ppermute | solution.py:819
  177.8 2.4 %own_block.2.kept_ref = bf16[512,1024]{1,0:T(8,128)(2,1)S(1)} custom-call(s32[6]{0:T(128)S(1)} %stack.27._.places, bf16[512,1024]{1,0:T(8,128)(2,1)S(1)} %get-tuple-element.100.normed_ref, bf16[1024,4096]{1,0:T(8,128)(2,1)S(1)} %bitcast.7, bf16[512,1024]{1,0:T(8,128)(2,1)S(1)} %collective-permute-done.23.refs_0_.y_ref, ...), custom_call_target="tpu_custom_call" | custom-call | flops 1 | bytes 1 | tf_op jit(solution)/shard_map/own_block/pallas_call | solution.py:43
  180.2 3.0 %own_block.3.above_ref = bf16[1024,1024]{1,0:T(8,128)(2,1)} custom-call(s32[6]{0:T(128)S(1)} %stack.27._.places, bf16[512,1024]{1,0:T(8,128)(2,1)S(1)} %get-tuple-element.95.normed_ref, bf16[1024,4096]{1,0:T(8,128)(2,1)S(1)} %bitcast.7, bf16[512,1024]{1,0:T(8,128)(2,1)S(1)} %collective-permute-done.20.y_ref.refs_0_, ...), custom_call_target="tpu_custom_call" | custom-call | flops 1 | bytes 1 | tf_op jit(solution)/shard_map/own_block/pallas_call | solution.py:43
  183.3 4.4 %collective-permute-done.25.a_ref = bf16[256,1024]{1,0:T(8,128)(2,1)S(1)} collective-permute-done((bf16[256,1024]{1,0:T(8,128)(2,1)S(1)}, bf16[256,1024]{1,0:T(8,128)(2,1)S(1)}, u32[]{:S(2)}, u32[]{:S(2)}) %collective-permute-start.25) | collective-permute-done | bytes 524320 | tf_op jit(solution)/shard_map/ppermute | solution.py:821
  (58 shorter events, 21.1 us)
Async XLA Ops:
  2.2 15.1 %collective-permute-start = (bf16[256,1024]{1,0:T(8,128)(2,1)}, bf16[256,1024]{1,0:T(8,128)(2,1)S(1)}, u32[]{:S(2)}, u32[]{:S(2)}) collective-permute-start(bf16[256,1024]{1,0:T(8,128)(2,1)} %get-tuple-element.56), channel_id=1, source_target_pairs={{0,1},{1,0},{2,3},{3,2},{4,5},{5,4},{6,7},{7,6},{8,9},{9,8},{10,11... | collective-permute-start | bytes 1572872 | tf_op jit(solution)/shard_map/ppermute | solution.py:717
  3.7 15.1 %collective-permute-start.1 = (bf16[256,1024]{1,0:T(8,128)(2,1)}, bf16[256,1024]{1,0:T(8,128)(2,1)S(1)}, u32[]{:S(2)}, u32[]{:S(2)}) collective-permute-start(bf16[256,1024]{1,0:T(8,128)(2,1)} %get-tuple-element.57), channel_id=1, source_target_pairs={{0,2},{1,3},{2,0},{3,1},{4,6},{5,7},{6,4},{7,5},{8,10},{9,11},{10,... | collective-permute-start | bytes 1572872 | tf_op jit(solution)/shard_map/ppermute | solution.py:717
  5.3 25.3 %collective-permute-start.2 = (bf16[256,1024]{1,0:T(8,128)(2,1)}, bf16[256,1024]{1,0:T(8,128)(2,1)S(1)}, u32[]{:S(2)}, u32[]{:S(2)}) collective-permute-start(bf16[256,1024]{1,0:T(8,128)(2,1)} %get-tuple-element.57), channel_id=1, source_target_pairs={{0,1},{1,0},{2,3},{3,2},{4,5},{5,4},{6,7},{7,6},{8,9},{9,8},{10,11... | collective-permute-start | bytes 1572872 | tf_op jit(solution)/shard_map/ppermute | solution.py:717
  5.8 24.7 %collective-permute-start.3 = (bf16[256,1024]{1,0:T(8,128)(2,1)}, bf16[256,1024]{1,0:T(8,128)(2,1)S(1)}, u32[]{:S(2)}, u32[]{:S(2)}) collective-permute-start(bf16[256,1024]{1,0:T(8,128)(2,1)} %get-tuple-element.56), channel_id=1, source_target_pairs={{0,2},{1,3},{2,0},{3,1},{4,6},{5,7},{6,4},{7,5},{8,10},{9,11},{10,... | collective-permute-start | bytes 1572872 | tf_op jit(solution)/shard_map/ppermute | solution.py:717
  18.8 11.1 %collective-permute-start.4 = (f32[8,128]{1,0:T(8,128)S(1)}, f32[8,128]{1,0:T(8,128)S(1)}, u32[]{:S(2)}, u32[]{:S(2)}) collective-permute-start(f32[8,128]{1,0:T(8,128)S(1)} %get-tuple-element.61.tail_ref), channel_id=1, source_target_pairs={{0,4},{4,0},{8,12},{12,8},{16,20},{20,16},{24,28},{28,24},{1,5},{5... | collective-permute-start | bytes 12296 | tf_op jit(solution)/shard_map/ppermute | solution.py:711
  27.8 17.4 %collective-permute-start.6 = (bf16[256,1024]{1,0:T(8,128)(2,1)S(1)}, bf16[256,1024]{1,0:T(8,128)(2,1)S(1)}, u32[]{:S(2)}, u32[]{:S(2)}) collective-permute-start(bf16[256,1024]{1,0:T(8,128)(2,1)S(1)} %collective-permute-done.xa), channel_id=1, source_target_pairs={{0,2},{1,3},{2,0},{3,1},{4,6},{5,7},{6,4},{7,5},{8,10},{9,11},{10,... | collective-permute-start | bytes 1572872 | tf_op jit(solution)/shard_map/ppermute | solution.py:720
  29.3 15.9 %collective-permute-start.7 = (bf16[256,1024]{1,0:T(8,128)(2,1)S(1)}, bf16[256,1024]{1,0:T(8,128)(2,1)S(1)}, u32[]{:S(2)}, u32[]{:S(2)}) collective-permute-start(bf16[256,1024]{1,0:T(8,128)(2,1)S(1)} %collective-permute-done.1.yb), channel_id=1, source_target_pairs={{0,1},{1,0},{2,3},{3,2},{4,5},{5,4},{6,7},{7,6},{8,9},{9,8},{10,11... | collective-permute-start | bytes 1572872 | tf_op jit(solution)/shard_map/ppermute | solution.py:720
  29.9 15.3 %collective-permute-start.11 = (f32[8,128]{1,0:T(8,128)S(1)}, f32[8,128]{1,0:T(8,128)S(1)}, u32[]{:S(2)}, u32[]{:S(2)}) collective-permute-start(f32[8,128]{1,0:T(8,128)S(1)} %add.10), channel_id=1, source_target_pairs={{16,24},{20,28},{17,25},{21,29},{18,26},{22,30},{19,27},{23,31}} | collective-permute-start | bytes 12296 | tf_op jit(solution)/shard_map/ppermute | solution.py:708
  30.6 28.0 %collective-permute-start.9 = (bf16[256,1024]{1,0:T(8,128)(2,1)}, bf16[256,1024]{1,0:T(8,128)(2,1)S(1)}, u32[]{:S(2)}, u32[]{:S(2)}) collective-permute-start(bf16[256,1024]{1,0:T(8,128)(2,1)} %get-tuple-element.72), channel_id=1, source_target_pairs={{0,2},{1,3},{2,0},{3,1},{4,6},{5,7},{6,4},{7,5},{8,10},{9,11},{10,... | collective-permute-start | bytes 1572872 | tf_op jit(solution)/shard_map/ppermute | solution.py:723
  31.1 14.1 %copy-start.4 = (bf16[256,1024]{1,0:T(8,128)(2,1)S(1)}, bf16[256,1024]{1,0:T(8,128)(2,1)}, u32[]{:S(2)}) copy-start(bf16[256,1024]{1,0:T(8,128)(2,1)} %get-tuple-element.73) | copy-start | bytes 1572868
  31.1 15.7 %copy-start.3 = (bf16[256,1024]{1,0:T(8,128)(2,1)S(1)}, bf16[256,1024]{1,0:T(8,128)(2,1)}, u32[]{:S(2)}) copy-start(bf16[256,1024]{1,0:T(8,128)(2,1)} %get-tuple-element.72) | copy-start | bytes 1572868
  31.1 29.0 %collective-permute-start.5 = (bf16[256,1024]{1,0:T(8,128)(2,1)}, bf16[256,1024]{1,0:T(8,128)(2,1)S(1)}, u32[]{:S(2)}, u32[]{:S(2)}) collective-permute-start(bf16[256,1024]{1,0:T(8,128)(2,1)} %get-tuple-element.73), channel_id=1, source_target_pairs={{0,1},{1,0},{2,3},{3,2},{4,5},{5,4},{6,7},{7,6},{8,9},{9,8},{10,11... | collective-permute-start | bytes 1572872 | tf_op jit(solution)/shard_map/ppermute | solution.py:722
  45.2 19.8 %collective-permute-start.13 = (bf16[256,1024]{1,0:T(8,128)(2,1)S(1)}, bf16[256,1024]{1,0:T(8,128)(2,1)S(1)}, u32[]{:S(2)}, u32[]{:S(2)}) collective-permute-start(bf16[256,1024]{1,0:T(8,128)(2,1)S(1)} %copy-done.4), channel_id=1, source_target_pairs={{0,2},{1,3},{2,0},{3,1},{4,6},{5,7},{6,4},{7,5},{8,10},{9,11},{10,... | collective-permute-start | bytes 1572872 | tf_op jit(solution)/shard_map/ppermute | solution.py:728
  46.8 19.7 %collective-permute-start.12 = (bf16[256,1024]{1,0:T(8,128)(2,1)S(1)}, bf16[256,1024]{1,0:T(8,128)(2,1)S(1)}, u32[]{:S(2)}, u32[]{:S(2)}) collective-permute-start(bf16[256,1024]{1,0:T(8,128)(2,1)S(1)} %copy-done.3), channel_id=1, source_target_pairs={{0,1},{1,0},{2,3},{3,2},{4,5},{5,4},{6,7},{7,6},{8,9},{9,8},{10,11... | collective-permute-start | bytes 1572872 | tf_op jit(solution)/shard_map/ppermute | solution.py:728
  58.6 21.9 %copy-start = (f32[8,128,128]{2,1,0:T(8,128)}, f32[8,128,128]{2,1,0:T(8,128)S(1)}, u32[]{:S(2)}) copy-start(f32[8,128,128]{2,1,0:T(8,128)S(1)} %get-tuple-element.91.refs_6_.refs_8_) | copy-start | bytes 1572868
  58.6 21.8 %collective-permute-start.10 = (bf16[256,1024]{1,0:T(8,128)(2,1)S(1)}, bf16[256,1024]{1,0:T(8,128)(2,1)S(1)}, u32[]{:S(2)}, u32[]{:S(2)}) collective-permute-start(bf16[256,1024]{1,0:T(8,128)(2,1)S(1)} %collective-permute-done.9.yb), channel_id=1, source_target_pairs={{0,1},{1,0},{2,3},{3,2},{4,5},{5,4},{6,7},{7,6},{8,9},{9,8},{10,11... | collective-permute-start | bytes 1572872 | tf_op jit(solution)/shard_map/ppermute | solution.py:742
  60.1 20.3 %collective-permute-start.8 = (bf16[256,1024]{1,0:T(8,128)(2,1)S(1)}, bf16[256,1024]{1,0:T(8,128)(2,1)S(1)}, u32[]{:S(2)}, u32[]{:S(2)}) collective-permute-start(bf16[256,1024]{1,0:T(8,128)(2,1)S(1)} %collective-permute-done.5.xa), channel_id=1, source_target_pairs={{0,2},{1,3},{2,0},{3,1},{4,6},{5,7},{6,4},{7,5},{8,10},{9,11},{10,... | collective-permute-start | bytes 1572872 | tf_op jit(solution)/shard_map/ppermute | solution.py:742
  80.4 29.1 %slice-start = ((s8[8388608]{0:T(1024)(128)(4,1)}), s8[4194304]{0:T(1024)(128)(4,1)S(1)}, s32[]{:S(2)}) async-start(s8[8388608]{0:T(1024)(128)(4,1)} %bitcast.6), calls=%async_computation | async-start | bytes 8388608
  80.5 29.1 %slice-start.1 = ((s8[8388608]{0:T(1024)(128)(4,1)}), s8[4194304]{0:T(1024)(128)(4,1)S(1)}, s32[]{:S(2)}) async-start(s8[8388608]{0:T(1024)(128)(4,1)} %bitcast.6), calls=%async_computation.1 | async-start | bytes 8388608
  89.6 1.3 collective-permute-start.14
  91.6 7.4 %collective-permute-start.15 = (bf16[4,128,128]{2,1,0:T(8,128)(2,1)S(1)}, bf16[4,128,128]{2,1,0:T(8,128)(2,1)S(1)}, u32[]{:S(2)}, u32[]{:S(2)}) collective-permute-start(bf16[4,128,128]{2,1,0:T(8,128)(2,1)S(1)} %get-tuple-element.84), channel_id=1, source_target_pairs={{0,8},{4,12},{16,24},{20,28},{1,9},{5,13},{17,25},{21,29},{2,10},{... | collective-permute-start | bytes 393224 | tf_op jit(solution)/shard_map/ppermute | solution.py:708
  99.6 5.5 %collective-permute-start.16 = (bf16[4,128,128]{2,1,0:T(8,128)(2,1)S(1)}, bf16[4,128,128]{2,1,0:T(8,128)(2,1)S(1)}, u32[]{:S(2)}, u32[]{:S(2)}) collective-permute-start(bf16[4,128,128]{2,1,0:T(8,128)(2,1)S(1)} %pass_on.1), channel_id=1, source_target_pairs={{8,16},{12,20},{9,17},{13,21},{10,18},{14,22},{11,19},{15,23}} | collective-permute-start | bytes 393224 | tf_op jit(solution)/shard_map/ppermute | solution.py:708
  102.2 5.3 %collective-permute-start.17 = (bf16[4,128,128]{2,1,0:T(8,128)(2,1)S(1)}, bf16[4,128,128]{2,1,0:T(8,128)(2,1)S(1)}, u32[]{:S(2)}, u32[]{:S(2)}) collective-permute-start(bf16[4,128,128]{2,1,0:T(8,128)(2,1)S(1)} %pass_on.1), channel_id=1, source_target_pairs={{8,24},{12,28},{9,25},{13,29},{10,26},{14,30},{11,27},{15,31}} | collective-permute-start | bytes 393224 | tf_op jit(solution)/shard_map/ppermute | solution.py:708
  108.2 1.4 collective-permute-start.18
  117.5 26.1 %collective-permute-start.19 = (bf16[512,1024]{1,0:T(8,128)(2,1)S(1)}, bf16[512,1024]{1,0:T(8,128)(2,1)S(1)}, u32[]{:S(2)}, u32[]{:S(2)}) collective-permute-start(bf16[512,1024]{1,0:T(8,128)(2,1)S(1)} %get-tuple-element.96), channel_id=1, source_target_pairs={{0,2},{1,3},{2,0},{3,1},{4,6},{5,7},{6,4},{7,5},{8,10},{9,11},{10,... | collective-permute-start | bytes 3145736 | tf_op jit(solution)/shard_map/ppermute | solution.py:809
  118.1 26.0 %collective-permute-start.20 = (bf16[512,1024]{1,0:T(8,128)(2,1)S(1)}, bf16[512,1024]{1,0:T(8,128)(2,1)S(1)}, u32[]{:S(2)}, u32[]{:S(2)}) collective-permute-start(bf16[512,1024]{1,0:T(8,128)(2,1)S(1)} %get-tuple-element.97), channel_id=1, source_target_pairs={{0,1},{1,0},{2,3},{3,2},{4,5},{5,4},{6,7},{7,6},{8,9},{9,8},{10,11... | collective-permute-start | bytes 3145736 | tf_op jit(solution)/shard_map/ppermute | solution.py:809
  133.6 32.4 %collective-permute-start.24 = (bf16[512,1024]{1,0:T(8,128)(2,1)S(1)}, bf16[512,1024]{1,0:T(8,128)(2,1)S(1)}, u32[]{:S(2)}, u32[]{:S(2)}) collective-permute-start(bf16[512,1024]{1,0:T(8,128)(2,1)S(1)} %get-tuple-element.103), channel_id=1, source_target_pairs={{0,2},{1,3},{2,0},{3,1},{4,6},{5,7},{6,4},{7,5},{8,10},{9,11},{10,... | collective-permute-start | bytes 3145736 | tf_op jit(solution)/shard_map/ppermute | solution.py:816
  135.2 31.4 %collective-permute-start.23 = (bf16[512,1024]{1,0:T(8,128)(2,1)S(1)}, bf16[512,1024]{1,0:T(8,128)(2,1)S(1)}, u32[]{:S(2)}, u32[]{:S(2)}) collective-permute-start(bf16[512,1024]{1,0:T(8,128)(2,1)S(1)} %get-tuple-element.101), channel_id=1, source_target_pairs={{0,1},{1,0},{2,3},{3,2},{4,5},{5,4},{6,7},{7,6},{8,9},{9,8},{10,11... | collective-permute-start | bytes 3145736 | tf_op jit(solution)/shard_map/ppermute | solution.py:816
  146.4 31.4 %collective-permute-start.21 = (bf16[256,1024]{1,0:T(8,128)(2,1)S(1)}, bf16[256,1024]{1,0:T(8,128)(2,1)S(1)}, u32[]{:S(2)}, u32[]{:S(2)}) collective-permute-start(bf16[256,1024]{1,0:T(8,128)(2,1)S(1)} %get-tuple-element.98), channel_id=1, source_target_pairs={{0,1},{1,0},{2,3},{3,2},{4,5},{5,4},{6,7},{7,6},{8,9},{9,8},{10,11... | collective-permute-start | bytes 1572872 | tf_op jit(solution)/shard_map/ppermute | solution.py:819
  147.1 30.8 %collective-permute-start.22 = (bf16[256,1024]{1,0:T(8,128)(2,1)S(1)}, bf16[256,1024]{1,0:T(8,128)(2,1)S(1)}, u32[]{:S(2)}, u32[]{:S(2)}) collective-permute-start(bf16[256,1024]{1,0:T(8,128)(2,1)S(1)} %get-tuple-element.99), channel_id=1, source_target_pairs={{0,2},{1,3},{2,0},{3,1},{4,6},{5,7},{6,4},{7,5},{8,10},{9,11},{10,... | collective-permute-start | bytes 1572872 | tf_op jit(solution)/shard_map/ppermute | solution.py:819
  168.9 18.8 %collective-permute-start.25 = (bf16[256,1024]{1,0:T(8,128)(2,1)S(1)}, bf16[256,1024]{1,0:T(8,128)(2,1)S(1)}, u32[]{:S(2)}, u32[]{:S(2)}) collective-permute-start(bf16[256,1024]{1,0:T(8,128)(2,1)S(1)} %get-tuple-element.105), channel_id=1, source_target_pairs={{0,2},{1,3},{2,0},{3,1},{4,6},{5,7},{6,4},{7,5},{8,10},{9,11},{10,... | collective-permute-start | bytes 1572872 | tf_op jit(solution)/shard_map/ppermute | solution.py:821
  170.5 17.4 %collective-permute-start.26 = (bf16[256,1024]{1,0:T(8,128)(2,1)S(1)}, bf16[256,1024]{1,0:T(8,128)(2,1)S(1)}, u32[]{:S(2)}, u32[]{:S(2)}) collective-permute-start(bf16[256,1024]{1,0:T(8,128)(2,1)S(1)} %get-tuple-element.106), channel_id=1, source_target_pairs={{0,1},{1,0},{2,3},{3,2},{4,5},{5,4},{6,7},{7,6},{8,9},{9,8},{10,11... | collective-permute-start | bytes 1572872 | tf_op jit(solution)/shard_map/ppermute | solution.py:821
  (2 other events, 11.3 us)

commit v9 on v7

--- a/solution.py
+++ b/solution.py
@@ -65,7 +65,7 @@
     b_ref[...] = x_ref[tall:, :]
 
 
-def cut_call(x):
+def cut_call(x, half, cost):
     rows, width = x.shape
     quarter = (rows // 4, width)
     return call(
@@ -74,10 +74,10 @@
         1,
         jnp.zeros((1,), jnp.int32),
         (x,),
-        [fixed((rows // 2, width))],
+        [pl.BlockSpec((rows // 2, width), lambda j, o: (half, 0))],
         (struct(quarter, x.dtype),) * 2,
         [fixed(quarter)] * 2,
-        1,
+        cost,
     )
 
 
@@ -231,35 +231,25 @@
     )
 
 
-def own_part_kernel(_, x_ref, w_ref, out_ref, *cut_refs):
-    @pl.when(pl.program_id(0) == 0)
-    def _():
-        for i, ref in enumerate(cut_refs):
-            tall = ref.shape[0]
-            ref[...] = x_ref[i * tall : (i + 1) * tall, :]
-
+def own_part_kernel(_, x_ref, w_ref, out_ref):
     for c in range(3):
         out_ref[c] = dot(x_ref[...], w_ref[c])
 
 
-def own_part_call(places, tokens, w_qkv, cols, half, cuts):
-    rows, depth = tokens.shape[0] // 2, tokens.shape[1]
+def own_part_call(places, tokens, w_qkv, cols):
+    rows, depth = tokens.shape
     width = w_qkv.shape[2]
-    quarter = (rows // 2, depth)
     return call(
         own_part_kernel,
         "own_part",
         width // cols,
         places,
         (tokens, w_qkv),
-        [
-            pl.BlockSpec((rows, depth), lambda j, o: (half, 0)),
-            pl.BlockSpec((3, depth, cols), lambda j, o: (0, o[0], j)),
-        ],
-        (pltpu.HBM((3, rows, width), F32), *[pltpu.HBM(quarter, BF16)] * cuts),
-        [pl.BlockSpec((3, rows, cols), lambda j, o: (0, 0, j))] + [fixed(quarter)] * cuts,
+        [fixed((rows, depth)), pl.BlockSpec((3, depth, cols), lambda j, o: (0, o[0], j))],
+        (pltpu.HBM((3, rows, width), F32),),
+        [pl.BlockSpec((3, rows, cols), lambda j, o: (0, 0, j))],
         2 * rows * depth * width * 3,
-    )
+    )[0]
 
 
 def part_kernel(layout, outs, _, *refs):
@@ -286,7 +276,7 @@
         ref[at] = total + before_ref[c]
 
 
-def part_call(places, blocks, pieces, w_qkv, rows, cols, before, apart=False):
+def part_call(places, blocks, pieces, w_qkv, rows, cols, before, at, apart=False):
     flat = [p for piece in pieces for p in piece]
     depth = flat[0].shape[1]
     width = w_qkv.shape[2]
@@ -299,7 +289,7 @@
         pl.BlockSpec((rows // len(piece), depth), lambda j, o: (0, 0)) for piece in pieces for _ in piece
     ] + [block(i) for i in range(len(pieces))]
     ins.append(before)
-    specs.append(pl.BlockSpec((3, rows, cols), lambda j, o: (0, 0, j)))
+    specs.append(pl.BlockSpec((3, rows, cols), lambda j, o: (0, at, j)))
     outs = [struct((3, rows, width), F32)]
     if apart:
         outs = [pltpu.HBM((1, rows, width), F32), struct((2, rows, width), F32)]
@@ -337,7 +327,7 @@
     for a in range(group):
         head = pl.ds(j * group + a, 1)
         lanes = slice(a * size, (a + 1) * size)
-        scaled = (k_all[:, lanes].astype(F32).T * end_ref[head, :]).astype(BF16)
+        scaled = (k_all[:, lanes].T.astype(F32) * end_ref[head, :]).astype(BF16)
         end = half_ref[head, :] * state_ref[a] + dot(scaled, v_all[:, lanes])
         out_ref[a] = end
         ends.append(end.astype(BF16))
@@ -513,14 +503,22 @@
     return small_call(enter_kernel, "enter", places, ins, outs)
 
 
-def head_kernel(places, q_ref, within_ref, here_ref, there_ref, down_ref, w_ref, normed_ref, *out_refs):
+def columns(w_ref, block, width):
+    return w_ref[:, pl.ds(pl.multiple_of(block * width, width), width)]
+
+
+WHOLE = pl.BlockSpec(memory_space=pltpu.VMEM)
+
+
+def head_kernel(blocks, places, q_ref, within_ref, here_ref, there_ref, down_ref, w_ref, *refs):
+    normed_ref, out_refs, held = refs[0], refs[1:3], refs[3]
     share, size = here_ref.shape[0], here_ref.shape[1]
-    tall = q_ref.shape[0]
+    tall, width = out_refs[0].shape
+    step = pl.program_id(0)
     for p, out_ref in enumerate(out_refs):
-        rows = slice(p * tall, (p + 1) * tall)
-
-        @pl.when(pl.program_id(0) == p)
-        def _(rows=rows, out_ref=out_ref):
+
+        @pl.when(step == p)
+        def _(p=p, out_ref=out_ref):
             fade = jnp.exp(-down_ref[...])
             for a in range(2 * share):
                 lanes = slice(a * size, (a + 1) * size)
@@ -529,14 +527,13 @@
                 seen = dot(q_ref[:, lanes], entering) * fade[:, a : a + 1]
                 combined = within_ref[:, lanes] + seen
                 power = jnp.mean(combined * combined, axis=1, keepdims=True)
-                normed_ref[rows, lanes] = (combined * lax.rsqrt(power + 1e-06)).astype(BF16)
-            out_ref[:tall, :] = dot(normed_ref[rows, :], w_ref[...]).astype(BF16)
-
-        if out_ref.shape[0] > tall:
-
-            @pl.when(pl.program_id(0) == 2 + p)
-            def _(rows=rows, out_ref=out_ref):
-                out_ref[tall:, :] = dot(normed_ref[rows, :], w_ref[...]).astype(BF16)
+                held[p, :, lanes] = (combined * lax.rsqrt(power + 1e-06)).astype(BF16)
+            normed_ref[...] = held[p]
+            out_ref[...] = dot(held[p], columns(w_ref, places[blocks[0]], width)).astype(BF16)
+
+        @pl.when(step == 2 + p)
+        def _(p=p, out_ref=out_ref):
+            out_ref[...] = dot(held[p], columns(w_ref, places[blocks[1 + p]], width)).astype(BF16)
 
 
 def head_call(places, blocks, q, within, entering, down, w_out, width, at):
@@ -544,18 +541,10 @@
     tall = rows // 2
     heads = down.shape[1]
     part = pl.BlockSpec((tall, cols), lambda i, o: (jnp.minimum(i, 1), 0))
-    near = len(blocks) > 1
-    out = (tall * (2 if near else 1), width)
-
-    def columns(i, o):
-        if not near:
-            return 0, o[blocks[0]]
-        return 0, o[jnp.where(i < 2, blocks[0], jnp.where(i == 2, blocks[1], blocks[2]))]
-
-    return call(
-        head_kernel,
+    return call(
+        functools.partial(head_kernel, blocks),
         "heads",
-        4 if near else 2,
+        4,
         places,
         (q, within, *entering, down, w_out),
         [
@@ -564,25 +553,32 @@
             fixed(entering[0].shape),
             fixed(entering[1].shape),
             pl.BlockSpec((tall, heads), lambda i, o: (2 * at + jnp.minimum(i, 1), 0)),
-            pl.BlockSpec((cols, width), columns),
+            WHOLE,
         ],
-        (struct((rows, cols), BF16), *[struct(out, BF16)] * 2),
-        [fixed((rows, cols))] + [fixed(out)] * 2,
+        (struct((rows, cols), BF16), *[struct((rows, width), BF16)] * 2),
+        [
+            part,
+            pl.BlockSpec((tall, width), lambda i, o: (i // 2, 0)),
+            pl.BlockSpec((tall, width), lambda i, o: (jnp.maximum(i - 2, 0), 0)),
+        ],
         2 * rows * cols * (2 * width + 128),
+        scratch=[pltpu.VMEM((2, tall, cols), BF16)],
         light=True,
     )
 
 
-def pair_kernel(_, normed_ref, x_ref, y_ref, w_ref, out_x_ref, out_y_ref):
-    tall = x_ref.shape[0]
+def pair_kernel(places, normed_ref, x_ref, y_ref, w_ref, out_x_ref, out_y_ref):
+    tall, width = out_x_ref.shape
 
     @pl.when(pl.program_id(0) == 0)
     def _():
-        out_x_ref[...] = (dot(normed_ref[tall:, :], w_ref[...]) + x_ref[...].astype(F32)).astype(BF16)
+        total = dot(normed_ref[tall:, :], columns(w_ref, places[1], width)) + x_ref[...].astype(F32)
+        out_x_ref[...] = total.astype(BF16)
 
     @pl.when(pl.program_id(0) == 1)
     def _():
-        out_y_ref[...] = (dot(normed_ref[:tall, :], w_ref[...]) + y_ref[...].astype(F32)).astype(BF16)
+        total = dot(normed_ref[:tall, :], columns(w_ref, places[2], width)) + y_ref[...].astype(F32)
+        out_y_ref[...] = total.astype(BF16)
 
 
 def pair_call(places, normed, for_x, for_y, w_out, width):
@@ -594,12 +590,7 @@
         2,
         places,
         (normed, for_x, for_y, w_out),
-        [
-            fixed((rows, cols)),
-            fixed(quarter),
-            fixed(quarter),
-            pl.BlockSpec((cols, width), lambda i, o: (0, o[1 + i])),
-        ],
+        [fixed((rows, cols)), fixed(quarter), fixed(quarter), WHOLE],
         (struct(quarter, BF16),) * 2,
         [fixed(quarter)] * 2,
         2 * rows * cols * width,
@@ -607,16 +598,16 @@
     )
 
 
-def own_kernel(_, normed_ref, w_ref, *refs):
+def own_kernel(places, normed_ref, w_ref, *refs):
     out_ref = refs[-1]
-    tall = out_ref.shape[0]
+    tall, width = out_ref.shape
     each = len(refs) // 2
     for p in range(2):
         rows = slice(p * tall, (p + 1) * tall)
 
         @pl.when(pl.program_id(0) == p)
         def _(p=p, rows=rows):
-            total = dot(normed_ref[rows, :], w_ref[...])
+            total = dot(normed_ref[rows, :], columns(w_ref, places[0], width))
             for ref in refs[p * each : (p + 1) * each]:
                 total = total + ref[...].astype(F32)
             out_ref[...] = total.astype(BF16)
@@ -631,7 +622,7 @@
         2,
         places,
         (normed, w_out, *[a for a, _ in (*first, *second)]),
-        [fixed((rows, cols)), pl.BlockSpec((cols, width), lambda i, o: (0, o[0]))]
+        [fixed((rows, cols)), WHOLE]
         + [pl.BlockSpec(quarter, lambda i, o, at=at: (at, 0)) for _, at in (*first, *second)],
         (struct((rows * height, width), BF16),),
         [pl.BlockSpec(quarter, lambda i, o: (i, 0))],
@@ -704,12 +695,13 @@
 
     if square:
         tokens = stay(tokens)
-        q0, q1 = cut_call(tokens)
-        x0, y1, x1, y0 = over_x(q0), over_y(q1), over_x(q1), over_y(q0)
-        (acc_a,) = own_part_call(places, tokens, w_qkv, cols, 0, 0)
-        acc_b, q2, q3 = own_part_call(places, stay(after(tokens, acc_a, x0, y1)), w_qkv, cols, 1, 2)
+        q0, q1 = cut_call(tokens, 0, 1)
+        x0, y1 = over_x(q0), over_y(q1)
+        x1, y0 = over_x(after(q1, tail)), over_y(after(q0, tail))
+        acc = own_part_call(places, tokens, w_qkv, cols)
+        q2, q3 = cut_call(stay(after(tokens, acc, x0, y1)), 1, 10**10)
         fy0, fx1 = over_y(x0), over_x(y1)
-        tail_other, tail_chip, tail_below = chip_tails(after(tail, acc_a, x0, y1))
+        tail_other, tail_chip, tail_below = chip_tails(after(tail, acc, x0, y1))
         x2 = over_x(after(q2, x1, y0, tail_chip))
         y3 = over_y(after(q3, x1, y0, tail_chip))
         acc_a = part_call(
@@ -719,7 +711,8 @@
             w_qkv,
             2 * quarter,
             cols,
-            before=stay(after(acc_a, tail_chip, acc_b)),
+            before=stay(after(acc, tail_chip)),
+            at=0,
         )
         earlier = (fy0, fx1, acc_a) if tail_below is None else (fy0, fx1, acc_a, tail_below)
         x3, y2 = over_x(after(q3, *earlier)), over_y(after(q2, *earlier))
@@ -744,7 +737,8 @@
             w_qkv,
             2 * quarter,
             cols,
-            before=stay(acc_b),
+            before=stay(acc),
+            at=1,
             apart=True,
         )
         far = (fy2, fx3)
@@ -792,11 +786,12 @@
         passed = jnp.where(core == 0, other, chip_entering).astype(BF16)
     entering = (here, swap(passed))
 
+    w_whole, w_out = w_out, near(w_out)
     if not square:
         halves = [
             head_call(
                 places,
-                (0,),
+                (0, 0, 0),
                 query[r * rows // 2 : (r + 1) * rows // 2],
                 within[r * rows // 2 : (r + 1) * rows // 2],
                 entering,
@@ -807,7 +802,7 @@
             )[0]
             for r in range(2)
         ]
-        partial = dot(jnp.concatenate(halves), w_out).astype(BF16)
+        partial = dot(jnp.concatenate(halves), w_whole).astype(BF16)
         return lax.psum_scatter(partial, "head", scatter_dimension=1, tiled=True)
 
     na, by_x, by_y = head_call(

time: 186 us -> 185 us (level)
  waiting for transfers between devices: 57.4 us -> 62.6 us
  Pallas kernels: 98.3 us -> 93.4 us
    pallas_call x16, Pallas kernels: 96.4 us -> 91.5 us  [call(): pl.pallas_call(kernel, out_shape=tuple(outs), grid_spec=pltpu.PrefetchSca...]
    ppermute x4, waiting for transfers between devices: 1.99 us -> 4.92 us  [the longest x2 4.91 us: local(): x1, y0 = (over_x(after(q1, tail)), over_y(after(q0, tail)))]
    ppermute x2, waiting for transfers between devices: 7.07 us -> 4.83 us  [local(): x3, y2 = (over_x(after(q3, *earlier)), over_y(after(q2, *earlier)))]
  transfers between devices with their start and end apart: 27 -> 27, of which waited for: 16 -> 15; matrix products, arithmetic and copies ran while one was open for 0% -> 0% of each run, Pallas kernels for 42% -> 40%
where the time goes in v9:
time: 185 us; the launch traced here: 183 us
  Pallas kernels  93.4 us (50%)
  waiting for transfers between devices  62.6 us (34%)
  starting transfers between devices  27.1 us (15%)
    pallas_call x16, Pallas kernels, call(): pl.pallas_call(kernel, out_shape=tuple(outs), grid_spec=pltpu.PrefetchSca...  91.5 us
    ppermute x2, waiting for transfers between devices, local(): by_x2, by_y2 = (over_x(by_x2), over_y(by_y2))  19.3 us
    ppermute x2, waiting for transfers between devices, local(): by_x, by_y = (over_x(by_x), over_y(by_y))  8.83 us
    ppermute x4, waiting for transfers between devices, hop(): return lax.ppermute(x, 'seq', perm=perm)  8.82 us
    ppermute x2, waiting for transfers between devices, local(): sum1, sum0 = (over_x(sum1), over_y(sum0))  8.07 us
    ppermute x4, starting transfers between devices, hop(): return lax.ppermute(x, 'seq', perm=perm)  7.11 us
    ppermute x2, waiting for transfers between devices, local(): sum3, sum2 = (over_x(sum3), over_y(sum2))  5.17 us
    ppermute x2, waiting for transfers between devices, local(): x1, y0 = (over_x(after(q1, tail)), over_y(after(q0, tail)))  4.91 us
  transfers between devices with their start and end apart: 27, of which 15 were waited for; matrix products, arithmetic and copies ran while one was open for 0% of the time, Pallas kernels for 40%

profile of v9, /device:TPU:8, one launch (start us, length us, event | category | flops | bytes accessed | tf_op | source)
XLA Modules:
  0.0 183.4 jit_solution(8679362556405200258)
XLA Ops:
  0.0 2.2 %cut.2 = (bf16[256,1024]{1,0:T(8,128)(2,1)}, bf16[256,1024]{1,0:T(8,128)(2,1)}) custom-call(s32[1]{0:T(128)} %constant.29.clone.1._, bf16[1024,1024]{1,0:T(8,128)(2,1)} %x_ref.4), custom_call_target="tpu_custom_call" | custom-call | flops 1 | bytes 3145728 | tf_op jit(solution)/shard_map/cut/pallas_call | solution.py:43
  3.7 1.5 collective-permute-start.1
  7.5 12.5 %own_part.1.refs_6_ = f32[3,1024,1024]{2,1,0:T(8,128)} custom-call(s32[6]{0:T(128)S(1)} %stack.27._.places, bf16[1024,1024]{1,0:T(8,128)(2,1)} %x_ref.4, bf16[3,4096,1024]{2,1,0:T(8,128)(2,1)} %refs_2_.5), custom_call_target="tpu_custom_call" | custom-call | flops 6442450944 | bytes 39845888 | tf_op jit(solution)/shard_map/own_part/pallas_call | solution.py:43
  21.4 1.6 collective-permute-start.6
  25.1 3.4 %collective-permute-done.2.refs_1_ = bf16[256,1024]{1,0:T(8,128)(2,1)S(1)} collective-permute-done((bf16[256,1024]{1,0:T(8,128)(2,1)}, bf16[256,1024]{1,0:T(8,128)(2,1)S(1)}, u32[]{:S(2)}, u32[]{:S(2)}) %collective-permute-start.2) | collective-permute-done | bytes 524320 | tf_op jit(solution)/shard_map/ppermute | solution.py:700
  28.5 1.5 collective-permute-done.3.refs_2_
  32.1 11.5 %part.2.refs_3_ = f32[3,512,1024]{2,1,0:T(8,128)S(1)} custom-call(s32[6]{0:T(128)S(1)} %stack.27._.places, bf16[256,1024]{1,0:T(8,128)(2,1)S(1)} %collective-permute-done.refs_0_, bf16[256,1024]{1,0:T(8,128)(2,1)S(1)} %collective-permute-done.2.refs_1_, bf16[256,1024]{1,0:T(8,128)(2,1)S(1)} %collective-permute-done.3.refs_2_, ...), custom_call_target="tpu_custom_call" | custom-call | flops 6442450944 | bytes 71303168 | tf_op jit(solution)/shard_map/part/pallas_call | solution.py:43
  43.6 1.6 collective-permute-start.12
  45.7 11.1 %first.1 = (bf16[512,1024]{1,0:T(8,128)(2,1)}, f32[512,1024]{1,0:T(8,128)}, f32[8,128,128]{2,1,0:T(8,128)S(1)}) custom-call(s32[6]{0:T(128)S(1)} %stack.27._.places, bf16[256,1024]{1,0:T(8,128)(2,1)S(1)} %collective-permute-done.6.refs_0_, bf16[256,1024]{1,0:T(8,128)(2,1)S(1)} %collective-permute-done.7.refs_1_, bf16[3,4096,1024]{2,1,0:T(8,128)(2,1)} %refs_2_.5, ...), custom_call_target="tpu_custom_call" | custom-call | flops 3221225472 | bytes 36241408 | tf_op jit(solution)/shard_map/first/pallas_call | solution.py:43
  56.8 1.6 collective-permute-start.8
  58.9 3.3 %collective-permute-done.12.refs_1_ = bf16[256,1024]{1,0:T(8,128)(2,1)S(1)} collective-permute-done((bf16[256,1024]{1,0:T(8,128)(2,1)S(1)}, bf16[256,1024]{1,0:T(8,128)(2,1)S(1)}, u32[]{:S(2)}, u32[]{:S(2)}) %collective-permute-start.12) | collective-permute-done | bytes 524320 | tf_op jit(solution)/shard_map/ppermute | solution.py:718
  62.2 1.5 collective-permute-done.13.refs_2_
  63.7 11.7 %part.3 = (f32[1,512,1024]{2,1,0:T(8,128)}, f32[2,512,1024]{2,1,0:T(8,128)S(1)}) custom-call(s32[6]{0:T(128)S(1)} %stack.27._.places, bf16[256,1024]{1,0:T(8,128)(2,1)S(1)} %collective-permute-done.5.refs_0_, bf16[256,1024]{1,0:T(8,128)(2,1)S(1)} %collective-permute-done.12.refs_1_, bf16[256,1024]{1,0:T(8,128)(2,1)S(1)} %collective-permute-done.13.refs_2_, ...), custom_call_target="tpu_custom_call" | custom-call | flops 6442450944 | bytes 71303168 | tf_op jit(solution)/shard_map/part/pallas_call | solution.py:43
  75.5 7.5 %states.1 = (bf16[512,1024]{1,0:T(8,128)(2,1)}, bf16[512,1024]{1,0:T(8,128)(2,1)}, f32[8,128,128]{2,1,0:T(8,128)S(1)}, bf16[4,128,128]{2,1,0:T(8,128)(2,1)S(1)}) custom-call(s32[6]{0:T(128)S(1)} %stack.27._.places, bf16[256,1024]{1,0:T(8,128)(2,1)S(1)} %collective-permute-done.8.refs_0_, bf16[256,1024]{1,0:T(8,128)(2,1)S(1)} %collective-permute-done.10.refs_1_, ...), custom_call_target="tpu_custom_call" | custom-call | flops 2147483648 | bytes 63082496 | tf_op jit(solution)/shard_map/states/pallas_call | solution.py:43
  86.3 6.1 %collective-permute-done.15.come_ref = bf16[4,128,128]{2,1,0:T(8,128)(2,1)S(1)} collective-permute-done((bf16[4,128,128]{2,1,0:T(8,128)(2,1)S(1)}, bf16[4,128,128]{2,1,0:T(8,128)(2,1)S(1)}, u32[]{:S(2)}, u32[]{:S(2)}) %collective-permute-start.15) | collective-permute-done | bytes 131104 | tf_op jit(solution)/shard_map/ppermute | solution.py:690
  93.0 2.6 %collective-permute-start.16 = (bf16[4,128,128]{2,1,0:T(8,128)(2,1)S(1)}, bf16[4,128,128]{2,1,0:T(8,128)(2,1)S(1)}, u32[]{:S(2)}, u32[]{:S(2)}) collective-permute-start(bf16[4,128,128]{2,1,0:T(8,128)(2,1)S(1)} %pass_on.1), channel_id=1, source_target_pairs={{8,16},{12,20},{9,17},{13,21},{10,18},{14,22},{11,19},{15,23}} | collective-permute-start | bytes 393224 | tf_op jit(solution)/shard_map/ppermute | solution.py:690
  95.6 2.6 %collective-permute-start.17 = (bf16[4,128,128]{2,1,0:T(8,128)(2,1)S(1)}, bf16[4,128,128]{2,1,0:T(8,128)(2,1)S(1)}, u32[]{:S(2)}, u32[]{:S(2)}) collective-permute-start(bf16[4,128,128]{2,1,0:T(8,128)(2,1)S(1)} %pass_on.1), channel_id=1, source_target_pairs={{8,24},{12,28},{9,25},{13,29},{10,26},{14,30},{11,27},{15,31}} | collective-permute-start | bytes 393224 | tf_op jit(solution)/shard_map/ppermute | solution.py:690
  98.5 2.3 %collective-permute-done.17.third_ref = bf16[4,128,128]{2,1,0:T(8,128)(2,1)S(1)} collective-permute-done((bf16[4,128,128]{2,1,0:T(8,128)(2,1)S(1)}, bf16[4,128,128]{2,1,0:T(8,128)(2,1)S(1)}, u32[]{:S(2)}, u32[]{:S(2)}) %collective-permute-start.17) | collective-permute-done | bytes 131104 | tf_op jit(solution)/shard_map/ppermute | solution.py:690
  103.0 7.9 %heads.2 = (bf16[512,1024]{1,0:T(8,128)(2,1)S(1)}, bf16[512,1024]{1,0:T(8,128)(2,1)S(1)}, bf16[512,1024]{1,0:T(8,128)(2,1)S(1)}) custom-call(s32[6]{0:T(128)S(1)} %stack.27._.places, bf16[512,1024]{1,0:T(8,128)(2,1)} %get-tuple-element.82.q_ref, f32[512,1024]{1,0:T(8,128)} %get-tuple-element.83.within_ref, ...), custom_call_target="tpu_custom_call" | custom-call | flops 1 | bytes 1 | tf_op jit(solution)/shard_map/heads/pallas_call | solution.py:43
  110.9 1.6 collective-permute-start.19
  113.0 8.3 %later.1 = (bf16[512,1024]{1,0:T(8,128)(2,1)S(1)}, f32[512,1024]{1,0:T(8,128)S(1)}) custom-call(s32[6]{0:T(128)S(1)} %stack.27._.places, bf16[256,1024]{1,0:T(8,128)(2,1)S(1)} %collective-permute-done.8.refs_0_, bf16[256,1024]{1,0:T(8,128)(2,1)S(1)} %collective-permute-done.10.refs_1_, bf16[3,4096,1024]{2,1,0:T(8,128)(2,1)} %refs_2_.5, ...), custom_call_target="tpu_custom_call" | custom-call | flops 1879048192 | bytes 34144256 | tf_op jit(solution)/shard_map/later/pallas_call | solution.py:43
  121.3 6.3 %heads.3 = (bf16[512,1024]{1,0:T(8,128)(2,1)S(1)}, bf16[512,1024]{1,0:T(8,128)(2,1)S(1)}, bf16[512,1024]{1,0:T(8,128)(2,1)S(1)}) custom-call(s32[6]{0:T(128)S(1)} %stack.27._.places, bf16[512,1024]{1,0:T(8,128)(2,1)S(1)} %get-tuple-element.94.q_ref, f32[512,1024]{1,0:T(8,128)S(1)} %get-tuple-element.95.within_ref, ...), custom_call_target="tpu_custom_call" | custom-call | flops 1 | bytes 1 | tf_op jit(solution)/shard_map/heads/pallas_call | solution.py:43
  127.6 1.5 collective-permute-start.23
  129.7 7.3 %collective-permute-done.19.x_ref.refs_2_ = bf16[512,1024]{1,0:T(8,128)(2,1)S(1)} collective-permute-done((bf16[512,1024]{1,0:T(8,128)(2,1)S(1)}, bf16[512,1024]{1,0:T(8,128)(2,1)S(1)}, u32[]{:S(2)}, u32[]{:S(2)}) %collective-permute-start.19) | collective-permute-done | bytes 1048608 | tf_op jit(solution)/shard_map/ppermute | solution.py:812
  137.0 1.6 collective-permute-done.20.y_ref.refs_0_
  138.5 2.0 %sum_pair.2 = (bf16[256,1024]{1,0:T(8,128)(2,1)S(1)}, bf16[256,1024]{1,0:T(8,128)(2,1)S(1)}) custom-call(s32[6]{0:T(128)S(1)} %stack.27._.places, bf16[512,1024]{1,0:T(8,128)(2,1)S(1)} %get-tuple-element.97.normed_ref, bf16[512,1024]{1,0:T(8,128)(2,1)S(1)} %collective-permute-done.19.x_ref.refs_2_, ...), custom_call_target="tpu_custom_call" | custom-call | flops 1 | bytes 1 | tf_op jit(solution)/shard_map/sum_pair/pallas_call | solution.py:43
  141.7 19.3 %collective-permute-done.23.refs_0_.y_ref = bf16[512,1024]{1,0:T(8,128)(2,1)S(1)} collective-permute-done((bf16[512,1024]{1,0:T(8,128)(2,1)S(1)}, bf16[512,1024]{1,0:T(8,128)(2,1)S(1)}, u32[]{:S(2)}, u32[]{:S(2)}) %collective-permute-start.23) | collective-permute-done | bytes 1048608 | tf_op jit(solution)/shard_map/ppermute | solution.py:819
  161.0 2.0 %sum_pair.3 = (bf16[256,1024]{1,0:T(8,128)(2,1)S(1)}, bf16[256,1024]{1,0:T(8,128)(2,1)S(1)}) custom-call(s32[6]{0:T(128)S(1)} %stack.27._.places, bf16[512,1024]{1,0:T(8,128)(2,1)S(1)} %get-tuple-element.102.normed_ref, bf16[512,1024]{1,0:T(8,128)(2,1)S(1)} %collective-permute-done.24.refs_1_.x_ref, ...), custom_call_target="tpu_custom_call" | custom-call | flops 1 | bytes 1 | tf_op jit(solution)/shard_map/sum_pair/pallas_call | solution.py:43
  164.2 8.1 %collective-permute-done.21.refs_3_ = bf16[256,1024]{1,0:T(8,128)(2,1)S(1)} collective-permute-done((bf16[256,1024]{1,0:T(8,128)(2,1)S(1)}, bf16[256,1024]{1,0:T(8,128)(2,1)S(1)}, u32[]{:S(2)}, u32[]{:S(2)}) %collective-permute-start.21) | collective-permute-done | bytes 524320 | tf_op jit(solution)/shard_map/ppermute | solution.py:822
  172.2 2.0 %own_block.2.kept_ref = bf16[512,1024]{1,0:T(8,128)(2,1)S(1)} custom-call(s32[6]{0:T(128)S(1)} %stack.27._.places, bf16[512,1024]{1,0:T(8,128)(2,1)S(1)} %get-tuple-element.102.normed_ref, bf16[1024,4096]{1,0:T(8,128)(2,1)S(1)} %bitcast.7, bf16[512,1024]{1,0:T(8,128)(2,1)S(1)} %collective-permute-done.23.refs_0_.y_ref, ...), custom_call_target="tpu_custom_call" | custom-call | flops 1 | bytes 1 | tf_op jit(solution)/shard_map/own_block/pallas_call | solution.py:43
  174.3 2.9 %own_block.3.above_ref = bf16[1024,1024]{1,0:T(8,128)(2,1)} custom-call(s32[6]{0:T(128)S(1)} %stack.27._.places, bf16[512,1024]{1,0:T(8,128)(2,1)S(1)} %get-tuple-element.97.normed_ref, bf16[1024,4096]{1,0:T(8,128)(2,1)S(1)} %bitcast.7, bf16[512,1024]{1,0:T(8,128)(2,1)S(1)} %collective-permute-done.20.y_ref.refs_0_, ...), custom_call_target="tpu_custom_call" | custom-call | flops 1 | bytes 1 | tf_op jit(solution)/shard_map/own_block/pallas_call | solution.py:43
  177.2 3.9 %collective-permute-done.25.a_ref = bf16[256,1024]{1,0:T(8,128)(2,1)S(1)} collective-permute-done((bf16[256,1024]{1,0:T(8,128)(2,1)S(1)}, bf16[256,1024]{1,0:T(8,128)(2,1)S(1)}, u32[]{:S(2)}, u32[]{:S(2)}) %collective-permute-start.25) | collective-permute-done | bytes 524320 | tf_op jit(solution)/shard_map/ppermute | solution.py:824
  (54 shorter events, 22.2 us)
Async XLA Ops:
  0.0 5.3 %copy-start.2 = (f32[8,1024]{1,0:T(8,128)S(1)}, f32[8,1024]{1,0:T(8,128)}, u32[]{:S(2)}) copy-start(f32[8,1024]{1,0:T(8,128)} %rate_ref.1) | copy-start | bytes 98308
  2.3 17.8 %collective-permute-start = (bf16[256,1024]{1,0:T(8,128)(2,1)}, bf16[256,1024]{1,0:T(8,128)(2,1)S(1)}, u32[]{:S(2)}, u32[]{:S(2)}) collective-permute-start(bf16[256,1024]{1,0:T(8,128)(2,1)} %get-tuple-element.63), channel_id=1, source_target_pairs={{0,1},{1,0},{2,3},{3,2},{4,5},{5,4},{6,7},{7,6},{8,9},{9,8},{10,11... | collective-permute-start | bytes 1572872 | tf_op jit(solution)/shard_map/ppermute | solution.py:699
  3.7 16.3 %collective-permute-start.1 = (bf16[256,1024]{1,0:T(8,128)(2,1)}, bf16[256,1024]{1,0:T(8,128)(2,1)S(1)}, u32[]{:S(2)}, u32[]{:S(2)}) collective-permute-start(bf16[256,1024]{1,0:T(8,128)(2,1)} %get-tuple-element.62), channel_id=1, source_target_pairs={{0,2},{1,3},{2,0},{3,1},{4,6},{5,7},{6,4},{7,5},{8,10},{9,11},{10,... | collective-permute-start | bytes 1572872 | tf_op jit(solution)/shard_map/ppermute | solution.py:699
  6.3 22.2 %collective-permute-start.2 = (bf16[256,1024]{1,0:T(8,128)(2,1)}, bf16[256,1024]{1,0:T(8,128)(2,1)S(1)}, u32[]{:S(2)}, u32[]{:S(2)}) collective-permute-start(bf16[256,1024]{1,0:T(8,128)(2,1)} %get-tuple-element.62), channel_id=1, source_target_pairs={{0,1},{1,0},{2,3},{3,2},{4,5},{5,4},{6,7},{7,6},{8,9},{9,8},{10,11... | collective-permute-start | bytes 1572872 | tf_op jit(solution)/shard_map/ppermute | solution.py:700
  6.9 23.2 %collective-permute-start.3 = (bf16[256,1024]{1,0:T(8,128)(2,1)}, bf16[256,1024]{1,0:T(8,128)(2,1)S(1)}, u32[]{:S(2)}, u32[]{:S(2)}) collective-permute-start(bf16[256,1024]{1,0:T(8,128)(2,1)} %get-tuple-element.63), channel_id=1, source_target_pairs={{0,2},{1,3},{2,0},{3,1},{4,6},{5,7},{6,4},{7,5},{8,10},{9,11},{10,... | collective-permute-start | bytes 1572872 | tf_op jit(solution)/shard_map/ppermute | solution.py:700
  20.0 4.5 %collective-permute-start.4 = (f32[8,128]{1,0:T(8,128)S(1)}, f32[8,128]{1,0:T(8,128)S(1)}, u32[]{:S(2)}, u32[]{:S(2)}) collective-permute-start(f32[8,128]{1,0:T(8,128)S(1)} %get-tuple-element.64.tail_ref), channel_id=1, source_target_pairs={{0,4},{4,0},{8,12},{12,8},{16,20},{20,16},{24,28},{28,24},{1,5},{5... | collective-permute-start | bytes 12296 | tf_op jit(solution)/shard_map/ppermute | solution.py:693
  21.4 22.2 %collective-permute-start.6 = (bf16[256,1024]{1,0:T(8,128)(2,1)S(1)}, bf16[256,1024]{1,0:T(8,128)(2,1)S(1)}, u32[]{:S(2)}, u32[]{:S(2)}) collective-permute-start(bf16[256,1024]{1,0:T(8,128)(2,1)S(1)} %collective-permute-done.refs_0_), channel_id=1, source_target_pairs={{0,2},{1,3},{2,0},{3,1},{4,6},{5,7},{6,4},{7,5},{8,10},{9,11},{10,... | collective-permute-start | bytes 1572872 | tf_op jit(solution)/shard_map/ppermute | solution.py:703
  23.0 20.6 %collective-permute-start.7 = (bf16[256,1024]{1,0:T(8,128)(2,1)S(1)}, bf16[256,1024]{1,0:T(8,128)(2,1)S(1)}, u32[]{:S(2)}, u32[]{:S(2)}) collective-permute-start(bf16[256,1024]{1,0:T(8,128)(2,1)S(1)} %collective-permute-done.1.refs_3_), channel_id=1, source_target_pairs={{0,1},{1,0},{2,3},{3,2},{4,5},{5,4},{6,7},{7,6},{8,9},{9,8},{10,11... | collective-permute-start | bytes 1572872 | tf_op jit(solution)/shard_map/ppermute | solution.py:703
  24.5 19.1 %collective-permute-start.11 = (f32[8,128]{1,0:T(8,128)S(1)}, f32[8,128]{1,0:T(8,128)S(1)}, u32[]{:S(2)}, u32[]{:S(2)}) collective-permute-start(f32[8,128]{1,0:T(8,128)S(1)} %add.10), channel_id=1, source_target_pairs={{16,24},{20,28},{17,25},{21,29},{18,26},{22,30},{19,27},{23,31}} | collective-permute-start | bytes 12296 | tf_op jit(solution)/shard_map/ppermute | solution.py:690
  30.0 26.8 %collective-permute-start.5 = (bf16[256,1024]{1,0:T(8,128)(2,1)S(1)}, bf16[256,1024]{1,0:T(8,128)(2,1)S(1)}, u32[]{:S(2)}, u32[]{:S(2)}) collective-permute-start(bf16[256,1024]{1,0:T(8,128)(2,1)S(1)} %get-tuple-element.75), channel_id=1, source_target_pairs={{0,1},{1,0},{2,3},{3,2},{4,5},{5,4},{6,7},{7,6},{8,9},{9,8},{10,11... | collective-permute-start | bytes 1572872 | tf_op jit(solution)/shard_map/ppermute | solution.py:705
  30.6 27.8 %collective-permute-start.9 = (bf16[256,1024]{1,0:T(8,128)(2,1)S(1)}, bf16[256,1024]{1,0:T(8,128)(2,1)S(1)}, u32[]{:S(2)}, u32[]{:S(2)}) collective-permute-start(bf16[256,1024]{1,0:T(8,128)(2,1)S(1)} %get-tuple-element.74), channel_id=1, source_target_pairs={{0,2},{1,3},{2,0},{3,1},{4,6},{5,7},{6,4},{7,5},{8,10},{9,11},{10,... | collective-permute-start | bytes 1572872 | tf_op jit(solution)/shard_map/ppermute | solution.py:706
  43.6 18.6 %collective-permute-start.12 = (bf16[256,1024]{1,0:T(8,128)(2,1)S(1)}, bf16[256,1024]{1,0:T(8,128)(2,1)S(1)}, u32[]{:S(2)}, u32[]{:S(2)}) collective-permute-start(bf16[256,1024]{1,0:T(8,128)(2,1)S(1)} %get-tuple-element.74), channel_id=1, source_target_pairs={{0,1},{1,0},{2,3},{3,2},{4,5},{5,4},{6,7},{7,6},{8,9},{9,8},{10,11... | collective-permute-start | bytes 1572872 | tf_op jit(solution)/shard_map/ppermute | solution.py:718
  45.1 18.6 %collective-permute-start.13 = (bf16[256,1024]{1,0:T(8,128)(2,1)S(1)}, bf16[256,1024]{1,0:T(8,128)(2,1)S(1)}, u32[]{:S(2)}, u32[]{:S(2)}) collective-permute-start(bf16[256,1024]{1,0:T(8,128)(2,1)S(1)} %get-tuple-element.75), channel_id=1, source_target_pairs={{0,2},{1,3},{2,0},{3,1},{4,6},{5,7},{6,4},{7,5},{8,10},{9,11},{10,... | collective-permute-start | bytes 1572872 | tf_op jit(solution)/shard_map/ppermute | solution.py:718
  56.8 18.7 %copy-start = (f32[8,128,128]{2,1,0:T(8,128)}, f32[8,128,128]{2,1,0:T(8,128)S(1)}, u32[]{:S(2)}) copy-start(f32[8,128,128]{2,1,0:T(8,128)S(1)} %get-tuple-element.93.refs_8_) | copy-start | bytes 1572868
  56.8 18.6 %collective-permute-start.8 = (bf16[256,1024]{1,0:T(8,128)(2,1)S(1)}, bf16[256,1024]{1,0:T(8,128)(2,1)S(1)}, u32[]{:S(2)}, u32[]{:S(2)}) collective-permute-start(bf16[256,1024]{1,0:T(8,128)(2,1)S(1)} %collective-permute-done.5.refs_0_), channel_id=1, source_target_pairs={{0,2},{1,3},{2,0},{3,1},{4,6},{5,7},{6,4},{7,5},{8,10},{9,11},{10,... | collective-permute-start | bytes 1572872 | tf_op jit(solution)/shard_map/ppermute | solution.py:732
  58.4 17.1 %collective-permute-start.10 = (bf16[256,1024]{1,0:T(8,128)(2,1)S(1)}, bf16[256,1024]{1,0:T(8,128)(2,1)S(1)}, u32[]{:S(2)}, u32[]{:S(2)}) collective-permute-start(bf16[256,1024]{1,0:T(8,128)(2,1)S(1)} %collective-permute-done.9.refs_3_), channel_id=1, source_target_pairs={{0,1},{1,0},{2,3},{3,2},{4,5},{5,4},{6,7},{7,6},{8,9},{9,8},{10,11... | collective-permute-start | bytes 1572872 | tf_op jit(solution)/shard_map/ppermute | solution.py:732
  75.4 27.5 %slice-start = ((s8[8388608]{0:T(1024)(128)(4,1)}), s8[4194304]{0:T(1024)(128)(4,1)S(1)}, s32[]{:S(2)}) async-start(s8[8388608]{0:T(1024)(128)(4,1)} %bitcast.6), calls=%async_computation | async-start | bytes 8388608
  75.5 8.9 %copy-start.1 = (f32[8,128,128]{2,1,0:T(8,128)S(1)}, f32[8,128,128]{2,1,0:T(8,128)}, u32[]{:S(2)}) copy-start(f32[8,128,128]{2,1,0:T(8,128)} %prior_ref.3) | copy-start | bytes 1572868
  75.5 27.5 %slice-start.1 = ((s8[8388608]{0:T(1024)(128)(4,1)}), s8[4194304]{0:T(1024)(128)(4,1)S(1)}, s32[]{:S(2)}) async-start(s8[8388608]{0:T(1024)(128)(4,1)} %bitcast.6), calls=%async_computation.1 | async-start | bytes 8388608
  83.0 1.3 collective-permute-start.14
  85.0 7.4 %collective-permute-start.15 = (bf16[4,128,128]{2,1,0:T(8,128)(2,1)S(1)}, bf16[4,128,128]{2,1,0:T(8,128)(2,1)S(1)}, u32[]{:S(2)}, u32[]{:S(2)}) collective-permute-start(bf16[4,128,128]{2,1,0:T(8,128)(2,1)S(1)} %get-tuple-element.86), channel_id=1, source_target_pairs={{0,8},{4,12},{16,24},{20,28},{1,9},{5,13},{17,25},{21,29},{2,10},{... | collective-permute-start | bytes 393224 | tf_op jit(solution)/shard_map/ppermute | solution.py:690
  93.0 5.5 %collective-permute-start.16 = (bf16[4,128,128]{2,1,0:T(8,128)(2,1)S(1)}, bf16[4,128,128]{2,1,0:T(8,128)(2,1)S(1)}, u32[]{:S(2)}, u32[]{:S(2)}) collective-permute-start(bf16[4,128,128]{2,1,0:T(8,128)(2,1)S(1)} %pass_on.1), channel_id=1, source_target_pairs={{8,16},{12,20},{9,17},{13,21},{10,18},{14,22},{11,19},{15,23}} | collective-permute-start | bytes 393224 | tf_op jit(solution)/shard_map/ppermute | solution.py:690
  95.6 5.3 %collective-permute-start.17 = (bf16[4,128,128]{2,1,0:T(8,128)(2,1)S(1)}, bf16[4,128,128]{2,1,0:T(8,128)(2,1)S(1)}, u32[]{:S(2)}, u32[]{:S(2)}) collective-permute-start(bf16[4,128,128]{2,1,0:T(8,128)(2,1)S(1)} %pass_on.1), channel_id=1, source_target_pairs={{8,24},{12,28},{9,25},{13,29},{10,26},{14,30},{11,27},{15,31}} | collective-permute-start | bytes 393224 | tf_op jit(solution)/shard_map/ppermute | solution.py:690
  101.5 1.4 collective-permute-start.18
  110.9 26.1 %collective-permute-start.19 = (bf16[512,1024]{1,0:T(8,128)(2,1)S(1)}, bf16[512,1024]{1,0:T(8,128)(2,1)S(1)}, u32[]{:S(2)}, u32[]{:S(2)}) collective-permute-start(bf16[512,1024]{1,0:T(8,128)(2,1)S(1)} %get-tuple-element.98), channel_id=1, source_target_pairs={{0,2},{1,3},{2,0},{3,1},{4,6},{5,7},{6,4},{7,5},{8,10},{9,11},{10,... | collective-permute-start | bytes 3145736 | tf_op jit(solution)/shard_map/ppermute | solution.py:812
  112.5 26.0 %collective-permute-start.20 = (bf16[512,1024]{1,0:T(8,128)(2,1)S(1)}, bf16[512,1024]{1,0:T(8,128)(2,1)S(1)}, u32[]{:S(2)}, u32[]{:S(2)}) collective-permute-start(bf16[512,1024]{1,0:T(8,128)(2,1)S(1)} %get-tuple-element.99), channel_id=1, source_target_pairs={{0,1},{1,0},{2,3},{3,2},{4,5},{5,4},{6,7},{7,6},{8,9},{9,8},{10,11... | collective-permute-start | bytes 3145736 | tf_op jit(solution)/shard_map/ppermute | solution.py:812
  127.6 33.4 %collective-permute-start.23 = (bf16[512,1024]{1,0:T(8,128)(2,1)S(1)}, bf16[512,1024]{1,0:T(8,128)(2,1)S(1)}, u32[]{:S(2)}, u32[]{:S(2)}) collective-permute-start(bf16[512,1024]{1,0:T(8,128)(2,1)S(1)} %get-tuple-element.103), channel_id=1, source_target_pairs={{0,1},{1,0},{2,3},{3,2},{4,5},{5,4},{6,7},{7,6},{8,9},{9,8},{10,11... | collective-permute-start | bytes 3145736 | tf_op jit(solution)/shard_map/ppermute | solution.py:819
  129.2 31.8 %collective-permute-start.24 = (bf16[512,1024]{1,0:T(8,128)(2,1)S(1)}, bf16[512,1024]{1,0:T(8,128)(2,1)S(1)}, u32[]{:S(2)}, u32[]{:S(2)}) collective-permute-start(bf16[512,1024]{1,0:T(8,128)(2,1)S(1)} %get-tuple-element.105), channel_id=1, source_target_pairs={{0,2},{1,3},{2,0},{3,1},{4,6},{5,7},{6,4},{7,5},{8,10},{9,11},{10,... | collective-permute-start | bytes 3145736 | tf_op jit(solution)/shard_map/ppermute | solution.py:819
  140.6 31.7 %collective-permute-start.21 = (bf16[256,1024]{1,0:T(8,128)(2,1)S(1)}, bf16[256,1024]{1,0:T(8,128)(2,1)S(1)}, u32[]{:S(2)}, u32[]{:S(2)}) collective-permute-start(bf16[256,1024]{1,0:T(8,128)(2,1)S(1)} %get-tuple-element.100), channel_id=1, source_target_pairs={{0,1},{1,0},{2,3},{3,2},{4,5},{5,4},{6,7},{7,6},{8,9},{9,8},{10,11... | collective-permute-start | bytes 1572872 | tf_op jit(solution)/shard_map/ppermute | solution.py:822
  141.2 31.1 %collective-permute-start.22 = (bf16[256,1024]{1,0:T(8,128)(2,1)S(1)}, bf16[256,1024]{1,0:T(8,128)(2,1)S(1)}, u32[]{:S(2)}, u32[]{:S(2)}) collective-permute-start(bf16[256,1024]{1,0:T(8,128)(2,1)S(1)} %get-tuple-element.101), channel_id=1, source_target_pairs={{0,2},{1,3},{2,0},{3,1},{4,6},{5,7},{6,4},{7,5},{8,10},{9,11},{10,... | collective-permute-start | bytes 1572872 | tf_op jit(solution)/shard_map/ppermute | solution.py:822
  163.0 18.1 %collective-permute-start.25 = (bf16[256,1024]{1,0:T(8,128)(2,1)S(1)}, bf16[256,1024]{1,0:T(8,128)(2,1)S(1)}, u32[]{:S(2)}, u32[]{:S(2)}) collective-permute-start(bf16[256,1024]{1,0:T(8,128)(2,1)S(1)} %get-tuple-element.107), channel_id=1, source_target_pairs={{0,2},{1,3},{2,0},{3,1},{4,6},{5,7},{6,4},{7,5},{8,10},{9,11},{10,... | collective-permute-start | bytes 1572872 | tf_op jit(solution)/shard_map/ppermute | solution.py:824
  163.6 18.7 %collective-permute-start.26 = (bf16[256,1024]{1,0:T(8,128)(2,1)S(1)}, bf16[256,1024]{1,0:T(8,128)(2,1)S(1)}, u32[]{:S(2)}, u32[]{:S(2)}) collective-permute-start(bf16[256,1024]{1,0:T(8,128)(2,1)S(1)} %get-tuple-element.108), channel_id=1, source_target_pairs={{0,1},{1,0},{2,3},{3,2},{4,5},{5,4},{6,7},{7,6},{8,9},{9,8},{10,11... | collective-permute-start | bytes 1572872 | tf_op jit(solution)/shard_map/ppermute | solution.py:824

commit v10 on v9

--- a/solution.py
+++ b/solution.py
@@ -148,6 +148,10 @@
     return dot(weights, v) + dot(q, state.astype(BF16)) * jnp.exp(-down)
 
 
+def faded(q, down):
+    return (q.astype(F32) * jnp.exp(-down)).astype(BF16)
+
+
 def advance(k, v, down, state):
     last = down[down.shape[0] - 1 :, :]
     scaled = (k.astype(F32) * jnp.exp(down - last)).astype(BF16)
@@ -179,18 +183,18 @@
         return total.astype(BF16)
 
     q_all, k_all, v_all = project(0), project(1), project(2)
-    q_ref[...] = q_all
     for a in range(group):
         head = j * group + a
         lanes = slice(a * size, (a + 1) * size)
-        state = jnp.zeros((size, size), F32)
+        state, base = jnp.zeros((size, size), F32), jnp.zeros((1, 1), F32)
         for c in range(rows // chunk):
             here = slice(c * chunk, (c + 1) * chunk)
             q, k, v = q_all[here, lanes], k_all[here, lanes], v_all[here, lanes]
             down = column(inside_ref[here, :], head)
             along = along_ref[pl.ds(head, 1), here]
-            within_ref[here, lanes] = scores(q, k, v, along, down, state)
-            state = advance(k, v, down, state)
+            q_ref[here, lanes] = faded(q, base + down)
+            within_ref[here, lanes] = scores(q, k, v, along, down, state).astype(BF16)
+            state, base = advance(k, v, down, state), base + down[chunk - 1 :, :]
         state_ref[a] = state
 
 
@@ -222,7 +226,7 @@
         + [fixed((heads, rows)), fixed((rows, heads))],
         (
             pltpu.HBM((rows, heads * size), BF16),
-            pltpu.HBM((rows, heads * size), F32),
+            pltpu.HBM((rows, heads * size), BF16),
             struct((heads, size, size), F32),
         ),
         [wide, wide, pl.BlockSpec((group, size, size), lambda j, o: (j, 0, 0))],
@@ -374,7 +378,8 @@
 
 
 def later_kernel(chunk, group, size, _, *refs):
-    xa, xb, wq, acc_q, k_ref, v_ref, along_ref, inside_ref, state_ref, q_ref, within_ref, held = refs
+    xa, xb, wq, acc_q, k_ref, v_ref, along_ref, inside_ref, down_ref, state_ref = refs[:10]
+    q_ref, within_ref, held = refs[10:]
     j = pl.program_id(0)
     rows = held.shape[0]
 
@@ -384,7 +389,6 @@
         held[rows // 2 :, :] = xb[...]
 
     q_all = (acc_q[0] + dot(held[...], wq[0])).astype(BF16)
-    q_ref[...] = q_all
     for a in range(group):
         head = j * group + a
         lanes = slice(a * size, (a + 1) * size)
@@ -393,12 +397,13 @@
             here = slice(c * chunk, (c + 1) * chunk)
             q, k, v = q_all[here, lanes], k_ref[here, lanes], v_ref[here, lanes]
             along, down = along_ref[pl.ds(head, 1), here], column(inside_ref[here, :], head)
-            within_ref[here, lanes] = scores(q, k, v, along, down, state)
+            q_ref[here, lanes] = faded(q, column(down_ref[here, :], head))
+            within_ref[here, lanes] = scores(q, k, v, along, down, state).astype(BF16)
             if c + 1 < rows // chunk:
                 state = advance(k, v, down, state)
 
 
-def later_call(places, far, w_qkv, acc, k, v, along, inside, state, chunk, group):
+def later_call(places, far, w_qkv, acc, k, v, along, inside, down, state, chunk, group):
     _, rows, width = acc.shape
     heads, size = state.shape[0], state.shape[1]
     depth = far[0].shape[1]
@@ -409,7 +414,7 @@
         "later",
         heads // group,
         places,
-        (*far, w_qkv, acc, k, v, along, inside, state),
+        (*far, w_qkv, acc, k, v, along, inside, down, state),
         [
             fixed(far[0].shape),
             fixed(far[1].shape),
@@ -419,9 +424,10 @@
             wide,
             pl.BlockSpec((heads, rows), lambda j, o: (0, 1)),
             pl.BlockSpec((rows, heads), lambda j, o: (1, 0)),
+            pl.BlockSpec((rows, heads), lambda j, o: (1, 0)),
             pl.BlockSpec((group, size, size), lambda j, o: (j, 0, 0)),
         ],
-        (struct((rows, width), BF16), struct((rows, width), F32)),
+        (struct((rows, width), BF16), struct((rows, width), BF16)),
         [wide, wide],
         2 * rows * depth * width + 4 * rows * (chunk + size) * width,
         scratch=[pltpu.VMEM((rows, depth), BF16)],
@@ -510,7 +516,7 @@
 WHOLE = pl.BlockSpec(memory_space=pltpu.VMEM)
 
 
-def head_kernel(blocks, places, q_ref, within_ref, here_ref, there_ref, down_ref, w_ref, *refs):
+def head_kernel(blocks, places, q_ref, within_ref, here_ref, there_ref, w_ref, *refs):
     normed_ref, out_refs, held = refs[0], refs[1:3], refs[3]
     share, size = here_ref.shape[0], here_ref.shape[1]
     tall, width = out_refs[0].shape
@@ -519,14 +525,16 @@
 
         @pl.when(step == p)
         def _(p=p, out_ref=out_ref):
-            fade = jnp.exp(-down_ref[...])
+            ones = jnp.ones((size, size), BF16)
             for a in range(2 * share):
                 lanes = slice(a * size, (a + 1) * size)
                 ours = places[4] == a // share
                 entering = jnp.where(ours, here_ref[a % share], there_ref[a % share])
-                seen = dot(q_ref[:, lanes], entering) * fade[:, a : a + 1]
-                combined = within_ref[:, lanes] + seen
-                power = jnp.mean(combined * combined, axis=1, keepdims=True)
+                combined = within_ref[:, lanes].astype(F32) + dot(q_ref[:, lanes], entering)
+                square = combined * combined
+                high = square.astype(BF16)
+                low = (square - high.astype(F32)).astype(BF16)
+                power = (dot(high, ones) + dot(low, ones)) * (1.0 / size)
                 held[p, :, lanes] = (combined * lax.rsqrt(power + 1e-06)).astype(BF16)
             normed_ref[...] = held[p]
             out_ref[...] = dot(held[p], columns(w_ref, places[blocks[0]], width)).astype(BF16)
@@ -536,23 +544,21 @@
             out_ref[...] = dot(held[p], columns(w_ref, places[blocks[1 + p]], width)).astype(BF16)
 
 
-def head_call(places, blocks, q, within, entering, down, w_out, width, at):
+def head_call(places, blocks, q, within, entering, w_out, width):
     rows, cols = q.shape
     tall = rows // 2
-    heads = down.shape[1]
     part = pl.BlockSpec((tall, cols), lambda i, o: (jnp.minimum(i, 1), 0))
     return call(
         functools.partial(head_kernel, blocks),
         "heads",
         4,
         places,
-        (q, within, *entering, down, w_out),
+        (q, within, *entering, w_out),
         [
             part,
             part,
             fixed(entering[0].shape),
             fixed(entering[1].shape),
-            pl.BlockSpec((tall, heads), lambda i, o: (2 * at + jnp.minimum(i, 1), 0)),
             WHOLE,
         ],
         (struct((rows, cols), BF16), *[struct((rows, width), BF16)] * 2),
@@ -795,10 +801,8 @@
                 query[r * rows // 2 : (r + 1) * rows // 2],
                 within[r * rows // 2 : (r + 1) * rows // 2],
                 entering,
-                down,
                 w_out,
                 width,
-                r,
             )[0]
             for r in range(2)
         ]
@@ -806,15 +810,15 @@
         return lax.psum_scatter(partial, "head", scatter_dimension=1, tiled=True)
 
     na, by_x, by_y = head_call(
-        places, (3, 1, 2), stay(query_a), stay(within_a), entering, down, w_out, width, 0
+        places, (3, 1, 2), stay(query_a), stay(within_a), entering, w_out, width
     )
     middle = stay(after(middle, na))
     by_x, by_y = over_x(by_x), over_y(by_y)
     query_b, within_b = later_call(
-        places, far, w_qkv, stay(acc_q), stay(k), stay(v), along, inside, middle, quarter, group
+        places, far, w_qkv, stay(acc_q), stay(k), stay(v), along, inside, down, middle, quarter, group
     )
     nb, by_x2, by_y2 = head_call(
-        places, (3, 1, 2), query_b, within_b, entering, down, w_out, width, 1
+        places, (3, 1, 2), query_b, within_b, entering, w_out, width
     )
     by_x2, by_y2 = over_x(by_x2), over_y(by_y2)
     sum1, sum0 = pair_call(places, after(na, nb), by_y, by_x, w_out, width)

time: 185 us -> 183 us (0.989)
  Pallas kernels: 93.4 us -> 91.4 us
    pallas_call x16, Pallas kernels: 91.5 us -> 89.5 us  [call(): pl.pallas_call(kernel, out_shape=tuple(outs), grid_spec=pltpu.PrefetchSca...]
  transfers between devices with their start and end apart: 27 -> 27, of which waited for: 15 -> 15; matrix products, arithmetic and copies ran while one was open for 0% -> 0% of each run, Pallas kernels for 40% -> 39%
where the time goes in v10:
time: 183 us; the launch traced here: 182 us
  Pallas kernels  91.4 us (50%)
  waiting for transfers between devices  62.5 us (34%)
  starting transfers between devices  27.2 us (15%)
    pallas_call x16, Pallas kernels, call(): pl.pallas_call(kernel, out_shape=tuple(outs), grid_spec=pltpu.PrefetchSca...  89.5 us
    ppermute x2, waiting for transfers between devices, local(): by_x2, by_y2 = (over_x(by_x2), over_y(by_y2))  19.3 us
    ppermute x2, waiting for transfers between devices, local(): by_x, by_y = (over_x(by_x), over_y(by_y))  9.71 us
    ppermute x4, waiting for transfers between devices, hop(): return lax.ppermute(x, 'seq', perm=perm)  8.64 us
    ppermute x2, waiting for transfers between devices, local(): sum1, sum0 = (over_x(sum1), over_y(sum0))  8.07 us
    ppermute x4, starting transfers between devices, hop(): return lax.ppermute(x, 'seq', perm=perm)  7.29 us
    ppermute x2, waiting for transfers between devices, local(): sum3, sum2 = (over_x(sum3), over_y(sum2))  5.14 us
    ppermute x2, waiting for transfers between devices, local(): x3, y2 = (over_x(after(q3, *earlier)), over_y(after(q2, *earlier)))  4.78 us
  transfers between devices with their start and end apart: 27, of which 15 were waited for; matrix products, arithmetic and copies ran while one was open for 0% of the time, Pallas kernels for 39%

profile of v10, /device:TPU:8, one launch (start us, length us, event | category | flops | bytes accessed | tf_op | source)
XLA Modules:
  0.0 182.2 jit_solution(8282826761564443760)
XLA Ops:
  0.0 2.2 %cut.2 = (bf16[256,1024]{1,0:T(8,128)(2,1)}, bf16[256,1024]{1,0:T(8,128)(2,1)}) custom-call(s32[1]{0:T(128)} %constant.29.clone.1._, bf16[1024,1024]{1,0:T(8,128)(2,1)} %x_ref.4), custom_call_target="tpu_custom_call" | custom-call | flops 1 | bytes 3145728 | tf_op jit(solution)/shard_map/cut/pallas_call | solution.py:43
  3.7 1.5 collective-permute-start.1
  8.2 12.5 %own_part.1.refs_6_ = f32[3,1024,1024]{2,1,0:T(8,128)} custom-call(s32[6]{0:T(128)S(1)} %stack.27._.places, bf16[1024,1024]{1,0:T(8,128)(2,1)} %x_ref.4, bf16[3,4096,1024]{2,1,0:T(8,128)(2,1)} %refs_2_.5), custom_call_target="tpu_custom_call" | custom-call | flops 6442450944 | bytes 39845888 | tf_op jit(solution)/shard_map/own_part/pallas_call | solution.py:43
  22.1 1.6 collective-permute-start.6
  25.9 2.2 %collective-permute-done.2.refs_1_ = bf16[256,1024]{1,0:T(8,128)(2,1)S(1)} collective-permute-done((bf16[256,1024]{1,0:T(8,128)(2,1)}, bf16[256,1024]{1,0:T(8,128)(2,1)S(1)}, u32[]{:S(2)}, u32[]{:S(2)}) %collective-permute-start.2) | collective-permute-done | bytes 524320 | tf_op jit(solution)/shard_map/ppermute | solution.py:706
  28.1 1.9 %collective-permute-done.3.refs_2_ = bf16[256,1024]{1,0:T(8,128)(2,1)S(1)} collective-permute-done((bf16[256,1024]{1,0:T(8,128)(2,1)}, bf16[256,1024]{1,0:T(8,128)(2,1)S(1)}, u32[]{:S(2)}, u32[]{:S(2)}) %collective-permute-start.3) | collective-permute-done | bytes 524320 | tf_op jit(solution)/shard_map/ppermute | solution.py:706
  32.1 11.5 %part.2.refs_3_ = f32[3,512,1024]{2,1,0:T(8,128)S(1)} custom-call(s32[6]{0:T(128)S(1)} %stack.27._.places, bf16[256,1024]{1,0:T(8,128)(2,1)S(1)} %collective-permute-done.refs_0_, bf16[256,1024]{1,0:T(8,128)(2,1)S(1)} %collective-permute-done.2.refs_1_, bf16[256,1024]{1,0:T(8,128)(2,1)S(1)} %collective-permute-done.3.refs_2_, ...), custom_call_target="tpu_custom_call" | custom-call | flops 6442450944 | bytes 71303168 | tf_op jit(solution)/shard_map/part/pallas_call | solution.py:43
  43.6 1.6 collective-permute-start.12
  45.6 11.2 %first.1 = (bf16[512,1024]{1,0:T(8,128)(2,1)}, bf16[512,1024]{1,0:T(8,128)(2,1)}, f32[8,128,128]{2,1,0:T(8,128)S(1)}) custom-call(s32[6]{0:T(128)S(1)} %stack.27._.places, bf16[256,1024]{1,0:T(8,128)(2,1)S(1)} %collective-permute-done.6.refs_0_, bf16[256,1024]{1,0:T(8,128)(2,1)S(1)} %collective-permute-done.7.refs_1_, bf16[3,4096,1024]{2,1,0:T(8,128)(2,1)} %refs_2_.5, ...), custom_call_target="tpu_custom_call" | custom-call | flops 3221225472 | bytes 35192832 | tf_op jit(solution)/shard_map/first/pallas_call | solution.py:43
  56.8 1.6 collective-permute-start.8
  59.0 2.9 %collective-permute-done.12.refs_1_ = bf16[256,1024]{1,0:T(8,128)(2,1)S(1)} collective-permute-done((bf16[256,1024]{1,0:T(8,128)(2,1)S(1)}, bf16[256,1024]{1,0:T(8,128)(2,1)S(1)}, u32[]{:S(2)}, u32[]{:S(2)}) %collective-permute-start.12) | collective-permute-done | bytes 524320 | tf_op jit(solution)/shard_map/ppermute | solution.py:724
  61.8 1.9 %collective-permute-done.13.refs_2_ = bf16[256,1024]{1,0:T(8,128)(2,1)S(1)} collective-permute-done((bf16[256,1024]{1,0:T(8,128)(2,1)S(1)}, bf16[256,1024]{1,0:T(8,128)(2,1)S(1)}, u32[]{:S(2)}, u32[]{:S(2)}) %collective-permute-start.13) | collective-permute-done | bytes 524320 | tf_op jit(solution)/shard_map/ppermute | solution.py:724
  63.7 11.7 %part.3 = (f32[1,512,1024]{2,1,0:T(8,128)}, f32[2,512,1024]{2,1,0:T(8,128)S(1)}) custom-call(s32[6]{0:T(128)S(1)} %stack.27._.places, bf16[256,1024]{1,0:T(8,128)(2,1)S(1)} %collective-permute-done.5.refs_0_, bf16[256,1024]{1,0:T(8,128)(2,1)S(1)} %collective-permute-done.12.refs_1_, bf16[256,1024]{1,0:T(8,128)(2,1)S(1)} %collective-permute-done.13.refs_2_, ...), custom_call_target="tpu_custom_call" | custom-call | flops 6442450944 | bytes 71303168 | tf_op jit(solution)/shard_map/part/pallas_call | solution.py:43
  75.5 7.5 %states.1 = (bf16[512,1024]{1,0:T(8,128)(2,1)}, bf16[512,1024]{1,0:T(8,128)(2,1)}, f32[8,128,128]{2,1,0:T(8,128)S(1)}, bf16[4,128,128]{2,1,0:T(8,128)(2,1)S(1)}) custom-call(s32[6]{0:T(128)S(1)} %stack.27._.places, bf16[256,1024]{1,0:T(8,128)(2,1)S(1)} %collective-permute-done.8.refs_0_, bf16[256,1024]{1,0:T(8,128)(2,1)S(1)} %collective-permute-done.10.refs_1_, ...), custom_call_target="tpu_custom_call" | custom-call | flops 2147483648 | bytes 63082496 | tf_op jit(solution)/shard_map/states/pallas_call | solution.py:43
  86.3 6.1 %collective-permute-done.15.come_ref = bf16[4,128,128]{2,1,0:T(8,128)(2,1)S(1)} collective-permute-done((bf16[4,128,128]{2,1,0:T(8,128)(2,1)S(1)}, bf16[4,128,128]{2,1,0:T(8,128)(2,1)S(1)}, u32[]{:S(2)}, u32[]{:S(2)}) %collective-permute-start.15) | collective-permute-done | bytes 131104 | tf_op jit(solution)/shard_map/ppermute | solution.py:696
  93.0 2.6 %collective-permute-start.16 = (bf16[4,128,128]{2,1,0:T(8,128)(2,1)S(1)}, bf16[4,128,128]{2,1,0:T(8,128)(2,1)S(1)}, u32[]{:S(2)}, u32[]{:S(2)}) collective-permute-start(bf16[4,128,128]{2,1,0:T(8,128)(2,1)S(1)} %pass_on.1), channel_id=1, source_target_pairs={{8,16},{12,20},{9,17},{13,21},{10,18},{14,22},{11,19},{15,23}} | collective-permute-start | bytes 393224 | tf_op jit(solution)/shard_map/ppermute | solution.py:696
  95.6 2.8 %collective-permute-start.17 = (bf16[4,128,128]{2,1,0:T(8,128)(2,1)S(1)}, bf16[4,128,128]{2,1,0:T(8,128)(2,1)S(1)}, u32[]{:S(2)}, u32[]{:S(2)}) collective-permute-start(bf16[4,128,128]{2,1,0:T(8,128)(2,1)S(1)} %pass_on.1), channel_id=1, source_target_pairs={{8,24},{12,28},{9,25},{13,29},{10,26},{14,30},{11,27},{15,31}} | collective-permute-start | bytes 393224 | tf_op jit(solution)/shard_map/ppermute | solution.py:696
  98.5 2.3 %collective-permute-done.17.third_ref = bf16[4,128,128]{2,1,0:T(8,128)(2,1)S(1)} collective-permute-done((bf16[4,128,128]{2,1,0:T(8,128)(2,1)S(1)}, bf16[4,128,128]{2,1,0:T(8,128)(2,1)S(1)}, u32[]{:S(2)}, u32[]{:S(2)}) %collective-permute-start.17) | collective-permute-done | bytes 131104 | tf_op jit(solution)/shard_map/ppermute | solution.py:696
  102.9 6.7 %heads.2 = (bf16[512,1024]{1,0:T(8,128)(2,1)S(1)}, bf16[512,1024]{1,0:T(8,128)(2,1)S(1)}, bf16[512,1024]{1,0:T(8,128)(2,1)S(1)}) custom-call(s32[6]{0:T(128)S(1)} %stack.27._.places, bf16[512,1024]{1,0:T(8,128)(2,1)} %get-tuple-element.83.q_ref, bf16[512,1024]{1,0:T(8,128)(2,1)} %get-tuple-element.84.within_ref, ...), custom_call_target="tpu_custom_call" | custom-call | flops 1 | bytes 1 | tf_op jit(solution)/shard_map/heads/pallas_call | solution.py:43
  109.7 1.6 collective-permute-start.19
  111.8 8.2 %later.1 = (bf16[512,1024]{1,0:T(8,128)(2,1)S(1)}, bf16[512,1024]{1,0:T(8,128)(2,1)S(1)}) custom-call(s32[6]{0:T(128)S(1)} %stack.27._.places, bf16[256,1024]{1,0:T(8,128)(2,1)S(1)} %collective-permute-done.8.refs_0_, bf16[256,1024]{1,0:T(8,128)(2,1)S(1)} %collective-permute-done.10.refs_1_, bf16[3,4096,1024]{2,1,0:T(8,128)(2,1)} %refs_2_.5, ...), custom_call_target="tpu_custom_call" | custom-call | flops 1879048192 | bytes 33128448 | tf_op jit(solution)/shard_map/later/pallas_call | solution.py:43
  120.0 5.5 %heads.3 = (bf16[512,1024]{1,0:T(8,128)(2,1)S(1)}, bf16[512,1024]{1,0:T(8,128)(2,1)S(1)}, bf16[512,1024]{1,0:T(8,128)(2,1)S(1)}) custom-call(s32[6]{0:T(128)S(1)} %stack.27._.places, bf16[512,1024]{1,0:T(8,128)(2,1)S(1)} %get-tuple-element.94.q_ref, bf16[512,1024]{1,0:T(8,128)(2,1)S(1)} %get-tuple-element.95.within_ref, ...), custom_call_target="tpu_custom_call" | custom-call | flops 1 | bytes 1 | tf_op jit(solution)/shard_map/heads/pallas_call | solution.py:43
  125.5 1.6 collective-permute-start.23
  127.6 8.1 %collective-permute-done.19.x_ref.refs_2_ = bf16[512,1024]{1,0:T(8,128)(2,1)S(1)} collective-permute-done((bf16[512,1024]{1,0:T(8,128)(2,1)S(1)}, bf16[512,1024]{1,0:T(8,128)(2,1)S(1)}, u32[]{:S(2)}, u32[]{:S(2)}) %collective-permute-start.19) | collective-permute-done | bytes 1048608 | tf_op jit(solution)/shard_map/ppermute | solution.py:816
  135.7 1.6 collective-permute-done.20.y_ref.refs_0_
  137.3 2.0 %sum_pair.2 = (bf16[256,1024]{1,0:T(8,128)(2,1)S(1)}, bf16[256,1024]{1,0:T(8,128)(2,1)S(1)}) custom-call(s32[6]{0:T(128)S(1)} %stack.27._.places, bf16[512,1024]{1,0:T(8,128)(2,1)S(1)} %get-tuple-element.97.normed_ref, bf16[512,1024]{1,0:T(8,128)(2,1)S(1)} %collective-permute-done.19.x_ref.refs_2_, ...), custom_call_target="tpu_custom_call" | custom-call | flops 1 | bytes 1 | tf_op jit(solution)/shard_map/sum_pair/pallas_call | solution.py:43
  140.4 19.3 %collective-permute-done.23.refs_0_.y_ref = bf16[512,1024]{1,0:T(8,128)(2,1)S(1)} collective-permute-done((bf16[512,1024]{1,0:T(8,128)(2,1)S(1)}, bf16[512,1024]{1,0:T(8,128)(2,1)S(1)}, u32[]{:S(2)}, u32[]{:S(2)}) %collective-permute-start.23) | collective-permute-done | bytes 1048608 | tf_op jit(solution)/shard_map/ppermute | solution.py:823
  159.8 2.1 %sum_pair.3 = (bf16[256,1024]{1,0:T(8,128)(2,1)S(1)}, bf16[256,1024]{1,0:T(8,128)(2,1)S(1)}) custom-call(s32[6]{0:T(128)S(1)} %stack.27._.places, bf16[512,1024]{1,0:T(8,128)(2,1)S(1)} %get-tuple-element.102.normed_ref, bf16[512,1024]{1,0:T(8,128)(2,1)S(1)} %collective-permute-done.24.refs_1_.x_ref, ...), custom_call_target="tpu_custom_call" | custom-call | flops 1 | bytes 1 | tf_op jit(solution)/shard_map/sum_pair/pallas_call | solution.py:43
  162.9 8.1 %collective-permute-done.21.refs_3_ = bf16[256,1024]{1,0:T(8,128)(2,1)S(1)} collective-permute-done((bf16[256,1024]{1,0:T(8,128)(2,1)S(1)}, bf16[256,1024]{1,0:T(8,128)(2,1)S(1)}, u32[]{:S(2)}, u32[]{:S(2)}) %collective-permute-start.21) | collective-permute-done | bytes 524320 | tf_op jit(solution)/shard_map/ppermute | solution.py:826
  171.0 2.1 %own_block.2.kept_ref = bf16[512,1024]{1,0:T(8,128)(2,1)S(1)} custom-call(s32[6]{0:T(128)S(1)} %stack.27._.places, bf16[512,1024]{1,0:T(8,128)(2,1)S(1)} %get-tuple-element.102.normed_ref, bf16[1024,4096]{1,0:T(8,128)(2,1)S(1)} %bitcast.7, bf16[512,1024]{1,0:T(8,128)(2,1)S(1)} %collective-permute-done.23.refs_0_.y_ref, ...), custom_call_target="tpu_custom_call" | custom-call | flops 1 | bytes 1 | tf_op jit(solution)/shard_map/own_block/pallas_call | solution.py:43
  173.1 2.9 %own_block.3.above_ref = bf16[1024,1024]{1,0:T(8,128)(2,1)} custom-call(s32[6]{0:T(128)S(1)} %stack.27._.places, bf16[512,1024]{1,0:T(8,128)(2,1)S(1)} %get-tuple-element.97.normed_ref, bf16[1024,4096]{1,0:T(8,128)(2,1)S(1)} %bitcast.7, bf16[512,1024]{1,0:T(8,128)(2,1)S(1)} %collective-permute-done.20.y_ref.refs_0_, ...), custom_call_target="tpu_custom_call" | custom-call | flops 1 | bytes 1 | tf_op jit(solution)/shard_map/own_block/pallas_call | solution.py:43
  176.0 3.9 %collective-permute-done.25.a_ref = bf16[256,1024]{1,0:T(8,128)(2,1)S(1)} collective-permute-done((bf16[256,1024]{1,0:T(8,128)(2,1)S(1)}, bf16[256,1024]{1,0:T(8,128)(2,1)S(1)}, u32[]{:S(2)}, u32[]{:S(2)}) %collective-permute-start.25) | collective-permute-done | bytes 524320 | tf_op jit(solution)/shard_map/ppermute | solution.py:828
  (54 shorter events, 22.7 us)
Async XLA Ops:
  2.2 18.5 %collective-permute-start = (bf16[256,1024]{1,0:T(8,128)(2,1)}, bf16[256,1024]{1,0:T(8,128)(2,1)S(1)}, u32[]{:S(2)}, u32[]{:S(2)}) collective-permute-start(bf16[256,1024]{1,0:T(8,128)(2,1)} %get-tuple-element.63), channel_id=1, source_target_pairs={{0,1},{1,0},{2,3},{3,2},{4,5},{5,4},{6,7},{7,6},{8,9},{9,8},{10,11... | collective-permute-start | bytes 1572872 | tf_op jit(solution)/shard_map/ppermute | solution.py:705
  3.7 17.0 %collective-permute-start.1 = (bf16[256,1024]{1,0:T(8,128)(2,1)}, bf16[256,1024]{1,0:T(8,128)(2,1)S(1)}, u32[]{:S(2)}, u32[]{:S(2)}) collective-permute-start(bf16[256,1024]{1,0:T(8,128)(2,1)} %get-tuple-element.62), channel_id=1, source_target_pairs={{0,2},{1,3},{2,0},{3,1},{4,6},{5,7},{6,4},{7,5},{8,10},{9,11},{10,... | collective-permute-start | bytes 1572872 | tf_op jit(solution)/shard_map/ppermute | solution.py:705
  5.3 0.8 copy-start.2
  7.0 21.1 %collective-permute-start.2 = (bf16[256,1024]{1,0:T(8,128)(2,1)}, bf16[256,1024]{1,0:T(8,128)(2,1)S(1)}, u32[]{:S(2)}, u32[]{:S(2)}) collective-permute-start(bf16[256,1024]{1,0:T(8,128)(2,1)} %get-tuple-element.62), channel_id=1, source_target_pairs={{0,1},{1,0},{2,3},{3,2},{4,5},{5,4},{6,7},{7,6},{8,9},{9,8},{10,11... | collective-permute-start | bytes 1572872 | tf_op jit(solution)/shard_map/ppermute | solution.py:706
  7.6 22.4 %collective-permute-start.3 = (bf16[256,1024]{1,0:T(8,128)(2,1)}, bf16[256,1024]{1,0:T(8,128)(2,1)S(1)}, u32[]{:S(2)}, u32[]{:S(2)}) collective-permute-start(bf16[256,1024]{1,0:T(8,128)(2,1)} %get-tuple-element.63), channel_id=1, source_target_pairs={{0,2},{1,3},{2,0},{3,1},{4,6},{5,7},{6,4},{7,5},{8,10},{9,11},{10,... | collective-permute-start | bytes 1572872 | tf_op jit(solution)/shard_map/ppermute | solution.py:706
  20.7 4.5 %collective-permute-start.4 = (f32[8,128]{1,0:T(8,128)S(1)}, f32[8,128]{1,0:T(8,128)S(1)}, u32[]{:S(2)}, u32[]{:S(2)}) collective-permute-start(f32[8,128]{1,0:T(8,128)S(1)} %get-tuple-element.64.tail_ref), channel_id=1, source_target_pairs={{0,4},{4,0},{8,12},{12,8},{16,20},{20,16},{24,28},{28,24},{1,5},{5... | collective-permute-start | bytes 12296 | tf_op jit(solution)/shard_map/ppermute | solution.py:699
  22.1 21.4 %collective-permute-start.6 = (bf16[256,1024]{1,0:T(8,128)(2,1)S(1)}, bf16[256,1024]{1,0:T(8,128)(2,1)S(1)}, u32[]{:S(2)}, u32[]{:S(2)}) collective-permute-start(bf16[256,1024]{1,0:T(8,128)(2,1)S(1)} %collective-permute-done.refs_0_), channel_id=1, source_target_pairs={{0,2},{1,3},{2,0},{3,1},{4,6},{5,7},{6,4},{7,5},{8,10},{9,11},{10,... | collective-permute-start | bytes 1572872 | tf_op jit(solution)/shard_map/ppermute | solution.py:709
  23.7 19.9 %collective-permute-start.7 = (bf16[256,1024]{1,0:T(8,128)(2,1)S(1)}, bf16[256,1024]{1,0:T(8,128)(2,1)S(1)}, u32[]{:S(2)}, u32[]{:S(2)}) collective-permute-start(bf16[256,1024]{1,0:T(8,128)(2,1)S(1)} %collective-permute-done.1.refs_3_), channel_id=1, source_target_pairs={{0,1},{1,0},{2,3},{3,2},{4,5},{5,4},{6,7},{7,6},{8,9},{9,8},{10,11... | collective-permute-start | bytes 1572872 | tf_op jit(solution)/shard_map/ppermute | solution.py:709
  25.2 18.3 %collective-permute-start.11 = (f32[8,128]{1,0:T(8,128)S(1)}, f32[8,128]{1,0:T(8,128)S(1)}, u32[]{:S(2)}, u32[]{:S(2)}) collective-permute-start(f32[8,128]{1,0:T(8,128)S(1)} %add.10), channel_id=1, source_target_pairs={{16,24},{20,28},{17,25},{21,29},{18,26},{22,30},{19,27},{23,31}} | collective-permute-start | bytes 12296 | tf_op jit(solution)/shard_map/ppermute | solution.py:696
  30.0 26.8 %collective-permute-start.5 = (bf16[256,1024]{1,0:T(8,128)(2,1)S(1)}, bf16[256,1024]{1,0:T(8,128)(2,1)S(1)}, u32[]{:S(2)}, u32[]{:S(2)}) collective-permute-start(bf16[256,1024]{1,0:T(8,128)(2,1)S(1)} %get-tuple-element.75), channel_id=1, source_target_pairs={{0,1},{1,0},{2,3},{3,2},{4,5},{5,4},{6,7},{7,6},{8,9},{9,8},{10,11... | collective-permute-start | bytes 1572872 | tf_op jit(solution)/shard_map/ppermute | solution.py:711
  30.6 27.8 %collective-permute-start.9 = (bf16[256,1024]{1,0:T(8,128)(2,1)S(1)}, bf16[256,1024]{1,0:T(8,128)(2,1)S(1)}, u32[]{:S(2)}, u32[]{:S(2)}) collective-permute-start(bf16[256,1024]{1,0:T(8,128)(2,1)S(1)} %get-tuple-element.74), channel_id=1, source_target_pairs={{0,2},{1,3},{2,0},{3,1},{4,6},{5,7},{6,4},{7,5},{8,10},{9,11},{10,... | collective-permute-start | bytes 1572872 | tf_op jit(solution)/shard_map/ppermute | solution.py:712
  43.6 18.2 %collective-permute-start.12 = (bf16[256,1024]{1,0:T(8,128)(2,1)S(1)}, bf16[256,1024]{1,0:T(8,128)(2,1)S(1)}, u32[]{:S(2)}, u32[]{:S(2)}) collective-permute-start(bf16[256,1024]{1,0:T(8,128)(2,1)S(1)} %get-tuple-element.74), channel_id=1, source_target_pairs={{0,1},{1,0},{2,3},{3,2},{4,5},{5,4},{6,7},{7,6},{8,9},{9,8},{10,11... | collective-permute-start | bytes 1572872 | tf_op jit(solution)/shard_map/ppermute | solution.py:724
  45.1 18.6 %collective-permute-start.13 = (bf16[256,1024]{1,0:T(8,128)(2,1)S(1)}, bf16[256,1024]{1,0:T(8,128)(2,1)S(1)}, u32[]{:S(2)}, u32[]{:S(2)}) collective-permute-start(bf16[256,1024]{1,0:T(8,128)(2,1)S(1)} %get-tuple-element.75), channel_id=1, source_target_pairs={{0,2},{1,3},{2,0},{3,1},{4,6},{5,7},{6,4},{7,5},{8,10},{9,11},{10,... | collective-permute-start | bytes 1572872 | tf_op jit(solution)/shard_map/ppermute | solution.py:724
  56.8 18.6 %copy-start = (f32[8,128,128]{2,1,0:T(8,128)}, f32[8,128,128]{2,1,0:T(8,128)S(1)}, u32[]{:S(2)}) copy-start(f32[8,128,128]{2,1,0:T(8,128)S(1)} %get-tuple-element.93.refs_8_.refs_9_) | copy-start | bytes 1572868
  56.8 18.6 %collective-permute-start.8 = (bf16[256,1024]{1,0:T(8,128)(2,1)S(1)}, bf16[256,1024]{1,0:T(8,128)(2,1)S(1)}, u32[]{:S(2)}, u32[]{:S(2)}) collective-permute-start(bf16[256,1024]{1,0:T(8,128)(2,1)S(1)} %collective-permute-done.5.refs_0_), channel_id=1, source_target_pairs={{0,2},{1,3},{2,0},{3,1},{4,6},{5,7},{6,4},{7,5},{8,10},{9,11},{10,... | collective-permute-start | bytes 1572872 | tf_op jit(solution)/shard_map/ppermute | solution.py:738
  58.4 17.0 %collective-permute-start.10 = (bf16[256,1024]{1,0:T(8,128)(2,1)S(1)}, bf16[256,1024]{1,0:T(8,128)(2,1)S(1)}, u32[]{:S(2)}, u32[]{:S(2)}) collective-permute-start(bf16[256,1024]{1,0:T(8,128)(2,1)S(1)} %collective-permute-done.9.refs_3_), channel_id=1, source_target_pairs={{0,1},{1,0},{2,3},{3,2},{4,5},{5,4},{6,7},{7,6},{8,9},{9,8},{10,11... | collective-permute-start | bytes 1572872 | tf_op jit(solution)/shard_map/ppermute | solution.py:738
  75.4 27.5 %slice-start = ((s8[8388608]{0:T(1024)(128)(4,1)}), s8[4194304]{0:T(1024)(128)(4,1)S(1)}, s32[]{:S(2)}) async-start(s8[8388608]{0:T(1024)(128)(4,1)} %bitcast.6), calls=%async_computation | async-start | bytes 8388608
  75.5 8.9 %copy-start.1 = (f32[8,128,128]{2,1,0:T(8,128)S(1)}, f32[8,128,128]{2,1,0:T(8,128)}, u32[]{:S(2)}) copy-start(f32[8,128,128]{2,1,0:T(8,128)} %prior_ref.3) | copy-start | bytes 1572868
  75.5 27.5 %slice-start.1 = ((s8[8388608]{0:T(1024)(128)(4,1)}), s8[4194304]{0:T(1024)(128)(4,1)S(1)}, s32[]{:S(2)}) async-start(s8[8388608]{0:T(1024)(128)(4,1)} %bitcast.6), calls=%async_computation.1 | async-start | bytes 8388608
  83.0 1.3 collective-permute-start.14
  85.0 7.4 %collective-permute-start.15 = (bf16[4,128,128]{2,1,0:T(8,128)(2,1)S(1)}, bf16[4,128,128]{2,1,0:T(8,128)(2,1)S(1)}, u32[]{:S(2)}, u32[]{:S(2)}) collective-permute-start(bf16[4,128,128]{2,1,0:T(8,128)(2,1)S(1)} %get-tuple-element.87), channel_id=1, source_target_pairs={{0,8},{4,12},{16,24},{20,28},{1,9},{5,13},{17,25},{21,29},{2,10},{... | collective-permute-start | bytes 393224 | tf_op jit(solution)/shard_map/ppermute | solution.py:696
  93.0 5.5 %collective-permute-start.16 = (bf16[4,128,128]{2,1,0:T(8,128)(2,1)S(1)}, bf16[4,128,128]{2,1,0:T(8,128)(2,1)S(1)}, u32[]{:S(2)}, u32[]{:S(2)}) collective-permute-start(bf16[4,128,128]{2,1,0:T(8,128)(2,1)S(1)} %pass_on.1), channel_id=1, source_target_pairs={{8,16},{12,20},{9,17},{13,21},{10,18},{14,22},{11,19},{15,23}} | collective-permute-start | bytes 393224 | tf_op jit(solution)/shard_map/ppermute | solution.py:696
  95.6 5.3 %collective-permute-start.17 = (bf16[4,128,128]{2,1,0:T(8,128)(2,1)S(1)}, bf16[4,128,128]{2,1,0:T(8,128)(2,1)S(1)}, u32[]{:S(2)}, u32[]{:S(2)}) collective-permute-start(bf16[4,128,128]{2,1,0:T(8,128)(2,1)S(1)} %pass_on.1), channel_id=1, source_target_pairs={{8,24},{12,28},{9,25},{13,29},{10,26},{14,30},{11,27},{15,31}} | collective-permute-start | bytes 393224 | tf_op jit(solution)/shard_map/ppermute | solution.py:696
  101.5 1.4 collective-permute-start.18
  109.7 26.1 %collective-permute-start.19 = (bf16[512,1024]{1,0:T(8,128)(2,1)S(1)}, bf16[512,1024]{1,0:T(8,128)(2,1)S(1)}, u32[]{:S(2)}, u32[]{:S(2)}) collective-permute-start(bf16[512,1024]{1,0:T(8,128)(2,1)S(1)} %get-tuple-element.98), channel_id=1, source_target_pairs={{0,2},{1,3},{2,0},{3,1},{4,6},{5,7},{6,4},{7,5},{8,10},{9,11},{10,... | collective-permute-start | bytes 3145736 | tf_op jit(solution)/shard_map/ppermute | solution.py:816
  111.2 26.0 %collective-permute-start.20 = (bf16[512,1024]{1,0:T(8,128)(2,1)S(1)}, bf16[512,1024]{1,0:T(8,128)(2,1)S(1)}, u32[]{:S(2)}, u32[]{:S(2)}) collective-permute-start(bf16[512,1024]{1,0:T(8,128)(2,1)S(1)} %get-tuple-element.99), channel_id=1, source_target_pairs={{0,1},{1,0},{2,3},{3,2},{4,5},{5,4},{6,7},{7,6},{8,9},{9,8},{10,11... | collective-permute-start | bytes 3145736 | tf_op jit(solution)/shard_map/ppermute | solution.py:816
  125.5 34.2 %collective-permute-start.23 = (bf16[512,1024]{1,0:T(8,128)(2,1)S(1)}, bf16[512,1024]{1,0:T(8,128)(2,1)S(1)}, u32[]{:S(2)}, u32[]{:S(2)}) collective-permute-start(bf16[512,1024]{1,0:T(8,128)(2,1)S(1)} %get-tuple-element.103), channel_id=1, source_target_pairs={{0,1},{1,0},{2,3},{3,2},{4,5},{5,4},{6,7},{7,6},{8,9},{9,8},{10,11... | collective-permute-start | bytes 3145736 | tf_op jit(solution)/shard_map/ppermute | solution.py:823
  127.1 32.7 %collective-permute-start.24 = (bf16[512,1024]{1,0:T(8,128)(2,1)S(1)}, bf16[512,1024]{1,0:T(8,128)(2,1)S(1)}, u32[]{:S(2)}, u32[]{:S(2)}) collective-permute-start(bf16[512,1024]{1,0:T(8,128)(2,1)S(1)} %get-tuple-element.105), channel_id=1, source_target_pairs={{0,2},{1,3},{2,0},{3,1},{4,6},{5,7},{6,4},{7,5},{8,10},{9,11},{10,... | collective-permute-start | bytes 3145736 | tf_op jit(solution)/shard_map/ppermute | solution.py:823
  139.3 31.7 %collective-permute-start.21 = (bf16[256,1024]{1,0:T(8,128)(2,1)S(1)}, bf16[256,1024]{1,0:T(8,128)(2,1)S(1)}, u32[]{:S(2)}, u32[]{:S(2)}) collective-permute-start(bf16[256,1024]{1,0:T(8,128)(2,1)S(1)} %get-tuple-element.100), channel_id=1, source_target_pairs={{0,1},{1,0},{2,3},{3,2},{4,5},{5,4},{6,7},{7,6},{8,9},{9,8},{10,11... | collective-permute-start | bytes 1572872 | tf_op jit(solution)/shard_map/ppermute | solution.py:826
  139.9 31.1 %collective-permute-start.22 = (bf16[256,1024]{1,0:T(8,128)(2,1)S(1)}, bf16[256,1024]{1,0:T(8,128)(2,1)S(1)}, u32[]{:S(2)}, u32[]{:S(2)}) collective-permute-start(bf16[256,1024]{1,0:T(8,128)(2,1)S(1)} %get-tuple-element.101), channel_id=1, source_target_pairs={{0,2},{1,3},{2,0},{3,1},{4,6},{5,7},{6,4},{7,5},{8,10},{9,11},{10,... | collective-permute-start | bytes 1572872 | tf_op jit(solution)/shard_map/ppermute | solution.py:826
  161.8 18.0 %collective-permute-start.25 = (bf16[256,1024]{1,0:T(8,128)(2,1)S(1)}, bf16[256,1024]{1,0:T(8,128)(2,1)S(1)}, u32[]{:S(2)}, u32[]{:S(2)}) collective-permute-start(bf16[256,1024]{1,0:T(8,128)(2,1)S(1)} %get-tuple-element.107), channel_id=1, source_target_pairs={{0,2},{1,3},{2,0},{3,1},{4,6},{5,7},{6,4},{7,5},{8,10},{9,11},{10,... | collective-permute-start | bytes 1572872 | tf_op jit(solution)/shard_map/ppermute | solution.py:828
  162.4 18.7 %collective-permute-start.26 = (bf16[256,1024]{1,0:T(8,128)(2,1)S(1)}, bf16[256,1024]{1,0:T(8,128)(2,1)S(1)}, u32[]{:S(2)}, u32[]{:S(2)}) collective-permute-start(bf16[256,1024]{1,0:T(8,128)(2,1)S(1)} %get-tuple-element.108), channel_id=1, source_target_pairs={{0,1},{1,0},{2,3},{3,2},{4,5},{5,4},{6,7},{7,6},{8,9},{9,8},{10,11... | collective-permute-start | bytes 1572872 | tf_op jit(solution)/shard_map/ppermute | solution.py:828

commit v11 on v10

--- a/solution.py
+++ b/solution.py
@@ -377,7 +377,7 @@
     )
 
 
-def later_kernel(chunk, group, size, _, *refs):
+def later_kernel(first, chunk, group, size, _, *refs):
     xa, xb, wq, acc_q, k_ref, v_ref, along_ref, inside_ref, down_ref, state_ref = refs[:10]
     q_ref, within_ref, held = refs[10:]
     j = pl.program_id(0)
@@ -390,7 +390,7 @@
 
     q_all = (acc_q[0] + dot(held[...], wq[0])).astype(BF16)
     for a in range(group):
-        head = j * group + a
+        head = (first + j) * group + a
         lanes = slice(a * size, (a + 1) * size)
         state = state_ref[a]
         for c in range(rows // chunk):
@@ -403,33 +403,36 @@
                 state = advance(k, v, down, state)
 
 
-def later_call(places, far, w_qkv, acc, k, v, along, inside, down, state, chunk, group):
+def later_call(places, far, w_qkv, acc, k, v, along, inside, down, state, chunk, group, half):
     _, rows, width = acc.shape
     heads, size = state.shape[0], state.shape[1]
     depth = far[0].shape[1]
     cols = group * size
-    wide = pl.BlockSpec((rows, cols), lambda j, o: (0, j))
-    return call(
-        functools.partial(later_kernel, chunk, group, size),
+    steps = heads // group // 2
+    first = half * steps
+    wide = pl.BlockSpec((rows, cols), lambda j, o: (0, first + j))
+    out = pl.BlockSpec((rows, cols), lambda j, o: (0, j))
+    return call(
+        functools.partial(later_kernel, first, chunk, group, size),
         "later",
-        heads // group,
+        steps,
         places,
         (*far, w_qkv, acc, k, v, along, inside, down, state),
         [
             fixed(far[0].shape),
             fixed(far[1].shape),
-            pl.BlockSpec((1, depth, cols), lambda j, o: (0, o[3], j)),
-            pl.BlockSpec((1, rows, cols), lambda j, o: (0, 0, j)),
+            pl.BlockSpec((1, depth, cols), lambda j, o: (0, o[3], first + j)),
+            pl.BlockSpec((1, rows, cols), lambda j, o: (0, 0, first + j)),
             wide,
             wide,
             pl.BlockSpec((heads, rows), lambda j, o: (0, 1)),
             pl.BlockSpec((rows, heads), lambda j, o: (1, 0)),
             pl.BlockSpec((rows, heads), lambda j, o: (1, 0)),
-            pl.BlockSpec((group, size, size), lambda j, o: (j, 0, 0)),
+            pl.BlockSpec((group, size, size), lambda j, o: (first + j, 0, 0)),
         ],
-        (struct((rows, width), BF16), struct((rows, width), BF16)),
-        [wide, wide],
-        2 * rows * depth * width + 4 * rows * (chunk + size) * width,
+        (struct((rows, width // 2), BF16), struct((rows, width // 2), BF16)),
+        [out, out],
+        rows * depth * width + 2 * rows * (chunk + size) * width,
         scratch=[pltpu.VMEM((rows, depth), BF16)],
     )
 
@@ -516,8 +519,10 @@
 WHOLE = pl.BlockSpec(memory_space=pltpu.VMEM)
 
 
-def head_kernel(blocks, places, q_ref, within_ref, here_ref, there_ref, w_ref, *refs):
-    normed_ref, out_refs, held = refs[0], refs[1:3], refs[3]
+def head_kernel(count, blocks, places, *refs):
+    q_refs, within_refs, refs = refs[:count], refs[count : 2 * count], refs[2 * count :]
+    here_ref, there_ref, w_ref, normed_ref = refs[:4]
+    out_refs, held = refs[4:6], refs[6]
     share, size = here_ref.shape[0], here_ref.shape[1]
     tall, width = out_refs[0].shape
     step = pl.program_id(0)
@@ -527,41 +532,43 @@
         def _(p=p, out_ref=out_ref):
             ones = jnp.ones((size, size), BF16)
             for a in range(2 * share):
-                lanes = slice(a * size, (a + 1) * size)
+                part, at = divmod(a, 2 * share // count)
+                here = slice(at * size, (at + 1) * size)
                 ours = places[4] == a // share
                 entering = jnp.where(ours, here_ref[a % share], there_ref[a % share])
-                combined = within_ref[:, lanes].astype(F32) + dot(q_ref[:, lanes], entering)
+                seen = dot(q_refs[part][:, here], entering)
+                combined = within_refs[part][:, here].astype(F32) + seen
                 square = combined * combined
                 high = square.astype(BF16)
                 low = (square - high.astype(F32)).astype(BF16)
                 power = (dot(high, ones) + dot(low, ones)) * (1.0 / size)
+                lanes = slice(a * size, (a + 1) * size)
                 held[p, :, lanes] = (combined * lax.rsqrt(power + 1e-06)).astype(BF16)
             normed_ref[...] = held[p]
             out_ref[...] = dot(held[p], columns(w_ref, places[blocks[0]], width)).astype(BF16)
 
-        @pl.when(step == 2 + p)
-        def _(p=p, out_ref=out_ref):
-            out_ref[...] = dot(held[p], columns(w_ref, places[blocks[1 + p]], width)).astype(BF16)
+        if len(blocks) > 1:
+
+            @pl.when(step == 2 + p)
+            def _(p=p, out_ref=out_ref):
+                out_ref[...] = dot(held[p], columns(w_ref, places[blocks[1 + p]], width)).astype(BF16)
 
 
 def head_call(places, blocks, q, within, entering, w_out, width):
-    rows, cols = q.shape
+    rows, cols = q[0].shape[0], w_out.shape[0]
     tall = rows // 2
+    near = len(blocks) > 1
     part = pl.BlockSpec((tall, cols), lambda i, o: (jnp.minimum(i, 1), 0))
-    return call(
-        functools.partial(head_kernel, blocks),
+    some = pl.BlockSpec((tall, cols // len(q)), lambda i, o: (jnp.minimum(i, 1), 0))
+    out = struct((rows if near else tall, width), BF16)
+    return call(
+        functools.partial(head_kernel, len(q), blocks),
         "heads",
-        4,
+        4 if near else 2,
         places,
-        (q, within, *entering, w_out),
-        [
-            part,
-            part,
-            fixed(entering[0].shape),
-            fixed(entering[1].shape),
-            WHOLE,
-        ],
-        (struct((rows, cols), BF16), *[struct((rows, width), BF16)] * 2),
+        (*q, *within, *entering, w_out),
+        [some] * (2 * len(q)) + [fixed(entering[0].shape), fixed(entering[1].shape), WHOLE],
+        (struct((rows, cols), BF16), out, out),
         [
             part,
             pl.BlockSpec((tall, width), lambda i, o: (i // 2, 0)),
@@ -569,6 +576,35 @@
         ],
         2 * rows * cols * (2 * width + 128),
         scratch=[pltpu.VMEM((2, tall, cols), BF16)],
+        light=True,
+    )
+
+
+def mixed_kernel(places, normed_ref, x_ref, y_ref, w_ref, out_x_ref, out_y_ref):
+    tall, width = x_ref.shape
+    for p, (out_ref, come_ref) in enumerate(((out_x_ref, x_ref), (out_y_ref, y_ref))):
+
+        @pl.when(pl.program_id(0) == p)
+        def _(p=p, out_ref=out_ref, come_ref=come_ref):
+            total = dot(normed_ref[...], columns(w_ref, places[1 + p], width))
+            summed = total[(1 - p) * tall : (2 - p) * tall] + come_ref[...].astype(F32)
+            out_ref[:tall, :] = summed.astype(BF16)
+            out_ref[tall:, :] = total[p * tall : (p + 1) * tall].astype(BF16)
+
+
+def mixed_call(places, normed, for_x, for_y, w_out, width):
+    rows, cols = normed.shape
+    quarter, half = (rows // 2, width), (rows, width)
+    return call(
+        mixed_kernel,
+        "sum_and_near",
+        2,
+        places,
+        (normed, for_x, for_y, w_out),
+        [fixed((rows, cols)), fixed(quarter), fixed(quarter), WHOLE],
+        (struct(half, BF16),) * 2,
+        [fixed(half)] * 2,
+        4 * rows * cols * width,
         light=True,
     )
 
@@ -760,11 +796,22 @@
         )
 
     tails = (tail, tail_other)
+
+    def scores_of_later(half, *earlier):
+        start = stay(after(middle, *earlier))
+        ins = (far, w_qkv, stay(acc_q), stay(k), stay(v), along, inside, down, start)
+        return later_call(places, *ins, quarter, group, half)
+
     if square and n_chips == 4:
         leaving, chip_state, first = chip_call(places, state, near(swap(sent)), tails, prior_state)
-        arriving = near(hop(leaving, (0, 1), (2, 3)))
+        arriving = hop(leaving, (0, 1), (2, 3))
+        query_b, within_b = scores_of_later(0, leaving)
+        arriving = near(after(arriving, query_b))
         leaving = pass_call(places, arriving, chip_state, tails)
-        to_third, to_second = near(hop(leaving, (1, 3))), near(hop(leaving, (1, 2)))
+        to_third, to_second = hop(leaving, (1, 3)), hop(leaving, (1, 2))
+        query_c, within_c = scores_of_later(1, leaving)
+        to_third, to_second, _ = lax.optimization_barrier((to_third, to_second, query_c))
+        to_third, to_second = near(to_third), near(to_second)
         here, passed = enter_call(
             places, arriving, to_second, to_third, first, tails, tail_below, prior_state
         )
@@ -797,9 +844,9 @@
         halves = [
             head_call(
                 places,
-                (0, 0, 0),
-                query[r * rows // 2 : (r + 1) * rows // 2],
-                within[r * rows // 2 : (r + 1) * rows // 2],
+                (0,),
+                (query[r * rows // 2 : (r + 1) * rows // 2],),
+                (within[r * rows // 2 : (r + 1) * rows // 2],),
                 entering,
                 w_out,
                 width,
@@ -809,27 +856,24 @@
         partial = dot(jnp.concatenate(halves), w_whole).astype(BF16)
         return lax.psum_scatter(partial, "head", scatter_dimension=1, tiled=True)
 
-    na, by_x, by_y = head_call(
-        places, (3, 1, 2), stay(query_a), stay(within_a), entering, w_out, width
-    )
-    middle = stay(after(middle, na))
+    if n_chips != 4:
+        (query_b, within_b), (query_c, within_c) = scores_of_later(0), scores_of_later(1)
+    na, far0, far1 = head_call(
+        places, (3,), (stay(query_a),), (stay(within_a),), entering, w_out, width
+    )
+    query_b = after(query_b, na)
+    far0, far1 = over_x(far0), over_y(far1)
+    nb, by_x2, by_y2 = head_call(
+        places, (3, 1, 2), (query_b, query_c), (within_b, within_c), entering, w_out, width
+    )
+    by_x2, by_y2 = over_x(by_x2), over_y(by_y2)
+    by_x, by_y = mixed_call(places, after(na, nb), far1, far0, w_out, width)
+    by_x2, by_y2 = after(by_x2, by_x), after(by_y2, by_x)
     by_x, by_y = over_x(by_x), over_y(by_y)
-    query_b, within_b = later_call(
-        places, far, w_qkv, stay(acc_q), stay(k), stay(v), along, inside, down, middle, quarter, group
-    )
-    nb, by_x2, by_y2 = head_call(
-        places, (3, 1, 2), query_b, within_b, entering, w_out, width
-    )
-    by_x2, by_y2 = over_x(by_x2), over_y(by_y2)
-    sum1, sum0 = pair_call(places, after(na, nb), by_y, by_x, w_out, width)
-    by_x2, by_y2 = after(by_x2, sum1), after(by_y2, sum1)
-    sum1, sum0 = over_x(sum1), over_y(sum0)
     sum3, sum2 = pair_call(places, nb, by_y2, by_x2, w_out, width)
     sum3, sum2 = over_x(sum3), over_y(sum2)
-    below = own_call(places, after(nb, sum1, sum0), ((by_x2, 1),), ((by_y2, 1),), w_out, width, 1)
-    above = own_call(
-        places, na, ((by_x, 1), (sum0, 0)), ((by_y, 1), (sum1, 0)), w_out, width, 2
-    )
+    below = own_call(places, after(nb, by_x, by_y), ((by_x2, 1),), ((by_y2, 1),), w_out, width, 1)
+    above = own_call(places, na, ((by_x, 1), (by_y, 0)), ((by_y, 1), (by_x, 0)), w_out, width, 2)
     return last_call(below, sum2, sum3, above)
 
 

time: 183 us -> 184 us (level)
    ppermute x2, waiting for transfers between devices: 9.71 us -> 19.3 us  [local(): by_x, by_y = (over_x(by_x), over_y(by_y))]
    ppermute x4, waiting for transfers between devices: 8.64 us -> 1.05 us  [hop(): return lax.ppermute(x, 'seq', perm=perm)]
    pallas_call x16 -> x17, Pallas kernels: 89.5 us -> 90.6 us  [call(): pl.pallas_call(kernel, out_shape=tuple(outs), grid_spec=pltpu.PrefetchSca...]
  transfers between devices with their start and end apart: 27 -> 27, of which waited for: 15 -> 13; matrix products, arithmetic and copies ran while one was open for 0% -> 0% of each run, Pallas kernels for 39% -> 41%
where the time goes in v11:
time: 184 us
  Pallas kernels  92.4 us (50%)
  waiting for transfers between devices  62.2 us (34%)
  starting transfers between devices  28.2 us (15%)
    pallas_call x17, Pallas kernels, call(): pl.pallas_call(kernel, out_shape=tuple(outs), grid_spec=pltpu.PrefetchSca...  90.6 us
    ppermute x2, waiting for transfers between devices, local(): by_x, by_y = (over_x(by_x), over_y(by_y))  19.3 us
    ppermute x2, waiting for transfers between devices, local(): by_x2, by_y2 = (over_x(by_x2), over_y(by_y2))  18.2 us
    ppermute x4, starting transfers between devices, hop(): return lax.ppermute(x, 'seq', perm=perm)  8.18 us
    ppermute x2, waiting for transfers between devices, local(): far0, far1 = (over_x(far0), over_y(far1))  6.71 us
    ppermute x2, waiting for transfers between devices, local(): sum3, sum2 = (over_x(sum3), over_y(sum2))  5.17 us
    ppermute x2, waiting for transfers between devices, local(): x3, y2 = (over_x(after(q3, *earlier)), over_y(after(q2, *earlier)))  4.77 us
    ppermute x2, waiting for transfers between devices, local(): x1, y0 = (over_x(after(q1, tail)), over_y(after(q0, tail)))  4.22 us
  transfers between devices with their start and end apart: 27, of which 13 were waited for; matrix products, arithmetic and copies ran while one was open for 0% of the time, Pallas kernels for 41%

profile of v11, /device:TPU:8, one launch (start us, length us, event | category | flops | bytes accessed | tf_op | source)
XLA Modules:
  0.0 183.9 jit_solution(1250826303246586902)
XLA Ops:
  0.0 2.2 %cut.2 = (bf16[256,1024]{1,0:T(8,128)(2,1)}, bf16[256,1024]{1,0:T(8,128)(2,1)}) custom-call(s32[1]{0:T(128)} %constant.29.clone.1._, bf16[1024,1024]{1,0:T(8,128)(2,1)} %x_ref.4), custom_call_target="tpu_custom_call" | custom-call | flops 1 | bytes 3145728 | tf_op jit(solution)/shard_map/cut/pallas_call | solution.py:43
  2.2 1.5 collective-permute-start
  3.7 1.5 collective-permute-start.1
  8.2 12.5 %own_part.1.refs_6_ = f32[3,1024,1024]{2,1,0:T(8,128)} custom-call(s32[6]{0:T(128)S(1)} %stack.27._.places, bf16[1024,1024]{1,0:T(8,128)(2,1)} %x_ref.4, bf16[3,4096,1024]{2,1,0:T(8,128)(2,1)} %refs_2_.7), custom_call_target="tpu_custom_call" | custom-call | flops 6442450944 | bytes 39845888 | tf_op jit(solution)/shard_map/own_part/pallas_call | solution.py:43
  22.1 1.6 collective-permute-start.6
  25.8 2.4 %collective-permute-done.2.refs_1_ = bf16[256,1024]{1,0:T(8,128)(2,1)S(1)} collective-permute-done((bf16[256,1024]{1,0:T(8,128)(2,1)}, bf16[256,1024]{1,0:T(8,128)(2,1)S(1)}, u32[]{:S(2)}, u32[]{:S(2)}) %collective-permute-start.2) | collective-permute-done | bytes 524320 | tf_op jit(solution)/shard_map/ppermute | solution.py:742
  28.2 1.9 %collective-permute-done.3.refs_2_ = bf16[256,1024]{1,0:T(8,128)(2,1)S(1)} collective-permute-done((bf16[256,1024]{1,0:T(8,128)(2,1)}, bf16[256,1024]{1,0:T(8,128)(2,1)S(1)}, u32[]{:S(2)}, u32[]{:S(2)}) %collective-permute-start.3) | collective-permute-done | bytes 524320 | tf_op jit(solution)/shard_map/ppermute | solution.py:742
  30.6 1.5 collective-permute-start.9
  32.1 11.5 %part.2.refs_3_ = f32[3,512,1024]{2,1,0:T(8,128)S(1)} custom-call(s32[6]{0:T(128)S(1)} %stack.27._.places, bf16[256,1024]{1,0:T(8,128)(2,1)S(1)} %collective-permute-done.refs_0_, bf16[256,1024]{1,0:T(8,128)(2,1)S(1)} %collective-permute-done.2.refs_1_, bf16[256,1024]{1,0:T(8,128)(2,1)S(1)} %collective-permute-done.3.refs_2_, ...), custom_call_target="tpu_custom_call" | custom-call | flops 6442450944 | bytes 71303168 | tf_op jit(solution)/shard_map/part/pallas_call | solution.py:43
  43.6 1.6 collective-permute-start.12
  45.6 11.2 %first.1 = (bf16[512,1024]{1,0:T(8,128)(2,1)}, bf16[512,1024]{1,0:T(8,128)(2,1)}, f32[8,128,128]{2,1,0:T(8,128)S(1)}) custom-call(s32[6]{0:T(128)S(1)} %stack.27._.places, bf16[256,1024]{1,0:T(8,128)(2,1)S(1)} %collective-permute-done.6.refs_0_, bf16[256,1024]{1,0:T(8,128)(2,1)S(1)} %collective-permute-done.7.refs_1_, bf16[3,4096,1024]{2,1,0:T(8,128)(2,1)} %refs_2_.7, ...), custom_call_target="tpu_custom_call" | custom-call | flops 3221225472 | bytes 35192832 | tf_op jit(solution)/shard_map/first/pallas_call | solution.py:43
  56.8 1.6 collective-permute-start.8
  59.0 2.9 %collective-permute-done.12.refs_1_ = bf16[256,1024]{1,0:T(8,128)(2,1)S(1)} collective-permute-done((bf16[256,1024]{1,0:T(8,128)(2,1)S(1)}, bf16[256,1024]{1,0:T(8,128)(2,1)S(1)}, u32[]{:S(2)}, u32[]{:S(2)}) %collective-permute-start.12) | collective-permute-done | bytes 524320 | tf_op jit(solution)/shard_map/ppermute | solution.py:760
  61.9 1.9 %collective-permute-done.13.refs_2_ = bf16[256,1024]{1,0:T(8,128)(2,1)S(1)} collective-permute-done((bf16[256,1024]{1,0:T(8,128)(2,1)S(1)}, bf16[256,1024]{1,0:T(8,128)(2,1)S(1)}, u32[]{:S(2)}, u32[]{:S(2)}) %collective-permute-start.13) | collective-permute-done | bytes 524320 | tf_op jit(solution)/shard_map/ppermute | solution.py:760
  63.7 11.7 %part.3 = (f32[1,512,1024]{2,1,0:T(8,128)}, f32[2,512,1024]{2,1,0:T(8,128)S(1)}) custom-call(s32[6]{0:T(128)S(1)} %stack.27._.places, bf16[256,1024]{1,0:T(8,128)(2,1)S(1)} %collective-permute-done.5.refs_0_, bf16[256,1024]{1,0:T(8,128)(2,1)S(1)} %collective-permute-done.12.refs_1_, bf16[256,1024]{1,0:T(8,128)(2,1)S(1)} %collective-permute-done.13.refs_2_, ...), custom_call_target="tpu_custom_call" | custom-call | flops 6442450944 | bytes 71303168 | tf_op jit(solution)/shard_map/part/pallas_call | solution.py:43
  75.4 7.2 %states.1 = (bf16[512,1024]{1,0:T(8,128)(2,1)}, bf16[512,1024]{1,0:T(8,128)(2,1)}, f32[8,128,128]{2,1,0:T(8,128)S(1)}, bf16[4,128,128]{2,1,0:T(8,128)(2,1)S(1)}) custom-call(s32[6]{0:T(128)S(1)} %stack.27._.places, bf16[256,1024]{1,0:T(8,128)(2,1)S(1)} %collective-permute-done.8.refs_0_, bf16[256,1024]{1,0:T(8,128)(2,1)S(1)} %collective-permute-done.10.refs_1_, ...), custom_call_target="tpu_custom_call" | custom-call | flops 2147483648 | bytes 63082496 | tf_op jit(solution)/shard_map/states/pallas_call | solution.py:43
  85.9 5.1 %later.2 = (bf16[512,512]{1,0:T(8,128)(2,1)S(1)}, bf16[512,512]{1,0:T(8,128)(2,1)S(1)}) custom-call(s32[6]{0:T(128)S(1)} %stack.27._.places, bf16[256,1024]{1,0:T(8,128)(2,1)S(1)} %collective-permute-done.8.refs_0_, bf16[256,1024]{1,0:T(8,128)(2,1)S(1)} %collective-permute-done.10.refs_1_, bf16[3,4096,1024]{2,1,0:T(8,128)(2,1)} %refs_2_.7, ...), custom_call_target="tpu_custom_call" | custom-call | flops 939524096 | bytes 32079872 | tf_op jit(solution)/shard_map/later/pallas_call | solution.py:43
  92.7 4.8 %collective-permute-start.16 = (bf16[4,128,128]{2,1,0:T(8,128)(2,1)S(1)}, bf16[4,128,128]{2,1,0:T(8,128)(2,1)S(1)}, u32[]{:S(2)}, u32[]{:S(2)}) collective-permute-start(bf16[4,128,128]{2,1,0:T(8,128)(2,1)S(1)} %pass_on.1), channel_id=1, source_target_pairs={{8,24},{12,28},{9,25},{13,29},{10,26},{14,30},{11,27},{15,31}} | collective-permute-start | bytes 393224 | tf_op jit(solution)/shard_map/ppermute | solution.py:732
  98.9 5.1 %later.3 = (bf16[512,512]{1,0:T(8,128)(2,1)S(1)}, bf16[512,512]{1,0:T(8,128)(2,1)S(1)}) custom-call(s32[6]{0:T(128)S(1)} %stack.27._.places, bf16[256,1024]{1,0:T(8,128)(2,1)S(1)} %collective-permute-done.8.refs_0_, bf16[256,1024]{1,0:T(8,128)(2,1)S(1)} %collective-permute-done.10.refs_1_, bf16[3,4096,1024]{2,1,0:T(8,128)(2,1)} %refs_2_.7, ...), custom_call_target="tpu_custom_call" | custom-call | flops 939524096 | bytes 32079872 | tf_op jit(solution)/shard_map/later/pallas_call | solution.py:43
  106.2 5.2 %heads.2 = (bf16[512,1024]{1,0:T(8,128)(2,1)S(1)}, bf16[256,1024]{1,0:T(8,128)(2,1)S(1)}, bf16[256,1024]{1,0:T(8,128)(2,1)S(1)}) custom-call(s32[6]{0:T(128)S(1)} %stack.27._.places, bf16[512,1024]{1,0:T(8,128)(2,1)} %get-tuple-element.95.refs_0_, bf16[512,1024]{1,0:T(8,128)(2,1)} %get-tuple-element.96.refs_1_, ...), custom_call_target="tpu_custom_call" | custom-call | flops 1 | bytes 1 | tf_op jit(solution)/shard_map/heads/pallas_call | solution.py:43
  111.3 1.6 collective-permute-start.19
  113.5 5.5 %heads.3 = (bf16[512,1024]{1,0:T(8,128)(2,1)S(1)}, bf16[512,1024]{1,0:T(8,128)(2,1)S(1)}, bf16[512,1024]{1,0:T(8,128)(2,1)S(1)}) custom-call(s32[6]{0:T(128)S(1)} %stack.27._.places, bf16[512,512]{1,0:T(8,128)(2,1)S(1)} %get-tuple-element.107.refs_0_, bf16[512,512]{1,0:T(8,128)(2,1)S(1)} %get-tuple-element.100.refs_1_, ...), custom_call_target="tpu_custom_call" | custom-call | flops 1 | bytes 1 | tf_op jit(solution)/shard_map/heads/pallas_call | solution.py:43
  119.0 1.6 collective-permute-start.23
  121.0 5.2 %collective-permute-done.19.x_ref = bf16[256,1024]{1,0:T(8,128)(2,1)S(1)} collective-permute-done((bf16[256,1024]{1,0:T(8,128)(2,1)S(1)}, bf16[256,1024]{1,0:T(8,128)(2,1)S(1)}, u32[]{:S(2)}, u32[]{:S(2)}) %collective-permute-start.19) | collective-permute-done | bytes 524320 | tf_op jit(solution)/shard_map/ppermute | solution.py:865
  126.2 1.6 collective-permute-done.20.y_ref
  127.7 3.1 %sum_and_near.1 = (bf16[512,1024]{1,0:T(8,128)(2,1)S(1)}, bf16[512,1024]{1,0:T(8,128)(2,1)S(1)}) custom-call(s32[6]{0:T(128)S(1)} %stack.27._.places, bf16[512,1024]{1,0:T(8,128)(2,1)S(1)} %get-tuple-element.111.normed_ref, bf16[256,1024]{1,0:T(8,128)(2,1)S(1)} %collective-permute-done.19.x_ref, bf16[256,1024]{1,0:T(8,128)(2,1)S(1)} %collective-permute-done.20.y_ref, ...), custom_call_target="tpu_custom_call" | custom-call | flops 1 | bytes 1 | tf_op jit(solution)/shard_map/sum_and_near/pallas_call | solution.py:43
  132.0 18.2 %collective-permute-done.23.refs_0_.y_ref = bf16[512,1024]{1,0:T(8,128)(2,1)S(1)} collective-permute-done((bf16[512,1024]{1,0:T(8,128)(2,1)S(1)}, bf16[512,1024]{1,0:T(8,128)(2,1)S(1)}, u32[]{:S(2)}, u32[]{:S(2)}) %collective-permute-start.23) | collective-permute-done | bytes 1048608 | tf_op jit(solution)/shard_map/ppermute | solution.py:869
  150.2 2.0 %sum_pair.1 = (bf16[256,1024]{1,0:T(8,128)(2,1)S(1)}, bf16[256,1024]{1,0:T(8,128)(2,1)S(1)}) custom-call(s32[6]{0:T(128)S(1)} %stack.27._.places, bf16[512,1024]{1,0:T(8,128)(2,1)S(1)} %get-tuple-element.116.normed_ref, bf16[512,1024]{1,0:T(8,128)(2,1)S(1)} %collective-permute-done.24.refs_1_.x_ref, ...), custom_call_target="tpu_custom_call" | custom-call | flops 1 | bytes 1 | tf_op jit(solution)/shard_map/sum_pair/pallas_call | solution.py:43
  153.4 19.3 %collective-permute-done.21.refs_0_.refs_3_ = bf16[512,1024]{1,0:T(8,128)(2,1)S(1)} collective-permute-done((bf16[512,1024]{1,0:T(8,128)(2,1)S(1)}, bf16[512,1024]{1,0:T(8,128)(2,1)S(1)}, u32[]{:S(2)}, u32[]{:S(2)}) %collective-permute-start.21) | collective-permute-done | bytes 1048608 | tf_op jit(solution)/shard_map/ppermute | solution.py:872
  172.7 2.0 %own_block.2.kept_ref = bf16[512,1024]{1,0:T(8,128)(2,1)S(1)} custom-call(s32[6]{0:T(128)S(1)} %stack.27._.places, bf16[512,1024]{1,0:T(8,128)(2,1)S(1)} %get-tuple-element.116.normed_ref, bf16[1024,4096]{1,0:T(8,128)(2,1)S(1)} %bitcast.7, bf16[512,1024]{1,0:T(8,128)(2,1)S(1)} %collective-permute-done.23.refs_0_.y_ref, ...), custom_call_target="tpu_custom_call" | custom-call | flops 1 | bytes 1 | tf_op jit(solution)/shard_map/own_block/pallas_call | solution.py:43
  174.7 2.9 %own_block.3.above_ref = bf16[1024,1024]{1,0:T(8,128)(2,1)} custom-call(s32[6]{0:T(128)S(1)} %stack.27._.places, bf16[512,1024]{1,0:T(8,128)(2,1)S(1)} %get-tuple-element.111.normed_ref, bf16[1024,4096]{1,0:T(8,128)(2,1)S(1)} %bitcast.7, bf16[512,1024]{1,0:T(8,128)(2,1)S(1)} %collective-permute-done.21.refs_0_.refs_3_, ...), custom_call_target="tpu_custom_call" | custom-call | flops 1 | bytes 1 | tf_op jit(solution)/shard_map/own_block/pallas_call | solution.py:43
  177.6 3.9 %collective-permute-done.25.a_ref = bf16[256,1024]{1,0:T(8,128)(2,1)S(1)} collective-permute-done((bf16[256,1024]{1,0:T(8,128)(2,1)S(1)}, bf16[256,1024]{1,0:T(8,128)(2,1)S(1)}, u32[]{:S(2)}, u32[]{:S(2)}) %collective-permute-start.25) | collective-permute-done | bytes 524320 | tf_op jit(solution)/shard_map/ppermute | solution.py:874
  (55 shorter events, 22.1 us)
Async XLA Ops:
  2.2 18.4 %collective-permute-start = (bf16[256,1024]{1,0:T(8,128)(2,1)}, bf16[256,1024]{1,0:T(8,128)(2,1)S(1)}, u32[]{:S(2)}, u32[]{:S(2)}) collective-permute-start(bf16[256,1024]{1,0:T(8,128)(2,1)} %get-tuple-element.70), channel_id=1, source_target_pairs={{0,1},{1,0},{2,3},{3,2},{4,5},{5,4},{6,7},{7,6},{8,9},{9,8},{10,11... | collective-permute-start | bytes 1572872 | tf_op jit(solution)/shard_map/ppermute | solution.py:741
  3.7 17.0 %collective-permute-start.1 = (bf16[256,1024]{1,0:T(8,128)(2,1)}, bf16[256,1024]{1,0:T(8,128)(2,1)S(1)}, u32[]{:S(2)}, u32[]{:S(2)}) collective-permute-start(bf16[256,1024]{1,0:T(8,128)(2,1)} %get-tuple-element.69), channel_id=1, source_target_pairs={{0,2},{1,3},{2,0},{3,1},{4,6},{5,7},{6,4},{7,5},{8,10},{9,11},{10,... | collective-permute-start | bytes 1572872 | tf_op jit(solution)/shard_map/ppermute | solution.py:741
  5.2 0.8 copy-start.2
  7.0 21.2 %collective-permute-start.2 = (bf16[256,1024]{1,0:T(8,128)(2,1)}, bf16[256,1024]{1,0:T(8,128)(2,1)S(1)}, u32[]{:S(2)}, u32[]{:S(2)}) collective-permute-start(bf16[256,1024]{1,0:T(8,128)(2,1)} %get-tuple-element.69), channel_id=1, source_target_pairs={{0,1},{1,0},{2,3},{3,2},{4,5},{5,4},{6,7},{7,6},{8,9},{9,8},{10,11... | collective-permute-start | bytes 1572872 | tf_op jit(solution)/shard_map/ppermute | solution.py:742
  7.6 22.4 %collective-permute-start.3 = (bf16[256,1024]{1,0:T(8,128)(2,1)}, bf16[256,1024]{1,0:T(8,128)(2,1)S(1)}, u32[]{:S(2)}, u32[]{:S(2)}) collective-permute-start(bf16[256,1024]{1,0:T(8,128)(2,1)} %get-tuple-element.70), channel_id=1, source_target_pairs={{0,2},{1,3},{2,0},{3,1},{4,6},{5,7},{6,4},{7,5},{8,10},{9,11},{10,... | collective-permute-start | bytes 1572872 | tf_op jit(solution)/shard_map/ppermute | solution.py:742
  20.7 4.5 %collective-permute-start.4 = (f32[8,128]{1,0:T(8,128)S(1)}, f32[8,128]{1,0:T(8,128)S(1)}, u32[]{:S(2)}, u32[]{:S(2)}) collective-permute-start(f32[8,128]{1,0:T(8,128)S(1)} %get-tuple-element.71.tail_ref), channel_id=1, source_target_pairs={{0,4},{4,0},{8,12},{12,8},{16,20},{20,16},{24,28},{28,24},{1,5},{5... | collective-permute-start | bytes 12296 | tf_op jit(solution)/shard_map/ppermute | solution.py:735
  22.1 21.5 %collective-permute-start.6 = (bf16[256,1024]{1,0:T(8,128)(2,1)S(1)}, bf16[256,1024]{1,0:T(8,128)(2,1)S(1)}, u32[]{:S(2)}, u32[]{:S(2)}) collective-permute-start(bf16[256,1024]{1,0:T(8,128)(2,1)S(1)} %collective-permute-done.refs_0_), channel_id=1, source_target_pairs={{0,2},{1,3},{2,0},{3,1},{4,6},{5,7},{6,4},{7,5},{8,10},{9,11},{10,... | collective-permute-start | bytes 1572872 | tf_op jit(solution)/shard_map/ppermute | solution.py:745
  23.7 19.9 %collective-permute-start.7 = (bf16[256,1024]{1,0:T(8,128)(2,1)S(1)}, bf16[256,1024]{1,0:T(8,128)(2,1)S(1)}, u32[]{:S(2)}, u32[]{:S(2)}) collective-permute-start(bf16[256,1024]{1,0:T(8,128)(2,1)S(1)} %collective-permute-done.1.refs_3_), channel_id=1, source_target_pairs={{0,1},{1,0},{2,3},{3,2},{4,5},{5,4},{6,7},{7,6},{8,9},{9,8},{10,11... | collective-permute-start | bytes 1572872 | tf_op jit(solution)/shard_map/ppermute | solution.py:745
  25.1 18.4 %collective-permute-start.11 = (f32[8,128]{1,0:T(8,128)S(1)}, f32[8,128]{1,0:T(8,128)S(1)}, u32[]{:S(2)}, u32[]{:S(2)}) collective-permute-start(f32[8,128]{1,0:T(8,128)S(1)} %add.10), channel_id=1, source_target_pairs={{16,24},{20,28},{17,25},{21,29},{18,26},{22,30},{19,27},{23,31}} | collective-permute-start | bytes 12296 | tf_op jit(solution)/shard_map/ppermute | solution.py:732
  30.0 26.8 %collective-permute-start.5 = (bf16[256,1024]{1,0:T(8,128)(2,1)S(1)}, bf16[256,1024]{1,0:T(8,128)(2,1)S(1)}, u32[]{:S(2)}, u32[]{:S(2)}) collective-permute-start(bf16[256,1024]{1,0:T(8,128)(2,1)S(1)} %get-tuple-element.82), channel_id=1, source_target_pairs={{0,1},{1,0},{2,3},{3,2},{4,5},{5,4},{6,7},{7,6},{8,9},{9,8},{10,11... | collective-permute-start | bytes 1572872 | tf_op jit(solution)/shard_map/ppermute | solution.py:747
  30.6 27.9 %collective-permute-start.9 = (bf16[256,1024]{1,0:T(8,128)(2,1)S(1)}, bf16[256,1024]{1,0:T(8,128)(2,1)S(1)}, u32[]{:S(2)}, u32[]{:S(2)}) collective-permute-start(bf16[256,1024]{1,0:T(8,128)(2,1)S(1)} %get-tuple-element.81), channel_id=1, source_target_pairs={{0,2},{1,3},{2,0},{3,1},{4,6},{5,7},{6,4},{7,5},{8,10},{9,11},{10,... | collective-permute-start | bytes 1572872 | tf_op jit(solution)/shard_map/ppermute | solution.py:748
  43.6 18.3 %collective-permute-start.12 = (bf16[256,1024]{1,0:T(8,128)(2,1)S(1)}, bf16[256,1024]{1,0:T(8,128)(2,1)S(1)}, u32[]{:S(2)}, u32[]{:S(2)}) collective-permute-start(bf16[256,1024]{1,0:T(8,128)(2,1)S(1)} %get-tuple-element.81), channel_id=1, source_target_pairs={{0,1},{1,0},{2,3},{3,2},{4,5},{5,4},{6,7},{7,6},{8,9},{9,8},{10,11... | collective-permute-start | bytes 1572872 | tf_op jit(solution)/shard_map/ppermute | solution.py:760
  45.1 18.6 %collective-permute-start.13 = (bf16[256,1024]{1,0:T(8,128)(2,1)S(1)}, bf16[256,1024]{1,0:T(8,128)(2,1)S(1)}, u32[]{:S(2)}, u32[]{:S(2)}) collective-permute-start(bf16[256,1024]{1,0:T(8,128)(2,1)S(1)} %get-tuple-element.82), channel_id=1, source_target_pairs={{0,2},{1,3},{2,0},{3,1},{4,6},{5,7},{6,4},{7,5},{8,10},{9,11},{10,... | collective-permute-start | bytes 1572872 | tf_op jit(solution)/shard_map/ppermute | solution.py:760
  56.8 18.6 %copy-start = (f32[8,128,128]{2,1,0:T(8,128)}, f32[8,128,128]{2,1,0:T(8,128)S(1)}, u32[]{:S(2)}) copy-start(f32[8,128,128]{2,1,0:T(8,128)S(1)} %get-tuple-element.99.refs_8_.refs_9_) | copy-start | bytes 1572868
  56.8 18.6 %collective-permute-start.8 = (bf16[256,1024]{1,0:T(8,128)(2,1)S(1)}, bf16[256,1024]{1,0:T(8,128)(2,1)S(1)}, u32[]{:S(2)}, u32[]{:S(2)}) collective-permute-start(bf16[256,1024]{1,0:T(8,128)(2,1)S(1)} %collective-permute-done.5.refs_0_), channel_id=1, source_target_pairs={{0,2},{1,3},{2,0},{3,1},{4,6},{5,7},{6,4},{7,5},{8,10},{9,11},{10,... | collective-permute-start | bytes 1572872 | tf_op jit(solution)/shard_map/ppermute | solution.py:774
  58.4 17.0 %collective-permute-start.10 = (bf16[256,1024]{1,0:T(8,128)(2,1)S(1)}, bf16[256,1024]{1,0:T(8,128)(2,1)S(1)}, u32[]{:S(2)}, u32[]{:S(2)}) collective-permute-start(bf16[256,1024]{1,0:T(8,128)(2,1)S(1)} %collective-permute-done.9.refs_3_), channel_id=1, source_target_pairs={{0,1},{1,0},{2,3},{3,2},{4,5},{5,4},{6,7},{7,6},{8,9},{9,8},{10,11... | collective-permute-start | bytes 1572872 | tf_op jit(solution)/shard_map/ppermute | solution.py:774
  75.4 8.5 %copy-start.1 = (f32[8,128,128]{2,1,0:T(8,128)S(1)}, f32[8,128,128]{2,1,0:T(8,128)}, u32[]{:S(2)}) copy-start(f32[8,128,128]{2,1,0:T(8,128)} %prior_ref.3) | copy-start | bytes 1572868
  82.6 1.3 collective-permute-start.14
  84.6 7.4 %collective-permute-start.15 = (bf16[4,128,128]{2,1,0:T(8,128)(2,1)S(1)}, bf16[4,128,128]{2,1,0:T(8,128)(2,1)S(1)}, u32[]{:S(2)}, u32[]{:S(2)}) collective-permute-start(bf16[4,128,128]{2,1,0:T(8,128)(2,1)S(1)} %get-tuple-element.92), channel_id=1, source_target_pairs={{0,8},{4,12},{16,24},{20,28},{1,9},{5,13},{17,25},{21,29},{2,10},{... | collective-permute-start | bytes 393224 | tf_op jit(solution)/shard_map/ppermute | solution.py:732
  92.1 14.1 %slice-start = ((s8[8388608]{0:T(1024)(128)(4,1)}), s8[4194304]{0:T(1024)(128)(4,1)S(1)}, s32[]{:S(2)}) async-start(s8[8388608]{0:T(1024)(128)(4,1)} %bitcast.6), calls=%async_computation | async-start | bytes 8388608
  92.7 13.5 %slice-start.1 = ((s8[8388608]{0:T(1024)(128)(4,1)}), s8[4194304]{0:T(1024)(128)(4,1)S(1)}, s32[]{:S(2)}) async-start(s8[8388608]{0:T(1024)(128)(4,1)} %bitcast.6), calls=%async_computation.1 | async-start | bytes 8388608
  92.7 11.4 %collective-permute-start.16 = (bf16[4,128,128]{2,1,0:T(8,128)(2,1)S(1)}, bf16[4,128,128]{2,1,0:T(8,128)(2,1)S(1)}, u32[]{:S(2)}, u32[]{:S(2)}) collective-permute-start(bf16[4,128,128]{2,1,0:T(8,128)(2,1)S(1)} %pass_on.1), channel_id=1, source_target_pairs={{8,24},{12,28},{9,25},{13,29},{10,26},{14,30},{11,27},{15,31}} | collective-permute-start | bytes 393224 | tf_op jit(solution)/shard_map/ppermute | solution.py:732
  97.4 6.6 %collective-permute-start.17 = (bf16[4,128,128]{2,1,0:T(8,128)(2,1)S(1)}, bf16[4,128,128]{2,1,0:T(8,128)(2,1)S(1)}, u32[]{:S(2)}, u32[]{:S(2)}) collective-permute-start(bf16[4,128,128]{2,1,0:T(8,128)(2,1)S(1)} %pass_on.1), channel_id=1, source_target_pairs={{8,16},{12,20},{9,17},{13,21},{10,18},{14,22},{11,19},{15,23}} | collective-permute-start | bytes 393224 | tf_op jit(solution)/shard_map/ppermute | solution.py:732
  104.7 1.4 collective-permute-start.18
  111.3 14.8 %collective-permute-start.19 = (bf16[256,1024]{1,0:T(8,128)(2,1)S(1)}, bf16[256,1024]{1,0:T(8,128)(2,1)S(1)}, u32[]{:S(2)}, u32[]{:S(2)}) collective-permute-start(bf16[256,1024]{1,0:T(8,128)(2,1)S(1)} %get-tuple-element.112), channel_id=1, source_target_pairs={{0,2},{1,3},{2,0},{3,1},{4,6},{5,7},{6,4},{7,5},{8,10},{9,11},{10,... | collective-permute-start | bytes 1572872 | tf_op jit(solution)/shard_map/ppermute | solution.py:865
  112.9 14.8 %collective-permute-start.20 = (bf16[256,1024]{1,0:T(8,128)(2,1)S(1)}, bf16[256,1024]{1,0:T(8,128)(2,1)S(1)}, u32[]{:S(2)}, u32[]{:S(2)}) collective-permute-start(bf16[256,1024]{1,0:T(8,128)(2,1)S(1)} %get-tuple-element.113), channel_id=1, source_target_pairs={{0,1},{1,0},{2,3},{3,2},{4,5},{5,4},{6,7},{7,6},{8,9},{9,8},{10,11... | collective-permute-start | bytes 1572872 | tf_op jit(solution)/shard_map/ppermute | solution.py:865
  119.0 31.2 %collective-permute-start.23 = (bf16[512,1024]{1,0:T(8,128)(2,1)S(1)}, bf16[512,1024]{1,0:T(8,128)(2,1)S(1)}, u32[]{:S(2)}, u32[]{:S(2)}) collective-permute-start(bf16[512,1024]{1,0:T(8,128)(2,1)S(1)} %get-tuple-element.117), channel_id=1, source_target_pairs={{0,1},{1,0},{2,3},{3,2},{4,5},{5,4},{6,7},{7,6},{8,9},{9,8},{10,11... | collective-permute-start | bytes 3145736 | tf_op jit(solution)/shard_map/ppermute | solution.py:869
  120.5 29.7 %collective-permute-start.24 = (bf16[512,1024]{1,0:T(8,128)(2,1)S(1)}, bf16[512,1024]{1,0:T(8,128)(2,1)S(1)}, u32[]{:S(2)}, u32[]{:S(2)}) collective-permute-start(bf16[512,1024]{1,0:T(8,128)(2,1)S(1)} %get-tuple-element.119), channel_id=1, source_target_pairs={{0,2},{1,3},{2,0},{3,1},{4,6},{5,7},{6,4},{7,5},{8,10},{9,11},{10,... | collective-permute-start | bytes 3145736 | tf_op jit(solution)/shard_map/ppermute | solution.py:869
  130.8 41.8 %collective-permute-start.21 = (bf16[512,1024]{1,0:T(8,128)(2,1)S(1)}, bf16[512,1024]{1,0:T(8,128)(2,1)S(1)}, u32[]{:S(2)}, u32[]{:S(2)}) collective-permute-start(bf16[512,1024]{1,0:T(8,128)(2,1)S(1)} %get-tuple-element.114), channel_id=1, source_target_pairs={{0,1},{1,0},{2,3},{3,2},{4,5},{5,4},{6,7},{7,6},{8,9},{9,8},{10,11... | collective-permute-start | bytes 3145736 | tf_op jit(solution)/shard_map/ppermute | solution.py:872
  131.4 41.2 %collective-permute-start.22 = (bf16[512,1024]{1,0:T(8,128)(2,1)S(1)}, bf16[512,1024]{1,0:T(8,128)(2,1)S(1)}, u32[]{:S(2)}, u32[]{:S(2)}) collective-permute-start(bf16[512,1024]{1,0:T(8,128)(2,1)S(1)} %get-tuple-element.115), channel_id=1, source_target_pairs={{0,2},{1,3},{2,0},{3,1},{4,6},{5,7},{6,4},{7,5},{8,10},{9,11},{10,... | collective-permute-start | bytes 3145736 | tf_op jit(solution)/shard_map/ppermute | solution.py:872
  152.2 29.3 %collective-permute-start.25 = (bf16[256,1024]{1,0:T(8,128)(2,1)S(1)}, bf16[256,1024]{1,0:T(8,128)(2,1)S(1)}, u32[]{:S(2)}, u32[]{:S(2)}) collective-permute-start(bf16[256,1024]{1,0:T(8,128)(2,1)S(1)} %get-tuple-element.121), channel_id=1, source_target_pairs={{0,2},{1,3},{2,0},{3,1},{4,6},{5,7},{6,4},{7,5},{8,10},{9,11},{10,... | collective-permute-start | bytes 1572872 | tf_op jit(solution)/shard_map/ppermute | solution.py:874
  152.8 30.0 %collective-permute-start.26 = (bf16[256,1024]{1,0:T(8,128)(2,1)S(1)}, bf16[256,1024]{1,0:T(8,128)(2,1)S(1)}, u32[]{:S(2)}, u32[]{:S(2)}) collective-permute-start(bf16[256,1024]{1,0:T(8,128)(2,1)S(1)} %get-tuple-element.122), channel_id=1, source_target_pairs={{0,1},{1,0},{2,3},{3,2},{4,5},{5,4},{6,7},{7,6},{8,9},{9,8},{10,11... | collective-permute-start | bytes 1572872 | tf_op jit(solution)/shard_map/ppermute | solution.py:874

commit v12 on v11

--- a/solution.py
+++ b/solution.py
@@ -444,8 +444,8 @@
 
 
 def chip_kernel(places, state_ref, come_ref, tail_ref, other_ref, prior_ref, *out_refs):
-    leaving_ref, chip_ref, first_ref = out_refs
-    core, chip = places[4], places[5]
+    leaving_ref, alone_ref, chip_ref, first_ref = out_refs
+    core = places[4]
     share = come_ref.shape[0]
     for i in range(share):
         head = core * share + i
@@ -455,7 +455,8 @@
         total = second_fade * first + second
         first_ref[i] = first
         chip_ref[i] = total
-        leaving_ref[i] = jnp.where(chip == 2, total, fade * prior_ref[head] + total).astype(BF16)
+        alone_ref[i] = total.astype(BF16)
+        leaving_ref[i] = (fade * prior_ref[head] + total).astype(BF16)
 
 
 def pass_kernel(places, come_ref, chip_ref, tail_ref, other_ref, leaving_ref):
@@ -466,18 +467,18 @@
 
 
 def enter_kernel(
-    places, come_ref, second_ref, third_ref, first_ref, tail_ref, other_ref, below_ref, prior_ref, *out_refs
+    places, come_ref, alone_ref, second_ref, third_ref, first_ref, tail_ref, other_ref, below_ref, prior_ref, *out_refs
 ):
     here_ref, passed_ref = out_refs
     core, chip = places[4], places[5]
     share = come_ref.shape[0]
     for i in range(share):
         head = core * share + i
-        come = come_ref[i].astype(F32)
         below = jnp.exp(-below_ref[pl.ds(head, 1), :])
-        state = jnp.where(chip == 0, prior_ref[head], come)
+        through = below * third_ref[i].astype(F32) + alone_ref[i].astype(F32)
+        state = jnp.where(chip == 0, prior_ref[head], come_ref[i].astype(F32))
         state = jnp.where(chip == 2, second_ref[i].astype(F32), state)
-        state = jnp.where(chip == 3, below * third_ref[i].astype(F32) + come, state)
+        state = jnp.where(chip == 3, through, state)
         later = fades(tail_ref, other_ref, core, head)[0] * state + first_ref[i]
         here_ref[i] = jnp.where(core == 0, state, later).astype(BF16)
         passed_ref[i] = jnp.where(core == 0, later, state).astype(BF16)
@@ -497,7 +498,7 @@
 
 
 def chip_call(places, state, come, tails, prior):
-    outs = (struct(come.shape, BF16), struct(come.shape, F32), struct(come.shape, F32))
+    outs = [struct(come.shape, kind) for kind in (BF16, BF16, F32, F32)]
     return small_call(chip_kernel, "chip_state", places, (state, come, *tails, prior), outs)
 
 
@@ -506,9 +507,9 @@
     return small_call(pass_kernel, "pass_on", places, (come, chip_state, *tails), outs)[0]
 
 
-def enter_call(places, come, second, third, first, tails, below, prior):
+def enter_call(places, come, alone, second, third, first, tails, below, prior):
     outs = (struct(come.shape, BF16),) * 2
-    ins = (come, second, third, first, *tails, below, prior)
+    ins = (come, alone, second, third, first, *tails, below, prior)
     return small_call(enter_kernel, "enter", places, ins, outs)
 
 
@@ -803,17 +804,25 @@
         return later_call(places, *ins, quarter, group, half)
 
     if square and n_chips == 4:
-        leaving, chip_state, first = chip_call(places, state, near(swap(sent)), tails, prior_state)
-        arriving = hop(leaving, (0, 1), (2, 3))
-        query_b, within_b = scores_of_later(0, leaving)
-        arriving = near(after(arriving, query_b))
+        leaving, alone, chip_state, first = chip_call(
+            places, state, near(swap(sent)), tails, prior_state
+        )
+        alone = hop(alone, (2, 3))
+        arriving = near(hop(leaving, (0, 1)))
         leaving = pass_call(places, arriving, chip_state, tails)
         to_third, to_second = hop(leaving, (1, 3)), hop(leaving, (1, 2))
-        query_c, within_c = scores_of_later(1, leaving)
-        to_third, to_second, _ = lax.optimization_barrier((to_third, to_second, query_c))
-        to_third, to_second = near(to_third), near(to_second)
+        query_b, within_b = scores_of_later(0, leaving)
+        alone, to_third, to_second, _ = lax.optimization_barrier((alone, to_third, to_second, query_b))
         here, passed = enter_call(
-            places, arriving, to_second, to_third, first, tails, tail_below, prior_state
+            places,
+            arriving,
+            near(alone),
+            near(to_second),
+            near(to_third),
+            first,
+            tails,
+            tail_below,
+            prior_state,
         )
     else:
         share = heads // 2
@@ -857,11 +866,11 @@
         return lax.psum_scatter(partial, "head", scatter_dimension=1, tiled=True)
 
     if n_chips != 4:
-        (query_b, within_b), (query_c, within_c) = scores_of_later(0), scores_of_later(1)
+        query_b, within_b = scores_of_later(0)
     na, far0, far1 = head_call(
         places, (3,), (stay(query_a),), (stay(within_a),), entering, w_out, width
     )
-    query_b = after(query_b, na)
+    query_c, within_c = scores_of_later(1, na)
     far0, far1 = over_x(far0), over_y(far1)
     nb, by_x2, by_y2 = head_call(
         places, (3, 1, 2), (query_b, query_c), (within_b, within_c), entering, w_out, width

time: 184 us -> 182 us (0.989)
  starting transfers between devices: 28.2 us -> 25.6 us
    ppermute x2, waiting for transfers between devices: 6.71 us -> 0.74 us  [local(): far0, far1 = (over_x(far0), over_y(far1))]
    ppermute x4 -> x5, waiting for transfers between devices: 1.05 us -> 5.48 us  [hop(): return lax.ppermute(x, 'seq', perm=perm)]
    ppermute x4 -> x5, starting transfers between devices: 8.18 us -> 5.39 us  [hop(): return lax.ppermute(x, 'seq', perm=perm)]
    ppermute x2, waiting for transfers between devices: 18.2 us -> 20.4 us  [local(): by_x2, by_y2 = (over_x(by_x2), over_y(by_y2))]
  transfers between devices with their start and end apart: 27 -> 28, of which waited for: 13 -> 13; matrix products, arithmetic and copies ran while one was open for 0% -> 0% of each run, Pallas kernels for 41% -> 42%
where the time goes in v12:
time: 182 us
  Pallas kernels  93 us (51%)
  waiting for transfers between devices  61.9 us (34%)
  starting transfers between devices  25.6 us (14%)
    pallas_call x17, Pallas kernels, call(): pl.pallas_call(kernel, out_shape=tuple(outs), grid_spec=pltpu.PrefetchSca...  91.1 us
    ppermute x2, waiting for transfers between devices, local(): by_x2, by_y2 = (over_x(by_x2), over_y(by_y2))  20.4 us
    ppermute x2, waiting for transfers between devices, local(): by_x, by_y = (over_x(by_x), over_y(by_y))  19.1 us
    ppermute x5, waiting for transfers between devices, hop(): return lax.ppermute(x, 'seq', perm=perm)  5.48 us
    ppermute x5, starting transfers between devices, hop(): return lax.ppermute(x, 'seq', perm=perm)  5.39 us
    ppermute x2, waiting for transfers between devices, local(): x3, y2 = (over_x(after(q3, *earlier)), over_y(after(q2, *earlier)))  4.77 us
    ppermute x2, waiting for transfers between devices, local(): sum3, sum2 = (over_x(sum3), over_y(sum2))  4.55 us
    ppermute x2, waiting for transfers between devices, local(): x1, y0 = (over_x(after(q1, tail)), over_y(after(q0, tail)))  4.16 us
  transfers between devices with their start and end apart: 28, of which 13 were waited for; matrix products, arithmetic and copies ran while one was open for 0% of the time, Pallas kernels for 42%

profile of v12, /device:TPU:8, one launch (start us, length us, event | category | flops | bytes accessed | tf_op | source)
XLA Modules:
  0.0 181.7 jit_solution(4681988831258537521)
XLA Ops:
  0.0 2.2 %cut.2 = (bf16[256,1024]{1,0:T(8,128)(2,1)}, bf16[256,1024]{1,0:T(8,128)(2,1)}) custom-call(s32[1]{0:T(128)} %constant.29.clone.1._, bf16[1024,1024]{1,0:T(8,128)(2,1)} %x_ref.4), custom_call_target="tpu_custom_call" | custom-call | flops 1 | bytes 3145728 | tf_op jit(solution)/shard_map/cut/pallas_call | solution.py:43
  2.2 1.5 collective-permute-start
  3.7 1.5 collective-permute-start.1
  8.2 12.5 %own_part.1.refs_6_ = f32[3,1024,1024]{2,1,0:T(8,128)} custom-call(s32[6]{0:T(128)S(1)} %stack.27._.places, bf16[1024,1024]{1,0:T(8,128)(2,1)} %x_ref.4, bf16[3,4096,1024]{2,1,0:T(8,128)(2,1)} %refs_2_.7), custom_call_target="tpu_custom_call" | custom-call | flops 6442450944 | bytes 39845888 | tf_op jit(solution)/shard_map/own_part/pallas_call | solution.py:43
  22.1 1.6 collective-permute-start.6
  25.9 2.3 %collective-permute-done.2.refs_1_ = bf16[256,1024]{1,0:T(8,128)(2,1)S(1)} collective-permute-done((bf16[256,1024]{1,0:T(8,128)(2,1)}, bf16[256,1024]{1,0:T(8,128)(2,1)S(1)}, u32[]{:S(2)}, u32[]{:S(2)}) %collective-permute-start.2) | collective-permute-done | bytes 524320 | tf_op jit(solution)/shard_map/ppermute | solution.py:743
  28.1 1.9 %collective-permute-done.3.refs_2_ = bf16[256,1024]{1,0:T(8,128)(2,1)S(1)} collective-permute-done((bf16[256,1024]{1,0:T(8,128)(2,1)}, bf16[256,1024]{1,0:T(8,128)(2,1)S(1)}, u32[]{:S(2)}, u32[]{:S(2)}) %collective-permute-start.3) | collective-permute-done | bytes 524320 | tf_op jit(solution)/shard_map/ppermute | solution.py:743
  30.6 1.5 collective-permute-start.9
  32.1 11.5 %part.2.refs_3_ = f32[3,512,1024]{2,1,0:T(8,128)S(1)} custom-call(s32[6]{0:T(128)S(1)} %stack.27._.places, bf16[256,1024]{1,0:T(8,128)(2,1)S(1)} %collective-permute-done.refs_0_, bf16[256,1024]{1,0:T(8,128)(2,1)S(1)} %collective-permute-done.2.refs_1_, bf16[256,1024]{1,0:T(8,128)(2,1)S(1)} %collective-permute-done.3.refs_2_, ...), custom_call_target="tpu_custom_call" | custom-call | flops 6442450944 | bytes 71303168 | tf_op jit(solution)/shard_map/part/pallas_call | solution.py:43
  43.6 1.6 collective-permute-start.12
  45.6 11.2 %first.1 = (bf16[512,1024]{1,0:T(8,128)(2,1)}, bf16[512,1024]{1,0:T(8,128)(2,1)}, f32[8,128,128]{2,1,0:T(8,128)S(1)}) custom-call(s32[6]{0:T(128)S(1)} %stack.27._.places, bf16[256,1024]{1,0:T(8,128)(2,1)S(1)} %collective-permute-done.6.refs_0_, bf16[256,1024]{1,0:T(8,128)(2,1)S(1)} %collective-permute-done.7.refs_1_, bf16[3,4096,1024]{2,1,0:T(8,128)(2,1)} %refs_2_.7, ...), custom_call_target="tpu_custom_call" | custom-call | flops 3221225472 | bytes 35192832 | tf_op jit(solution)/shard_map/first/pallas_call | solution.py:43
  56.8 1.6 collective-permute-start.8
  59.0 2.9 %collective-permute-done.12.refs_1_ = bf16[256,1024]{1,0:T(8,128)(2,1)S(1)} collective-permute-done((bf16[256,1024]{1,0:T(8,128)(2,1)S(1)}, bf16[256,1024]{1,0:T(8,128)(2,1)S(1)}, u32[]{:S(2)}, u32[]{:S(2)}) %collective-permute-start.12) | collective-permute-done | bytes 524320 | tf_op jit(solution)/shard_map/ppermute | solution.py:761
  61.8 1.9 %collective-permute-done.13.refs_2_ = bf16[256,1024]{1,0:T(8,128)(2,1)S(1)} collective-permute-done((bf16[256,1024]{1,0:T(8,128)(2,1)S(1)}, bf16[256,1024]{1,0:T(8,128)(2,1)S(1)}, u32[]{:S(2)}, u32[]{:S(2)}) %collective-permute-start.13) | collective-permute-done | bytes 524320 | tf_op jit(solution)/shard_map/ppermute | solution.py:761
  63.7 11.7 %part.3 = (f32[1,512,1024]{2,1,0:T(8,128)}, f32[2,512,1024]{2,1,0:T(8,128)S(1)}) custom-call(s32[6]{0:T(128)S(1)} %stack.27._.places, bf16[256,1024]{1,0:T(8,128)(2,1)S(1)} %collective-permute-done.5.refs_0_, bf16[256,1024]{1,0:T(8,128)(2,1)S(1)} %collective-permute-done.12.refs_1_, bf16[256,1024]{1,0:T(8,128)(2,1)S(1)} %collective-permute-done.13.refs_2_, ...), custom_call_target="tpu_custom_call" | custom-call | flops 6442450944 | bytes 71303168 | tf_op jit(solution)/shard_map/part/pallas_call | solution.py:43
  75.5 7.2 %states.1 = (bf16[512,1024]{1,0:T(8,128)(2,1)}, bf16[512,1024]{1,0:T(8,128)(2,1)}, f32[8,128,128]{2,1,0:T(8,128)S(1)}, bf16[4,128,128]{2,1,0:T(8,128)(2,1)S(1)}) custom-call(s32[6]{0:T(128)S(1)} %stack.27._.places, bf16[256,1024]{1,0:T(8,128)(2,1)S(1)} %collective-permute-done.8.refs_0_, bf16[256,1024]{1,0:T(8,128)(2,1)S(1)} %collective-permute-done.10.refs_1_, ...), custom_call_target="tpu_custom_call" | custom-call | flops 2147483648 | bytes 63082496 | tf_op jit(solution)/shard_map/states/pallas_call | solution.py:43
  86.6 5.5 %collective-permute-done.15.come_ref = bf16[4,128,128]{2,1,0:T(8,128)(2,1)S(1)} collective-permute-done((bf16[4,128,128]{2,1,0:T(8,128)(2,1)S(1)}, bf16[4,128,128]{2,1,0:T(8,128)(2,1)S(1)}, u32[]{:S(2)}, u32[]{:S(2)}) %collective-permute-start.15) | collective-permute-done | bytes 131104 | tf_op jit(solution)/shard_map/ppermute | solution.py:733
  95.5 5.4 %later.2 = (bf16[512,512]{1,0:T(8,128)(2,1)S(1)}, bf16[512,512]{1,0:T(8,128)(2,1)S(1)}) custom-call(s32[6]{0:T(128)S(1)} %stack.27._.places, bf16[256,1024]{1,0:T(8,128)(2,1)S(1)} %collective-permute-done.8.refs_0_, bf16[256,1024]{1,0:T(8,128)(2,1)S(1)} %collective-permute-done.10.refs_1_, bf16[3,4096,1024]{2,1,0:T(8,128)(2,1)} %refs_2_.7, ...), custom_call_target="tpu_custom_call" | custom-call | flops 939524096 | bytes 32079872 | tf_op jit(solution)/shard_map/later/pallas_call | solution.py:43
  103.0 5.2 %heads.2 = (bf16[512,1024]{1,0:T(8,128)(2,1)S(1)}, bf16[256,1024]{1,0:T(8,128)(2,1)S(1)}, bf16[256,1024]{1,0:T(8,128)(2,1)S(1)}) custom-call(s32[6]{0:T(128)S(1)} %stack.27._.places, bf16[512,1024]{1,0:T(8,128)(2,1)} %get-tuple-element.96.refs_0_, bf16[512,1024]{1,0:T(8,128)(2,1)} %get-tuple-element.97.refs_1_, ...), custom_call_target="tpu_custom_call" | custom-call | flops 1 | bytes 1 | tf_op jit(solution)/shard_map/heads/pallas_call | solution.py:43
  108.2 1.6 collective-permute-start.20
  110.3 5.1 %later.3 = (bf16[512,512]{1,0:T(8,128)(2,1)S(1)}, bf16[512,512]{1,0:T(8,128)(2,1)S(1)}) custom-call(s32[6]{0:T(128)S(1)} %stack.27._.places, bf16[256,1024]{1,0:T(8,128)(2,1)S(1)} %collective-permute-done.8.refs_0_, bf16[256,1024]{1,0:T(8,128)(2,1)S(1)} %collective-permute-done.10.refs_1_, bf16[3,4096,1024]{2,1,0:T(8,128)(2,1)} %refs_2_.7, ...), custom_call_target="tpu_custom_call" | custom-call | flops 939524096 | bytes 32079872 | tf_op jit(solution)/shard_map/later/pallas_call | solution.py:43
  115.4 5.5 %heads.3 = (bf16[512,1024]{1,0:T(8,128)(2,1)S(1)}, bf16[512,1024]{1,0:T(8,128)(2,1)S(1)}, bf16[512,1024]{1,0:T(8,128)(2,1)S(1)}) custom-call(s32[6]{0:T(128)S(1)} %stack.27._.places, bf16[512,512]{1,0:T(8,128)(2,1)S(1)} %get-tuple-element.95.refs_0_, bf16[512,512]{1,0:T(8,128)(2,1)S(1)} %get-tuple-element.107.refs_1_, ...), custom_call_target="tpu_custom_call" | custom-call | flops 1 | bytes 1 | tf_op jit(solution)/shard_map/heads/pallas_call | solution.py:43
  120.9 1.6 collective-permute-start.24
  123.7 3.1 %sum_and_near.1 = (bf16[512,1024]{1,0:T(8,128)(2,1)S(1)}, bf16[512,1024]{1,0:T(8,128)(2,1)S(1)}) custom-call(s32[6]{0:T(128)S(1)} %stack.27._.places, bf16[512,1024]{1,0:T(8,128)(2,1)S(1)} %get-tuple-element.111.normed_ref, bf16[256,1024]{1,0:T(8,128)(2,1)S(1)} %collective-permute-done.20.x_ref, bf16[256,1024]{1,0:T(8,128)(2,1)S(1)} %collective-permute-done.21.y_ref, ...), custom_call_target="tpu_custom_call" | custom-call | flops 1 | bytes 1 | tf_op jit(solution)/shard_map/sum_and_near/pallas_call | solution.py:43
  128.2 18.8 %collective-permute-done.24.refs_0_.y_ref = bf16[512,1024]{1,0:T(8,128)(2,1)S(1)} collective-permute-done((bf16[512,1024]{1,0:T(8,128)(2,1)S(1)}, bf16[512,1024]{1,0:T(8,128)(2,1)S(1)}, u32[]{:S(2)}, u32[]{:S(2)}) %collective-permute-start.24) | collective-permute-done | bytes 1048608 | tf_op jit(solution)/shard_map/ppermute | solution.py:878
  147.1 1.5 collective-permute-done.25.refs_1_.x_ref
  148.6 2.2 %sum_pair.1 = (bf16[256,1024]{1,0:T(8,128)(2,1)S(1)}, bf16[256,1024]{1,0:T(8,128)(2,1)S(1)}) custom-call(s32[6]{0:T(128)S(1)} %stack.27._.places, bf16[512,1024]{1,0:T(8,128)(2,1)S(1)} %get-tuple-element.116.normed_ref, bf16[512,1024]{1,0:T(8,128)(2,1)S(1)} %collective-permute-done.25.refs_1_.x_ref, ...), custom_call_target="tpu_custom_call" | custom-call | flops 1 | bytes 1 | tf_op jit(solution)/shard_map/sum_pair/pallas_call | solution.py:43
  151.9 17.6 %collective-permute-done.22.refs_0_.refs_3_ = bf16[512,1024]{1,0:T(8,128)(2,1)S(1)} collective-permute-done((bf16[512,1024]{1,0:T(8,128)(2,1)S(1)}, bf16[512,1024]{1,0:T(8,128)(2,1)S(1)}, u32[]{:S(2)}, u32[]{:S(2)}) %collective-permute-start.22) | collective-permute-done | bytes 1048608 | tf_op jit(solution)/shard_map/ppermute | solution.py:881
  169.5 1.5 collective-permute-done.23.refs_1_.refs_2_
  171.1 2.0 %own_block.2.kept_ref = bf16[512,1024]{1,0:T(8,128)(2,1)S(1)} custom-call(s32[6]{0:T(128)S(1)} %stack.27._.places, bf16[512,1024]{1,0:T(8,128)(2,1)S(1)} %get-tuple-element.116.normed_ref, bf16[1024,4096]{1,0:T(8,128)(2,1)S(1)} %bitcast.7, bf16[512,1024]{1,0:T(8,128)(2,1)S(1)} %collective-permute-done.24.refs_0_.y_ref, ...), custom_call_target="tpu_custom_call" | custom-call | flops 1 | bytes 1 | tf_op jit(solution)/shard_map/own_block/pallas_call | solution.py:43
  173.1 2.9 %own_block.3.above_ref = bf16[1024,1024]{1,0:T(8,128)(2,1)} custom-call(s32[6]{0:T(128)S(1)} %stack.27._.places, bf16[512,1024]{1,0:T(8,128)(2,1)S(1)} %get-tuple-element.111.normed_ref, bf16[1024,4096]{1,0:T(8,128)(2,1)S(1)} %bitcast.7, bf16[512,1024]{1,0:T(8,128)(2,1)S(1)} %collective-permute-done.22.refs_0_.refs_3_, ...), custom_call_target="tpu_custom_call" | custom-call | flops 1 | bytes 1 | tf_op jit(solution)/shard_map/own_block/pallas_call | solution.py:43
  176.0 4.5 %collective-permute-done.26.a_ref = bf16[256,1024]{1,0:T(8,128)(2,1)S(1)} collective-permute-done((bf16[256,1024]{1,0:T(8,128)(2,1)S(1)}, bf16[256,1024]{1,0:T(8,128)(2,1)S(1)}, u32[]{:S(2)}, u32[]{:S(2)}) %collective-permute-start.26) | collective-permute-done | bytes 524320 | tf_op jit(solution)/shard_map/ppermute | solution.py:883
  (57 shorter events, 22.8 us)
Async XLA Ops:
  2.2 18.5 %collective-permute-start = (bf16[256,1024]{1,0:T(8,128)(2,1)}, bf16[256,1024]{1,0:T(8,128)(2,1)S(1)}, u32[]{:S(2)}, u32[]{:S(2)}) collective-permute-start(bf16[256,1024]{1,0:T(8,128)(2,1)} %get-tuple-element.70), channel_id=1, source_target_pairs={{0,1},{1,0},{2,3},{3,2},{4,5},{5,4},{6,7},{7,6},{8,9},{9,8},{10,11... | collective-permute-start | bytes 1572872 | tf_op jit(solution)/shard_map/ppermute | solution.py:742
  3.7 17.0 %collective-permute-start.1 = (bf16[256,1024]{1,0:T(8,128)(2,1)}, bf16[256,1024]{1,0:T(8,128)(2,1)S(1)}, u32[]{:S(2)}, u32[]{:S(2)}) collective-permute-start(bf16[256,1024]{1,0:T(8,128)(2,1)} %get-tuple-element.69), channel_id=1, source_target_pairs={{0,2},{1,3},{2,0},{3,1},{4,6},{5,7},{6,4},{7,5},{8,10},{9,11},{10,... | collective-permute-start | bytes 1572872 | tf_op jit(solution)/shard_map/ppermute | solution.py:742
  7.0 21.1 %collective-permute-start.2 = (bf16[256,1024]{1,0:T(8,128)(2,1)}, bf16[256,1024]{1,0:T(8,128)(2,1)S(1)}, u32[]{:S(2)}, u32[]{:S(2)}) collective-permute-start(bf16[256,1024]{1,0:T(8,128)(2,1)} %get-tuple-element.69), channel_id=1, source_target_pairs={{0,1},{1,0},{2,3},{3,2},{4,5},{5,4},{6,7},{7,6},{8,9},{9,8},{10,11... | collective-permute-start | bytes 1572872 | tf_op jit(solution)/shard_map/ppermute | solution.py:743
  7.6 22.4 %collective-permute-start.3 = (bf16[256,1024]{1,0:T(8,128)(2,1)}, bf16[256,1024]{1,0:T(8,128)(2,1)S(1)}, u32[]{:S(2)}, u32[]{:S(2)}) collective-permute-start(bf16[256,1024]{1,0:T(8,128)(2,1)} %get-tuple-element.70), channel_id=1, source_target_pairs={{0,2},{1,3},{2,0},{3,1},{4,6},{5,7},{6,4},{7,5},{8,10},{9,11},{10,... | collective-permute-start | bytes 1572872 | tf_op jit(solution)/shard_map/ppermute | solution.py:743
  20.8 4.5 %collective-permute-start.4 = (f32[8,128]{1,0:T(8,128)S(1)}, f32[8,128]{1,0:T(8,128)S(1)}, u32[]{:S(2)}, u32[]{:S(2)}) collective-permute-start(f32[8,128]{1,0:T(8,128)S(1)} %get-tuple-element.71.tail_ref), channel_id=1, source_target_pairs={{0,4},{4,0},{8,12},{12,8},{16,20},{20,16},{24,28},{28,24},{1,5},{5... | collective-permute-start | bytes 12296 | tf_op jit(solution)/shard_map/ppermute | solution.py:736
  22.1 21.4 %collective-permute-start.6 = (bf16[256,1024]{1,0:T(8,128)(2,1)S(1)}, bf16[256,1024]{1,0:T(8,128)(2,1)S(1)}, u32[]{:S(2)}, u32[]{:S(2)}) collective-permute-start(bf16[256,1024]{1,0:T(8,128)(2,1)S(1)} %collective-permute-done.refs_0_), channel_id=1, source_target_pairs={{0,2},{1,3},{2,0},{3,1},{4,6},{5,7},{6,4},{7,5},{8,10},{9,11},{10,... | collective-permute-start | bytes 1572872 | tf_op jit(solution)/shard_map/ppermute | solution.py:746
  23.7 19.9 %collective-permute-start.7 = (bf16[256,1024]{1,0:T(8,128)(2,1)S(1)}, bf16[256,1024]{1,0:T(8,128)(2,1)S(1)}, u32[]{:S(2)}, u32[]{:S(2)}) collective-permute-start(bf16[256,1024]{1,0:T(8,128)(2,1)S(1)} %collective-permute-done.1.refs_3_), channel_id=1, source_target_pairs={{0,1},{1,0},{2,3},{3,2},{4,5},{5,4},{6,7},{7,6},{8,9},{9,8},{10,11... | collective-permute-start | bytes 1572872 | tf_op jit(solution)/shard_map/ppermute | solution.py:746
  25.2 18.3 %collective-permute-start.11 = (f32[8,128]{1,0:T(8,128)S(1)}, f32[8,128]{1,0:T(8,128)S(1)}, u32[]{:S(2)}, u32[]{:S(2)}) collective-permute-start(f32[8,128]{1,0:T(8,128)S(1)} %add.10), channel_id=1, source_target_pairs={{16,24},{20,28},{17,25},{21,29},{18,26},{22,30},{19,27},{23,31}} | collective-permute-start | bytes 12296 | tf_op jit(solution)/shard_map/ppermute | solution.py:733
  30.0 26.8 %collective-permute-start.5 = (bf16[256,1024]{1,0:T(8,128)(2,1)S(1)}, bf16[256,1024]{1,0:T(8,128)(2,1)S(1)}, u32[]{:S(2)}, u32[]{:S(2)}) collective-permute-start(bf16[256,1024]{1,0:T(8,128)(2,1)S(1)} %get-tuple-element.82), channel_id=1, source_target_pairs={{0,1},{1,0},{2,3},{3,2},{4,5},{5,4},{6,7},{7,6},{8,9},{9,8},{10,11... | collective-permute-start | bytes 1572872 | tf_op jit(solution)/shard_map/ppermute | solution.py:748
  30.6 27.9 %collective-permute-start.9 = (bf16[256,1024]{1,0:T(8,128)(2,1)S(1)}, bf16[256,1024]{1,0:T(8,128)(2,1)S(1)}, u32[]{:S(2)}, u32[]{:S(2)}) collective-permute-start(bf16[256,1024]{1,0:T(8,128)(2,1)S(1)} %get-tuple-element.81), channel_id=1, source_target_pairs={{0,2},{1,3},{2,0},{3,1},{4,6},{5,7},{6,4},{7,5},{8,10},{9,11},{10,... | collective-permute-start | bytes 1572872 | tf_op jit(solution)/shard_map/ppermute | solution.py:749
  43.6 18.2 %collective-permute-start.12 = (bf16[256,1024]{1,0:T(8,128)(2,1)S(1)}, bf16[256,1024]{1,0:T(8,128)(2,1)S(1)}, u32[]{:S(2)}, u32[]{:S(2)}) collective-permute-start(bf16[256,1024]{1,0:T(8,128)(2,1)S(1)} %get-tuple-element.81), channel_id=1, source_target_pairs={{0,1},{1,0},{2,3},{3,2},{4,5},{5,4},{6,7},{7,6},{8,9},{9,8},{10,11... | collective-permute-start | bytes 1572872 | tf_op jit(solution)/shard_map/ppermute | solution.py:761
  45.1 18.6 %collective-permute-start.13 = (bf16[256,1024]{1,0:T(8,128)(2,1)S(1)}, bf16[256,1024]{1,0:T(8,128)(2,1)S(1)}, u32[]{:S(2)}, u32[]{:S(2)}) collective-permute-start(bf16[256,1024]{1,0:T(8,128)(2,1)S(1)} %get-tuple-element.82), channel_id=1, source_target_pairs={{0,2},{1,3},{2,0},{3,1},{4,6},{5,7},{6,4},{7,5},{8,10},{9,11},{10,... | collective-permute-start | bytes 1572872 | tf_op jit(solution)/shard_map/ppermute | solution.py:761
  56.8 18.6 %copy-start = (f32[8,128,128]{2,1,0:T(8,128)}, f32[8,128,128]{2,1,0:T(8,128)S(1)}, u32[]{:S(2)}) copy-start(f32[8,128,128]{2,1,0:T(8,128)S(1)} %get-tuple-element.106.refs_8_.refs_9_) | copy-start | bytes 1572868
  56.8 18.6 %collective-permute-start.8 = (bf16[256,1024]{1,0:T(8,128)(2,1)S(1)}, bf16[256,1024]{1,0:T(8,128)(2,1)S(1)}, u32[]{:S(2)}, u32[]{:S(2)}) collective-permute-start(bf16[256,1024]{1,0:T(8,128)(2,1)S(1)} %collective-permute-done.5.refs_0_), channel_id=1, source_target_pairs={{0,2},{1,3},{2,0},{3,1},{4,6},{5,7},{6,4},{7,5},{8,10},{9,11},{10,... | collective-permute-start | bytes 1572872 | tf_op jit(solution)/shard_map/ppermute | solution.py:775
  58.4 17.0 %collective-permute-start.10 = (bf16[256,1024]{1,0:T(8,128)(2,1)S(1)}, bf16[256,1024]{1,0:T(8,128)(2,1)S(1)}, u32[]{:S(2)}, u32[]{:S(2)}) collective-permute-start(bf16[256,1024]{1,0:T(8,128)(2,1)S(1)} %collective-permute-done.9.refs_3_), channel_id=1, source_target_pairs={{0,1},{1,0},{2,3},{3,2},{4,5},{5,4},{6,7},{7,6},{8,9},{9,8},{10,11... | collective-permute-start | bytes 1572872 | tf_op jit(solution)/shard_map/ppermute | solution.py:775
  75.4 8.5 %copy-start.1 = (f32[8,128,128]{2,1,0:T(8,128)S(1)}, f32[8,128,128]{2,1,0:T(8,128)}, u32[]{:S(2)}) copy-start(f32[8,128,128]{2,1,0:T(8,128)} %prior_ref.3) | copy-start | bytes 1572868
  82.6 1.3 collective-permute-start.14
  84.6 7.4 %collective-permute-start.15 = (bf16[4,128,128]{2,1,0:T(8,128)(2,1)S(1)}, bf16[4,128,128]{2,1,0:T(8,128)(2,1)S(1)}, u32[]{:S(2)}, u32[]{:S(2)}) collective-permute-start(bf16[4,128,128]{2,1,0:T(8,128)(2,1)S(1)} %get-tuple-element.92), channel_id=1, source_target_pairs={{0,8},{4,12},{1,9},{5,13},{2,10},{6,14},{3,11},{7,15}} | collective-permute-start | bytes 393224 | tf_op jit(solution)/shard_map/ppermute | solution.py:733
  85.9 14.9 %collective-permute-start.16 = (bf16[4,128,128]{2,1,0:T(8,128)(2,1)S(1)}, bf16[4,128,128]{2,1,0:T(8,128)(2,1)S(1)}, u32[]{:S(2)}, u32[]{:S(2)}) collective-permute-start(bf16[4,128,128]{2,1,0:T(8,128)(2,1)S(1)} %get-tuple-element.98), channel_id=1, source_target_pairs={{16,24},{20,28},{17,25},{21,29},{18,26},{22,30},{19,27},{23,31}} | collective-permute-start | bytes 393224 | tf_op jit(solution)/shard_map/ppermute | solution.py:733
  92.7 8.2 %collective-permute-start.17 = (bf16[4,128,128]{2,1,0:T(8,128)(2,1)S(1)}, bf16[4,128,128]{2,1,0:T(8,128)(2,1)S(1)}, u32[]{:S(2)}, u32[]{:S(2)}) collective-permute-start(bf16[4,128,128]{2,1,0:T(8,128)(2,1)S(1)} %pass_on.1), channel_id=1, source_target_pairs={{8,24},{12,28},{9,25},{13,29},{10,26},{14,30},{11,27},{15,31}} | collective-permute-start | bytes 393224 | tf_op jit(solution)/shard_map/ppermute | solution.py:733
  94.0 6.9 %collective-permute-start.18 = (bf16[4,128,128]{2,1,0:T(8,128)(2,1)S(1)}, bf16[4,128,128]{2,1,0:T(8,128)(2,1)S(1)}, u32[]{:S(2)}, u32[]{:S(2)}) collective-permute-start(bf16[4,128,128]{2,1,0:T(8,128)(2,1)S(1)} %pass_on.1), channel_id=1, source_target_pairs={{8,16},{12,20},{9,17},{13,21},{10,18},{14,22},{11,19},{15,23}} | collective-permute-start | bytes 393224 | tf_op jit(solution)/shard_map/ppermute | solution.py:733
  95.5 7.5 %slice-start = ((s8[8388608]{0:T(1024)(128)(4,1)}), s8[4194304]{0:T(1024)(128)(4,1)S(1)}, s32[]{:S(2)}) async-start(s8[8388608]{0:T(1024)(128)(4,1)} %bitcast.6), calls=%async_computation | async-start | bytes 8388608
  95.5 7.5 %slice-start.1 = ((s8[8388608]{0:T(1024)(128)(4,1)}), s8[4194304]{0:T(1024)(128)(4,1)S(1)}, s32[]{:S(2)}) async-start(s8[8388608]{0:T(1024)(128)(4,1)} %bitcast.6), calls=%async_computation.1 | async-start | bytes 8388608
  101.6 1.4 collective-permute-start.19
  108.2 14.8 %collective-permute-start.20 = (bf16[256,1024]{1,0:T(8,128)(2,1)S(1)}, bf16[256,1024]{1,0:T(8,128)(2,1)S(1)}, u32[]{:S(2)}, u32[]{:S(2)}) collective-permute-start(bf16[256,1024]{1,0:T(8,128)(2,1)S(1)} %get-tuple-element.112), channel_id=1, source_target_pairs={{0,2},{1,3},{2,0},{3,1},{4,6},{5,7},{6,4},{7,5},{8,10},{9,11},{10,... | collective-permute-start | bytes 1572872 | tf_op jit(solution)/shard_map/ppermute | solution.py:874
  109.8 13.9 %collective-permute-start.21 = (bf16[256,1024]{1,0:T(8,128)(2,1)S(1)}, bf16[256,1024]{1,0:T(8,128)(2,1)S(1)}, u32[]{:S(2)}, u32[]{:S(2)}) collective-permute-start(bf16[256,1024]{1,0:T(8,128)(2,1)S(1)} %get-tuple-element.113), channel_id=1, source_target_pairs={{0,1},{1,0},{2,3},{3,2},{4,5},{5,4},{6,7},{7,6},{8,9},{9,8},{10,11... | collective-permute-start | bytes 1572872 | tf_op jit(solution)/shard_map/ppermute | solution.py:874
  120.9 26.1 %collective-permute-start.24 = (bf16[512,1024]{1,0:T(8,128)(2,1)S(1)}, bf16[512,1024]{1,0:T(8,128)(2,1)S(1)}, u32[]{:S(2)}, u32[]{:S(2)}) collective-permute-start(bf16[512,1024]{1,0:T(8,128)(2,1)S(1)} %get-tuple-element.117), channel_id=1, source_target_pairs={{0,1},{1,0},{2,3},{3,2},{4,5},{5,4},{6,7},{7,6},{8,9},{9,8},{10,11... | collective-permute-start | bytes 3145736 | tf_op jit(solution)/shard_map/ppermute | solution.py:878
  122.5 26.1 %collective-permute-start.25 = (bf16[512,1024]{1,0:T(8,128)(2,1)S(1)}, bf16[512,1024]{1,0:T(8,128)(2,1)S(1)}, u32[]{:S(2)}, u32[]{:S(2)}) collective-permute-start(bf16[512,1024]{1,0:T(8,128)(2,1)S(1)} %get-tuple-element.119), channel_id=1, source_target_pairs={{0,2},{1,3},{2,0},{3,1},{4,6},{5,7},{6,4},{7,5},{8,10},{9,11},{10,... | collective-permute-start | bytes 3145736 | tf_op jit(solution)/shard_map/ppermute | solution.py:878
  126.9 42.7 %collective-permute-start.22 = (bf16[512,1024]{1,0:T(8,128)(2,1)S(1)}, bf16[512,1024]{1,0:T(8,128)(2,1)S(1)}, u32[]{:S(2)}, u32[]{:S(2)}) collective-permute-start(bf16[512,1024]{1,0:T(8,128)(2,1)S(1)} %get-tuple-element.114), channel_id=1, source_target_pairs={{0,1},{1,0},{2,3},{3,2},{4,5},{5,4},{6,7},{7,6},{8,9},{9,8},{10,11... | collective-permute-start | bytes 3145736 | tf_op jit(solution)/shard_map/ppermute | solution.py:881
  127.2 43.9 %collective-permute-start.23 = (bf16[512,1024]{1,0:T(8,128)(2,1)S(1)}, bf16[512,1024]{1,0:T(8,128)(2,1)S(1)}, u32[]{:S(2)}, u32[]{:S(2)}) collective-permute-start(bf16[512,1024]{1,0:T(8,128)(2,1)S(1)} %get-tuple-element.115), channel_id=1, source_target_pairs={{0,2},{1,3},{2,0},{3,1},{4,6},{5,7},{6,4},{7,5},{8,10},{9,11},{10,... | collective-permute-start | bytes 3145736 | tf_op jit(solution)/shard_map/ppermute | solution.py:881
  150.8 29.7 %collective-permute-start.26 = (bf16[256,1024]{1,0:T(8,128)(2,1)S(1)}, bf16[256,1024]{1,0:T(8,128)(2,1)S(1)}, u32[]{:S(2)}, u32[]{:S(2)}) collective-permute-start(bf16[256,1024]{1,0:T(8,128)(2,1)S(1)} %get-tuple-element.121), channel_id=1, source_target_pairs={{0,2},{1,3},{2,0},{3,1},{4,6},{5,7},{6,4},{7,5},{8,10},{9,11},{10,... | collective-permute-start | bytes 1572872 | tf_op jit(solution)/shard_map/ppermute | solution.py:883
  151.4 29.2 %collective-permute-start.27 = (bf16[256,1024]{1,0:T(8,128)(2,1)S(1)}, bf16[256,1024]{1,0:T(8,128)(2,1)S(1)}, u32[]{:S(2)}, u32[]{:S(2)}) collective-permute-start(bf16[256,1024]{1,0:T(8,128)(2,1)S(1)} %get-tuple-element.122), channel_id=1, source_target_pairs={{0,1},{1,0},{2,3},{3,2},{4,5},{5,4},{6,7},{7,6},{8,9},{9,8},{10,11... | collective-permute-start | bytes 1572872 | tf_op jit(solution)/shard_map/ppermute | solution.py:883
  (1 other events, 0.8 us)

commit v13 on v12

--- a/solution.py
+++ b/solution.py
@@ -51,7 +51,7 @@
             scratch_shapes=list(scratch),
         ),
         input_output_aliases=aliases or {},
-        compiler_params=pltpu.CompilerParams(vmem_limit_bytes=(24 if light else 32) * MIB),
+        compiler_params=pltpu.CompilerParams(vmem_limit_bytes=(16 if light else 24) * MIB),
         cost_estimate=pl.CostEstimate(
             flops=1 if light else flops, bytes_accessed=1 if light else moved, transcendentals=0
         ),
@@ -161,7 +161,10 @@
 def first_kernel(layout, added, chunk, group, size, _, *refs):
     count = sum(layout)
     x_refs, w_refs, refs = refs[:count], refs[count : count + len(layout)], refs[count + len(layout) :]
-    along_ref, inside_ref, q_ref, within_ref, state_ref, held = refs[-6:]
+    passed_refs, held = refs[added + 5 : -1], refs[-1]
+    along_ref, inside_ref, q_ref, within_ref, state_ref = refs[added : added + 5]
+    for ref in passed_refs:
+        ref[...] = w_refs[0][1:]
     j = pl.program_id(0)
     rows = held.shape[1]
 
@@ -225,11 +228,13 @@
         + [pl.BlockSpec((3, rows, cols), lambda j, o: (0, 0, j)) for _ in before]
         + [fixed((heads, rows)), fixed((rows, heads))],
         (
-            pltpu.HBM((rows, heads * size), BF16),
-            pltpu.HBM((rows, heads * size), BF16),
+            struct((rows, heads * size), BF16),
+            struct((rows, heads * size), BF16),
             struct((heads, size, size), F32),
+            *[struct((2, depth, heads * size), BF16) for _ in before],
         ),
-        [wide, wide, pl.BlockSpec((group, size, size), lambda j, o: (j, 0, 0))],
+        [wide, wide, pl.BlockSpec((group, size, size), lambda j, o: (j, 0, 0))]
+        + [pl.BlockSpec((2, depth, cols), lambda j, o: (0, 0, j)) for _ in before],
         2 * rows * 3 * heads * size * depth * len(pieces),
         scratch=[pltpu.VMEM((len(pieces), rows, depth), BF16)],
     )
@@ -312,69 +317,43 @@
     return out if apart else out[0]
 
 
-def state_kernel(group, size, places, *refs):
-    xa, xb, wk, wv, acc_k, acc_v, end_ref, half_ref, state_ref = refs[:9]
-    k_ref, v_ref, out_ref, sent_ref, held = refs[9:]
-    j = pl.program_id(0)
-    rows = held.shape[0]
-
-    @pl.when(j == 0)
-    def _():
-        held[: rows // 2, :] = xa[...]
-        held[rows // 2 :, :] = xb[...]
-
-    k_all = (acc_k[0] + dot(held[...], wk[0])).astype(BF16)
-    v_all = (acc_v[0] + dot(held[...], wv[0])).astype(BF16)
-    k_ref[...] = k_all
-    v_ref[...] = v_all
-    ends = []
-    for a in range(group):
-        head = pl.ds(j * group + a, 1)
-        lanes = slice(a * size, (a + 1) * size)
-        scaled = (k_all[:, lanes].T.astype(F32) * end_ref[head, :]).astype(BF16)
-        end = half_ref[head, :] * state_ref[a] + dot(scaled, v_all[:, lanes])
-        out_ref[a] = end
-        ends.append(end.astype(BF16))
-    half = pl.num_programs(0) // 2
-
-    @pl.when(jnp.where(places[4] == 0, j >= half, j < half))
-    def _():
-        for a in range(group):
-            sent_ref[a] = ends[a]
-
-
-def state_call(places, far, w_qkv, acc, to_end, half_fade, state, group):
+def state_kernel(places, xa, xb, w_ref, acc_ref, end_ref, half_ref, state_ref, *refs):
+    k_ref, v_ref, out_ref, sent_ref, held = refs
+    tall = xa.shape[0]
+    heads, size = state_ref.shape[0], state_ref.shape[1]
+    held[:tall, :] = xa[...]
+    held[tall:, :] = xb[...]
+    for pair in range(heads // 2):
+        cols = slice(2 * pair * size, 2 * (pair + 1) * size)
+        keys = (acc_ref[0, :, cols] + dot(held[...], w_ref[0, :, cols])).astype(BF16)
+        values = (acc_ref[1, :, cols] + dot(held[...], w_ref[1, :, cols])).astype(BF16)
+        k_ref[:, cols] = keys
+        v_ref[:, cols] = values
+        for a in range(2):
+            head = 2 * pair + a
+            lanes = slice(a * size, (a + 1) * size)
+            scaled = (keys[:, lanes].T.astype(F32) * end_ref[head : head + 1, tall * 2 :]).astype(BF16)
+            end = half_ref[head : head + 1, :] * state_ref[head] + dot(scaled, values[:, lanes])
+            out_ref[head] = end
+
+            @pl.when(places[4] != 2 * head // heads)
+            def _(head=head, end=end):
+                sent_ref[head % (heads // 2)] = end.astype(BF16)
+
+
+def state_call(places, far, w_far, acc, to_end, half_fade, state):
     _, rows, width = acc.shape
     heads, size = state.shape[0], state.shape[1]
     depth = far[0].shape[1]
-    cols = group * size
-    wide = pl.BlockSpec((rows, cols), lambda j, o: (0, j))
-    small = pl.BlockSpec((group, size, size), lambda j, o: (j, 0, 0))
-    half = heads // group // 2
-
-    def sent_block(j, o):
-        return jnp.where(o[4] == 0, jnp.maximum(j - half, 0), jnp.minimum(j, half - 1)), 0, 0
-
-    return call(
-        functools.partial(state_kernel, group, size),
-        "states",
-        heads // group,
-        places,
-        (*far, w_qkv, w_qkv, acc, acc, to_end, half_fade, state),
-        [fixed(far[0].shape), fixed(far[1].shape)]
-        + [pl.BlockSpec((1, depth, cols), lambda j, o, c=c: (c, o[3], j)) for c in (1, 2)]
-        + [pl.BlockSpec((1, rows, cols), lambda j, o, c=c: (c, 0, j)) for c in (0, 1)]
-        + [pl.BlockSpec((heads, rows), lambda j, o: (0, 1)), fixed(half_fade.shape), small],
-        (
-            pltpu.HBM((rows, width), BF16),
-            pltpu.HBM((rows, width), BF16),
-            struct(state.shape, F32),
-            struct((heads // 2, size, size), BF16),
-        ),
-        [wide, wide, small, pl.BlockSpec((group, size, size), sent_block)],
-        4 * rows * depth * width,
-        scratch=[pltpu.VMEM((rows, depth), BF16)],
-    )
+    ins = [near(x) for x in (*far, w_far, acc)] + [to_end, half_fade, near(state)]
+    outs = (
+        struct((rows, width), BF16),
+        struct((rows, width), BF16),
+        struct(state.shape, F32),
+        struct((heads // 2, size, size), BF16),
+    )
+    scratch = [pltpu.VMEM((rows, depth), BF16)]
+    return small_call(state_kernel, "states", places, ins, outs, 16, scratch)
 
 
 def later_kernel(first, chunk, group, size, _, *refs):
@@ -484,14 +463,15 @@
         passed_ref[i] = jnp.where(core == 0, later, state).astype(BF16)
 
 
-def small_call(kernel, name, places, ins, outs):
+def small_call(kernel, name, places, ins, outs, limit=4, scratch=()):
     whole = pl.BlockSpec(memory_space=pltpu.VMEM)
     return pl.pallas_call(
         kernel,
         out_shape=tuple(outs),
         in_specs=[pl.BlockSpec(memory_space=pltpu.SMEM)] + [whole] * len(ins),
         out_specs=[whole] * len(outs),
-        compiler_params=pltpu.CompilerParams(vmem_limit_bytes=4 * MIB),
+        scratch_shapes=list(scratch),
+        compiler_params=pltpu.CompilerParams(vmem_limit_bytes=limit * MIB),
         cost_estimate=pl.CostEstimate(flops=1, bytes_accessed=1, transcendentals=0),
         name=name,
     )(places, *ins)
@@ -520,31 +500,48 @@
 WHOLE = pl.BlockSpec(memory_space=pltpu.VMEM)
 
 
+def normalise(core, q_refs, within_refs, here_ref, there_ref, rows, out_ref):
+    share, size = here_ref.shape[0], here_ref.shape[1]
+    ones = jnp.ones((size, size), BF16)
+    for a in range(2 * share):
+        part, at = divmod(a, 2 * share // len(q_refs))
+        here = slice(at * size, (at + 1) * size)
+        entering = jnp.where(core == a // share, here_ref[a % share], there_ref[a % share])
+        seen = dot(q_refs[part][rows, here], entering)
+        combined = within_refs[part][rows, here].astype(F32) + seen
+        square = combined * combined
+        high = square.astype(BF16)
+        low = (square - high.astype(F32)).astype(BF16)
+        power = (dot(high, ones) + dot(low, ones)) * (1.0 / size)
+        out_ref[:, a * size : (a + 1) * size] = (combined * lax.rsqrt(power + 1e-06)).astype(BF16)
+
+
+def far_kernel(places, q_ref, within_ref, here_ref, there_ref, w_ref, normed_ref, *out_refs):
+    tall, width = out_refs[0].shape
+    for p, out_ref in enumerate(out_refs):
+        rows = slice(p * tall, (p + 1) * tall)
+        normed = normed_ref.at[rows]
+        normalise(places[4], (q_ref,), (within_ref,), here_ref, there_ref, rows, normed)
+        out_ref[...] = dot(normed[...], columns(w_ref, places[3], width)).astype(BF16)
+
+
+def far_call(places, q, within, entering, w_out, width):
+    out = struct((q.shape[0] // 2, width), BF16)
+    ins = (near(q), near(within), *[near(e) for e in entering], w_out)
+    return small_call(far_kernel, "heads_far", places, ins, (struct(q.shape, BF16), out, out), 8)
+
+
 def head_kernel(count, blocks, places, *refs):
     q_refs, within_refs, refs = refs[:count], refs[count : 2 * count], refs[2 * count :]
     here_ref, there_ref, w_ref, normed_ref = refs[:4]
     out_refs, held = refs[4:6], refs[6]
-    share, size = here_ref.shape[0], here_ref.shape[1]
-    tall, width = out_refs[0].shape
+    width = out_refs[0].shape[1]
     step = pl.program_id(0)
     for p, out_ref in enumerate(out_refs):
 
         @pl.when(step == p)
         def _(p=p, out_ref=out_ref):
-            ones = jnp.ones((size, size), BF16)
-            for a in range(2 * share):
-                part, at = divmod(a, 2 * share // count)
-                here = slice(at * size, (at + 1) * size)
-                ours = places[4] == a // share
-                entering = jnp.where(ours, here_ref[a % share], there_ref[a % share])
-                seen = dot(q_refs[part][:, here], entering)
-                combined = within_refs[part][:, here].astype(F32) + seen
-                square = combined * combined
-                high = square.astype(BF16)
-                low = (square - high.astype(F32)).astype(BF16)
-                power = (dot(high, ones) + dot(low, ones)) * (1.0 / size)
-                lanes = slice(a * size, (a + 1) * size)
-                held[p, :, lanes] = (combined * lax.rsqrt(power + 1e-06)).astype(BF16)
+            normalise(places[4], q_refs, within_refs, here_ref, there_ref, slice(None), held.at[p])
             normed_ref[...] = held[p]
             out_ref[...] = dot(held[p], columns(w_ref, places[blocks[0]], width)).astype(BF16)
 
@@ -737,7 +734,7 @@
         return other, tail + other, hop(tail + other, (2, 3)) if n_chips == 4 else None
 
     if square:
-        tokens = stay(tokens)
+        tokens, w_qkv = stay(tokens), stay(w_qkv)
         q0, q1 = cut_call(tokens, 0, 1)
         x0, y1 = over_x(q0), over_y(q1)
         x1, y0 = over_x(after(q1, tail)), over_y(after(q0, tail))
@@ -759,7 +756,7 @@
         )
         earlier = (fy0, fx1, acc_a) if tail_below is None else (fy0, fx1, acc_a, tail_below)
         x3, y2 = over_x(after(q3, *earlier)), over_y(after(q2, *earlier))
-        query_a, within_a, state = first_call(
+        query_a, within_a, state, w_far = first_call(
             places,
             (3,),
             [(fy0, fx1)],
@@ -786,9 +783,7 @@
         )
         far = (fy2, fx3)
         middle = state
-        k, v, state, sent = state_call(
-            places, far, w_qkv, acc_kv, to_end, half_fade, middle, group
-        )
+        k, v, state, sent = state_call(places, far, w_far, acc_kv, to_end, half_fade, middle)
     else:
         tail_other, tail_chip, tail_below = chip_tails(tail)
         gathered = lax.all_gather(tokens, "head", axis=1, tiled=True)
@@ -799,8 +794,8 @@
     tails = (tail, tail_other)
 
     def scores_of_later(half, *earlier):
-        start = stay(after(middle, *earlier))
-        ins = (far, w_qkv, stay(acc_q), stay(k), stay(v), along, inside, down, start)
+        start = after(middle, *earlier)
+        ins = (far, w_qkv, stay(acc_q), k, v, along, inside, down, start)
         return later_call(places, *ins, quarter, group, half)
 
     if square and n_chips == 4:
@@ -867,9 +862,7 @@
 
     if n_chips != 4:
         query_b, within_b = scores_of_later(0)
-    na, far0, far1 = head_call(
-        places, (3,), (stay(query_a),), (stay(within_a),), entering, w_out, width
-    )
+    na, far0, far1 = far_call(places, query_a, within_a, entering, w_out, width)
     query_c, within_c = scores_of_later(1, na)
     far0, far1 = over_x(far0), over_y(far1)
     nb, by_x2, by_y2 = head_call(

time: 182 us -> 178 us (0.978)
  Pallas kernels: 93 us -> 89.1 us
    pallas_call x17 -> x15, Pallas kernels: 91.1 us -> 78.4 us  [call(): pl.pallas_call(kernel, out_shape=tuple(outs), grid_spec=pltpu.PrefetchSca...]
    pallas_call x3 -> x5, Pallas kernels: 1.9 us -> 10.8 us  [small_call(): pl.pallas_call(kernel, out_shape=tuple(outs), in_specs=[pl.BlockSpec(memo...]
  transfers between devices with their start and end apart: 28 -> 28, of which waited for: 13 -> 12; matrix products, arithmetic and copies ran while one was open for 0% -> 0% of each run, Pallas kernels for 42% -> 43%
where the time goes in v13:
time: 178 us
  Pallas kernels  89.1 us (50%)
  waiting for transfers between devices  62.2 us (35%)
  starting transfers between devices  25.3 us (14%)
    pallas_call x15, Pallas kernels, call(): pl.pallas_call(kernel, out_shape=tuple(outs), grid_spec=pltpu.PrefetchSca...  78.4 us
    ppermute x2, waiting for transfers between devices, local(): by_x2, by_y2 = (over_x(by_x2), over_y(by_y2))  20.3 us
    ppermute x2, waiting for transfers between devices, local(): by_x, by_y = (over_x(by_x), over_y(by_y))  19.3 us
    pallas_call x5, Pallas kernels, small_call(): pl.pallas_call(kernel, out_shape=tuple(outs), in_specs=[pl.BlockSpec(memo...  10.8 us
    ppermute x5, waiting for transfers between devices, hop(): return lax.ppermute(x, 'seq', perm=perm)  5.48 us
    ppermute x5, starting transfers between devices, hop(): return lax.ppermute(x, 'seq', perm=perm)  5.39 us
    ppermute x2, waiting for transfers between devices, local(): sum3, sum2 = (over_x(sum3), over_y(sum2))  4.56 us
    ppermute x2, waiting for transfers between devices, local(): x3, y2 = (over_x(after(q3, *earlier)), over_y(after(q2, *earlier)))  4.44 us
  transfers between devices with their start and end apart: 28, of which 12 were waited for; matrix products, arithmetic and copies ran while one was open for 0% of the time, Pallas kernels for 43%

profile of v13, /device:TPU:8, one launch (start us, length us, event | category | flops | bytes accessed | tf_op | source)
XLA Modules:
  0.0 177.8 jit_solution(17810117074706213287)
XLA Ops:
  0.0 2.2 %cut.2 = (bf16[256,1024]{1,0:T(8,128)(2,1)}, bf16[256,1024]{1,0:T(8,128)(2,1)}) custom-call(s32[1]{0:T(128)} %constant.29.clone.1._, bf16[1024,1024]{1,0:T(8,128)(2,1)} %x_ref.4), custom_call_target="tpu_custom_call" | custom-call | flops 1 | bytes 3145728 | tf_op jit(solution)/shard_map/cut/pallas_call | solution.py:43
  2.2 1.5 collective-permute-start
  3.7 1.5 collective-permute-start.1
  8.2 12.5 %own_part.1.refs_6_ = f32[3,1024,1024]{2,1,0:T(8,128)} custom-call(s32[6]{0:T(128)S(1)} %stack.27._.places, bf16[1024,1024]{1,0:T(8,128)(2,1)} %x_ref.4, bf16[3,4096,1024]{2,1,0:T(8,128)(2,1)} %refs_2_.5), custom_call_target="tpu_custom_call" | custom-call | flops 6442450944 | bytes 39845888 | tf_op jit(solution)/shard_map/own_part/pallas_call | solution.py:43
  22.1 1.6 collective-permute-start.6
  23.7 1.5 collective-permute-start.7
  25.8 2.4 %collective-permute-done.2.refs_1_ = bf16[256,1024]{1,0:T(8,128)(2,1)S(1)} collective-permute-done((bf16[256,1024]{1,0:T(8,128)(2,1)}, bf16[256,1024]{1,0:T(8,128)(2,1)S(1)}, u32[]{:S(2)}, u32[]{:S(2)}) %collective-permute-start.2) | collective-permute-done | bytes 524320 | tf_op jit(solution)/shard_map/ppermute | solution.py:740
  28.2 1.9 %collective-permute-done.3.refs_2_ = bf16[256,1024]{1,0:T(8,128)(2,1)S(1)} collective-permute-done((bf16[256,1024]{1,0:T(8,128)(2,1)}, bf16[256,1024]{1,0:T(8,128)(2,1)S(1)}, u32[]{:S(2)}, u32[]{:S(2)}) %collective-permute-start.3) | collective-permute-done | bytes 524320 | tf_op jit(solution)/shard_map/ppermute | solution.py:740
  30.0 1.5 collective-permute-start.9
  32.1 11.5 %part.2.refs_3_ = f32[3,512,1024]{2,1,0:T(8,128)S(1)} custom-call(s32[6]{0:T(128)S(1)} %stack.27._.places, bf16[256,1024]{1,0:T(8,128)(2,1)S(1)} %collective-permute-done.refs_0_, bf16[256,1024]{1,0:T(8,128)(2,1)S(1)} %collective-permute-done.2.refs_1_, bf16[256,1024]{1,0:T(8,128)(2,1)S(1)} %collective-permute-done.3.refs_2_, ...), custom_call_target="tpu_custom_call" | custom-call | flops 6442450944 | bytes 71303168 | tf_op jit(solution)/shard_map/part/pallas_call | solution.py:43
  43.6 1.6 collective-permute-start.12
  45.6 11.5 %first.1 = (bf16[512,1024]{1,0:T(8,128)(2,1)S(1)}, bf16[512,1024]{1,0:T(8,128)(2,1)S(1)}, f32[8,128,128]{2,1,0:T(8,128)S(1)}, bf16[2,1024,1024]{2,1,0:T(8,128)(2,1)S(1)}) custom-call(s32[6]{0:T(128)S(1)} %stack.27._.places, bf16[256,1024]{1,0:T(8,128)(2,1)S(1)} %collective-permute-done.6.refs_0_, bf16[256,1024]{1,0:T(8,128)(2,1)S(1)} %collective-permute-done.7.refs_1_, ...), custom_call_target="tpu_custom_call" | custom-call | flops 3221225472 | bytes 39387136 | tf_op jit(solution)/shard_map/first/pallas_call | solution.py:43
  57.2 1.6 collective-permute-start.8
  59.3 2.6 %collective-permute-done.12.refs_1_ = bf16[256,1024]{1,0:T(8,128)(2,1)S(1)} collective-permute-done((bf16[256,1024]{1,0:T(8,128)(2,1)S(1)}, bf16[256,1024]{1,0:T(8,128)(2,1)S(1)}, u32[]{:S(2)}, u32[]{:S(2)}) %collective-permute-start.12) | collective-permute-done | bytes 524320 | tf_op jit(solution)/shard_map/ppermute | solution.py:758
  61.9 1.9 %collective-permute-done.13.refs_2_ = bf16[256,1024]{1,0:T(8,128)(2,1)S(1)} collective-permute-done((bf16[256,1024]{1,0:T(8,128)(2,1)S(1)}, bf16[256,1024]{1,0:T(8,128)(2,1)S(1)}, u32[]{:S(2)}, u32[]{:S(2)}) %collective-permute-start.13) | collective-permute-done | bytes 524320 | tf_op jit(solution)/shard_map/ppermute | solution.py:758
  63.7 11.7 %part.3 = (f32[1,512,1024]{2,1,0:T(8,128)}, f32[2,512,1024]{2,1,0:T(8,128)S(1)}) custom-call(s32[6]{0:T(128)S(1)} %stack.27._.places, bf16[256,1024]{1,0:T(8,128)(2,1)S(1)} %collective-permute-done.5.refs_0_, bf16[256,1024]{1,0:T(8,128)(2,1)S(1)} %collective-permute-done.12.refs_1_, bf16[256,1024]{1,0:T(8,128)(2,1)S(1)} %collective-permute-done.13.refs_2_, ...), custom_call_target="tpu_custom_call" | custom-call | flops 6442450944 | bytes 71303168 | tf_op jit(solution)/shard_map/part/pallas_call | solution.py:43
  75.4 5.2 %states.1 = (bf16[512,1024]{1,0:T(8,128)(2,1)S(1)}, bf16[512,1024]{1,0:T(8,128)(2,1)S(1)}, f32[8,128,128]{2,1,0:T(8,128)S(1)}, bf16[4,128,128]{2,1,0:T(8,128)(2,1)S(1)}) custom-call(s32[6]{0:T(128)S(1)} %stack.27._.places, bf16[256,1024]{1,0:T(8,128)(2,1)S(1)} %collective-permute-done.8.xa.refs_0_, bf16[256,1024]{1,0:T(8,128)(2,1)S(1)} %collective-permute-done.10.xb.refs_1_, ...), custom_call_target="tpu_custom_call" | custom-call | flops 1 | bytes 1 | tf_op jit(solution)/shard_map/states/pallas_call | solution.py:468
  84.7 5.5 %collective-permute-done.15.come_ref = bf16[4,128,128]{2,1,0:T(8,128)(2,1)S(1)} collective-permute-done((bf16[4,128,128]{2,1,0:T(8,128)(2,1)S(1)}, bf16[4,128,128]{2,1,0:T(8,128)(2,1)S(1)}, u32[]{:S(2)}, u32[]{:S(2)}) %collective-permute-start.15) | collective-permute-done | bytes 131104 | tf_op jit(solution)/shard_map/ppermute | solution.py:730
  93.6 5.2 %later.2 = (bf16[512,512]{1,0:T(8,128)(2,1)S(1)}, bf16[512,512]{1,0:T(8,128)(2,1)S(1)}) custom-call(s32[6]{0:T(128)S(1)} %stack.27._.places, bf16[256,1024]{1,0:T(8,128)(2,1)S(1)} %collective-permute-done.8.xa.refs_0_, bf16[256,1024]{1,0:T(8,128)(2,1)S(1)} %collective-permute-done.10.xb.refs_1_, bf16[3,4096,1024]{2,1,0:T(8,128)(2,1)} %refs_2_.5, ...), custom_call_target="tpu_custom_call" | custom-call | flops 939524096 | bytes 32079872 | tf_op jit(solution)/shard_map/later/pallas_call | solution.py:43
  100.9 3.6 %heads_far.1 = (bf16[512,1024]{1,0:T(8,128)(2,1)S(1)}, bf16[256,1024]{1,0:T(8,128)(2,1)S(1)}, bf16[256,1024]{1,0:T(8,128)(2,1)S(1)}) custom-call(s32[6]{0:T(128)S(1)} %stack.27._.places, bf16[512,1024]{1,0:T(8,128)(2,1)S(1)} %get-tuple-element.98.q_ref, bf16[512,1024]{1,0:T(8,128)(2,1)S(1)} %get-tuple-element.99.within_ref, ...), custom_call_target="tpu_custom_call" | custom-call | flops 1 | bytes 1 | tf_op jit(solution)/shard_map/heads_far/pallas_call | solution.py:468
  104.5 1.6 collective-permute-start.20
  106.7 4.9 %later.3 = (bf16[512,512]{1,0:T(8,128)(2,1)S(1)}, bf16[512,512]{1,0:T(8,128)(2,1)S(1)}) custom-call(s32[6]{0:T(128)S(1)} %stack.27._.places, bf16[256,1024]{1,0:T(8,128)(2,1)S(1)} %collective-permute-done.8.xa.refs_0_, bf16[256,1024]{1,0:T(8,128)(2,1)S(1)} %collective-permute-done.10.xb.refs_1_, bf16[3,4096,1024]{2,1,0:T(8,128)(2,1)} %refs_2_.5, ...), custom_call_target="tpu_custom_call" | custom-call | flops 939524096 | bytes 32079872 | tf_op jit(solution)/shard_map/later/pallas_call | solution.py:43
  111.6 5.5 %heads.1 = (bf16[512,1024]{1,0:T(8,128)(2,1)S(1)}, bf16[512,1024]{1,0:T(8,128)(2,1)S(1)}, bf16[512,1024]{1,0:T(8,128)(2,1)S(1)}) custom-call(s32[6]{0:T(128)S(1)} %stack.27._.places, bf16[512,512]{1,0:T(8,128)(2,1)S(1)} %get-tuple-element.97.refs_0_, bf16[512,512]{1,0:T(8,128)(2,1)S(1)} %get-tuple-element.109.refs_1_, ...), custom_call_target="tpu_custom_call" | custom-call | flops 1 | bytes 1 | tf_op jit(solution)/shard_map/heads/pallas_call | solution.py:43
  117.1 1.6 collective-permute-start.24
  120.3 3.1 %sum_and_near.1 = (bf16[512,1024]{1,0:T(8,128)(2,1)S(1)}, bf16[512,1024]{1,0:T(8,128)(2,1)S(1)}) custom-call(s32[6]{0:T(128)S(1)} %stack.27._.places, bf16[512,1024]{1,0:T(8,128)(2,1)S(1)} %get-tuple-element.113.normed_ref, bf16[256,1024]{1,0:T(8,128)(2,1)S(1)} %collective-permute-done.20.x_ref, bf16[256,1024]{1,0:T(8,128)(2,1)S(1)} %collective-permute-done.21.y_ref, ...), custom_call_target="tpu_custom_call" | custom-call | flops 1 | bytes 1 | tf_op jit(solution)/shard_map/sum_and_near/pallas_call | solution.py:43
  124.4 18.8 %collective-permute-done.24.refs_0_.y_ref = bf16[512,1024]{1,0:T(8,128)(2,1)S(1)} collective-permute-done((bf16[512,1024]{1,0:T(8,128)(2,1)S(1)}, bf16[512,1024]{1,0:T(8,128)(2,1)S(1)}, u32[]{:S(2)}, u32[]{:S(2)}) %collective-permute-start.24) | collective-permute-done | bytes 1048608 | tf_op jit(solution)/shard_map/ppermute | solution.py:871
  143.2 1.5 collective-permute-done.25.refs_1_.x_ref
  144.7 2.0 %sum_pair.1 = (bf16[256,1024]{1,0:T(8,128)(2,1)S(1)}, bf16[256,1024]{1,0:T(8,128)(2,1)S(1)}) custom-call(s32[6]{0:T(128)S(1)} %stack.27._.places, bf16[512,1024]{1,0:T(8,128)(2,1)S(1)} %get-tuple-element.118.normed_ref, bf16[512,1024]{1,0:T(8,128)(2,1)S(1)} %collective-permute-done.25.refs_1_.x_ref, ...), custom_call_target="tpu_custom_call" | custom-call | flops 1 | bytes 1 | tf_op jit(solution)/shard_map/sum_pair/pallas_call | solution.py:43
  147.9 19.3 %collective-permute-done.23.refs_1_.refs_2_ = bf16[512,1024]{1,0:T(8,128)(2,1)S(1)} collective-permute-done((bf16[512,1024]{1,0:T(8,128)(2,1)S(1)}, bf16[512,1024]{1,0:T(8,128)(2,1)S(1)}, u32[]{:S(2)}, u32[]{:S(2)}) %collective-permute-start.23) | collective-permute-done | bytes 1048608 | tf_op jit(solution)/shard_map/ppermute | solution.py:874
  167.2 2.0 %own_block.2.kept_ref = bf16[512,1024]{1,0:T(8,128)(2,1)S(1)} custom-call(s32[6]{0:T(128)S(1)} %stack.27._.places, bf16[512,1024]{1,0:T(8,128)(2,1)S(1)} %get-tuple-element.118.normed_ref, bf16[1024,4096]{1,0:T(8,128)(2,1)S(1)} %bitcast.7, bf16[512,1024]{1,0:T(8,128)(2,1)S(1)} %collective-permute-done.24.refs_0_.y_ref, ...), custom_call_target="tpu_custom_call" | custom-call | flops 1 | bytes 1 | tf_op jit(solution)/shard_map/own_block/pallas_call | solution.py:43
  169.2 2.9 %own_block.3.above_ref = bf16[1024,1024]{1,0:T(8,128)(2,1)} custom-call(s32[6]{0:T(128)S(1)} %stack.27._.places, bf16[512,1024]{1,0:T(8,128)(2,1)S(1)} %get-tuple-element.113.normed_ref, bf16[1024,4096]{1,0:T(8,128)(2,1)S(1)} %bitcast.7, bf16[512,1024]{1,0:T(8,128)(2,1)S(1)} %collective-permute-done.22.refs_0_.refs_3_, ...), custom_call_target="tpu_custom_call" | custom-call | flops 1 | bytes 1 | tf_op jit(solution)/shard_map/own_block/pallas_call | solution.py:43
  172.2 4.6 %collective-permute-done.26.a_ref = bf16[256,1024]{1,0:T(8,128)(2,1)S(1)} collective-permute-done((bf16[256,1024]{1,0:T(8,128)(2,1)S(1)}, bf16[256,1024]{1,0:T(8,128)(2,1)S(1)}, u32[]{:S(2)}, u32[]{:S(2)}) %collective-permute-start.26) | collective-permute-done | bytes 524320 | tf_op jit(solution)/shard_map/ppermute | solution.py:876
  (55 shorter events, 21.4 us)
Async XLA Ops:
  2.2 18.4 %collective-permute-start = (bf16[256,1024]{1,0:T(8,128)(2,1)}, bf16[256,1024]{1,0:T(8,128)(2,1)S(1)}, u32[]{:S(2)}, u32[]{:S(2)}) collective-permute-start(bf16[256,1024]{1,0:T(8,128)(2,1)} %get-tuple-element.71), channel_id=1, source_target_pairs={{0,1},{1,0},{2,3},{3,2},{4,5},{5,4},{6,7},{7,6},{8,9},{9,8},{10,11... | collective-permute-start | bytes 1572872 | tf_op jit(solution)/shard_map/ppermute | solution.py:739
  3.7 17.0 %collective-permute-start.1 = (bf16[256,1024]{1,0:T(8,128)(2,1)}, bf16[256,1024]{1,0:T(8,128)(2,1)S(1)}, u32[]{:S(2)}, u32[]{:S(2)}) collective-permute-start(bf16[256,1024]{1,0:T(8,128)(2,1)} %get-tuple-element.70), channel_id=1, source_target_pairs={{0,2},{1,3},{2,0},{3,1},{4,6},{5,7},{6,4},{7,5},{8,10},{9,11},{10,... | collective-permute-start | bytes 1572872 | tf_op jit(solution)/shard_map/ppermute | solution.py:739
  5.2 0.8 copy-start.1
  7.0 21.2 %collective-permute-start.2 = (bf16[256,1024]{1,0:T(8,128)(2,1)}, bf16[256,1024]{1,0:T(8,128)(2,1)S(1)}, u32[]{:S(2)}, u32[]{:S(2)}) collective-permute-start(bf16[256,1024]{1,0:T(8,128)(2,1)} %get-tuple-element.70), channel_id=1, source_target_pairs={{0,1},{1,0},{2,3},{3,2},{4,5},{5,4},{6,7},{7,6},{8,9},{9,8},{10,11... | collective-permute-start | bytes 1572872 | tf_op jit(solution)/shard_map/ppermute | solution.py:740
  7.6 22.4 %collective-permute-start.3 = (bf16[256,1024]{1,0:T(8,128)(2,1)}, bf16[256,1024]{1,0:T(8,128)(2,1)S(1)}, u32[]{:S(2)}, u32[]{:S(2)}) collective-permute-start(bf16[256,1024]{1,0:T(8,128)(2,1)} %get-tuple-element.71), channel_id=1, source_target_pairs={{0,2},{1,3},{2,0},{3,1},{4,6},{5,7},{6,4},{7,5},{8,10},{9,11},{10,... | collective-permute-start | bytes 1572872 | tf_op jit(solution)/shard_map/ppermute | solution.py:740
  20.7 4.5 %collective-permute-start.4 = (f32[8,128]{1,0:T(8,128)S(1)}, f32[8,128]{1,0:T(8,128)S(1)}, u32[]{:S(2)}, u32[]{:S(2)}) collective-permute-start(f32[8,128]{1,0:T(8,128)S(1)} %get-tuple-element.72.tail_ref), channel_id=1, source_target_pairs={{0,4},{4,0},{8,12},{12,8},{16,20},{20,16},{24,28},{28,24},{1,5},{5... | collective-permute-start | bytes 12296 | tf_op jit(solution)/shard_map/ppermute | solution.py:733
  22.1 21.5 %collective-permute-start.6 = (bf16[256,1024]{1,0:T(8,128)(2,1)S(1)}, bf16[256,1024]{1,0:T(8,128)(2,1)S(1)}, u32[]{:S(2)}, u32[]{:S(2)}) collective-permute-start(bf16[256,1024]{1,0:T(8,128)(2,1)S(1)} %collective-permute-done.refs_0_), channel_id=1, source_target_pairs={{0,2},{1,3},{2,0},{3,1},{4,6},{5,7},{6,4},{7,5},{8,10},{9,11},{10,... | collective-permute-start | bytes 1572872 | tf_op jit(solution)/shard_map/ppermute | solution.py:743
  23.7 19.9 %collective-permute-start.7 = (bf16[256,1024]{1,0:T(8,128)(2,1)S(1)}, bf16[256,1024]{1,0:T(8,128)(2,1)S(1)}, u32[]{:S(2)}, u32[]{:S(2)}) collective-permute-start(bf16[256,1024]{1,0:T(8,128)(2,1)S(1)} %collective-permute-done.1.refs_3_), channel_id=1, source_target_pairs={{0,1},{1,0},{2,3},{3,2},{4,5},{5,4},{6,7},{7,6},{8,9},{9,8},{10,11... | collective-permute-start | bytes 1572872 | tf_op jit(solution)/shard_map/ppermute | solution.py:743
  25.1 18.4 %collective-permute-start.11 = (f32[8,128]{1,0:T(8,128)S(1)}, f32[8,128]{1,0:T(8,128)S(1)}, u32[]{:S(2)}, u32[]{:S(2)}) collective-permute-start(f32[8,128]{1,0:T(8,128)S(1)} %add.10), channel_id=1, source_target_pairs={{16,24},{20,28},{17,25},{21,29},{18,26},{22,30},{19,27},{23,31}} | collective-permute-start | bytes 12296 | tf_op jit(solution)/shard_map/ppermute | solution.py:730
  30.0 27.1 %collective-permute-start.9 = (bf16[256,1024]{1,0:T(8,128)(2,1)S(1)}, bf16[256,1024]{1,0:T(8,128)(2,1)S(1)}, u32[]{:S(2)}, u32[]{:S(2)}) collective-permute-start(bf16[256,1024]{1,0:T(8,128)(2,1)S(1)} %get-tuple-element.82), channel_id=1, source_target_pairs={{0,2},{1,3},{2,0},{3,1},{4,6},{5,7},{6,4},{7,5},{8,10},{9,11},{10,... | collective-permute-start | bytes 1572872 | tf_op jit(solution)/shard_map/ppermute | solution.py:746
  31.5 25.6 %collective-permute-start.5 = (bf16[256,1024]{1,0:T(8,128)(2,1)S(1)}, bf16[256,1024]{1,0:T(8,128)(2,1)S(1)}, u32[]{:S(2)}, u32[]{:S(2)}) collective-permute-start(bf16[256,1024]{1,0:T(8,128)(2,1)S(1)} %get-tuple-element.83), channel_id=1, source_target_pairs={{0,1},{1,0},{2,3},{3,2},{4,5},{5,4},{6,7},{7,6},{8,9},{9,8},{10,11... | collective-permute-start | bytes 1572872 | tf_op jit(solution)/shard_map/ppermute | solution.py:745
  43.6 18.3 %collective-permute-start.12 = (bf16[256,1024]{1,0:T(8,128)(2,1)S(1)}, bf16[256,1024]{1,0:T(8,128)(2,1)S(1)}, u32[]{:S(2)}, u32[]{:S(2)}) collective-permute-start(bf16[256,1024]{1,0:T(8,128)(2,1)S(1)} %get-tuple-element.82), channel_id=1, source_target_pairs={{0,1},{1,0},{2,3},{3,2},{4,5},{5,4},{6,7},{7,6},{8,9},{9,8},{10,11... | collective-permute-start | bytes 1572872 | tf_op jit(solution)/shard_map/ppermute | solution.py:758
  45.1 18.6 %collective-permute-start.13 = (bf16[256,1024]{1,0:T(8,128)(2,1)S(1)}, bf16[256,1024]{1,0:T(8,128)(2,1)S(1)}, u32[]{:S(2)}, u32[]{:S(2)}) collective-permute-start(bf16[256,1024]{1,0:T(8,128)(2,1)S(1)} %get-tuple-element.83), channel_id=1, source_target_pairs={{0,2},{1,3},{2,0},{3,1},{4,6},{5,7},{6,4},{7,5},{8,10},{9,11},{10,... | collective-permute-start | bytes 1572872 | tf_op jit(solution)/shard_map/ppermute | solution.py:758
  57.2 18.2 %collective-permute-start.8 = (bf16[256,1024]{1,0:T(8,128)(2,1)S(1)}, bf16[256,1024]{1,0:T(8,128)(2,1)S(1)}, u32[]{:S(2)}, u32[]{:S(2)}) collective-permute-start(bf16[256,1024]{1,0:T(8,128)(2,1)S(1)} %collective-permute-done.5.refs_0_), channel_id=1, source_target_pairs={{0,2},{1,3},{2,0},{3,1},{4,6},{5,7},{6,4},{7,5},{8,10},{9,11},{10,... | collective-permute-start | bytes 1572872 | tf_op jit(solution)/shard_map/ppermute | solution.py:772
  58.8 16.7 %collective-permute-start.10 = (bf16[256,1024]{1,0:T(8,128)(2,1)S(1)}, bf16[256,1024]{1,0:T(8,128)(2,1)S(1)}, u32[]{:S(2)}, u32[]{:S(2)}) collective-permute-start(bf16[256,1024]{1,0:T(8,128)(2,1)S(1)} %collective-permute-done.9.refs_3_), channel_id=1, source_target_pairs={{0,1},{1,0},{2,3},{3,2},{4,5},{5,4},{6,7},{7,6},{8,9},{9,8},{10,11... | collective-permute-start | bytes 1572872 | tf_op jit(solution)/shard_map/ppermute | solution.py:772
  75.4 6.7 %copy-start = (f32[8,128,128]{2,1,0:T(8,128)S(1)}, f32[8,128,128]{2,1,0:T(8,128)}, u32[]{:S(2)}) copy-start(f32[8,128,128]{2,1,0:T(8,128)} %prior_ref.3) | copy-start | bytes 1572868
  80.7 1.4 collective-permute-start.14
  82.7 7.4 %collective-permute-start.15 = (bf16[4,128,128]{2,1,0:T(8,128)(2,1)S(1)}, bf16[4,128,128]{2,1,0:T(8,128)(2,1)S(1)}, u32[]{:S(2)}, u32[]{:S(2)}) collective-permute-start(bf16[4,128,128]{2,1,0:T(8,128)(2,1)S(1)} %get-tuple-element.94), channel_id=1, source_target_pairs={{0,8},{4,12},{1,9},{5,13},{2,10},{6,14},{3,11},{7,15}} | collective-permute-start | bytes 393224 | tf_op jit(solution)/shard_map/ppermute | solution.py:730
  84.0 14.7 %collective-permute-start.16 = (bf16[4,128,128]{2,1,0:T(8,128)(2,1)S(1)}, bf16[4,128,128]{2,1,0:T(8,128)(2,1)S(1)}, u32[]{:S(2)}, u32[]{:S(2)}) collective-permute-start(bf16[4,128,128]{2,1,0:T(8,128)(2,1)S(1)} %get-tuple-element.100), channel_id=1, source_target_pairs={{16,24},{20,28},{17,25},{21,29},{18,26},{22,30},{19,27},{23,31}} | collective-permute-start | bytes 393224 | tf_op jit(solution)/shard_map/ppermute | solution.py:730
  90.8 8.0 %collective-permute-start.18 = (bf16[4,128,128]{2,1,0:T(8,128)(2,1)S(1)}, bf16[4,128,128]{2,1,0:T(8,128)(2,1)S(1)}, u32[]{:S(2)}, u32[]{:S(2)}) collective-permute-start(bf16[4,128,128]{2,1,0:T(8,128)(2,1)S(1)} %pass_on.1), channel_id=1, source_target_pairs={{8,16},{12,20},{9,17},{13,21},{10,18},{14,22},{11,19},{15,23}} | collective-permute-start | bytes 393224 | tf_op jit(solution)/shard_map/ppermute | solution.py:730
  92.1 6.7 %collective-permute-start.17 = (bf16[4,128,128]{2,1,0:T(8,128)(2,1)S(1)}, bf16[4,128,128]{2,1,0:T(8,128)(2,1)S(1)}, u32[]{:S(2)}, u32[]{:S(2)}) collective-permute-start(bf16[4,128,128]{2,1,0:T(8,128)(2,1)S(1)} %pass_on.1), channel_id=1, source_target_pairs={{8,24},{12,28},{9,25},{13,29},{10,26},{14,30},{11,27},{15,31}} | collective-permute-start | bytes 393224 | tf_op jit(solution)/shard_map/ppermute | solution.py:730
  93.6 7.3 %slice-start = ((s8[8388608]{0:T(1024)(128)(4,1)}), s8[4194304]{0:T(1024)(128)(4,1)S(1)}, s32[]{:S(2)}) async-start(s8[8388608]{0:T(1024)(128)(4,1)} %bitcast.6), calls=%async_computation | async-start | bytes 8388608
  93.6 7.3 %slice-start.1 = ((s8[8388608]{0:T(1024)(128)(4,1)}), s8[4194304]{0:T(1024)(128)(4,1)S(1)}, s32[]{:S(2)}) async-start(s8[8388608]{0:T(1024)(128)(4,1)} %bitcast.6), calls=%async_computation.1 | async-start | bytes 8388608
  99.5 1.4 collective-permute-start.19
  104.5 14.6 %collective-permute-start.20 = (bf16[256,1024]{1,0:T(8,128)(2,1)S(1)}, bf16[256,1024]{1,0:T(8,128)(2,1)S(1)}, u32[]{:S(2)}, u32[]{:S(2)}) collective-permute-start(bf16[256,1024]{1,0:T(8,128)(2,1)S(1)} %get-tuple-element.114), channel_id=1, source_target_pairs={{0,2},{1,3},{2,0},{3,1},{4,6},{5,7},{6,4},{7,5},{8,10},{9,11},{10,... | collective-permute-start | bytes 1572872 | tf_op jit(solution)/shard_map/ppermute | solution.py:867
  106.1 14.1 %collective-permute-start.21 = (bf16[256,1024]{1,0:T(8,128)(2,1)S(1)}, bf16[256,1024]{1,0:T(8,128)(2,1)S(1)}, u32[]{:S(2)}, u32[]{:S(2)}) collective-permute-start(bf16[256,1024]{1,0:T(8,128)(2,1)S(1)} %get-tuple-element.115), channel_id=1, source_target_pairs={{0,1},{1,0},{2,3},{3,2},{4,5},{5,4},{6,7},{7,6},{8,9},{9,8},{10,11... | collective-permute-start | bytes 1572872 | tf_op jit(solution)/shard_map/ppermute | solution.py:867
  117.1 26.1 %collective-permute-start.24 = (bf16[512,1024]{1,0:T(8,128)(2,1)S(1)}, bf16[512,1024]{1,0:T(8,128)(2,1)S(1)}, u32[]{:S(2)}, u32[]{:S(2)}) collective-permute-start(bf16[512,1024]{1,0:T(8,128)(2,1)S(1)} %get-tuple-element.119), channel_id=1, source_target_pairs={{0,1},{1,0},{2,3},{3,2},{4,5},{5,4},{6,7},{7,6},{8,9},{9,8},{10,11... | collective-permute-start | bytes 3145736 | tf_op jit(solution)/shard_map/ppermute | solution.py:871
  118.6 26.1 %collective-permute-start.25 = (bf16[512,1024]{1,0:T(8,128)(2,1)S(1)}, bf16[512,1024]{1,0:T(8,128)(2,1)S(1)}, u32[]{:S(2)}, u32[]{:S(2)}) collective-permute-start(bf16[512,1024]{1,0:T(8,128)(2,1)S(1)} %get-tuple-element.121), channel_id=1, source_target_pairs={{0,2},{1,3},{2,0},{3,1},{4,6},{5,7},{6,4},{7,5},{8,10},{9,11},{10,... | collective-permute-start | bytes 3145736 | tf_op jit(solution)/shard_map/ppermute | solution.py:871
  123.4 43.8 %collective-permute-start.23 = (bf16[512,1024]{1,0:T(8,128)(2,1)S(1)}, bf16[512,1024]{1,0:T(8,128)(2,1)S(1)}, u32[]{:S(2)}, u32[]{:S(2)}) collective-permute-start(bf16[512,1024]{1,0:T(8,128)(2,1)S(1)} %get-tuple-element.117), channel_id=1, source_target_pairs={{0,2},{1,3},{2,0},{3,1},{4,6},{5,7},{6,4},{7,5},{8,10},{9,11},{10,... | collective-permute-start | bytes 3145736 | tf_op jit(solution)/shard_map/ppermute | solution.py:874
  124.0 43.2 %collective-permute-start.22 = (bf16[512,1024]{1,0:T(8,128)(2,1)S(1)}, bf16[512,1024]{1,0:T(8,128)(2,1)S(1)}, u32[]{:S(2)}, u32[]{:S(2)}) collective-permute-start(bf16[512,1024]{1,0:T(8,128)(2,1)S(1)} %get-tuple-element.116), channel_id=1, source_target_pairs={{0,1},{1,0},{2,3},{3,2},{4,5},{5,4},{6,7},{7,6},{8,9},{9,8},{10,11... | collective-permute-start | bytes 3145736 | tf_op jit(solution)/shard_map/ppermute | solution.py:874
  146.8 29.9 %collective-permute-start.26 = (bf16[256,1024]{1,0:T(8,128)(2,1)S(1)}, bf16[256,1024]{1,0:T(8,128)(2,1)S(1)}, u32[]{:S(2)}, u32[]{:S(2)}) collective-permute-start(bf16[256,1024]{1,0:T(8,128)(2,1)S(1)} %get-tuple-element.123), channel_id=1, source_target_pairs={{0,2},{1,3},{2,0},{3,1},{4,6},{5,7},{6,4},{7,5},{8,10},{9,11},{10,... | collective-permute-start | bytes 1572872 | tf_op jit(solution)/shard_map/ppermute | solution.py:876
  147.3 29.4 %collective-permute-start.27 = (bf16[256,1024]{1,0:T(8,128)(2,1)S(1)}, bf16[256,1024]{1,0:T(8,128)(2,1)S(1)}, u32[]{:S(2)}, u32[]{:S(2)}) collective-permute-start(bf16[256,1024]{1,0:T(8,128)(2,1)S(1)} %get-tuple-element.124), channel_id=1, source_target_pairs={{0,1},{1,0},{2,3},{3,2},{4,5},{5,4},{6,7},{7,6},{8,9},{9,8},{10,11... | collective-permute-start | bytes 1572872 | tf_op jit(solution)/shard_map/ppermute | solution.py:876

commit v14 on v13

--- a/solution.py
+++ b/solution.py
@@ -164,7 +164,7 @@
     passed_refs, held = refs[added + 5 : -1], refs[-1]
     along_ref, inside_ref, q_ref, within_ref, state_ref = refs[added : added + 5]
     for ref in passed_refs:
-        ref[...] = w_refs[0][1:]
+        ref[...] = w_refs[0][...]
     j = pl.program_id(0)
     rows = held.shape[1]
 
@@ -231,10 +231,10 @@
             struct((rows, heads * size), BF16),
             struct((rows, heads * size), BF16),
             struct((heads, size, size), F32),
-            *[struct((2, depth, heads * size), BF16) for _ in before],
+            *[struct((3, depth, heads * size), BF16) for _ in before],
         ),
         [wide, wide, pl.BlockSpec((group, size, size), lambda j, o: (j, 0, 0))]
-        + [pl.BlockSpec((2, depth, cols), lambda j, o: (0, 0, j)) for _ in before],
+        + [pl.BlockSpec((3, depth, cols), lambda j, o: (0, 0, j)) for _ in before],
         2 * rows * 3 * heads * size * depth * len(pieces),
         scratch=[pltpu.VMEM((len(pieces), rows, depth), BF16)],
     )
@@ -261,11 +261,10 @@
     )[0]
 
 
-def part_kernel(layout, outs, _, *refs):
+def part_kernel(layout, _, *refs):
     count = sum(layout)
     x_refs, w_refs = refs[:count], refs[count : count + len(layout)]
-    before_ref, out_refs, held = refs[-2 - outs], refs[-1 - outs : -1], refs[-1]
-    targets = [(ref, c) for ref in out_refs for c in range(ref.shape[0])]
+    before_ref, out_ref, held = refs[-3:]
     rows = held.shape[1]
 
     @pl.when(pl.program_id(0) == 0)
@@ -281,11 +280,10 @@
         total = dot(held[0], w_refs[0][c])
         for i in range(1, len(layout)):
             total = total + dot(held[i], w_refs[i][c])
-        ref, at = targets[c]
-        ref[at] = total + before_ref[c]
-
-
-def part_call(places, blocks, pieces, w_qkv, rows, cols, before, at, apart=False):
+        out_ref[c] = total + before_ref[c]
+
+
+def part_call(places, blocks, pieces, w_qkv, rows, cols, before, at):
     flat = [p for piece in pieces for p in piece]
     depth = flat[0].shape[1]
     width = w_qkv.shape[2]
@@ -299,22 +297,18 @@
     ] + [block(i) for i in range(len(pieces))]
     ins.append(before)
     specs.append(pl.BlockSpec((3, rows, cols), lambda j, o: (0, at, j)))
-    outs = [struct((3, rows, width), F32)]
-    if apart:
-        outs = [pltpu.HBM((1, rows, width), F32), struct((2, rows, width), F32)]
-    out = call(
-        functools.partial(part_kernel, tuple(len(p) for p in pieces), len(outs)),
+    return call(
+        functools.partial(part_kernel, tuple(len(p) for p in pieces)),
         "part",
         width // cols,
         places,
         ins,
         specs,
-        outs,
-        [pl.BlockSpec((o.shape[0], rows, cols), lambda j, o: (0, 0, j)) for o in outs],
+        (struct((3, rows, width), F32),),
+        [pl.BlockSpec((3, rows, cols), lambda j, o: (0, 0, j))],
         2 * rows * depth * len(pieces) * width * 3,
         scratch=[pltpu.VMEM((len(pieces), rows, depth), BF16)],
-    )
-    return out if apart else out[0]
+    )[0]
 
 
 def state_kernel(places, xa, xb, w_ref, acc_ref, end_ref, half_ref, state_ref, *refs):
@@ -325,8 +319,8 @@
     held[tall:, :] = xb[...]
     for pair in range(heads // 2):
         cols = slice(2 * pair * size, 2 * (pair + 1) * size)
-        keys = (acc_ref[0, :, cols] + dot(held[...], w_ref[0, :, cols])).astype(BF16)
-        values = (acc_ref[1, :, cols] + dot(held[...], w_ref[1, :, cols])).astype(BF16)
+        keys = (acc_ref[1, :, cols] + dot(held[...], w_ref[1, :, cols])).astype(BF16)
+        values = (acc_ref[2, :, cols] + dot(held[...], w_ref[2, :, cols])).astype(BF16)
         k_ref[:, cols] = keys
         v_ref[:, cols] = values
         for a in range(2):
@@ -356,64 +350,37 @@
     return small_call(state_kernel, "states", places, ins, outs, 16, scratch)
 
 
-def later_kernel(first, chunk, group, size, _, *refs):
-    xa, xb, wq, acc_q, k_ref, v_ref, along_ref, inside_ref, down_ref, state_ref = refs[:10]
-    q_ref, within_ref, held = refs[10:]
-    j = pl.program_id(0)
-    rows = held.shape[0]
-
-    @pl.when(j == 0)
-    def _():
-        held[: rows // 2, :] = xa[...]
-        held[rows // 2 :, :] = xb[...]
-
-    q_all = (acc_q[0] + dot(held[...], wq[0])).astype(BF16)
-    for a in range(group):
-        head = (first + j) * group + a
-        lanes = slice(a * size, (a + 1) * size)
-        state = state_ref[a]
+def later_kernel(half, chunk, _, xa, xb, w_ref, acc_ref, k_ref, v_ref, *refs):
+    along_ref, inside_ref, down_ref, state_ref, q_ref, within_ref, held = refs
+    tall, rows = xa.shape[0], held.shape[0]
+    heads, size = state_ref.shape[0], state_ref.shape[1]
+    held[:tall, :] = xa[...]
+    held[tall:, :] = xb[...]
+    for a in range(heads // 2):
+        head = half * heads // 2 + a
+        lanes, out = slice(head * size, (head + 1) * size), slice(a * size, (a + 1) * size)
+        if a % 2 == 0:
+            pair = slice(head * size, (head + 2) * size)
+            queries = (acc_ref[0, :, pair] + dot(held[...], w_ref[0, :, pair])).astype(BF16)
+        state = state_ref[head]
         for c in range(rows // chunk):
-            here = slice(c * chunk, (c + 1) * chunk)
-            q, k, v = q_all[here, lanes], k_ref[here, lanes], v_ref[here, lanes]
-            along, down = along_ref[pl.ds(head, 1), here], column(inside_ref[here, :], head)
-            q_ref[here, lanes] = faded(q, column(down_ref[here, :], head))
-            within_ref[here, lanes] = scores(q, k, v, along, down, state).astype(BF16)
+            here, there = slice(c * chunk, (c + 1) * chunk), slice(rows + c * chunk, rows + (c + 1) * chunk)
+            q = queries[here, (a % 2) * size : (a % 2 + 1) * size]
+            k, v = k_ref[here, lanes], v_ref[here, lanes]
+            along, down = along_ref[head : head + 1, there], inside_ref[there, head : head + 1]
+            q_ref[here, out] = faded(q, down_ref[there, head : head + 1])
+            within_ref[here, out] = scores(q, k, v, along, down, state).astype(BF16)
             if c + 1 < rows // chunk:
                 state = advance(k, v, down, state)
 
 
-def later_call(places, far, w_qkv, acc, k, v, along, inside, down, state, chunk, group, half):
+def later_call(places, far, w_far, acc, k, v, along, inside, down, state, chunk, half):
     _, rows, width = acc.shape
-    heads, size = state.shape[0], state.shape[1]
-    depth = far[0].shape[1]
-    cols = group * size
-    steps = heads // group // 2
-    first = half * steps
-    wide = pl.BlockSpec((rows, cols), lambda j, o: (0, first + j))
-    out = pl.BlockSpec((rows, cols), lambda j, o: (0, j))
-    return call(
-        functools.partial(later_kernel, first, chunk, group, size),
-        "later",
-        steps,
-        places,
-        (*far, w_qkv, acc, k, v, along, inside, down, state),
-        [
-            fixed(far[0].shape),
-            fixed(far[1].shape),
-            pl.BlockSpec((1, depth, cols), lambda j, o: (0, o[3], first + j)),
-            pl.BlockSpec((1, rows, cols), lambda j, o: (0, 0, first + j)),
-            wide,
-            wide,
-            pl.BlockSpec((heads, rows), lambda j, o: (0, 1)),
-            pl.BlockSpec((rows, heads), lambda j, o: (1, 0)),
-            pl.BlockSpec((rows, heads), lambda j, o: (1, 0)),
-            pl.BlockSpec((group, size, size), lambda j, o: (first + j, 0, 0)),
-        ],
-        (struct((rows, width // 2), BF16), struct((rows, width // 2), BF16)),
-        [out, out],
-        rows * depth * width + 2 * rows * (chunk + size) * width,
-        scratch=[pltpu.VMEM((rows, depth), BF16)],
-    )
+    ins = [near(x) for x in (*far, w_far, acc, k, v)] + [along, inside, down, near(state)]
+    outs = (struct((rows, width // 2), BF16),) * 2
+    scratch = [pltpu.VMEM((rows, far[0].shape[1]), BF16)]
+    kernel = functools.partial(later_kernel, half, chunk)
+    return small_call(kernel, "later", places, ins, outs, 16, scratch)
 
 
 def fades(tail_ref, other_ref, place, head):
@@ -516,66 +483,26 @@
         out_ref[:, a * size : (a + 1) * size] = (combined * lax.rsqrt(power + 1e-06)).astype(BF16)
 
 
-def far_kernel(places, q_ref, within_ref, here_ref, there_ref, w_ref, normed_ref, *out_refs):
-    tall, width = out_refs[0].shape
+def head_kernel(count, places, *refs):
+    q_refs, within_refs, refs = refs[:count], refs[count : 2 * count], refs[2 * count :]
+    here_ref, there_ref, w_ref, normed_ref = refs[:4]
+    out_refs = refs[4:]
+    tall, width = normed_ref.shape[0] // 2, out_refs[0].shape[1]
     for p, out_ref in enumerate(out_refs):
         rows = slice(p * tall, (p + 1) * tall)
         normed = normed_ref.at[rows]
-        normalise(places[4], (q_ref,), (within_ref,), here_ref, there_ref, rows, normed)
-        out_ref[...] = dot(normed[...], columns(w_ref, places[3], width)).astype(BF16)
-
-
-def far_call(places, q, within, entering, w_out, width):
-    out = struct((q.shape[0] // 2, width), BF16)
-    ins = (near(q), near(within), *[near(e) for e in entering], w_out)
-    return small_call(far_kernel, "heads_far", places, ins, (struct(q.shape, BF16), out, out), 8)
-
-
-def head_kernel(count, blocks, places, *refs):
-    q_refs, within_refs, refs = refs[:count], refs[count : 2 * count], refs[2 * count :]
-    here_ref, there_ref, w_ref, normed_ref = refs[:4]
-    out_refs, held = refs[4:6], refs[6]
-    width = out_refs[0].shape[1]
-    step = pl.program_id(0)
-    for p, out_ref in enumerate(out_refs):
-
-        @pl.when(step == p)
-        def _(p=p, out_ref=out_ref):
-            normalise(places[4], q_refs, within_refs, here_ref, there_ref, slice(None), held.at[p])
-            normed_ref[...] = held[p]
-            out_ref[...] = dot(held[p], columns(w_ref, places[blocks[0]], width)).astype(BF16)
-
-        if len(blocks) > 1:
-
-            @pl.when(step == 2 + p)
-            def _(p=p, out_ref=out_ref):
-                out_ref[...] = dot(held[p], columns(w_ref, places[blocks[1 + p]], width)).astype(BF16)
-
-
-def head_call(places, blocks, q, within, entering, w_out, width):
+        normalise(places[4], q_refs, within_refs, here_ref, there_ref, rows, normed)
+        out_ref[:tall, :] = dot(normed[...], columns(w_ref, places[3], width)).astype(BF16)
+        if out_ref.shape[0] > tall:
+            out_ref[tall:, :] = dot(normed[...], columns(w_ref, places[1 + p], width)).astype(BF16)
+
+
+def head_call(places, q, within, entering, w_out, width, near_too):
     rows, cols = q[0].shape[0], w_out.shape[0]
-    tall = rows // 2
-    near = len(blocks) > 1
-    part = pl.BlockSpec((tall, cols), lambda i, o: (jnp.minimum(i, 1), 0))
-    some = pl.BlockSpec((tall, cols // len(q)), lambda i, o: (jnp.minimum(i, 1), 0))
-    out = struct((rows if near else tall, width), BF16)
-    return call(
-        functools.partial(head_kernel, len(q), blocks),
-        "heads",
-        4 if near else 2,
-        places,
-        (*q, *within, *entering, w_out),
-        [some] * (2 * len(q)) + [fixed(entering[0].shape), fixed(entering[1].shape), WHOLE],
-        (struct((rows, cols), BF16), out, out),
-        [
-            part,
-            pl.BlockSpec((tall, width), lambda i, o: (i // 2, 0)),
-            pl.BlockSpec((tall, width), lambda i, o: (jnp.maximum(i - 2, 0), 0)),
-        ],
-        2 * rows * cols * (2 * width + 128),
-        scratch=[pltpu.VMEM((2, tall, cols), BF16)],
-        light=True,
-    )
+    out = struct((rows if near_too else rows // 2, width), BF16)
+    ins = [near(x) for x in (*q, *within, *entering)] + [w_out]
+    outs = (struct((rows, cols), BF16), out, out)
+    return small_call(functools.partial(head_kernel, len(q)), "heads", places, ins, outs, 12)
 
 
 def mixed_kernel(places, normed_ref, x_ref, y_ref, w_ref, out_x_ref, out_y_ref):
@@ -770,7 +697,7 @@
             group,
         )
         fy2, fx3 = over_y(after(x2, state)), over_x(after(y3, state))
-        acc_q, acc_kv = part_call(
+        acc_b = part_call(
             places,
             (1, 2),
             [(x2, x3), (y2, y3)],
@@ -779,11 +706,10 @@
             cols,
             before=stay(acc),
             at=1,
-            apart=True,
         )
         far = (fy2, fx3)
         middle = state
-        k, v, state, sent = state_call(places, far, w_far, acc_kv, to_end, half_fade, middle)
+        k, v, state, sent = state_call(places, far, w_far, acc_b, to_end, half_fade, middle)
     else:
         tail_other, tail_chip, tail_below = chip_tails(tail)
         gathered = lax.all_gather(tokens, "head", axis=1, tiled=True)
@@ -795,8 +721,7 @@
 
     def scores_of_later(half, *earlier):
         start = after(middle, *earlier)
-        ins = (far, w_qkv, stay(acc_q), k, v, along, inside, down, start)
-        return later_call(places, *ins, quarter, group, half)
+        return later_call(places, far, w_far, acc_b, k, v, along, inside, down, start, quarter, half)
 
     if square and n_chips == 4:
         leaving, alone, chip_state, first = chip_call(
@@ -848,12 +773,12 @@
         halves = [
             head_call(
                 places,
-                (0,),
                 (query[r * rows // 2 : (r + 1) * rows // 2],),
                 (within[r * rows // 2 : (r + 1) * rows // 2],),
                 entering,
                 w_out,
                 width,
+                False,
             )[0]
             for r in range(2)
         ]
@@ -862,11 +787,11 @@
 
     if n_chips != 4:
         query_b, within_b = scores_of_later(0)
-    na, far0, far1 = far_call(places, query_a, within_a, entering, w_out, width)
+    na, far0, far1 = head_call(places, (query_a,), (within_a,), entering, w_out, width, False)
     query_c, within_c = scores_of_later(1, na)
     far0, far1 = over_x(far0), over_y(far1)
     nb, by_x2, by_y2 = head_call(
-        places, (3, 1, 2), (query_b, query_c), (within_b, within_c), entering, w_out, width
+        places, (query_b, query_c), (within_b, within_c), entering, w_out, width, True
     )
     by_x2, by_y2 = over_x(by_x2), over_y(by_y2)
     by_x, by_y = mixed_call(places, after(na, nb), far1, far0, w_out, width)

time: 178 us -> 177 us (level)
  Pallas kernels: 89.1 us -> 85.3 us
    pallas_call x15 -> x12, Pallas kernels: 78.4 us -> 63.3 us  [call(): pl.pallas_call(kernel, out_shape=tuple(outs), grid_spec=pltpu.PrefetchSca...]
    pallas_call x5 -> x8, Pallas kernels: 10.8 us -> 21.9 us  [small_call(): pl.pallas_call(kernel, out_shape=tuple(outs), in_specs=[pl.BlockSpec(memo...]
    ppermute x2, waiting for transfers between devices: 1.16 us -> 4.27 us  [local(): far0, far1 = (over_x(far0), over_y(far1))]
    ppermute x2, waiting for transfers between devices: 20.3 us -> 18 us  [local(): by_x2, by_y2 = (over_x(by_x2), over_y(by_y2))]
  transfers between devices with their start and end apart: 28 -> 28, of which waited for: 12 -> 15; matrix products, arithmetic and copies ran while one was open for 0% -> 0% of each run, Pallas kernels for 43% -> 41%
where the time goes in v14:
time: 177 us; the launch traced here: 175 us
  Pallas kernels  85.3 us (48%)
  waiting for transfers between devices  63.7 us (36%)
  starting transfers between devices  25.4 us (14%)
    pallas_call x12, Pallas kernels, call(): pl.pallas_call(kernel, out_shape=tuple(outs), grid_spec=pltpu.PrefetchSca...  63.3 us
    pallas_call x8, Pallas kernels, small_call(): pl.pallas_call(kernel, out_shape=tuple(outs), in_specs=[pl.BlockSpec(memo...  21.9 us
    ppermute x2, waiting for transfers between devices, local(): by_x, by_y = (over_x(by_x), over_y(by_y))  19.3 us
    ppermute x2, waiting for transfers between devices, local(): by_x2, by_y2 = (over_x(by_x2), over_y(by_y2))  18 us
    ppermute x5, waiting for transfers between devices, hop(): return lax.ppermute(x, 'seq', perm=perm)  6.03 us
    ppermute x5, starting transfers between devices, hop(): return lax.ppermute(x, 'seq', perm=perm)  5.39 us
    ppermute x2, waiting for transfers between devices, local(): sum3, sum2 = (over_x(sum3), over_y(sum2))  5.17 us
    ppermute x2, waiting for transfers between devices, local(): far0, far1 = (over_x(far0), over_y(far1))  4.27 us
  transfers between devices with their start and end apart: 28, of which 15 were waited for; matrix products, arithmetic and copies ran while one was open for 0% of the time, Pallas kernels for 41%

profile of v14, /device:TPU:8, one launch (start us, length us, event | category | flops | bytes accessed | tf_op | source)
XLA Modules:
  0.0 175.5 jit_solution(949545933344722866)
XLA Ops:
  0.0 2.2 %cut.2 = (bf16[256,1024]{1,0:T(8,128)(2,1)}, bf16[256,1024]{1,0:T(8,128)(2,1)}) custom-call(s32[1]{0:T(128)} %constant.29.clone.1._, bf16[1024,1024]{1,0:T(8,128)(2,1)} %x_ref.4), custom_call_target="tpu_custom_call" | custom-call | flops 1 | bytes 3145728 | tf_op jit(solution)/shard_map/cut/pallas_call | solution.py:43
  3.7 1.5 collective-permute-start.1
  8.2 12.5 %own_part.1.refs_6_ = f32[3,1024,1024]{2,1,0:T(8,128)} custom-call(s32[6]{0:T(128)S(1)} %stack.27._.places, bf16[1024,1024]{1,0:T(8,128)(2,1)} %x_ref.4, bf16[3,4096,1024]{2,1,0:T(8,128)(2,1)} %refs_5_.3), custom_call_target="tpu_custom_call" | custom-call | flops 6442450944 | bytes 39845888 | tf_op jit(solution)/shard_map/own_part/pallas_call | solution.py:43
  22.1 1.6 collective-permute-start.6
  23.7 1.5 collective-permute-start.7
  25.9 2.2 %collective-permute-done.2.refs_1_ = bf16[256,1024]{1,0:T(8,128)(2,1)S(1)} collective-permute-done((bf16[256,1024]{1,0:T(8,128)(2,1)}, bf16[256,1024]{1,0:T(8,128)(2,1)S(1)}, u32[]{:S(2)}, u32[]{:S(2)}) %collective-permute-start.2) | collective-permute-done | bytes 524320 | tf_op jit(solution)/shard_map/ppermute | solution.py:667
  28.1 1.9 %collective-permute-done.3.refs_2_ = bf16[256,1024]{1,0:T(8,128)(2,1)S(1)} collective-permute-done((bf16[256,1024]{1,0:T(8,128)(2,1)}, bf16[256,1024]{1,0:T(8,128)(2,1)S(1)}, u32[]{:S(2)}, u32[]{:S(2)}) %collective-permute-start.3) | collective-permute-done | bytes 524320 | tf_op jit(solution)/shard_map/ppermute | solution.py:667
  30.0 1.5 collective-permute-start.9
  32.1 11.5 %part.2.refs_3_ = f32[3,512,1024]{2,1,0:T(8,128)S(1)} custom-call(s32[6]{0:T(128)S(1)} %stack.27._.places, bf16[256,1024]{1,0:T(8,128)(2,1)S(1)} %collective-permute-done.refs_0_, bf16[256,1024]{1,0:T(8,128)(2,1)S(1)} %collective-permute-done.2.refs_1_, bf16[256,1024]{1,0:T(8,128)(2,1)S(1)} %collective-permute-done.3.refs_2_, ...), custom_call_target="tpu_custom_call" | custom-call | flops 6442450944 | bytes 71303168 | tf_op jit(solution)/shard_map/part/pallas_call | solution.py:43
  43.6 1.6 collective-permute-start.12
  45.6 11.9 %first.1 = (bf16[512,1024]{1,0:T(8,128)(2,1)S(1)}, bf16[512,1024]{1,0:T(8,128)(2,1)S(1)}, f32[8,128,128]{2,1,0:T(8,128)S(1)}, bf16[3,1024,1024]{2,1,0:T(8,128)(2,1)S(1)}) custom-call(s32[6]{0:T(128)S(1)} %stack.27._.places, bf16[256,1024]{1,0:T(8,128)(2,1)S(1)} %collective-permute-done.6.refs_0_, bf16[256,1024]{1,0:T(8,128)(2,1)S(1)} %collective-permute-done.7.refs_1_, ...), custom_call_target="tpu_custom_call" | custom-call | flops 3221225472 | bytes 41484288 | tf_op jit(solution)/shard_map/first/pallas_call | solution.py:43
  57.6 1.6 collective-permute-start.8
  59.7 2.1 %collective-permute-done.12.refs_1_ = bf16[256,1024]{1,0:T(8,128)(2,1)S(1)} collective-permute-done((bf16[256,1024]{1,0:T(8,128)(2,1)S(1)}, bf16[256,1024]{1,0:T(8,128)(2,1)S(1)}, u32[]{:S(2)}, u32[]{:S(2)}) %collective-permute-start.12) | collective-permute-done | bytes 524320 | tf_op jit(solution)/shard_map/ppermute | solution.py:685
  61.8 1.9 %collective-permute-done.13.refs_2_ = bf16[256,1024]{1,0:T(8,128)(2,1)S(1)} collective-permute-done((bf16[256,1024]{1,0:T(8,128)(2,1)S(1)}, bf16[256,1024]{1,0:T(8,128)(2,1)S(1)}, u32[]{:S(2)}, u32[]{:S(2)}) %collective-permute-start.13) | collective-permute-done | bytes 524320 | tf_op jit(solution)/shard_map/ppermute | solution.py:685
  63.7 11.5 %part.3.acc_ref = f32[3,512,1024]{2,1,0:T(8,128)S(1)} custom-call(s32[6]{0:T(128)S(1)} %stack.27._.places, bf16[256,1024]{1,0:T(8,128)(2,1)S(1)} %collective-permute-done.5.refs_0_, bf16[256,1024]{1,0:T(8,128)(2,1)S(1)} %collective-permute-done.12.refs_1_, bf16[256,1024]{1,0:T(8,128)(2,1)S(1)} %collective-permute-done.13.refs_2_, ...), custom_call_target="tpu_custom_call" | custom-call | flops 6442450944 | bytes 71303168 | tf_op jit(solution)/shard_map/part/pallas_call | solution.py:43
  75.2 5.2 %states.1 = (bf16[512,1024]{1,0:T(8,128)(2,1)S(1)}, bf16[512,1024]{1,0:T(8,128)(2,1)S(1)}, f32[8,128,128]{2,1,0:T(8,128)S(1)}, bf16[4,128,128]{2,1,0:T(8,128)(2,1)S(1)}) custom-call(s32[6]{0:T(128)S(1)} %stack.27._.places, bf16[256,1024]{1,0:T(8,128)(2,1)S(1)} %collective-permute-done.8.xa, bf16[256,1024]{1,0:T(8,128)(2,1)S(1)} %collective-permute-done.10.xb, ...), custom_call_target="tpu_custom_call" | custom-call | flops 1 | bytes 1 | tf_op jit(solution)/shard_map/states/pallas_call | solution.py:435
  84.5 5.5 %collective-permute-done.15.come_ref = bf16[4,128,128]{2,1,0:T(8,128)(2,1)S(1)} collective-permute-done((bf16[4,128,128]{2,1,0:T(8,128)(2,1)S(1)}, bf16[4,128,128]{2,1,0:T(8,128)(2,1)S(1)}, u32[]{:S(2)}, u32[]{:S(2)}) %collective-permute-start.15) | collective-permute-done | bytes 131104 | tf_op jit(solution)/shard_map/ppermute | solution.py:657
  93.4 3.2 %later.2 = (bf16[512,512]{1,0:T(8,128)(2,1)S(1)}, bf16[512,512]{1,0:T(8,128)(2,1)S(1)}) custom-call(s32[6]{0:T(128)S(1)} %stack.27._.places, bf16[256,1024]{1,0:T(8,128)(2,1)S(1)} %collective-permute-done.8.xa, bf16[256,1024]{1,0:T(8,128)(2,1)S(1)} %collective-permute-done.10.xb, bf16[3,1024,1024]{2,1,0:T(8,128)(2,1)S(1)} %get-tuple-element.80.w_ref, ...), custom_call_target="tpu_custom_call" | custom-call | flops 1 | bytes 1 | tf_op jit(solution)/shard_map/later/pallas_call | solution.py:435
  99.3 3.6 %heads.2 = (bf16[512,1024]{1,0:T(8,128)(2,1)S(1)}, bf16[256,1024]{1,0:T(8,128)(2,1)S(1)}, bf16[256,1024]{1,0:T(8,128)(2,1)S(1)}) custom-call(s32[6]{0:T(128)S(1)} %stack.27._.places, bf16[512,1024]{1,0:T(8,128)(2,1)S(1)} %get-tuple-element.94.refs_0_, bf16[512,1024]{1,0:T(8,128)(2,1)S(1)} %get-tuple-element.95.refs_1_, ...), custom_call_target="tpu_custom_call" | custom-call | flops 1 | bytes 1 | tf_op jit(solution)/shard_map/heads/pallas_call | solution.py:435
  102.9 1.6 collective-permute-start.20
  105.1 3.2 %later.3 = (bf16[512,512]{1,0:T(8,128)(2,1)S(1)}, bf16[512,512]{1,0:T(8,128)(2,1)S(1)}) custom-call(s32[6]{0:T(128)S(1)} %stack.27._.places, bf16[256,1024]{1,0:T(8,128)(2,1)S(1)} %collective-permute-done.8.xa, bf16[256,1024]{1,0:T(8,128)(2,1)S(1)} %collective-permute-done.10.xb, bf16[3,1024,1024]{2,1,0:T(8,128)(2,1)S(1)} %get-tuple-element.80.w_ref, ...), custom_call_target="tpu_custom_call" | custom-call | flops 1 | bytes 1 | tf_op jit(solution)/shard_map/later/pallas_call | solution.py:435
  108.3 4.7 %heads.3 = (bf16[512,1024]{1,0:T(8,128)(2,1)S(1)}, bf16[512,1024]{1,0:T(8,128)(2,1)S(1)}, bf16[512,1024]{1,0:T(8,128)(2,1)S(1)}) custom-call(s32[6]{0:T(128)S(1)} %stack.27._.places, bf16[512,512]{1,0:T(8,128)(2,1)S(1)} %get-tuple-element.93.refs_0_, bf16[512,512]{1,0:T(8,128)(2,1)S(1)} %get-tuple-element.105.refs_1_, ...), custom_call_target="tpu_custom_call" | custom-call | flops 1 | bytes 1 | tf_op jit(solution)/shard_map/heads/pallas_call | solution.py:435
  113.0 1.6 collective-permute-start.24
  115.1 2.4 %collective-permute-done.20.x_ref = bf16[256,1024]{1,0:T(8,128)(2,1)S(1)} collective-permute-done((bf16[256,1024]{1,0:T(8,128)(2,1)S(1)}, bf16[256,1024]{1,0:T(8,128)(2,1)S(1)}, u32[]{:S(2)}, u32[]{:S(2)}) %collective-permute-start.20) | collective-permute-done | bytes 524320 | tf_op jit(solution)/shard_map/ppermute | solution.py:792
  117.5 1.9 %collective-permute-done.21.y_ref = bf16[256,1024]{1,0:T(8,128)(2,1)S(1)} collective-permute-done((bf16[256,1024]{1,0:T(8,128)(2,1)S(1)}, bf16[256,1024]{1,0:T(8,128)(2,1)S(1)}, u32[]{:S(2)}, u32[]{:S(2)}) %collective-permute-start.21) | collective-permute-done | bytes 524320 | tf_op jit(solution)/shard_map/ppermute | solution.py:792
  119.3 3.3 %sum_and_near.1 = (bf16[512,1024]{1,0:T(8,128)(2,1)S(1)}, bf16[512,1024]{1,0:T(8,128)(2,1)S(1)}) custom-call(s32[6]{0:T(128)S(1)} %stack.27._.places, bf16[512,1024]{1,0:T(8,128)(2,1)S(1)} %get-tuple-element.109.normed_ref, bf16[256,1024]{1,0:T(8,128)(2,1)S(1)} %collective-permute-done.20.x_ref, bf16[256,1024]{1,0:T(8,128)(2,1)S(1)} %collective-permute-done.21.y_ref, ...), custom_call_target="tpu_custom_call" | custom-call | flops 1 | bytes 1 | tf_op jit(solution)/shard_map/sum_and_near/pallas_call | solution.py:43
  123.8 18.0 %collective-permute-done.24.refs_0_.y_ref = bf16[512,1024]{1,0:T(8,128)(2,1)S(1)} collective-permute-done((bf16[512,1024]{1,0:T(8,128)(2,1)S(1)}, bf16[512,1024]{1,0:T(8,128)(2,1)S(1)}, u32[]{:S(2)}, u32[]{:S(2)}) %collective-permute-start.24) | collective-permute-done | bytes 1048608 | tf_op jit(solution)/shard_map/ppermute | solution.py:796
  141.8 2.0 %sum_pair.1 = (bf16[256,1024]{1,0:T(8,128)(2,1)S(1)}, bf16[256,1024]{1,0:T(8,128)(2,1)S(1)}) custom-call(s32[6]{0:T(128)S(1)} %stack.27._.places, bf16[512,1024]{1,0:T(8,128)(2,1)S(1)} %get-tuple-element.114.normed_ref, bf16[512,1024]{1,0:T(8,128)(2,1)S(1)} %collective-permute-done.25.refs_1_.x_ref, ...), custom_call_target="tpu_custom_call" | custom-call | flops 1 | bytes 1 | tf_op jit(solution)/shard_map/sum_pair/pallas_call | solution.py:43
  144.9 18.2 %collective-permute-done.23.refs_1_.refs_2_ = bf16[512,1024]{1,0:T(8,128)(2,1)S(1)} collective-permute-done((bf16[512,1024]{1,0:T(8,128)(2,1)S(1)}, bf16[512,1024]{1,0:T(8,128)(2,1)S(1)}, u32[]{:S(2)}, u32[]{:S(2)}) %collective-permute-start.23) | collective-permute-done | bytes 1048608 | tf_op jit(solution)/shard_map/ppermute | solution.py:799
  164.3 2.0 %own_block.2.kept_ref = bf16[512,1024]{1,0:T(8,128)(2,1)S(1)} custom-call(s32[6]{0:T(128)S(1)} %stack.27._.places, bf16[512,1024]{1,0:T(8,128)(2,1)S(1)} %get-tuple-element.114.normed_ref, bf16[1024,4096]{1,0:T(8,128)(2,1)S(1)} %bitcast.7, bf16[512,1024]{1,0:T(8,128)(2,1)S(1)} %collective-permute-done.24.refs_0_.y_ref, ...), custom_call_target="tpu_custom_call" | custom-call | flops 1 | bytes 1 | tf_op jit(solution)/shard_map/own_block/pallas_call | solution.py:43
  166.3 2.9 %own_block.3.above_ref = bf16[1024,1024]{1,0:T(8,128)(2,1)} custom-call(s32[6]{0:T(128)S(1)} %stack.27._.places, bf16[512,1024]{1,0:T(8,128)(2,1)S(1)} %get-tuple-element.109.normed_ref, bf16[1024,4096]{1,0:T(8,128)(2,1)S(1)} %bitcast.7, bf16[512,1024]{1,0:T(8,128)(2,1)S(1)} %collective-permute-done.22.refs_0_.refs_3_, ...), custom_call_target="tpu_custom_call" | custom-call | flops 1 | bytes 1 | tf_op jit(solution)/shard_map/own_block/pallas_call | solution.py:43
  169.2 3.9 %collective-permute-done.26.a_ref = bf16[256,1024]{1,0:T(8,128)(2,1)S(1)} collective-permute-done((bf16[256,1024]{1,0:T(8,128)(2,1)S(1)}, bf16[256,1024]{1,0:T(8,128)(2,1)S(1)}, u32[]{:S(2)}, u32[]{:S(2)}) %collective-permute-start.26) | collective-permute-done | bytes 524320 | tf_op jit(solution)/shard_map/ppermute | solution.py:801
  (55 shorter events, 24.8 us)
Async XLA Ops:
  2.2 18.5 %collective-permute-start = (bf16[256,1024]{1,0:T(8,128)(2,1)}, bf16[256,1024]{1,0:T(8,128)(2,1)S(1)}, u32[]{:S(2)}, u32[]{:S(2)}) collective-permute-start(bf16[256,1024]{1,0:T(8,128)(2,1)} %get-tuple-element.69), channel_id=1, source_target_pairs={{0,1},{1,0},{2,3},{3,2},{4,5},{5,4},{6,7},{7,6},{8,9},{9,8},{10,11... | collective-permute-start | bytes 1572872 | tf_op jit(solution)/shard_map/ppermute | solution.py:666
  3.7 17.0 %collective-permute-start.1 = (bf16[256,1024]{1,0:T(8,128)(2,1)}, bf16[256,1024]{1,0:T(8,128)(2,1)S(1)}, u32[]{:S(2)}, u32[]{:S(2)}) collective-permute-start(bf16[256,1024]{1,0:T(8,128)(2,1)} %get-tuple-element.68), channel_id=1, source_target_pairs={{0,2},{1,3},{2,0},{3,1},{4,6},{5,7},{6,4},{7,5},{8,10},{9,11},{10,... | collective-permute-start | bytes 1572872 | tf_op jit(solution)/shard_map/ppermute | solution.py:666
  5.3 0.8 copy-start.1
  7.0 21.1 %collective-permute-start.2 = (bf16[256,1024]{1,0:T(8,128)(2,1)}, bf16[256,1024]{1,0:T(8,128)(2,1)S(1)}, u32[]{:S(2)}, u32[]{:S(2)}) collective-permute-start(bf16[256,1024]{1,0:T(8,128)(2,1)} %get-tuple-element.68), channel_id=1, source_target_pairs={{0,1},{1,0},{2,3},{3,2},{4,5},{5,4},{6,7},{7,6},{8,9},{9,8},{10,11... | collective-permute-start | bytes 1572872 | tf_op jit(solution)/shard_map/ppermute | solution.py:667
  7.6 22.4 %collective-permute-start.3 = (bf16[256,1024]{1,0:T(8,128)(2,1)}, bf16[256,1024]{1,0:T(8,128)(2,1)S(1)}, u32[]{:S(2)}, u32[]{:S(2)}) collective-permute-start(bf16[256,1024]{1,0:T(8,128)(2,1)} %get-tuple-element.69), channel_id=1, source_target_pairs={{0,2},{1,3},{2,0},{3,1},{4,6},{5,7},{6,4},{7,5},{8,10},{9,11},{10,... | collective-permute-start | bytes 1572872 | tf_op jit(solution)/shard_map/ppermute | solution.py:667
  20.7 4.5 %collective-permute-start.4 = (f32[8,128]{1,0:T(8,128)S(1)}, f32[8,128]{1,0:T(8,128)S(1)}, u32[]{:S(2)}, u32[]{:S(2)}) collective-permute-start(f32[8,128]{1,0:T(8,128)S(1)} %get-tuple-element.70.tail_ref), channel_id=1, source_target_pairs={{0,4},{4,0},{8,12},{12,8},{16,20},{20,16},{24,28},{28,24},{1,5},{5... | collective-permute-start | bytes 12296 | tf_op jit(solution)/shard_map/ppermute | solution.py:660
  22.1 21.4 %collective-permute-start.6 = (bf16[256,1024]{1,0:T(8,128)(2,1)S(1)}, bf16[256,1024]{1,0:T(8,128)(2,1)S(1)}, u32[]{:S(2)}, u32[]{:S(2)}) collective-permute-start(bf16[256,1024]{1,0:T(8,128)(2,1)S(1)} %collective-permute-done.refs_0_), channel_id=1, source_target_pairs={{0,2},{1,3},{2,0},{3,1},{4,6},{5,7},{6,4},{7,5},{8,10},{9,11},{10,... | collective-permute-start | bytes 1572872 | tf_op jit(solution)/shard_map/ppermute | solution.py:670
  23.7 19.9 %collective-permute-start.7 = (bf16[256,1024]{1,0:T(8,128)(2,1)S(1)}, bf16[256,1024]{1,0:T(8,128)(2,1)S(1)}, u32[]{:S(2)}, u32[]{:S(2)}) collective-permute-start(bf16[256,1024]{1,0:T(8,128)(2,1)S(1)} %collective-permute-done.1.refs_3_), channel_id=1, source_target_pairs={{0,1},{1,0},{2,3},{3,2},{4,5},{5,4},{6,7},{7,6},{8,9},{9,8},{10,11... | collective-permute-start | bytes 1572872 | tf_op jit(solution)/shard_map/ppermute | solution.py:670
  25.2 18.3 %collective-permute-start.11 = (f32[8,128]{1,0:T(8,128)S(1)}, f32[8,128]{1,0:T(8,128)S(1)}, u32[]{:S(2)}, u32[]{:S(2)}) collective-permute-start(f32[8,128]{1,0:T(8,128)S(1)} %add.10), channel_id=1, source_target_pairs={{16,24},{20,28},{17,25},{21,29},{18,26},{22,30},{19,27},{23,31}} | collective-permute-start | bytes 12296 | tf_op jit(solution)/shard_map/ppermute | solution.py:657
  30.0 27.6 %collective-permute-start.9 = (bf16[256,1024]{1,0:T(8,128)(2,1)S(1)}, bf16[256,1024]{1,0:T(8,128)(2,1)S(1)}, u32[]{:S(2)}, u32[]{:S(2)}) collective-permute-start(bf16[256,1024]{1,0:T(8,128)(2,1)S(1)} %get-tuple-element.81), channel_id=1, source_target_pairs={{0,2},{1,3},{2,0},{3,1},{4,6},{5,7},{6,4},{7,5},{8,10},{9,11},{10,... | collective-permute-start | bytes 1572872 | tf_op jit(solution)/shard_map/ppermute | solution.py:673
  31.5 26.1 %collective-permute-start.5 = (bf16[256,1024]{1,0:T(8,128)(2,1)S(1)}, bf16[256,1024]{1,0:T(8,128)(2,1)S(1)}, u32[]{:S(2)}, u32[]{:S(2)}) collective-permute-start(bf16[256,1024]{1,0:T(8,128)(2,1)S(1)} %get-tuple-element.82), channel_id=1, source_target_pairs={{0,1},{1,0},{2,3},{3,2},{4,5},{5,4},{6,7},{7,6},{8,9},{9,8},{10,11... | collective-permute-start | bytes 1572872 | tf_op jit(solution)/shard_map/ppermute | solution.py:672
  43.6 18.2 %collective-permute-start.12 = (bf16[256,1024]{1,0:T(8,128)(2,1)S(1)}, bf16[256,1024]{1,0:T(8,128)(2,1)S(1)}, u32[]{:S(2)}, u32[]{:S(2)}) collective-permute-start(bf16[256,1024]{1,0:T(8,128)(2,1)S(1)} %get-tuple-element.81), channel_id=1, source_target_pairs={{0,1},{1,0},{2,3},{3,2},{4,5},{5,4},{6,7},{7,6},{8,9},{9,8},{10,11... | collective-permute-start | bytes 1572872 | tf_op jit(solution)/shard_map/ppermute | solution.py:685
  45.1 18.6 %collective-permute-start.13 = (bf16[256,1024]{1,0:T(8,128)(2,1)S(1)}, bf16[256,1024]{1,0:T(8,128)(2,1)S(1)}, u32[]{:S(2)}, u32[]{:S(2)}) collective-permute-start(bf16[256,1024]{1,0:T(8,128)(2,1)S(1)} %get-tuple-element.82), channel_id=1, source_target_pairs={{0,2},{1,3},{2,0},{3,1},{4,6},{5,7},{6,4},{7,5},{8,10},{9,11},{10,... | collective-permute-start | bytes 1572872 | tf_op jit(solution)/shard_map/ppermute | solution.py:685
  57.6 17.6 %collective-permute-start.8 = (bf16[256,1024]{1,0:T(8,128)(2,1)S(1)}, bf16[256,1024]{1,0:T(8,128)(2,1)S(1)}, u32[]{:S(2)}, u32[]{:S(2)}) collective-permute-start(bf16[256,1024]{1,0:T(8,128)(2,1)S(1)} %collective-permute-done.5.refs_0_), channel_id=1, source_target_pairs={{0,2},{1,3},{2,0},{3,1},{4,6},{5,7},{6,4},{7,5},{8,10},{9,11},{10,... | collective-permute-start | bytes 1572872 | tf_op jit(solution)/shard_map/ppermute | solution.py:699
  59.2 16.0 %collective-permute-start.10 = (bf16[256,1024]{1,0:T(8,128)(2,1)S(1)}, bf16[256,1024]{1,0:T(8,128)(2,1)S(1)}, u32[]{:S(2)}, u32[]{:S(2)}) collective-permute-start(bf16[256,1024]{1,0:T(8,128)(2,1)S(1)} %collective-permute-done.9.refs_3_), channel_id=1, source_target_pairs={{0,1},{1,0},{2,3},{3,2},{4,5},{5,4},{6,7},{7,6},{8,9},{9,8},{10,11... | collective-permute-start | bytes 1572872 | tf_op jit(solution)/shard_map/ppermute | solution.py:699
  75.2 6.7 %copy-start = (f32[8,128,128]{2,1,0:T(8,128)S(1)}, f32[8,128,128]{2,1,0:T(8,128)}, u32[]{:S(2)}) copy-start(f32[8,128,128]{2,1,0:T(8,128)} %prior_ref.3) | copy-start | bytes 1572868
  80.5 1.4 collective-permute-start.14
  82.5 7.4 %collective-permute-start.15 = (bf16[4,128,128]{2,1,0:T(8,128)(2,1)S(1)}, bf16[4,128,128]{2,1,0:T(8,128)(2,1)S(1)}, u32[]{:S(2)}, u32[]{:S(2)}) collective-permute-start(bf16[4,128,128]{2,1,0:T(8,128)(2,1)S(1)} %get-tuple-element.90), channel_id=1, source_target_pairs={{0,8},{4,12},{1,9},{5,13},{2,10},{6,14},{3,11},{7,15}} | collective-permute-start | bytes 393224 | tf_op jit(solution)/shard_map/ppermute | solution.py:657
  83.8 12.8 %collective-permute-start.16 = (bf16[4,128,128]{2,1,0:T(8,128)(2,1)S(1)}, bf16[4,128,128]{2,1,0:T(8,128)(2,1)S(1)}, u32[]{:S(2)}, u32[]{:S(2)}) collective-permute-start(bf16[4,128,128]{2,1,0:T(8,128)(2,1)S(1)} %get-tuple-element.96), channel_id=1, source_target_pairs={{16,24},{20,28},{17,25},{21,29},{18,26},{22,30},{19,27},{23,31}} | collective-permute-start | bytes 393224 | tf_op jit(solution)/shard_map/ppermute | solution.py:657
  90.6 6.0 %collective-permute-start.18 = (bf16[4,128,128]{2,1,0:T(8,128)(2,1)S(1)}, bf16[4,128,128]{2,1,0:T(8,128)(2,1)S(1)}, u32[]{:S(2)}, u32[]{:S(2)}) collective-permute-start(bf16[4,128,128]{2,1,0:T(8,128)(2,1)S(1)} %pass_on.1), channel_id=1, source_target_pairs={{8,16},{12,20},{9,17},{13,21},{10,18},{14,22},{11,19},{15,23}} | collective-permute-start | bytes 393224 | tf_op jit(solution)/shard_map/ppermute | solution.py:657
  91.9 5.3 %collective-permute-start.17 = (bf16[4,128,128]{2,1,0:T(8,128)(2,1)S(1)}, bf16[4,128,128]{2,1,0:T(8,128)(2,1)S(1)}, u32[]{:S(2)}, u32[]{:S(2)}) collective-permute-start(bf16[4,128,128]{2,1,0:T(8,128)(2,1)S(1)} %pass_on.1), channel_id=1, source_target_pairs={{8,24},{12,28},{9,25},{13,29},{10,26},{14,30},{11,27},{15,31}} | collective-permute-start | bytes 393224 | tf_op jit(solution)/shard_map/ppermute | solution.py:657
  93.4 5.9 %slice-start = ((s8[8388608]{0:T(1024)(128)(4,1)}), s8[4194304]{0:T(1024)(128)(4,1)S(1)}, s32[]{:S(2)}) async-start(s8[8388608]{0:T(1024)(128)(4,1)} %bitcast.6), calls=%async_computation | async-start | bytes 8388608
  93.4 5.9 %slice-start.1 = ((s8[8388608]{0:T(1024)(128)(4,1)}), s8[4194304]{0:T(1024)(128)(4,1)S(1)}, s32[]{:S(2)}) async-start(s8[8388608]{0:T(1024)(128)(4,1)} %bitcast.6), calls=%async_computation.1 | async-start | bytes 8388608
  97.9 1.4 collective-permute-start.19
  102.9 14.5 %collective-permute-start.20 = (bf16[256,1024]{1,0:T(8,128)(2,1)S(1)}, bf16[256,1024]{1,0:T(8,128)(2,1)S(1)}, u32[]{:S(2)}, u32[]{:S(2)}) collective-permute-start(bf16[256,1024]{1,0:T(8,128)(2,1)S(1)} %get-tuple-element.110), channel_id=1, source_target_pairs={{0,2},{1,3},{2,0},{3,1},{4,6},{5,7},{6,4},{7,5},{8,10},{9,11},{10,... | collective-permute-start | bytes 1572872 | tf_op jit(solution)/shard_map/ppermute | solution.py:792
  104.5 14.8 %collective-permute-start.21 = (bf16[256,1024]{1,0:T(8,128)(2,1)S(1)}, bf16[256,1024]{1,0:T(8,128)(2,1)S(1)}, u32[]{:S(2)}, u32[]{:S(2)}) collective-permute-start(bf16[256,1024]{1,0:T(8,128)(2,1)S(1)} %get-tuple-element.111), channel_id=1, source_target_pairs={{0,1},{1,0},{2,3},{3,2},{4,5},{5,4},{6,7},{7,6},{8,9},{9,8},{10,11... | collective-permute-start | bytes 1572872 | tf_op jit(solution)/shard_map/ppermute | solution.py:792
  113.0 28.8 %collective-permute-start.24 = (bf16[512,1024]{1,0:T(8,128)(2,1)S(1)}, bf16[512,1024]{1,0:T(8,128)(2,1)S(1)}, u32[]{:S(2)}, u32[]{:S(2)}) collective-permute-start(bf16[512,1024]{1,0:T(8,128)(2,1)S(1)} %get-tuple-element.115), channel_id=1, source_target_pairs={{0,1},{1,0},{2,3},{3,2},{4,5},{5,4},{6,7},{7,6},{8,9},{9,8},{10,11... | collective-permute-start | bytes 3145736 | tf_op jit(solution)/shard_map/ppermute | solution.py:796
  114.6 27.3 %collective-permute-start.25 = (bf16[512,1024]{1,0:T(8,128)(2,1)S(1)}, bf16[512,1024]{1,0:T(8,128)(2,1)S(1)}, u32[]{:S(2)}, u32[]{:S(2)}) collective-permute-start(bf16[512,1024]{1,0:T(8,128)(2,1)S(1)} %get-tuple-element.117), channel_id=1, source_target_pairs={{0,2},{1,3},{2,0},{3,1},{4,6},{5,7},{6,4},{7,5},{8,10},{9,11},{10,... | collective-permute-start | bytes 3145736 | tf_op jit(solution)/shard_map/ppermute | solution.py:796
  122.7 40.4 %collective-permute-start.23 = (bf16[512,1024]{1,0:T(8,128)(2,1)S(1)}, bf16[512,1024]{1,0:T(8,128)(2,1)S(1)}, u32[]{:S(2)}, u32[]{:S(2)}) collective-permute-start(bf16[512,1024]{1,0:T(8,128)(2,1)S(1)} %get-tuple-element.113), channel_id=1, source_target_pairs={{0,2},{1,3},{2,0},{3,1},{4,6},{5,7},{6,4},{7,5},{8,10},{9,11},{10,... | collective-permute-start | bytes 3145736 | tf_op jit(solution)/shard_map/ppermute | solution.py:799
  123.3 41.0 %collective-permute-start.22 = (bf16[512,1024]{1,0:T(8,128)(2,1)S(1)}, bf16[512,1024]{1,0:T(8,128)(2,1)S(1)}, u32[]{:S(2)}, u32[]{:S(2)}) collective-permute-start(bf16[512,1024]{1,0:T(8,128)(2,1)S(1)} %get-tuple-element.112), channel_id=1, source_target_pairs={{0,1},{1,0},{2,3},{3,2},{4,5},{5,4},{6,7},{7,6},{8,9},{9,8},{10,11... | collective-permute-start | bytes 3145736 | tf_op jit(solution)/shard_map/ppermute | solution.py:799
  143.8 29.3 %collective-permute-start.26 = (bf16[256,1024]{1,0:T(8,128)(2,1)S(1)}, bf16[256,1024]{1,0:T(8,128)(2,1)S(1)}, u32[]{:S(2)}, u32[]{:S(2)}) collective-permute-start(bf16[256,1024]{1,0:T(8,128)(2,1)S(1)} %get-tuple-element.119), channel_id=1, source_target_pairs={{0,2},{1,3},{2,0},{3,1},{4,6},{5,7},{6,4},{7,5},{8,10},{9,11},{10,... | collective-permute-start | bytes 1572872 | tf_op jit(solution)/shard_map/ppermute | solution.py:801
  144.4 30.0 %collective-permute-start.27 = (bf16[256,1024]{1,0:T(8,128)(2,1)S(1)}, bf16[256,1024]{1,0:T(8,128)(2,1)S(1)}, u32[]{:S(2)}, u32[]{:S(2)}) collective-permute-start(bf16[256,1024]{1,0:T(8,128)(2,1)S(1)} %get-tuple-element.120), channel_id=1, source_target_pairs={{0,1},{1,0},{2,3},{3,2},{4,5},{5,4},{6,7},{7,6},{8,9},{9,8},{10,11... | collective-permute-start | bytes 1572872 | tf_op jit(solution)/shard_map/ppermute | solution.py:801

commit v15 on v14

--- a/solution.py
+++ b/solution.py
@@ -311,46 +311,43 @@
     )[0]
 
 
-def state_kernel(places, xa, xb, w_ref, acc_ref, end_ref, half_ref, state_ref, *refs):
-    k_ref, v_ref, out_ref, sent_ref, held = refs
+def state_kernel(own, places, xa, xb, w_ref, acc_ref, end_ref, half_ref, state_ref, k_ref, v_ref, out_ref, held):
     tall = xa.shape[0]
-    heads, size = state_ref.shape[0], state_ref.shape[1]
+    share, size = out_ref.shape[0], out_ref.shape[1]
     held[:tall, :] = xa[...]
     held[tall:, :] = xb[...]
-    for pair in range(heads // 2):
-        cols = slice(2 * pair * size, 2 * (pair + 1) * size)
+    base = share * (places[4] if own else 1 - places[4])
+    for pair in range(0, share, 2):
+        cols = pl.ds(pl.multiple_of((base + pair) * size, 2 * size), 2 * size)
         keys = (acc_ref[1, :, cols] + dot(held[...], w_ref[1, :, cols])).astype(BF16)
         values = (acc_ref[2, :, cols] + dot(held[...], w_ref[2, :, cols])).astype(BF16)
-        k_ref[:, cols] = keys
-        v_ref[:, cols] = values
+        k_ref[:, pair * size : (pair + 2) * size] = keys
+        v_ref[:, pair * size : (pair + 2) * size] = values
         for a in range(2):
-            head = 2 * pair + a
+            head = pl.ds(base + pair + a, 1)
             lanes = slice(a * size, (a + 1) * size)
-            scaled = (keys[:, lanes].T.astype(F32) * end_ref[head : head + 1, tall * 2 :]).astype(BF16)
-            end = half_ref[head : head + 1, :] * state_ref[head] + dot(scaled, values[:, lanes])
-            out_ref[head] = end
-
-            @pl.when(places[4] != 2 * head // heads)
-            def _(head=head, end=end):
-                sent_ref[head % (heads // 2)] = end.astype(BF16)
-
-
-def state_call(places, far, w_far, acc, to_end, half_fade, state):
+            scaled = (keys[:, lanes].T.astype(F32) * end_ref[head, 2 * tall :]).astype(BF16)
+            end = half_ref[head, :] * state_ref[base + pair + a] + dot(scaled, values[:, lanes])
+            out_ref[pair + a] = end.astype(out_ref.dtype)
+
+
+def state_call(places, far, w_far, acc, to_end, half_fade, state, own):
     _, rows, width = acc.shape
     heads, size = state.shape[0], state.shape[1]
-    depth = far[0].shape[1]
     ins = [near(x) for x in (*far, w_far, acc)] + [to_end, half_fade, near(state)]
     outs = (
-        struct((rows, width), BF16),
-        struct((rows, width), BF16),
-        struct(state.shape, F32),
-        struct((heads // 2, size, size), BF16),
-    )
-    scratch = [pltpu.VMEM((rows, depth), BF16)]
-    return small_call(state_kernel, "states", places, ins, outs, 16, scratch)
-
-
-def later_kernel(half, chunk, _, xa, xb, w_ref, acc_ref, k_ref, v_ref, *refs):
+        struct((rows, width // 2), BF16),
+        struct((rows, width // 2), BF16),
+        struct((heads // 2, size, size), F32 if own else BF16),
+    )
+    scratch = [pltpu.VMEM((rows, far[0].shape[1]), BF16)]
+    kernel = functools.partial(state_kernel, own)
+    return small_call(kernel, "states", places, ins, outs, 16, scratch)
+
+
+def later_kernel(half, chunk, places, xa, xb, w_ref, acc_ref, *refs):
+    k_ref, v_ref, k_own_ref, v_own_ref, refs = *refs[:4], refs[4:]
+    own = places[4] == half
     along_ref, inside_ref, down_ref, state_ref, q_ref, within_ref, held = refs
     tall, rows = xa.shape[0], held.shape[0]
     heads, size = state_ref.shape[0], state_ref.shape[1]
@@ -358,7 +355,7 @@
     held[tall:, :] = xb[...]
     for a in range(heads // 2):
         head = half * heads // 2 + a
-        lanes, out = slice(head * size, (head + 1) * size), slice(a * size, (a + 1) * size)
+        out = slice(a * size, (a + 1) * size)
         if a % 2 == 0:
             pair = slice(head * size, (head + 2) * size)
             queries = (acc_ref[0, :, pair] + dot(held[...], w_ref[0, :, pair])).astype(BF16)
@@ -366,7 +363,8 @@
         for c in range(rows // chunk):
             here, there = slice(c * chunk, (c + 1) * chunk), slice(rows + c * chunk, rows + (c + 1) * chunk)
             q = queries[here, (a % 2) * size : (a % 2 + 1) * size]
-            k, v = k_ref[here, lanes], v_ref[here, lanes]
+            k = jnp.where(own, k_own_ref[here, out], k_ref[here, out])
+            v = jnp.where(own, v_own_ref[here, out], v_ref[here, out])
             along, down = along_ref[head : head + 1, there], inside_ref[there, head : head + 1]
             q_ref[here, out] = faded(q, down_ref[there, head : head + 1])
             within_ref[here, out] = scores(q, k, v, along, down, state).astype(BF16)
@@ -374,9 +372,9 @@
                 state = advance(k, v, down, state)
 
 
-def later_call(places, far, w_far, acc, k, v, along, inside, down, state, chunk, half):
+def later_call(places, far, w_far, acc, keys_values, along, inside, down, state, chunk, half):
     _, rows, width = acc.shape
-    ins = [near(x) for x in (*far, w_far, acc, k, v)] + [along, inside, down, near(state)]
+    ins = [near(x) for x in (*far, w_far, acc, *keys_values)] + [along, inside, down, near(state)]
     outs = (struct((rows, width // 2), BF16),) * 2
     scratch = [pltpu.VMEM((rows, far[0].shape[1]), BF16)]
     kernel = functools.partial(later_kernel, half, chunk)
@@ -396,7 +394,7 @@
     for i in range(share):
         head = core * share + i
         _, second_fade, fade = fades(tail_ref, other_ref, core, head)
-        ours, come = state_ref[head], come_ref[i].astype(F32)
+        ours, come = state_ref[i], come_ref[i].astype(F32)
         first, second = jnp.where(core == 0, ours, come), jnp.where(core == 0, come, ours)
         total = second_fade * first + second
         first_ref[i] = first
@@ -709,7 +707,11 @@
         )
         far = (fy2, fx3)
         middle = state
-        k, v, state, sent = state_call(places, far, w_far, acc_b, to_end, half_fade, middle)
+        k, v, sent = state_call(places, far, w_far, acc_b, to_end, half_fade, middle, False)
+        k_own, v_own, state = state_call(
+            places, far, w_far, acc_b, to_end, half_fade, after(middle, sent), True
+        )
+        keys_values = (k, v, k_own, v_own)
     else:
         tail_other, tail_chip, tail_below = chip_tails(tail)
         gathered = lax.all_gather(tokens, "head", axis=1, tiled=True)
@@ -721,11 +723,13 @@
 
     def scores_of_later(half, *earlier):
         start = after(middle, *earlier)
-        return later_call(places, far, w_far, acc_b, k, v, along, inside, down, start, quarter, half)
+        return later_call(
+            places, far, w_far, acc_b, keys_values, along, inside, down, start, quarter, half
+        )
 
     if square and n_chips == 4:
         leaving, alone, chip_state, first = chip_call(
-            places, state, near(swap(sent)), tails, prior_state
+            places, near(state), near(swap(sent)), tails, prior_state
         )
         alone = hop(alone, (2, 3))
         arriving = near(hop(leaving, (0, 1)))
@@ -753,8 +757,8 @@
         def decay(tail):
             return jnp.exp(-mine(tail)[:, :1, None])
 
-        ours = mine(state)
-        other = swap(mine(state, 1 - core).astype(BF16)).astype(F32)
+        ours = state if square else mine(state)
+        other = swap(sent if square else mine(state, 1 - core).astype(BF16)).astype(F32)
         first = jnp.where(core == 0, ours, other)
         second = jnp.where(core == 0, other, ours)
         chip_state = decay(jnp.where(core == 0, tail_other, tail)) * first + second

time: 177 us -> 175 us (0.989)
    pallas_call x8 -> x9, Pallas kernels: 21.9 us -> 21.3 us  [small_call(): pl.pallas_call(kernel, out_shape=tuple(outs), in_specs=[pl.BlockSpec(memo...]
  transfers between devices with their start and end apart: 28 -> 28, of which waited for: 15 -> 14; matrix products, arithmetic and copies ran while one was open for 0% -> 0% of each run, Pallas kernels for 41% -> 42%
where the time goes in v15:
time: 175 us; the launch traced here: 174 us
  Pallas kernels  84.6 us (48%)
  waiting for transfers between devices  63.1 us (36%)
  starting transfers between devices  25.4 us (15%)
    pallas_call x12, Pallas kernels, call(): pl.pallas_call(kernel, out_shape=tuple(outs), grid_spec=pltpu.PrefetchSca...  63.3 us
    pallas_call x9, Pallas kernels, small_call(): pl.pallas_call(kernel, out_shape=tuple(outs), in_specs=[pl.BlockSpec(memo...  21.3 us
    ppermute x2, waiting for transfers between devices, local(): by_x, by_y = (over_x(by_x), over_y(by_y))  19.3 us
    ppermute x2, waiting for transfers between devices, local(): by_x2, by_y2 = (over_x(by_x2), over_y(by_y2))  18 us
    ppermute x5, waiting for transfers between devices, hop(): return lax.ppermute(x, 'seq', perm=perm)  6.75 us
    ppermute x5, starting transfers between devices, hop(): return lax.ppermute(x, 'seq', perm=perm)  5.39 us
    ppermute x2, waiting for transfers between devices, local(): sum3, sum2 = (over_x(sum3), over_y(sum2))  5.17 us
    ppermute x2, waiting for transfers between devices, local(): far0, far1 = (over_x(far0), over_y(far1))  4.23 us
  transfers between devices with their start and end apart: 28, of which 14 were waited for; matrix products, arithmetic and copies ran while one was open for 0% of the time, Pallas kernels for 42%

profile of v15, /device:TPU:8, one launch (start us, length us, event | category | flops | bytes accessed | tf_op | source)
XLA Modules:
  0.0 174.3 jit_solution(15143983681837494461)
XLA Ops:
  0.0 2.2 %cut.2 = (bf16[256,1024]{1,0:T(8,128)(2,1)}, bf16[256,1024]{1,0:T(8,128)(2,1)}) custom-call(s32[1]{0:T(128)} %constant.29.clone.1._, bf16[1024,1024]{1,0:T(8,128)(2,1)} %x_ref.4), custom_call_target="tpu_custom_call" | custom-call | flops 1 | bytes 3145728 | tf_op jit(solution)/shard_map/cut/pallas_call | solution.py:43
  3.7 1.5 collective-permute-start.1
  8.2 12.5 %own_part.1.refs_6_ = f32[3,1024,1024]{2,1,0:T(8,128)} custom-call(s32[6]{0:T(128)S(1)} %stack.27._.places, bf16[1024,1024]{1,0:T(8,128)(2,1)} %x_ref.4, bf16[3,4096,1024]{2,1,0:T(8,128)(2,1)} %refs_5_.3), custom_call_target="tpu_custom_call" | custom-call | flops 6442450944 | bytes 39845888 | tf_op jit(solution)/shard_map/own_part/pallas_call | solution.py:43
  22.1 1.6 collective-permute-start.6
  25.8 2.4 %collective-permute-done.2.refs_1_ = bf16[256,1024]{1,0:T(8,128)(2,1)S(1)} collective-permute-done((bf16[256,1024]{1,0:T(8,128)(2,1)}, bf16[256,1024]{1,0:T(8,128)(2,1)S(1)}, u32[]{:S(2)}, u32[]{:S(2)}) %collective-permute-start.2) | collective-permute-done | bytes 524320 | tf_op jit(solution)/shard_map/ppermute | solution.py:665
  28.2 1.9 %collective-permute-done.3.refs_2_ = bf16[256,1024]{1,0:T(8,128)(2,1)S(1)} collective-permute-done((bf16[256,1024]{1,0:T(8,128)(2,1)}, bf16[256,1024]{1,0:T(8,128)(2,1)S(1)}, u32[]{:S(2)}, u32[]{:S(2)}) %collective-permute-start.3) | collective-permute-done | bytes 524320 | tf_op jit(solution)/shard_map/ppermute | solution.py:665
  30.0 1.5 collective-permute-start.9
  32.1 11.5 %part.2.refs_3_ = f32[3,512,1024]{2,1,0:T(8,128)S(1)} custom-call(s32[6]{0:T(128)S(1)} %stack.27._.places, bf16[256,1024]{1,0:T(8,128)(2,1)S(1)} %collective-permute-done.refs_0_, bf16[256,1024]{1,0:T(8,128)(2,1)S(1)} %collective-permute-done.2.refs_1_, bf16[256,1024]{1,0:T(8,128)(2,1)S(1)} %collective-permute-done.3.refs_2_, ...), custom_call_target="tpu_custom_call" | custom-call | flops 6442450944 | bytes 71303168 | tf_op jit(solution)/shard_map/part/pallas_call | solution.py:43
  43.6 1.6 collective-permute-start.12
  45.6 11.9 %first.1 = (bf16[512,1024]{1,0:T(8,128)(2,1)S(1)}, bf16[512,1024]{1,0:T(8,128)(2,1)S(1)}, f32[8,128,128]{2,1,0:T(8,128)S(1)}, bf16[3,1024,1024]{2,1,0:T(8,128)(2,1)S(1)}) custom-call(s32[6]{0:T(128)S(1)} %stack.27._.places, bf16[256,1024]{1,0:T(8,128)(2,1)S(1)} %collective-permute-done.6.refs_0_, bf16[256,1024]{1,0:T(8,128)(2,1)S(1)} %collective-permute-done.7.refs_1_, ...), custom_call_target="tpu_custom_call" | custom-call | flops 3221225472 | bytes 41484288 | tf_op jit(solution)/shard_map/first/pallas_call | solution.py:43
  57.6 1.6 collective-permute-start.8
  59.7 2.1 %collective-permute-done.12.refs_1_ = bf16[256,1024]{1,0:T(8,128)(2,1)S(1)} collective-permute-done((bf16[256,1024]{1,0:T(8,128)(2,1)S(1)}, bf16[256,1024]{1,0:T(8,128)(2,1)S(1)}, u32[]{:S(2)}, u32[]{:S(2)}) %collective-permute-start.12) | collective-permute-done | bytes 524320 | tf_op jit(solution)/shard_map/ppermute | solution.py:683
  61.9 1.9 %collective-permute-done.13.refs_2_ = bf16[256,1024]{1,0:T(8,128)(2,1)S(1)} collective-permute-done((bf16[256,1024]{1,0:T(8,128)(2,1)S(1)}, bf16[256,1024]{1,0:T(8,128)(2,1)S(1)}, u32[]{:S(2)}, u32[]{:S(2)}) %collective-permute-start.13) | collective-permute-done | bytes 524320 | tf_op jit(solution)/shard_map/ppermute | solution.py:683
  63.7 11.5 %part.3.acc_ref = f32[3,512,1024]{2,1,0:T(8,128)S(1)} custom-call(s32[6]{0:T(128)S(1)} %stack.27._.places, bf16[256,1024]{1,0:T(8,128)(2,1)S(1)} %collective-permute-done.5.refs_0_, bf16[256,1024]{1,0:T(8,128)(2,1)S(1)} %collective-permute-done.12.refs_1_, bf16[256,1024]{1,0:T(8,128)(2,1)S(1)} %collective-permute-done.13.refs_2_, ...), custom_call_target="tpu_custom_call" | custom-call | flops 6442450944 | bytes 71303168 | tf_op jit(solution)/shard_map/part/pallas_call | solution.py:43
  75.2 2.3 %states.2 = (bf16[512,512]{1,0:T(8,128)(2,1)S(1)}, bf16[512,512]{1,0:T(8,128)(2,1)S(1)}, bf16[4,128,128]{2,1,0:T(8,128)(2,1)S(1)}) custom-call(s32[6]{0:T(128)S(1)} %stack.27._.places, bf16[256,1024]{1,0:T(8,128)(2,1)S(1)} %collective-permute-done.8.xa, bf16[256,1024]{1,0:T(8,128)(2,1)S(1)} %collective-permute-done.10.xb, ...), custom_call_target="tpu_custom_call" | custom-call | flops 1 | bytes 1 | tf_op jit(solution)/shard_map/states/pallas_call | solution.py:433
  77.6 2.3 %states.3 = (bf16[512,512]{1,0:T(8,128)(2,1)S(1)}, bf16[512,512]{1,0:T(8,128)(2,1)S(1)}, f32[4,128,128]{2,1,0:T(8,128)S(1)}) custom-call(s32[6]{0:T(128)S(1)} %stack.27._.places, bf16[256,1024]{1,0:T(8,128)(2,1)S(1)} %collective-permute-done.8.xa, bf16[256,1024]{1,0:T(8,128)(2,1)S(1)} %collective-permute-done.10.xb, ...), custom_call_target="tpu_custom_call" | custom-call | flops 1 | bytes 1 | tf_op jit(solution)/shard_map/states/pallas_call | solution.py:433
  82.5 5.8 %collective-permute-done.15.come_ref = bf16[4,128,128]{2,1,0:T(8,128)(2,1)S(1)} collective-permute-done((bf16[4,128,128]{2,1,0:T(8,128)(2,1)S(1)}, bf16[4,128,128]{2,1,0:T(8,128)(2,1)S(1)}, u32[]{:S(2)}, u32[]{:S(2)}) %collective-permute-start.15) | collective-permute-done | bytes 131104 | tf_op jit(solution)/shard_map/ppermute | solution.py:655
  91.8 3.3 %later.2 = (bf16[512,512]{1,0:T(8,128)(2,1)S(1)}, bf16[512,512]{1,0:T(8,128)(2,1)S(1)}) custom-call(s32[6]{0:T(128)S(1)} %stack.27._.places, bf16[256,1024]{1,0:T(8,128)(2,1)S(1)} %collective-permute-done.8.xa, bf16[256,1024]{1,0:T(8,128)(2,1)S(1)} %collective-permute-done.10.xb, bf16[3,1024,1024]{2,1,0:T(8,128)(2,1)S(1)} %get-tuple-element.83.w_ref, ...), custom_call_target="tpu_custom_call" | custom-call | flops 1 | bytes 1 | tf_op jit(solution)/shard_map/later/pallas_call | solution.py:433
  98.1 3.7 %heads.2 = (bf16[512,1024]{1,0:T(8,128)(2,1)S(1)}, bf16[256,1024]{1,0:T(8,128)(2,1)S(1)}, bf16[256,1024]{1,0:T(8,128)(2,1)S(1)}) custom-call(s32[6]{0:T(128)S(1)} %stack.27._.places, bf16[512,1024]{1,0:T(8,128)(2,1)S(1)} %get-tuple-element.100.refs_0_, bf16[512,1024]{1,0:T(8,128)(2,1)S(1)} %get-tuple-element.101.refs_1_, ...), custom_call_target="tpu_custom_call" | custom-call | flops 1 | bytes 1 | tf_op jit(solution)/shard_map/heads/pallas_call | solution.py:433
  101.7 1.6 collective-permute-start.20
  103.9 3.3 %later.3 = (bf16[512,512]{1,0:T(8,128)(2,1)S(1)}, bf16[512,512]{1,0:T(8,128)(2,1)S(1)}) custom-call(s32[6]{0:T(128)S(1)} %stack.27._.places, bf16[256,1024]{1,0:T(8,128)(2,1)S(1)} %collective-permute-done.8.xa, bf16[256,1024]{1,0:T(8,128)(2,1)S(1)} %collective-permute-done.10.xb, bf16[3,1024,1024]{2,1,0:T(8,128)(2,1)S(1)} %get-tuple-element.83.w_ref, ...), custom_call_target="tpu_custom_call" | custom-call | flops 1 | bytes 1 | tf_op jit(solution)/shard_map/later/pallas_call | solution.py:433
  107.1 4.7 %heads.3 = (bf16[512,1024]{1,0:T(8,128)(2,1)S(1)}, bf16[512,1024]{1,0:T(8,128)(2,1)S(1)}, bf16[512,1024]{1,0:T(8,128)(2,1)S(1)}) custom-call(s32[6]{0:T(128)S(1)} %stack.27._.places, bf16[512,512]{1,0:T(8,128)(2,1)S(1)} %get-tuple-element.99.refs_0_, bf16[512,512]{1,0:T(8,128)(2,1)S(1)} %get-tuple-element.111.refs_1_, ...), custom_call_target="tpu_custom_call" | custom-call | flops 1 | bytes 1 | tf_op jit(solution)/shard_map/heads/pallas_call | solution.py:433
  111.8 1.6 collective-permute-start.24
  113.9 2.3 %collective-permute-done.20.x_ref = bf16[256,1024]{1,0:T(8,128)(2,1)S(1)} collective-permute-done((bf16[256,1024]{1,0:T(8,128)(2,1)S(1)}, bf16[256,1024]{1,0:T(8,128)(2,1)S(1)}, u32[]{:S(2)}, u32[]{:S(2)}) %collective-permute-start.20) | collective-permute-done | bytes 524320 | tf_op jit(solution)/shard_map/ppermute | solution.py:796
  116.2 1.9 %collective-permute-done.21.y_ref = bf16[256,1024]{1,0:T(8,128)(2,1)S(1)} collective-permute-done((bf16[256,1024]{1,0:T(8,128)(2,1)S(1)}, bf16[256,1024]{1,0:T(8,128)(2,1)S(1)}, u32[]{:S(2)}, u32[]{:S(2)}) %collective-permute-start.21) | collective-permute-done | bytes 524320 | tf_op jit(solution)/shard_map/ppermute | solution.py:796
  118.1 3.3 %sum_and_near.1 = (bf16[512,1024]{1,0:T(8,128)(2,1)S(1)}, bf16[512,1024]{1,0:T(8,128)(2,1)S(1)}) custom-call(s32[6]{0:T(128)S(1)} %stack.27._.places, bf16[512,1024]{1,0:T(8,128)(2,1)S(1)} %get-tuple-element.115.normed_ref, bf16[256,1024]{1,0:T(8,128)(2,1)S(1)} %collective-permute-done.20.x_ref, bf16[256,1024]{1,0:T(8,128)(2,1)S(1)} %collective-permute-done.21.y_ref, ...), custom_call_target="tpu_custom_call" | custom-call | flops 1 | bytes 1 | tf_op jit(solution)/shard_map/sum_and_near/pallas_call | solution.py:43
  122.6 18.0 %collective-permute-done.24.refs_0_.y_ref = bf16[512,1024]{1,0:T(8,128)(2,1)S(1)} collective-permute-done((bf16[512,1024]{1,0:T(8,128)(2,1)S(1)}, bf16[512,1024]{1,0:T(8,128)(2,1)S(1)}, u32[]{:S(2)}, u32[]{:S(2)}) %collective-permute-start.24) | collective-permute-done | bytes 1048608 | tf_op jit(solution)/shard_map/ppermute | solution.py:800
  140.6 2.0 %sum_pair.1 = (bf16[256,1024]{1,0:T(8,128)(2,1)S(1)}, bf16[256,1024]{1,0:T(8,128)(2,1)S(1)}) custom-call(s32[6]{0:T(128)S(1)} %stack.27._.places, bf16[512,1024]{1,0:T(8,128)(2,1)S(1)} %get-tuple-element.120.normed_ref, bf16[512,1024]{1,0:T(8,128)(2,1)S(1)} %collective-permute-done.25.refs_1_.x_ref, ...), custom_call_target="tpu_custom_call" | custom-call | flops 1 | bytes 1 | tf_op jit(solution)/shard_map/sum_pair/pallas_call | solution.py:43
  143.7 18.2 %collective-permute-done.23.refs_1_.refs_2_ = bf16[512,1024]{1,0:T(8,128)(2,1)S(1)} collective-permute-done((bf16[512,1024]{1,0:T(8,128)(2,1)S(1)}, bf16[512,1024]{1,0:T(8,128)(2,1)S(1)}, u32[]{:S(2)}, u32[]{:S(2)}) %collective-permute-start.23) | collective-permute-done | bytes 1048608 | tf_op jit(solution)/shard_map/ppermute | solution.py:803
  163.1 2.0 %own_block.2.kept_ref = bf16[512,1024]{1,0:T(8,128)(2,1)S(1)} custom-call(s32[6]{0:T(128)S(1)} %stack.27._.places, bf16[512,1024]{1,0:T(8,128)(2,1)S(1)} %get-tuple-element.120.normed_ref, bf16[1024,4096]{1,0:T(8,128)(2,1)S(1)} %bitcast.7, bf16[512,1024]{1,0:T(8,128)(2,1)S(1)} %collective-permute-done.24.refs_0_.y_ref, ...), custom_call_target="tpu_custom_call" | custom-call | flops 1 | bytes 1 | tf_op jit(solution)/shard_map/own_block/pallas_call | solution.py:43
  165.1 2.9 %own_block.3.above_ref = bf16[1024,1024]{1,0:T(8,128)(2,1)} custom-call(s32[6]{0:T(128)S(1)} %stack.27._.places, bf16[512,1024]{1,0:T(8,128)(2,1)S(1)} %get-tuple-element.115.normed_ref, bf16[1024,4096]{1,0:T(8,128)(2,1)S(1)} %bitcast.7, bf16[512,1024]{1,0:T(8,128)(2,1)S(1)} %collective-permute-done.22.refs_0_.refs_3_, ...), custom_call_target="tpu_custom_call" | custom-call | flops 1 | bytes 1 | tf_op jit(solution)/shard_map/own_block/pallas_call | solution.py:43
  168.0 3.9 %collective-permute-done.26.a_ref = bf16[256,1024]{1,0:T(8,128)(2,1)S(1)} collective-permute-done((bf16[256,1024]{1,0:T(8,128)(2,1)S(1)}, bf16[256,1024]{1,0:T(8,128)(2,1)S(1)}, u32[]{:S(2)}, u32[]{:S(2)}) %collective-permute-start.26) | collective-permute-done | bytes 524320 | tf_op jit(solution)/shard_map/ppermute | solution.py:805
  (56 shorter events, 25.3 us)
Async XLA Ops:
  2.2 18.4 %collective-permute-start = (bf16[256,1024]{1,0:T(8,128)(2,1)}, bf16[256,1024]{1,0:T(8,128)(2,1)S(1)}, u32[]{:S(2)}, u32[]{:S(2)}) collective-permute-start(bf16[256,1024]{1,0:T(8,128)(2,1)} %get-tuple-element.72), channel_id=1, source_target_pairs={{0,1},{1,0},{2,3},{3,2},{4,5},{5,4},{6,7},{7,6},{8,9},{9,8},{10,11... | collective-permute-start | bytes 1572872 | tf_op jit(solution)/shard_map/ppermute | solution.py:664
  3.7 17.0 %collective-permute-start.1 = (bf16[256,1024]{1,0:T(8,128)(2,1)}, bf16[256,1024]{1,0:T(8,128)(2,1)S(1)}, u32[]{:S(2)}, u32[]{:S(2)}) collective-permute-start(bf16[256,1024]{1,0:T(8,128)(2,1)} %get-tuple-element.71), channel_id=1, source_target_pairs={{0,2},{1,3},{2,0},{3,1},{4,6},{5,7},{6,4},{7,5},{8,10},{9,11},{10,... | collective-permute-start | bytes 1572872 | tf_op jit(solution)/shard_map/ppermute | solution.py:664
  5.2 0.8 copy-start.1
  7.0 21.2 %collective-permute-start.2 = (bf16[256,1024]{1,0:T(8,128)(2,1)}, bf16[256,1024]{1,0:T(8,128)(2,1)S(1)}, u32[]{:S(2)}, u32[]{:S(2)}) collective-permute-start(bf16[256,1024]{1,0:T(8,128)(2,1)} %get-tuple-element.71), channel_id=1, source_target_pairs={{0,1},{1,0},{2,3},{3,2},{4,5},{5,4},{6,7},{7,6},{8,9},{9,8},{10,11... | collective-permute-start | bytes 1572872 | tf_op jit(solution)/shard_map/ppermute | solution.py:665
  7.6 22.4 %collective-permute-start.3 = (bf16[256,1024]{1,0:T(8,128)(2,1)}, bf16[256,1024]{1,0:T(8,128)(2,1)S(1)}, u32[]{:S(2)}, u32[]{:S(2)}) collective-permute-start(bf16[256,1024]{1,0:T(8,128)(2,1)} %get-tuple-element.72), channel_id=1, source_target_pairs={{0,2},{1,3},{2,0},{3,1},{4,6},{5,7},{6,4},{7,5},{8,10},{9,11},{10,... | collective-permute-start | bytes 1572872 | tf_op jit(solution)/shard_map/ppermute | solution.py:665
  20.7 4.5 %collective-permute-start.4 = (f32[8,128]{1,0:T(8,128)S(1)}, f32[8,128]{1,0:T(8,128)S(1)}, u32[]{:S(2)}, u32[]{:S(2)}) collective-permute-start(f32[8,128]{1,0:T(8,128)S(1)} %get-tuple-element.73.tail_ref), channel_id=1, source_target_pairs={{0,4},{4,0},{8,12},{12,8},{16,20},{20,16},{24,28},{28,24},{1,5},{5... | collective-permute-start | bytes 12296 | tf_op jit(solution)/shard_map/ppermute | solution.py:658
  22.1 21.5 %collective-permute-start.6 = (bf16[256,1024]{1,0:T(8,128)(2,1)S(1)}, bf16[256,1024]{1,0:T(8,128)(2,1)S(1)}, u32[]{:S(2)}, u32[]{:S(2)}) collective-permute-start(bf16[256,1024]{1,0:T(8,128)(2,1)S(1)} %collective-permute-done.refs_0_), channel_id=1, source_target_pairs={{0,2},{1,3},{2,0},{3,1},{4,6},{5,7},{6,4},{7,5},{8,10},{9,11},{10,... | collective-permute-start | bytes 1572872 | tf_op jit(solution)/shard_map/ppermute | solution.py:668
  23.7 19.9 %collective-permute-start.7 = (bf16[256,1024]{1,0:T(8,128)(2,1)S(1)}, bf16[256,1024]{1,0:T(8,128)(2,1)S(1)}, u32[]{:S(2)}, u32[]{:S(2)}) collective-permute-start(bf16[256,1024]{1,0:T(8,128)(2,1)S(1)} %collective-permute-done.1.refs_3_), channel_id=1, source_target_pairs={{0,1},{1,0},{2,3},{3,2},{4,5},{5,4},{6,7},{7,6},{8,9},{9,8},{10,11... | collective-permute-start | bytes 1572872 | tf_op jit(solution)/shard_map/ppermute | solution.py:668
  25.1 18.4 %collective-permute-start.11 = (f32[8,128]{1,0:T(8,128)S(1)}, f32[8,128]{1,0:T(8,128)S(1)}, u32[]{:S(2)}, u32[]{:S(2)}) collective-permute-start(f32[8,128]{1,0:T(8,128)S(1)} %add.10), channel_id=1, source_target_pairs={{16,24},{20,28},{17,25},{21,29},{18,26},{22,30},{19,27},{23,31}} | collective-permute-start | bytes 12296 | tf_op jit(solution)/shard_map/ppermute | solution.py:655
  30.0 27.6 %collective-permute-start.9 = (bf16[256,1024]{1,0:T(8,128)(2,1)S(1)}, bf16[256,1024]{1,0:T(8,128)(2,1)S(1)}, u32[]{:S(2)}, u32[]{:S(2)}) collective-permute-start(bf16[256,1024]{1,0:T(8,128)(2,1)S(1)} %get-tuple-element.84), channel_id=1, source_target_pairs={{0,2},{1,3},{2,0},{3,1},{4,6},{5,7},{6,4},{7,5},{8,10},{9,11},{10,... | collective-permute-start | bytes 1572872 | tf_op jit(solution)/shard_map/ppermute | solution.py:671
  31.5 26.1 %collective-permute-start.5 = (bf16[256,1024]{1,0:T(8,128)(2,1)S(1)}, bf16[256,1024]{1,0:T(8,128)(2,1)S(1)}, u32[]{:S(2)}, u32[]{:S(2)}) collective-permute-start(bf16[256,1024]{1,0:T(8,128)(2,1)S(1)} %get-tuple-element.85), channel_id=1, source_target_pairs={{0,1},{1,0},{2,3},{3,2},{4,5},{5,4},{6,7},{7,6},{8,9},{9,8},{10,11... | collective-permute-start | bytes 1572872 | tf_op jit(solution)/shard_map/ppermute | solution.py:670
  43.6 18.3 %collective-permute-start.12 = (bf16[256,1024]{1,0:T(8,128)(2,1)S(1)}, bf16[256,1024]{1,0:T(8,128)(2,1)S(1)}, u32[]{:S(2)}, u32[]{:S(2)}) collective-permute-start(bf16[256,1024]{1,0:T(8,128)(2,1)S(1)} %get-tuple-element.84), channel_id=1, source_target_pairs={{0,1},{1,0},{2,3},{3,2},{4,5},{5,4},{6,7},{7,6},{8,9},{9,8},{10,11... | collective-permute-start | bytes 1572872 | tf_op jit(solution)/shard_map/ppermute | solution.py:683
  45.1 18.6 %collective-permute-start.13 = (bf16[256,1024]{1,0:T(8,128)(2,1)S(1)}, bf16[256,1024]{1,0:T(8,128)(2,1)S(1)}, u32[]{:S(2)}, u32[]{:S(2)}) collective-permute-start(bf16[256,1024]{1,0:T(8,128)(2,1)S(1)} %get-tuple-element.85), channel_id=1, source_target_pairs={{0,2},{1,3},{2,0},{3,1},{4,6},{5,7},{6,4},{7,5},{8,10},{9,11},{10,... | collective-permute-start | bytes 1572872 | tf_op jit(solution)/shard_map/ppermute | solution.py:683
  57.6 17.6 %collective-permute-start.8 = (bf16[256,1024]{1,0:T(8,128)(2,1)S(1)}, bf16[256,1024]{1,0:T(8,128)(2,1)S(1)}, u32[]{:S(2)}, u32[]{:S(2)}) collective-permute-start(bf16[256,1024]{1,0:T(8,128)(2,1)S(1)} %collective-permute-done.5.refs_0_), channel_id=1, source_target_pairs={{0,2},{1,3},{2,0},{3,1},{4,6},{5,7},{6,4},{7,5},{8,10},{9,11},{10,... | collective-permute-start | bytes 1572872 | tf_op jit(solution)/shard_map/ppermute | solution.py:697
  59.2 16.0 %collective-permute-start.10 = (bf16[256,1024]{1,0:T(8,128)(2,1)S(1)}, bf16[256,1024]{1,0:T(8,128)(2,1)S(1)}, u32[]{:S(2)}, u32[]{:S(2)}) collective-permute-start(bf16[256,1024]{1,0:T(8,128)(2,1)S(1)} %collective-permute-done.9.refs_3_), channel_id=1, source_target_pairs={{0,1},{1,0},{2,3},{3,2},{4,5},{5,4},{6,7},{7,6},{8,9},{9,8},{10,11... | collective-permute-start | bytes 1572872 | tf_op jit(solution)/shard_map/ppermute | solution.py:697
  77.5 2.4 %copy-start = (f32[8,128,128]{2,1,0:T(8,128)S(1)}, f32[8,128,128]{2,1,0:T(8,128)}, u32[]{:S(2)}) copy-start(f32[8,128,128]{2,1,0:T(8,128)} %prior_ref.3) | copy-start | bytes 1572868
  77.5 2.4 %collective-permute-start.14 = (bf16[4,128,128]{2,1,0:T(8,128)(2,1)S(1)}, bf16[4,128,128]{2,1,0:T(8,128)(2,1)S(1)}, u32[]{:S(2)}, u32[]{:S(2)}) collective-permute-start(bf16[4,128,128]{2,1,0:T(8,128)(2,1)S(1)} %get-tuple-element.90), channel_id=1, source_target_pairs={{0,4},{4,0},{8,12},{12,8},{16,20},{20,16},{24,28},{28,24},{1,5},{5... | collective-permute-start | bytes 393224 | tf_op jit(solution)/shard_map/ppermute | solution.py:732
  80.6 7.8 %collective-permute-start.15 = (bf16[4,128,128]{2,1,0:T(8,128)(2,1)S(1)}, bf16[4,128,128]{2,1,0:T(8,128)(2,1)S(1)}, u32[]{:S(2)}, u32[]{:S(2)}) collective-permute-start(bf16[4,128,128]{2,1,0:T(8,128)(2,1)S(1)} %get-tuple-element.96), channel_id=1, source_target_pairs={{0,8},{4,12},{1,9},{5,13},{2,10},{6,14},{3,11},{7,15}} | collective-permute-start | bytes 393224 | tf_op jit(solution)/shard_map/ppermute | solution.py:655
  81.9 13.2 %collective-permute-start.16 = (bf16[4,128,128]{2,1,0:T(8,128)(2,1)S(1)}, bf16[4,128,128]{2,1,0:T(8,128)(2,1)S(1)}, u32[]{:S(2)}, u32[]{:S(2)}) collective-permute-start(bf16[4,128,128]{2,1,0:T(8,128)(2,1)S(1)} %get-tuple-element.102), channel_id=1, source_target_pairs={{16,24},{20,28},{17,25},{21,29},{18,26},{22,30},{19,27},{23,31}} | collective-permute-start | bytes 393224 | tf_op jit(solution)/shard_map/ppermute | solution.py:655
  89.0 6.1 %collective-permute-start.18 = (bf16[4,128,128]{2,1,0:T(8,128)(2,1)S(1)}, bf16[4,128,128]{2,1,0:T(8,128)(2,1)S(1)}, u32[]{:S(2)}, u32[]{:S(2)}) collective-permute-start(bf16[4,128,128]{2,1,0:T(8,128)(2,1)S(1)} %pass_on.1), channel_id=1, source_target_pairs={{8,16},{12,20},{9,17},{13,21},{10,18},{14,22},{11,19},{15,23}} | collective-permute-start | bytes 393224 | tf_op jit(solution)/shard_map/ppermute | solution.py:655
  90.3 5.7 %collective-permute-start.17 = (bf16[4,128,128]{2,1,0:T(8,128)(2,1)S(1)}, bf16[4,128,128]{2,1,0:T(8,128)(2,1)S(1)}, u32[]{:S(2)}, u32[]{:S(2)}) collective-permute-start(bf16[4,128,128]{2,1,0:T(8,128)(2,1)S(1)} %pass_on.1), channel_id=1, source_target_pairs={{8,24},{12,28},{9,25},{13,29},{10,26},{14,30},{11,27},{15,31}} | collective-permute-start | bytes 393224 | tf_op jit(solution)/shard_map/ppermute | solution.py:655
  91.8 6.3 %slice-start = ((s8[8388608]{0:T(1024)(128)(4,1)}), s8[4194304]{0:T(1024)(128)(4,1)S(1)}, s32[]{:S(2)}) async-start(s8[8388608]{0:T(1024)(128)(4,1)} %bitcast.6), calls=%async_computation | async-start | bytes 8388608
  91.8 6.3 %slice-start.1 = ((s8[8388608]{0:T(1024)(128)(4,1)}), s8[4194304]{0:T(1024)(128)(4,1)S(1)}, s32[]{:S(2)}) async-start(s8[8388608]{0:T(1024)(128)(4,1)} %bitcast.6), calls=%async_computation.1 | async-start | bytes 8388608
  96.7 1.4 collective-permute-start.19
  101.7 14.5 %collective-permute-start.20 = (bf16[256,1024]{1,0:T(8,128)(2,1)S(1)}, bf16[256,1024]{1,0:T(8,128)(2,1)S(1)}, u32[]{:S(2)}, u32[]{:S(2)}) collective-permute-start(bf16[256,1024]{1,0:T(8,128)(2,1)S(1)} %get-tuple-element.116), channel_id=1, source_target_pairs={{0,2},{1,3},{2,0},{3,1},{4,6},{5,7},{6,4},{7,5},{8,10},{9,11},{10,... | collective-permute-start | bytes 1572872 | tf_op jit(solution)/shard_map/ppermute | solution.py:796
  103.3 14.8 %collective-permute-start.21 = (bf16[256,1024]{1,0:T(8,128)(2,1)S(1)}, bf16[256,1024]{1,0:T(8,128)(2,1)S(1)}, u32[]{:S(2)}, u32[]{:S(2)}) collective-permute-start(bf16[256,1024]{1,0:T(8,128)(2,1)S(1)} %get-tuple-element.117), channel_id=1, source_target_pairs={{0,1},{1,0},{2,3},{3,2},{4,5},{5,4},{6,7},{7,6},{8,9},{9,8},{10,11... | collective-permute-start | bytes 1572872 | tf_op jit(solution)/shard_map/ppermute | solution.py:796
  111.8 28.8 %collective-permute-start.24 = (bf16[512,1024]{1,0:T(8,128)(2,1)S(1)}, bf16[512,1024]{1,0:T(8,128)(2,1)S(1)}, u32[]{:S(2)}, u32[]{:S(2)}) collective-permute-start(bf16[512,1024]{1,0:T(8,128)(2,1)S(1)} %get-tuple-element.121), channel_id=1, source_target_pairs={{0,1},{1,0},{2,3},{3,2},{4,5},{5,4},{6,7},{7,6},{8,9},{9,8},{10,11... | collective-permute-start | bytes 3145736 | tf_op jit(solution)/shard_map/ppermute | solution.py:800
  113.4 27.2 %collective-permute-start.25 = (bf16[512,1024]{1,0:T(8,128)(2,1)S(1)}, bf16[512,1024]{1,0:T(8,128)(2,1)S(1)}, u32[]{:S(2)}, u32[]{:S(2)}) collective-permute-start(bf16[512,1024]{1,0:T(8,128)(2,1)S(1)} %get-tuple-element.123), channel_id=1, source_target_pairs={{0,2},{1,3},{2,0},{3,1},{4,6},{5,7},{6,4},{7,5},{8,10},{9,11},{10,... | collective-permute-start | bytes 3145736 | tf_op jit(solution)/shard_map/ppermute | solution.py:800
  121.5 40.5 %collective-permute-start.23 = (bf16[512,1024]{1,0:T(8,128)(2,1)S(1)}, bf16[512,1024]{1,0:T(8,128)(2,1)S(1)}, u32[]{:S(2)}, u32[]{:S(2)}) collective-permute-start(bf16[512,1024]{1,0:T(8,128)(2,1)S(1)} %get-tuple-element.119), channel_id=1, source_target_pairs={{0,2},{1,3},{2,0},{3,1},{4,6},{5,7},{6,4},{7,5},{8,10},{9,11},{10,... | collective-permute-start | bytes 3145736 | tf_op jit(solution)/shard_map/ppermute | solution.py:803
  122.0 41.0 %collective-permute-start.22 = (bf16[512,1024]{1,0:T(8,128)(2,1)S(1)}, bf16[512,1024]{1,0:T(8,128)(2,1)S(1)}, u32[]{:S(2)}, u32[]{:S(2)}) collective-permute-start(bf16[512,1024]{1,0:T(8,128)(2,1)S(1)} %get-tuple-element.118), channel_id=1, source_target_pairs={{0,1},{1,0},{2,3},{3,2},{4,5},{5,4},{6,7},{7,6},{8,9},{9,8},{10,11... | collective-permute-start | bytes 3145736 | tf_op jit(solution)/shard_map/ppermute | solution.py:803
  142.6 29.3 %collective-permute-start.26 = (bf16[256,1024]{1,0:T(8,128)(2,1)S(1)}, bf16[256,1024]{1,0:T(8,128)(2,1)S(1)}, u32[]{:S(2)}, u32[]{:S(2)}) collective-permute-start(bf16[256,1024]{1,0:T(8,128)(2,1)S(1)} %get-tuple-element.125), channel_id=1, source_target_pairs={{0,2},{1,3},{2,0},{3,1},{4,6},{5,7},{6,4},{7,5},{8,10},{9,11},{10,... | collective-permute-start | bytes 1572872 | tf_op jit(solution)/shard_map/ppermute | solution.py:805
  143.2 30.0 %collective-permute-start.27 = (bf16[256,1024]{1,0:T(8,128)(2,1)S(1)}, bf16[256,1024]{1,0:T(8,128)(2,1)S(1)}, u32[]{:S(2)}, u32[]{:S(2)}) collective-permute-start(bf16[256,1024]{1,0:T(8,128)(2,1)S(1)} %get-tuple-element.126), channel_id=1, source_target_pairs={{0,1},{1,0},{2,3},{3,2},{4,5},{5,4},{6,7},{7,6},{8,9},{9,8},{10,11... | collective-permute-start | bytes 1572872 | tf_op jit(solution)/shard_map/ppermute | solution.py:805
